TPU v7x, 32 devices: a whole 2x2x4 slice. The times are simulated.
32 devices in a mesh: term: 16 (over z, y, core), wave: 2 (over x).
Axes of the slice: x: 2, y: 2, z: 4, core: 2. Of those that a mesh axis runs over, the one named last changes fastest.
Arguments:
- spectral_state: bfloat16 [8, 512, 1280], P('wave', 'term'), may hold values from -6 to 6
- inverse: bfloat16 [16, 8, 2, 640, 640], P('term', 'wave'), may hold values from -0.15625 to 0.15625
- term_weights: float32 [16, 2], P('term'), may hold values from -4 to 4
- legendre: bfloat16 [8, 640, 1280], P('wave'), may hold values from -0.25 to 0.25
- slot_column: int32 [8], replicated, may hold values from 0 to 7, each once
Outputs:
- fourier: float32 [8, 2, 512, 1280], P(None, None, 'term', 'wave')
Inputs may be any that keep to these rules, and one draw needn't show every extreme that they name: `slot_column`: each column appears in exactly one slot.
All inputs are finite; a program needn't handle non-finite values.
Results may differ from a plain program's by a relative error of at most 0.0003.
Values may be sent and summed in bfloat16 or wider, within the bound.
No kernel may reach another device: no remote copies, remote signals or barrier semaphores. Data moves between devices by JAX's collectives and lax.ppermute only.
A program may use at most 128 MiB of HBM per device.

v0:
```python
import jax
import jax.numpy as jnp
from jax import lax
from jax.sharding import PartitionSpec as P


def exact_product(values, table):
    return jnp.einsum(
        "spcn,snl->spcl", values, table.astype(jnp.float32), precision=lax.Precision.HIGHEST
    )


def shards(spectral_state, inverse, term_weights, legendre, slot_column):
    whole = lax.all_gather(spectral_state, "term", axis=1, tiled=True)
    middle = whole.shape[2] // 2
    column_count = whole.shape[1]
    stacked = jnp.concatenate([whole[:, :, :middle], whole[:, :, middle:]], axis=1)
    real_image = jnp.einsum(
        "srn,ksno->ksro", stacked, inverse[:, :, 0], preferred_element_type=jnp.float32
    )
    imag_image = jnp.einsum(
        "srn,ksno->ksro", stacked, inverse[:, :, 1], preferred_element_type=jnp.float32
    )
    solved_re = real_image[:, :, :column_count] - imag_image[:, :, column_count:]
    solved_im = imag_image[:, :, :column_count] + real_image[:, :, column_count:]
    weight_re = term_weights[:, 0][:, None, None, None]
    weight_im = term_weights[:, 1][:, None, None, None]
    total_re = jnp.sum(weight_re * solved_re - weight_im * solved_im, axis=0)
    total_im = jnp.sum(weight_re * solved_im + weight_im * solved_re, axis=0)
    partial_value = jnp.stack([total_re, total_im], axis=1)
    mine = lax.psum_scatter(partial_value, "term", scatter_dimension=2, tiled=True)
    grid = exact_product(mine, legendre)
    bands = lax.all_to_all(grid, "wave", split_axis=3, concat_axis=0, tiled=True)
    slot_count = slot_column.shape[0]
    selector = (slot_column[:, None] == jnp.arange(slot_count, dtype=jnp.int32)[None, :]).astype(
        jnp.float32
    )
    return jnp.einsum("spcl,sq->qpcl", bands, selector, precision=lax.Precision.HIGHEST)


def solution(mesh):
    return jax.shard_map(
        shards,
        mesh=mesh,
        in_specs=(
            P("wave", "term", None),
            P("term", "wave", None, None, None),
            P("term", None),
            P("wave", None, None),
            P(),
        ),
        out_specs=P(None, None, "term", "wave"),
        check_vma=False,
    )
```

profile of v0, /device:TPU:0, one launch (start us, length us, event | category | flops | bytes accessed | tf_op | source)
XLA Modules:
  0.0 284.2 jit_solution(9971825960220185334)
XLA Ops:
  6.5 0.0 all-gather.2.cloned.1.call-start
  6.5 0.7 all-gather.2.cloned.1.call-update
  7.3 0.0 reduce-scatter.2.cloned.1.call-start
  7.3 1.3 fusion.14
  8.6 59.8 %all-gather.2.cloned.1.call-done = bf16[4,512,1280]{2,1,0:T(8,128)(2,1)} async-done(((bf16[4,32,1280]{2,1,0:T(8,128)(2,1)}), bf16[4,512,1280]{2,1,0:T(8,128)(2,1)}) %all-gather.2.cloned.1.call-update) | async-done | bytes 5242896 | tf_op jit(solution)/shard_map/all_gather | solution.py:14
  68.4 0.0 copy-start.1
  68.4 3.1 %fusion.13 = (bf16[4,512,640]{2,1,0:T(8,128)(2,1)S(1)}, bf16[4,512,640]{2,1,0:T(8,128)(2,1)S(1)}) fusion(bf16[4,512,1280]{2,1,0:T(8,128)(2,1)} %all-gather.2.cloned.1.call-done), kind=kLoop, calls=%fused_computation.21 | loop fusion | bytes 10485760 | tf_op jit(solution)/shard_map/slice | solution.py:17
  71.5 1.3 copy-done.1
  72.8 7.2 %convolution_bitcast_fusion.1 = f32[1,4,1024,640]{3,2,1,0:T(8,128)} fusion(bf16[4,512,640]{2,1,0:T(8,128)(2,1)S(1)} %get-tuple-element.8, bf16[4,512,640]{2,1,0:T(8,128)(2,1)S(1)} %get-tuple-element.7, bf16[1,4,2,640,640]{4,3,2,1,0:T(8,128)(2,1)S(1)} %copy-done.1), kind=kOutput, calls=%fused_computation.9 | convolution fusion | flops 3365928960 | bytes 19005440 | tf_op jit(solution)/shard_map/srn,ksno->ksro/dot_general | solution.py:18
  80.0 7.3 %convolution_bitcast_fusion = f32[1,4,1024,640]{3,2,1,0:T(8,128)} fusion(bf16[4,512,640]{2,1,0:T(8,128)(2,1)S(1)} %get-tuple-element.8, bf16[4,512,640]{2,1,0:T(8,128)(2,1)S(1)} %get-tuple-element.7, bf16[1,4,2,640,640]{4,3,2,1,0:T(8,128)(2,1)S(1)} %copy-done.1), kind=kOutput, calls=%fused_computation.8 | convolution fusion | flops 3365928960 | bytes 19005440 | tf_op jit(solution)/shard_map/srn,ksno->ksro/dot_general | solution.py:21
  87.3 9.1 %subtract_bitcast_fusion = (f32[4,1,512,640]{3,2,0,1:T(8,128)S(1)}, f32[4,1,512,640]{3,2,0,1:T(8,128)S(1)}) fusion(f32[]{:T(128)} %bitcast.11, f32[]{:T(128)} %bitcast.2, f32[1,4,1024,640]{3,2,1,0:T(8,128)} %convolution_bitcast_fusion, f32[1,4,1024,640]{3,2,1,0:T(8,128)} %convolution_bitcast_fusion.1), kind=kLoop, calls=%fused_computation.7 | loop fusion | flops 10485760 | bytes 31457288 | tf_op jit(solution)/shard_map/stack | solution.py:30
  96.4 4.7 %pad_maximum_fusion = f32[4,2,512,640]{3,2,0,1:T(8,128)} fusion(f32[4,1,512,640]{3,2,0,1:T(8,128)S(1)} %get-tuple-element.6, f32[4,1,512,640]{3,2,0,1:T(8,128)S(1)} %get-tuple-element.5), kind=kLoop, calls=%fused_computation | loop fusion | flops 2621440 | bytes 20971520 | tf_op jit(solution)/shard_map/stack | solution.py:30
  101.1 0.0 reduce-scatter.2.cloned.1.call-update
  101.1 117.8 %reduce-scatter.2.cloned.1.call-done = f32[4,2,32,640]{3,2,0,1:T(8,128)} async-done(((f32[4,2,512,640]{3,2,0,1:T(8,128)}), f32[4,2,32,640]{3,2,0,1:T(8,128)}) %reduce-scatter.2.cloned.1.call-update) | async-done | bytes 655376 | tf_op jit(solution)/shard_map/reduce_scatter | solution.py:31
  218.9 6.4 %fusion = f32[4,2,32,1280]{3,2,1,0:T(8,128)S(1)} fusion(bf16[4,640,1280]{2,1,0:T(8,128)(2,1)} %param.8, f32[4,2,32,640]{3,2,0,1:T(8,128)} %reduce-scatter.2.cloned.1.call-done), kind=kOutput, calls=%fused_computation.1 | convolution fusion | flops 2516582400 | bytes 8519680 | tf_op jit(solution)/shard_map/spcn,snl->spcl/dot_general | solution.py:8
  225.3 4.9 %copy.14 = f32[4,2,32,1280]{2,1,0,3:T(2,128)} copy(f32[4,2,32,1280]{3,2,1,0:T(8,128)S(1)} %fusion) | data formatting | bytes 2621440 | tf_op jit(solution)/shard_map/spcn,snl->spcl/dot_general | solution.py:8
  230.2 6.8 %reshape.25 = f32[2,1,163840]{2,1,0:T(1,128)S(1)} reshape(f32[1280,4,2,32]{3,2,1,0:T(2,128)} %bitcast.45) | data formatting | bytes 2621440
  237.1 19.1 %all_to_all.18 = f32[2,1,163840]{2,1,0:T(1,128)S(1)} all-to-all(f32[2,1,163840]{2,1,0:T(1,128)S(1)} %reshape.25), channel_id=1, replica_groups=mesh['term'=16,'wave'=2] {'wave'}, dimensions={0} | all-to-all | bytes 2621440 | tf_op jit(solution)/shard_map/all_to_all | solution.py:33
  256.1 0.5 broadcast.3
  256.7 4.5 %reduce = f32[2,163840]{1,0:T(2,128)S(1)} reduce(f32[2,1,163840]{2,1,0:T(1,128)S(1)} %all_to_all.18, f32[]{:T(128)} %broadcast.3), dimensions={1}, to_apply=%all_to_all.13.reduce_sub_computation | reduce | bytes 2621444 | tf_op jit(solution)/shard_map/all_to_all | solution.py:33
  261.2 7.2 %reshape.26 = f32[1280,4,2,32]{3,2,1,0:T(2,128)} reshape(f32[2,163840]{1,0:T(2,128)S(1)} %reduce) | data formatting | bytes 2621440
  268.3 0.0 copy-start
  268.3 6.6 %copy.15 = f32[4,2,32,2,640]{4,0,3,2,1:T(4,128)S(1)} copy(f32[4,2,32,2,640]{2,1,0,4,3:T(2,128)} %bitcast.46) | data formatting | bytes 2621440 | tf_op jit(solution)/shard_map/all_to_all | solution.py:33
  274.9 0.5 all_to_all.16
  275.4 0.0 copy-done
  275.4 0.7 fusion.8
  276.1 1.3 copy.16
Async XLA Ops:
  6.5 61.9 %all-gather.2.cloned.1.call-start = ((), (), s32[]{:S(2)}) async-start(), calls=%async_computation.2 | async-start | bytes 5570560 | tf_op jit(solution)/shard_map/all_gather | solution.py:14
  7.3 211.6 %reduce-scatter.2.cloned.1.call-start = ((), (), s32[]{:S(2)}) async-start(), calls=%async_computation.3 | async-start | bytes 11141120 | tf_op jit(solution)/shard_map/reduce_scatter | solution.py:31
  68.4 4.4 %copy-start.1 = (bf16[1,4,2,640,640]{4,3,2,1,0:T(8,128)(2,1)S(1)}, bf16[1,4,2,640,640]{4,3,2,1,0:T(8,128)(2,1)}, u32[]{:S(2)}) copy-start(bf16[1,4,2,640,640]{4,3,2,1,0:T(8,128)(2,1)} %param.6) | copy-start | bytes 19660804
  268.3 7.1 %copy-start = (s32[8]{0:T(128)S(1)}, s32[8]{0:T(128)}, u32[]{:S(2)}) copy-start(s32[8]{0:T(128)} %param.9) | copy-start | bytes 100
Sparse Core Ops, SparseCore 0:
  9.6 58.7 all-gather.1
  101.2 117.6 reduce-scatter.1
where the time goes:
time: 285 us; the launch traced here: 284 us
  waiting for transfers between devices  178 us (62%)
  local copies, waits for them, and re-layouts  33.5 us (12%)
  matrix products  21.6 us (8%)
  blocking collectives  19.1 us (7%)
  other arithmetic  18.3 us (6%)
  between operations  13.5 us (5%)
    reduce_scatter x1, waiting for transfers between devices, shards(): lax.psum_scatter(partial_value, 'term', scatter_dimension=2, tiled=True)  118 us
    all_gather x1, waiting for transfers between devices, shards(): whole = lax.all_gather(spectral_state, 'term', axis=1, tiled=True)  59.8 us
    all_to_all x1, blocking collectives, shards(): lax.all_to_all(grid, 'wave', split_axis=3, concat_axis=0, tiled=True)  19.1 us
    unnamed x6, local copies, waits for them, and re-layouts  15.3 us
    another operation x2, other arithmetic, shards(): partial_value = jnp.stack([total_re, total_im], axis=1)  13.8 us
    all_to_all x3, local copies, waits for them, and re-layouts, shards(): lax.all_to_all(grid, 'wave', split_axis=3, concat_axis=0, tiled=True)  7.54 us
    dot_general x1, matrix products, shards(): jnp.einsum('srn,ksno->ksro', stacked, inverse[:, :, 1], preferred_element...  7.29 us
    dot_general x1, matrix products, shards(): jnp.einsum('srn,ksno->ksro', stacked, inverse[:, :, 0], preferred_element...  7.2 us
  transfers between devices with their start and end apart: 2, of which 2 were waited for; matrix products, arithmetic and copies ran while one was open for 0% of the time, Pallas kernels for 0%

commit v1 on v0

v1 whole, which is shorter than its diff:
```python
import functools

import jax
import jax.numpy as jnp
from jax import lax
from jax.experimental import pallas as pl
from jax.experimental.pallas import tpu as pltpu
from jax.sharding import PartitionSpec as P

F32, BF16, I16, I32 = jnp.float32, jnp.bfloat16, jnp.int16, jnp.int32
LANES = 128
STEPS = 64.0
TOP = 32000.0
TINY = 1e-30


def params(mib=40):
    return pltpu.CompilerParams(vmem_limit_bytes=mib * 2**20)


def split(x):
    hi = x.astype(BF16)
    return hi, (x - hi.astype(F32)).astype(BF16)


def lane_block(width):
    return 256 if width % 256 == 0 else LANES


def encode(x):
    top = jnp.maximum(jnp.max(jnp.abs(x), axis=1, keepdims=True), TINY)
    step = jnp.ceil(jnp.log2(top / TOP) * STEPS)
    code = jnp.round(x * jnp.exp2(step * (-1.0 / STEPS)))
    return code.astype(I32).astype(I16), step


def put_steps(steps, rows):
    lane = lax.broadcasted_iota(I32, (rows, LANES), 1)
    out = jnp.zeros((rows, LANES), F32)
    for n, step in enumerate(steps):
        out = jnp.where(lane == n, step, out)
    return out.astype(I32).astype(I16)


def encode_rows(x):
    rows, width = x.shape
    nb = lane_block(width)
    pairs = [encode(x[:, i : i + nb]) for i in range(0, width, nb)]
    return [p[0] for p in pairs] + [put_steps([p[1] for p in pairs], rows)]


def decode_rows(coded, width):
    nb = lane_block(width)
    scale = jnp.exp2(coded[:, width:].astype(I32).astype(F32) * (1.0 / STEPS))
    return [
        coded[:, i : i + nb].astype(I32).astype(F32) * scale[:, n : n + 1]
        for n, i in enumerate(range(0, width, nb))
    ]


def operator_kernel(pos, w_own, w_got, own, got, out):
    size = own.shape[-1]
    real = jnp.zeros(own.shape[-2:], F32)
    imag = jnp.zeros(own.shape[-2:], F32)
    for k in range(own.shape[0]):
        for w, block in ((w_own, own[k, 0]), (w_got, got[k])):
            r, j = block[0].astype(F32), block[1].astype(F32)
            real += w[k, 0] * r - w[k, 1] * j
            imag += w[k, 0] * j + w[k, 1] * r
    for level, (r, j) in enumerate(zip(split(real), split(imag))):
        out[level, 0, :, :size] = r
        out[level, 0, :, size:] = j
        out[level, 1, :, :size] = -j
        out[level, 1, :, size:] = r


def make_operator(at, w_own, w_got, inverse, got):
    terms, _, _, size, _ = inverse.shape
    rows = LANES
    smem = pl.BlockSpec(memory_space=pltpu.SMEM)
    out = pl.pallas_call(
        operator_kernel,
        out_shape=jax.ShapeDtypeStruct((2, 2, size, 2 * size), BF16),
        grid_spec=pltpu.PrefetchScalarGridSpec(
            num_scalar_prefetch=1,
            grid=(size // rows,),
            in_specs=[
                smem,
                smem,
                pl.BlockSpec((terms, 1, 2, rows, size), lambda i, pos: (0, pos[0], 0, i, 0)),
                pl.BlockSpec((terms, 2, rows, size), lambda i, pos: (0, 0, i, 0)),
            ],
            out_specs=pl.BlockSpec((2, 2, rows, 2 * size), lambda i, pos: (0, 0, i, 0)),
        ),
        compiler_params=params(),
        cost_estimate=pl.CostEstimate(
            flops=16 * terms * size * size, bytes_accessed=24 * size * size, transcendentals=0
        ),
        name="operator",
    )(at, w_own, w_got, inverse, got)
    return out.reshape(2, 2 * size, 2 * size)


def product_kernel(coded, count, *refs):
    parts, op, out, full = refs[:count], refs[count], refs[count + 1], refs[count + 2]
    rows = parts[0].shape[0]
    n = pl.program_id(0)

    @pl.when(n == 0)
    def _():
        for i, part in enumerate(parts):
            full[i * rows : (i + 1) * rows, :] = part[...]

    x = full[...]
    acc = jnp.dot(x, op[0], preferred_element_type=F32)
    acc += jnp.dot(x, op[1], preferred_element_type=F32)
    if not coded:
        out[...] = acc
        return
    steps = refs[count + 3]
    width, nb = x.shape[1], op.shape[2]
    code, step = encode(acc)
    out[:, pl.ds(pl.multiple_of(n * nb, nb), nb)] = code
    lane = lax.broadcasted_iota(I32, steps.shape, 1)
    steps[...] = jnp.where(lane == n, step, steps[...])

    @pl.when(n == pl.num_programs(0) - 1)
    def _():
        out[:, width:] = steps[...].astype(I32).astype(I16)


def product(parts, op, coded):
    count = len(parts)
    part_rows, width = parts[0].shape
    rows = count * part_rows
    nb = lane_block(width)
    scratch = [pltpu.VMEM((rows, width), BF16)]
    if coded:
        out_shape = jax.ShapeDtypeStruct((rows, width + LANES), I16)
        out_spec = pl.BlockSpec((rows, width + LANES), lambda n: (0, 0))
        scratch.append(pltpu.VMEM((rows, LANES), F32))
    else:
        out_shape = jax.ShapeDtypeStruct((rows, width), F32)
        out_spec = pl.BlockSpec((rows, nb), lambda n: (0, n))
    return pl.pallas_call(
        functools.partial(product_kernel, coded, count),
        out_shape=out_shape,
        grid=(width // nb,),
        in_specs=[pl.BlockSpec((part_rows, width), lambda n: (0, 0))] * count
        + [pl.BlockSpec((2, width, nb), lambda n: (0, 0, n))],
        out_specs=out_spec,
        scratch_shapes=scratch,
        compiler_params=params(),
        cost_estimate=pl.CostEstimate(
            flops=4 * rows * width * width,
            bytes_accessed=4 * width * width + 4 * rows * width,
            transcendentals=0,
        ),
        name="product",
    )(*parts, op)


def fold_kernel(count, own, got, *outs):
    rows, width = outs[0].shape
    nb = lane_block(width)
    for q in range(count):
        at = slice(q * rows, (q + 1) * rows)
        pieces = decode_rows(got[at, :], width)
        total = [own[at, n * nb : (n + 1) * nb] + piece for n, piece in enumerate(pieces)]
        if q == 0:
            for n, piece in enumerate(total):
                outs[0][:, n * nb : (n + 1) * nb] = piece
        else:
            pairs = [encode(piece) for piece in total]
            for n, pair in enumerate(pairs):
                outs[q][:, n * nb : (n + 1) * nb] = pair[0]
            outs[q][:, width:] = put_steps([p[1] for p in pairs], rows)


def fold(own, got, count):
    rows, width = own.shape[0] // count, own.shape[1]
    return pl.pallas_call(
        functools.partial(fold_kernel, count),
        out_shape=[jax.ShapeDtypeStruct((rows, width), F32)]
        + [jax.ShapeDtypeStruct((rows, width + LANES), I16)] * (count - 1),
        compiler_params=params(),
        cost_estimate=pl.CostEstimate(
            flops=10 * own.size, bytes_accessed=10 * own.size, transcendentals=0
        ),
        name="fold",
    )(own, got)


def total_rows(own, got):
    width = own.shape[1]
    nb = lane_block(width)
    pieces = [own[:, i : i + nb] for i in range(0, width, nb)]
    for part in got:
        pieces = [a + b for a, b in zip(pieces, decode_rows(part[...], width))]
    return jnp.concatenate(pieces, axis=1)


def synthesis_kernel(bands, count, pos, own, *refs):
    got, table, outs, values = refs[:count], refs[count], refs[count + 1 : -1], refs[-1]
    rows, width = own.shape
    size = width // 2
    half = rows // 2
    band = pl.program_id(0)

    @pl.when(band == 0)
    def _():
        total = total_rows(own, got)
        for part in range(2):
            hi, lo = split(total[:, part * size : (part + 1) * size])
            values[0, part * rows : (part + 1) * rows, :] = hi
            values[1, part * rows : (part + 1) * rows, :] = lo

    grid = jnp.dot(values[0], table[0], preferred_element_type=F32)
    grid += jnp.dot(values[1], table[0], preferred_element_type=F32)
    for d in range(bands):

        @pl.when(band == d)
        def _():
            for side in range(2):
                for part in range(2):
                    start = part * rows + side * half
                    outs[2 * d + side][part] = grid[start : start + half]


def synthesis(at, own, got, legendre, bands):
    rows, width = own.shape
    size, nlat = legendre.shape[1:]
    band = nlat // bands
    piece = (2, rows // 2, band)
    return pl.pallas_call(
        functools.partial(synthesis_kernel, bands, len(got)),
        out_shape=[jax.ShapeDtypeStruct(piece, F32)] * (2 * bands),
        grid_spec=pltpu.PrefetchScalarGridSpec(
            num_scalar_prefetch=1,
            grid=(bands,),
            in_specs=[pl.BlockSpec((rows, width), lambda b, pos: (0, 0))]
            + [pl.BlockSpec((rows, width + LANES), lambda b, pos: (0, 0))] * len(got)
            + [pl.BlockSpec((1, size, band), lambda b, pos: (pos[0], 0, pos[1] ^ b))],
            out_specs=[pl.BlockSpec(piece, lambda b, pos: (0, 0, 0))] * (2 * bands),
            scratch_shapes=[pltpu.VMEM((2, 2 * rows, size), BF16)],
        ),
        compiler_params=params(),
        cost_estimate=pl.CostEstimate(
            flops=8 * rows * size * nlat,
            bytes_accessed=2 * size * nlat + 8 * rows * nlat,
            transcendentals=0,
        ),
        name="synthesis",
    )(at, own, *got, legendre)


def sum_kernel(own, *refs):
    refs[-1][...] = total_rows(own, refs[:-1])


def plain_synthesis(at, own, got, legendre, bands):
    rows, width = own.shape
    size, nlat = legendre.shape[1:]
    total = pl.pallas_call(
        sum_kernel, out_shape=jax.ShapeDtypeStruct(own.shape, F32), name="total"
    )(own, *got)
    table = lax.dynamic_index_in_dim(legendre, at[0], 0, keepdims=False)
    values = jnp.stack([total[:, :size], total[:, size:]])
    grid = sum(
        jnp.einsum("pcn,nl->pcl", v, table, preferred_element_type=F32) for v in split(values)
    )
    half, band = rows // 2, nlat // bands
    return [
        lax.dynamic_slice(
            grid, (0, side * half, (at[1] ^ d) * band), (2, half, band)
        )
        for d in range(bands)
        for side in range(2)
    ]


def place_kernel(count, dst, *refs):
    pieces, out = refs[:count], refs[count]
    for i in range(count):

        @pl.when(pl.program_id(0) == i)
        def _():
            out[0] = pieces[i][...]


def place(dst, pieces):
    count = len(pieces)
    shape = pieces[0].shape
    return pl.pallas_call(
        functools.partial(place_kernel, count),
        out_shape=jax.ShapeDtypeStruct((count,) + shape, F32),
        grid_spec=pltpu.PrefetchScalarGridSpec(
            num_scalar_prefetch=1,
            grid=(count,),
            in_specs=[pl.BlockSpec(shape, lambda i, dst: (0, 0, 0))] * count,
            out_specs=pl.BlockSpec((1,) + shape, lambda i, dst: (dst[i], 0, 0, 0)),
        ),
        compiler_params=params(),
        name="place",
    )(dst, *pieces)


def shards(mesh, spectral_state, inverse, term_weights, legendre, slot_column):
    terms, waves = mesh.shape["term"], mesh.shape["wave"]
    slots, cols, width = spectral_state.shape
    mine = slots // 2
    outer = terms // 4
    me, wave = lax.axis_index("term"), lax.axis_index("wave")
    core = me % 2

    def swap(x, term_bits, wave_bits=0):
        pairs = [
            (t * waves + w, (t ^ term_bits) * waves + (w ^ wave_bits))
            for t in range(terms)
            for w in range(waves)
        ]
        return lax.ppermute(x, ("term", "wave"), pairs)

    def half_of(x, which, dim):
        return lax.dynamic_slice_in_dim(x, which * mine, mine, dim)

    state_got = swap(half_of(spectral_state, 1 - core, 0), 1)
    state_own = half_of(spectral_state, core, 0)
    weights_got = swap(term_weights, 1)
    away = half_of(inverse, 1 - core, 1)
    blocks = [jnp.concatenate([state_own[j], state_got[j]], axis=0) for j in range(mine)]
    inverse_got = [swap(away[:, j], 1) for j in range(mine)]

    pieces = []
    for j in range(mine):
        at = jnp.stack([core * mine + j, wave]).astype(I32)
        op = make_operator(at, term_weights, weights_got, inverse, inverse_got[j])
        near = [blocks[j]] + [swap(blocks[j], q * 4) for q in range(1, outer)]
        far = [swap(block, 2) for block in near]
        sent = swap(product(far, op, True), 2)
        own = product(near, op, False)
        folded = fold(own, sent, outer)
        got = [swap(folded[q], q * 4) for q in range(1, outer)]
        make = synthesis if legendre.shape[2] // waves % LANES == 0 else plain_synthesis
        grid = make(at, folded[0], got, legendre, waves)
        for d in range(waves):
            for side in range(2):
                piece = grid[2 * d + side]
                if d or side:
                    piece = swap(piece, side, d)
                slot = (wave ^ d) * slots + (core ^ side) * mine + j
                pieces.append((slot, piece))

    dst = jnp.stack([slot_column[slot] for slot, _ in pieces])
    return place(dst, [piece for _, piece in pieces])


def solution(mesh):
    return jax.shard_map(
        functools.partial(shards, mesh),
        mesh=mesh,
        in_specs=(
            P("wave", "term", None),
            P("term", "wave", None, None, None),
            P("term", None),
            P("wave", None, None),
            P(),
        ),
        out_specs=P(None, None, "term", "wave"),
        check_vma=False,
    )
```

time: 285 us -> 126 us (0.44)
  waiting for transfers between devices: 178 us -> 40.1 us
  starting transfers between devices: 0.04 us -> 37 us
  Pallas kernels: 0 us -> 34.7 us
  matrix products: 21.6 us -> 0 us
  local copies, waits for them, and re-layouts: 33.5 us -> 13 us
  blocking collectives: 19.1 us -> 0 us
  other arithmetic: 18.3 us -> 0.17 us
  between operations: 13.5 us -> 0.28 us
    reduce_scatter x1 -> x0, waiting for transfers between devices: 118 us -> none  [shards(): lax.psum_scatter(partial_value, 'term', scatter_dimension=2, tiled=True)]
    all_gather x1 -> x0, waiting for transfers between devices: 59.8 us -> none  [shards(): whole = lax.all_gather(spectral_state, 'term', axis=1, tiled=True)]
    ppermute x0 -> x32, waiting for transfers between devices: none -> 40.1 us  [swap(): return lax.ppermute(x, ('term', 'wave'), pairs)]
    ppermute x0 -> x32, starting transfers between devices: none -> 37 us  [swap(): return lax.ppermute(x, ('term', 'wave'), pairs)]
    pallas_call x0 -> x11, Pallas kernels: none -> 34.7 us  [the longest x4 16.2 us: product(): pl.pallas_call(functools.partial(product_kernel, coded, count), out_shape...]
    dot_general x4 -> x0, matrix products: 21.6 us -> none  [the longest x1 7.29 us: shards(): jnp.einsum('srn,ksno->ksro', stacked, inverse[:, :, 1], preferred_element...]
    all_to_all x1 -> x0, blocking collectives: 19.1 us -> none  [shards(): lax.all_to_all(grid, 'wave', split_axis=3, concat_axis=0, tiled=True)]
    unnamed x6 -> x26, local copies, waits for them, and re-layouts: 15.3 us -> 0.72 us
  transfers between devices with their start and end apart: 2 -> 32, of which waited for: 2 -> 11; matrix products, arithmetic and copies ran while one was open for 0% -> 7% of each run, Pallas kernels for 0% -> 25%
where the time goes in v1:
time: 126 us; the launch traced here: 125 us
  waiting for transfers between devices  40.1 us (32%)
  starting transfers between devices  37 us (29%)
  Pallas kernels  34.7 us (28%)
  local copies, waits for them, and re-layouts  13 us (10%)
    ppermute x32, waiting for transfers between devices, swap(): return lax.ppermute(x, ('term', 'wave'), pairs)  40.1 us
    ppermute x32, starting transfers between devices, swap(): return lax.ppermute(x, ('term', 'wave'), pairs)  37 us
    pallas_call x4, Pallas kernels, product(): pl.pallas_call(functools.partial(product_kernel, coded, count), out_shape...  16.2 us
    pallas_call x2, Pallas kernels, make_operator(): pl.pallas_call(operator_kernel, out_shape=jax.ShapeDtypeStruct((2, 2, siz...  9.8 us
    another operation x1, local copies, waits for them, and re-layouts, shards(): dst = jnp.stack([slot_column[slot] for slot, _ in pieces])  5.15 us
    squeeze x1, local copies, waits for them, and re-layouts, shards(): inverse_got = [swap(away[:, j], 1) for j in range(mine)]  3.95 us
    pallas_call x2, Pallas kernels, synthesis(): pl.pallas_call(functools.partial(synthesis_kernel, bands, len(got)), out_...  3.93 us
    pallas_call x1, Pallas kernels, place(): pl.pallas_call(functools.partial(place_kernel, count), out_shape=jax.Shap...  3.42 us
  transfers between devices with their start and end apart: 32, of which 11 were waited for; matrix products, arithmetic and copies ran while one was open for 7% of the time, Pallas kernels for 25%

profile of v1, /device:TPU:0, one launch (start us, length us, event | category | flops | bytes accessed | tf_op | source)
XLA Modules:
  0.0 125.3 jit_solution(1914040707836791624)
XLA Ops:
  0.0 4.0 %dynamic-slice_bitcast_fusion = (bf16[1,2,640,640]{3,2,1,0:T(8,128)(2,1)}, bf16[1,2,640,640]{3,2,1,0:T(8,128)(2,1)}) fusion(bf16[1,4,2,640,640]{4,3,2,1,0:T(8,128)(2,1)} %own.3, s32[]{:T(128)S(6)} %add.97, s32[]{:T(128)S(6)} %select_n.48), kind=kLoop, calls=%fused_computation | loop fusion | bytes 6553608 | tf_op jit(solution)/shard_map/squeeze | solution.py:332
  4.0 0.5 collective-permute-start.20
  4.4 0.1 collective-permute-start.4
  4.5 0.5 collective-permute-start.5
  4.9 0.7 constant_dynamic-slice_fusion
  5.6 0.1 collective-permute-start
  5.7 0.9 dynamic-slice_bitcast_fusion.2
  6.6 1.7 %collective-permute-done = bf16[2,32,1280]{2,1,0:T(8,128)(2,1)} collective-permute-done((bf16[2,32,1280]{2,1,0:T(8,128)(2,1)}, bf16[2,32,1280]{2,1,0:T(8,128)(2,1)}, u32[]{:S(2)}, u32[]{:S(2)}) %collective-permute-start) | collective-permute-done | bytes 163872 | tf_op jit(solution)/shard_map/ppermute | solution.py:322
  8.4 0.9 slice_bitcast_fusion
  9.3 3.0 %collective-permute-start.17 = (bf16[64,1280]{1,0:T(8,128)(2,1)S(1)}, bf16[64,1280]{1,0:T(8,128)(2,1)}, u32[]{:S(2)}, u32[]{:S(2)}) collective-permute-start(bf16[64,1280]{1,0:T(8,128)(2,1)S(1)} %pad_maximum_fusion.1.refs_0_), channel_id=1, source_target_pairs={{0,8},{1,9},{2,10},{3,11},{4,12},{5,13},{6,14},{7,15},{8,0},{9,1},... | collective-permute-start | bytes 491528 | tf_op jit(solution)/shard_map/ppermute | solution.py:322
  12.3 2.6 %collective-permute-start.18 = (bf16[64,1280]{1,0:T(8,128)(2,1)S(1)}, bf16[64,1280]{1,0:T(8,128)(2,1)}, u32[]{:S(2)}, u32[]{:S(2)}) collective-permute-start(bf16[64,1280]{1,0:T(8,128)(2,1)S(1)} %pad_maximum_fusion.1.refs_0_), channel_id=1, source_target_pairs={{0,16},{1,17},{2,18},{3,19},{4,20},{5,21},{6,22},{7,23},{8,24},{9,... | collective-permute-start | bytes 491528 | tf_op jit(solution)/shard_map/ppermute | solution.py:322
  14.9 4.8 %collective-permute-done.17.refs_1_ = bf16[64,1280]{1,0:T(8,128)(2,1)} collective-permute-done((bf16[64,1280]{1,0:T(8,128)(2,1)S(1)}, bf16[64,1280]{1,0:T(8,128)(2,1)}, u32[]{:S(2)}, u32[]{:S(2)}) %collective-permute-start.17) | collective-permute-done | bytes 163872 | tf_op jit(solution)/shard_map/ppermute | solution.py:322
  19.8 1.7 %collective-permute-start.21 = (bf16[64,1280]{1,0:T(8,128)(2,1)S(1)}, bf16[64,1280]{1,0:T(8,128)(2,1)S(1)}, u32[]{:S(2)}, u32[]{:S(2)}) collective-permute-start(bf16[64,1280]{1,0:T(8,128)(2,1)S(1)} %pad_maximum_fusion.1.refs_0_), channel_id=1, source_target_pairs={{0,4},{1,5},{2,6},{3,7},{4,0},{5,1},{6,2},{7,3},{8,12},{9,13},{10,... | collective-permute-start | bytes 491528 | tf_op jit(solution)/shard_map/ppermute | solution.py:322
  21.5 6.0 %collective-permute-done.18.refs_2_ = bf16[64,1280]{1,0:T(8,128)(2,1)} collective-permute-done((bf16[64,1280]{1,0:T(8,128)(2,1)S(1)}, bf16[64,1280]{1,0:T(8,128)(2,1)}, u32[]{:S(2)}, u32[]{:S(2)}) %collective-permute-start.18) | collective-permute-done | bytes 163872 | tf_op jit(solution)/shard_map/ppermute | solution.py:322
  27.5 0.0 collective-permute-start.1
  27.5 0.0 collective-permute-done.19.refs_3_
  27.5 4.0 %collective-permute-start.2 = (bf16[64,1280]{1,0:T(8,128)(2,1)S(1)}, bf16[64,1280]{1,0:T(8,128)(2,1)S(1)}, u32[]{:S(2)}, u32[]{:S(2)}) collective-permute-start(bf16[64,1280]{1,0:T(8,128)(2,1)S(1)} %pad_maximum_fusion.refs_0_), channel_id=1, source_target_pairs={{0,16},{1,17},{2,18},{3,19},{4,20},{5,21},{6,22},{7,23},{8,24},{9,... | collective-permute-start | bytes 491528 | tf_op jit(solution)/shard_map/ppermute | solution.py:322
  31.5 0.0 collective-permute-done.21.refs_0_
  31.5 0.7 copy-done.6
  32.1 1.4 %collective-permute-start.3 = (bf16[64,1280]{1,0:T(8,128)(2,1)S(1)}, bf16[64,1280]{1,0:T(8,128)(2,1)}, u32[]{:S(2)}, u32[]{:S(2)}) collective-permute-start(bf16[64,1280]{1,0:T(8,128)(2,1)S(1)} %pad_maximum_fusion.refs_0_), channel_id=1, source_target_pairs={{0,24},{1,25},{2,26},{3,27},{4,28},{5,29},{6,30},{7,31},{8,16},{9,... | collective-permute-start | bytes 491528 | tf_op jit(solution)/shard_map/ppermute | solution.py:322
  33.5 1.1 collective-permute-done.1.refs_1_
  34.6 1.5 %collective-permute-start.22 = (bf16[64,1280]{1,0:T(8,128)(2,1)}, bf16[64,1280]{1,0:T(8,128)(2,1)}, u32[]{:S(2)}, u32[]{:S(2)}) collective-permute-start(bf16[64,1280]{1,0:T(8,128)(2,1)} %collective-permute-done.17.refs_1_), channel_id=1, source_target_pairs={{0,4},{1,5},{2,6},{3,7},{4,0},{5,1},{6,2},{7,3},{8,12},{9,13},{10,... | collective-permute-start | bytes 491528 | tf_op jit(solution)/shard_map/ppermute | solution.py:322
  36.2 7.2 %collective-permute-done.2.refs_2_ = bf16[64,1280]{1,0:T(8,128)(2,1)S(1)} collective-permute-done((bf16[64,1280]{1,0:T(8,128)(2,1)S(1)}, bf16[64,1280]{1,0:T(8,128)(2,1)S(1)}, u32[]{:S(2)}, u32[]{:S(2)}) %collective-permute-start.2) | collective-permute-done | bytes 163872 | tf_op jit(solution)/shard_map/ppermute | solution.py:322
  43.3 1.5 %collective-permute-start.23 = (bf16[64,1280]{1,0:T(8,128)(2,1)}, bf16[64,1280]{1,0:T(8,128)(2,1)}, u32[]{:S(2)}, u32[]{:S(2)}) collective-permute-start(bf16[64,1280]{1,0:T(8,128)(2,1)} %collective-permute-done.18.refs_2_), channel_id=1, source_target_pairs={{0,4},{1,5},{2,6},{3,7},{4,0},{5,1},{6,2},{7,3},{8,12},{9,13},{10,... | collective-permute-start | bytes 491528 | tf_op jit(solution)/shard_map/ppermute | solution.py:322
  44.9 0.7 collective-permute-start.24
  45.5 0.1 pad_add_fusion.1.pos
  45.6 4.9 %operator.3 = bf16[2,2,640,1280]{3,2,1,0:T(8,128)(2,1)S(1)} custom-call(s32[2]{0:T(128)S(1)} %pad_add_fusion.1.pos, f32[1,2]{1,0:T(1,128)S(1)} %copy-done.8, f32[1,2]{1,0:T(1,128)S(1)} %collective-permute-done.4.w_got, bf16[1,4,2,640,640]{4,3,2,1,0:T(8,128)(2,1)} %own.3, bf16[1,2,640,640]{3,2,1,0:T(8,128)(2,1)S(1)} %collective-permute-done.20.got), custom_call_target="tpu_custom_call" | custom-call | flops 6553600 | bytes 9830400 | tf_op jit(solution)/shard_map/operator/pallas_call | solution.py:81
  50.5 0.0 collective-permute-done.3.refs_3_
  50.5 1.5 %collective-permute-start.6 = (bf16[64,1280]{1,0:T(8,128)(2,1)S(1)}, bf16[64,1280]{1,0:T(8,128)(2,1)S(1)}, u32[]{:S(2)}, u32[]{:S(2)}) collective-permute-start(bf16[64,1280]{1,0:T(8,128)(2,1)S(1)} %pad_maximum_fusion.refs_0_), channel_id=1, source_target_pairs={{0,4},{1,5},{2,6},{3,7},{4,0},{5,1},{6,2},{7,3},{8,12},{9,13},{10,... | collective-permute-start | bytes 491528 | tf_op jit(solution)/shard_map/ppermute | solution.py:322
  52.0 0.6 collective-permute-start.7
  52.6 1.4 %collective-permute-start.8 = (bf16[64,1280]{1,0:T(8,128)(2,1)S(1)}, bf16[64,1280]{1,0:T(8,128)(2,1)S(1)}, u32[]{:S(2)}, u32[]{:S(2)}) collective-permute-start(bf16[64,1280]{1,0:T(8,128)(2,1)S(1)} %copy-done.5), channel_id=1, source_target_pairs={{0,4},{1,5},{2,6},{3,7},{4,0},{5,1},{6,2},{7,3},{8,12},{9,13},{10,... | collective-permute-start | bytes 491528 | tf_op jit(solution)/shard_map/ppermute | solution.py:322
  54.1 0.6 collective-permute-start.9
  54.7 4.6 %product.7 = s16[256,1408]{1,0:T(8,128)(2,1)S(1)} custom-call(bf16[64,1280]{1,0:T(8,128)(2,1)S(1)} %copy-done.7, bf16[64,1280]{1,0:T(8,128)(2,1)} %collective-permute-done.22.refs_1_, bf16[64,1280]{1,0:T(8,128)(2,1)} %collective-permute-done.23.refs_2_, bf16[64,1280]{1,0:T(8,128)(2,1)} %collective-permute-done.24.refs_3_, bf16[2,1280,1280]{2,1,0:T(8,128)(2,1)S(1)} %bitcast.17), custom_call_target="tpu_custom_call" | custom-call | flops 1677721600 | bytes 7864320 | tf_op jit(solution)/shard_map/product/pallas_call | solution.py:145
  59.3 1.5 %collective-permute-start.25 = (s16[256,1408]{1,0:T(8,128)(2,1)S(1)}, s16[256,1408]{1,0:T(8,128)(2,1)S(1)}, u32[]{:S(2)}, u32[]{:S(2)}) collective-permute-start(s16[256,1408]{1,0:T(8,128)(2,1)S(1)} %product.7), channel_id=1, source_target_pairs={{0,4},{1,5},{2,6},{3,7},{4,0},{5,1},{6,2},{7,3},{8,12},{9,13},{10,... | collective-permute-start | bytes 2162696 | tf_op jit(solution)/shard_map/ppermute | solution.py:322
  60.8 0.1 pad_add_fusion.pos
  60.8 4.9 %operator.2 = bf16[2,2,640,1280]{3,2,1,0:T(8,128)(2,1)S(1)} custom-call(s32[2]{0:T(128)S(1)} %pad_add_fusion.pos, f32[1,2]{1,0:T(1,128)S(1)} %copy-done.8, f32[1,2]{1,0:T(1,128)S(1)} %collective-permute-done.4.w_got, bf16[1,4,2,640,640]{4,3,2,1,0:T(8,128)(2,1)} %own.3, bf16[1,2,640,640]{3,2,1,0:T(8,128)(2,1)S(1)} %collective-permute-done.5.got), custom_call_target="tpu_custom_call" | custom-call | flops 6553600 | bytes 9830400 | tf_op jit(solution)/shard_map/operator/pallas_call | solution.py:81
  65.8 2.5 %collective-permute-done.9.refs_3_ = bf16[64,1280]{1,0:T(8,128)(2,1)S(1)} collective-permute-done((bf16[64,1280]{1,0:T(8,128)(2,1)}, bf16[64,1280]{1,0:T(8,128)(2,1)S(1)}, u32[]{:S(2)}, u32[]{:S(2)}) %collective-permute-start.9) | collective-permute-done | bytes 163872 | tf_op jit(solution)/shard_map/ppermute | solution.py:322
  68.3 3.6 %product.5 = s16[256,1408]{1,0:T(8,128)(2,1)S(1)} custom-call(bf16[64,1280]{1,0:T(8,128)(2,1)S(1)} %collective-permute-done.6.refs_0_, bf16[64,1280]{1,0:T(8,128)(2,1)S(1)} %collective-permute-done.7.refs_1_, bf16[64,1280]{1,0:T(8,128)(2,1)S(1)} %collective-permute-done.8.refs_2_, bf16[64,1280]{1,0:T(8,128)(2,1)S(1)} %collective-permute-done.9.refs_3_, ...), custom_call_target="tpu_custom_call" | custom-call | flops 1677721600 | bytes 7864320 | tf_op jit(solution)/shard_map/product/pallas_call | solution.py:145
  71.9 1.5 %collective-permute-start.10 = (s16[256,1408]{1,0:T(8,128)(2,1)S(1)}, s16[256,1408]{1,0:T(8,128)(2,1)S(1)}, u32[]{:S(2)}, u32[]{:S(2)}) collective-permute-start(s16[256,1408]{1,0:T(8,128)(2,1)S(1)} %product.5), channel_id=1, source_target_pairs={{0,4},{1,5},{2,6},{3,7},{4,0},{5,1},{6,2},{7,3},{8,12},{9,13},{10,... | collective-permute-start | bytes 2162696 | tf_op jit(solution)/shard_map/ppermute | solution.py:322
  73.4 4.1 %product.6.own = f32[256,1280]{1,0:T(8,128)S(1)} custom-call(bf16[64,1280]{1,0:T(8,128)(2,1)S(1)} %copy-done.1, bf16[64,1280]{1,0:T(8,128)(2,1)} %collective-permute-done.17.refs_1_, bf16[64,1280]{1,0:T(8,128)(2,1)} %collective-permute-done.18.refs_2_, bf16[64,1280]{1,0:T(8,128)(2,1)} %collective-permute-done.19.refs_3_, bf16[2,1280,1280]{2,1,0:T(8,128)(2,1)S(1)} %bitcast.18), custom_call_target="tpu_custom_call" | custom-call | flops 1677721600 | bytes 7864320 | tf_op jit(solution)/shard_map/product/pallas_call | solution.py:145
  77.5 6.2 %collective-permute-done.25.got = s16[256,1408]{1,0:T(8,128)(2,1)S(1)} collective-permute-done((s16[256,1408]{1,0:T(8,128)(2,1)S(1)}, s16[256,1408]{1,0:T(8,128)(2,1)S(1)}, u32[]{:S(2)}, u32[]{:S(2)}) %collective-permute-start.25) | collective-permute-done | bytes 720928 | tf_op jit(solution)/shard_map/ppermute | solution.py:322
  83.7 0.6 fold.3
  84.4 0.1 collective-permute-start.26
  84.4 2.1 %collective-permute-start.27 = (s16[64,1408]{1,0:T(8,128)(2,1)S(1)}, s16[64,1408]{1,0:T(8,128)(2,1)S(1)}, u32[]{:S(2)}, u32[]{:S(2)}) collective-permute-start(s16[64,1408]{1,0:T(8,128)(2,1)S(1)} %get-tuple-element.31), channel_id=1, source_target_pairs={{0,16},{1,17},{2,18},{3,19},{4,20},{5,21},{6,22},{7,23},{8,24},{9,... | collective-permute-start | bytes 540680 | tf_op jit(solution)/shard_map/ppermute | solution.py:322
  86.5 2.3 %collective-permute-start.28 = (s16[64,1408]{1,0:T(8,128)(2,1)S(1)}, s16[64,1408]{1,0:T(8,128)(2,1)S(1)}, u32[]{:S(2)}, u32[]{:S(2)}) collective-permute-start(s16[64,1408]{1,0:T(8,128)(2,1)S(1)} %get-tuple-element.32), channel_id=1, source_target_pairs={{0,24},{1,25},{2,26},{3,27},{4,28},{5,29},{6,30},{7,31},{8,16},{9,... | collective-permute-start | bytes 540680 | tf_op jit(solution)/shard_map/ppermute | solution.py:322
  88.8 3.9 %product.4.own = f32[256,1280]{1,0:T(8,128)S(1)} custom-call(bf16[64,1280]{1,0:T(8,128)(2,1)S(1)} %pad_maximum_fusion.refs_0_, bf16[64,1280]{1,0:T(8,128)(2,1)S(1)} %copy-done.3, bf16[64,1280]{1,0:T(8,128)(2,1)S(1)} %copy-done.5, bf16[64,1280]{1,0:T(8,128)(2,1)} %collective-permute-done.3.refs_3_, bf16[2,1280,1280]{2,1,0:T(8,128)(2,1)S(1)} %bitcast.20), custom_call_target="tpu_custom_call" | custom-call | flops 1677721600 | bytes 7864320 | tf_op jit(solution)/shard_map/product/pallas_call | solution.py:145
  92.8 2.8 %collective-permute-done.10.got = s16[256,1408]{1,0:T(8,128)(2,1)S(1)} collective-permute-done((s16[256,1408]{1,0:T(8,128)(2,1)S(1)}, s16[256,1408]{1,0:T(8,128)(2,1)S(1)}, u32[]{:S(2)}, u32[]{:S(2)}) %collective-permute-start.10) | collective-permute-done | bytes 720928 | tf_op jit(solution)/shard_map/ppermute | solution.py:322
  95.5 0.6 fold.2
  96.2 0.1 collective-permute-start.11
  96.3 0.1 collective-permute-start.12
  96.4 4.3 %collective-permute-start.13 = (s16[64,1408]{1,0:T(8,128)(2,1)S(1)}, s16[64,1408]{1,0:T(8,128)(2,1)S(1)}, u32[]{:S(2)}, u32[]{:S(2)}) collective-permute-start(s16[64,1408]{1,0:T(8,128)(2,1)S(1)} %get-tuple-element.24), channel_id=1, source_target_pairs={{0,24},{1,25},{2,26},{3,27},{4,28},{5,29},{6,30},{7,31},{8,16},{9,... | collective-permute-start | bytes 540680 | tf_op jit(solution)/shard_map/ppermute | solution.py:322
  100.7 2.0 %synthesis.3 = (f32[2,32,640]{2,1,0:T(8,128)S(1)}, f32[2,32,640]{2,1,0:T(8,128)S(1)}, f32[2,32,640]{2,1,0:T(8,128)S(1)}, f32[2,32,640]{2,1,0:T(8,128)S(1)}) custom-call(s32[2]{0:T(128)S(1)} %pad_add_fusion.1.pos, f32[64,1280]{1,0:T(8,128)S(1)} %get-tuple-element.29.own, s16[64,1408]{1,0:T(8,128)(2,1)S(1)} %collective-permute-done.26.refs_0_, ...), custom_call_target="tpu_custom_call" | custom-call | flops 419430400 | bytes 2293760 | tf_op jit(solution)/shard_map/synthesis/pallas_call | solution.py:235
  102.6 0.1 collective-permute-start.29
  102.7 1.6 %collective-permute-start.30 = (f32[2,32,640]{2,1,0:T(8,128)S(1)}, f32[2,32,640]{2,1,0:T(8,128)S(1)}, u32[]{:S(2)}, u32[]{:S(2)}) collective-permute-start(f32[2,32,640]{2,1,0:T(8,128)S(1)} %get-tuple-element.35), channel_id=1, source_target_pairs={{0,1},{1,0},{2,3},{3,2},{4,5},{5,4},{6,7},{7,6},{8,9},{9,8},{10,11... | collective-permute-start | bytes 491528 | tf_op jit(solution)/shard_map/ppermute | solution.py:322
  104.3 0.6 collective-permute-done.11.refs_0_
  104.8 5.3 %collective-permute-done.12.refs_1_ = s16[64,1408]{1,0:T(8,128)(2,1)S(1)} collective-permute-done((s16[64,1408]{1,0:T(8,128)(2,1)S(1)}, s16[64,1408]{1,0:T(8,128)(2,1)S(1)}, u32[]{:S(2)}, u32[]{:S(2)}) %collective-permute-start.12) | collective-permute-done | bytes 180256 | tf_op jit(solution)/shard_map/ppermute | solution.py:322
  110.1 2.0 %synthesis.2 = (f32[2,32,640]{2,1,0:T(8,128)S(1)}, f32[2,32,640]{2,1,0:T(8,128)S(1)}, f32[2,32,640]{2,1,0:T(8,128)S(1)}, f32[2,32,640]{2,1,0:T(8,128)S(1)}) custom-call(s32[2]{0:T(128)S(1)} %pad_add_fusion.pos, f32[64,1280]{1,0:T(8,128)S(1)} %get-tuple-element.21.own, s16[64,1408]{1,0:T(8,128)(2,1)S(1)} %collective-permute-done.11.refs_0_, ...), custom_call_target="tpu_custom_call" | custom-call | flops 419430400 | bytes 2293760 | tf_op jit(solution)/shard_map/synthesis/pallas_call | solution.py:235
  112.1 0.1 collective-permute-start.14
  112.2 1.6 %collective-permute-start.15 = (f32[2,32,640]{2,1,0:T(8,128)S(1)}, f32[2,32,640]{2,1,0:T(8,128)S(1)}, u32[]{:S(2)}, u32[]{:S(2)}) collective-permute-start(f32[2,32,640]{2,1,0:T(8,128)S(1)} %get-tuple-element.27), channel_id=1, source_target_pairs={{0,1},{1,0},{2,3},{3,2},{4,5},{5,4},{6,7},{7,6},{8,9},{9,8},{10,11... | collective-permute-start | bytes 491528 | tf_op jit(solution)/shard_map/ppermute | solution.py:322
  113.8 0.3 collective-permute-start.16
  114.1 0.7 fusion
  114.7 5.2 %stack.19.dst = s32[8]{0:T(128)S(1)} concatenate(s32[1]{0:T(128)} %get-tuple-element.49, s32[1]{0:T(128)} %get-tuple-element.48, s32[1]{0:T(128)} %get-tuple-element.47, s32[1]{0:T(128)} %get-tuple-element.46, s32[1]{0:T(128)} %get-tuple-element.45, s32[1]{0:T(128)} %get-tuple-element.44, s32[1]{0:T(128)} %get-tuple-element.50, s32[1]{0:T(128)} %get-tuple-element.43), dimensions={0} | concatenate | bytes 64 | tf_op jit(solution)/shard_map/stack | solution.py:354
  119.9 1.9 %collective-permute-done.16.refs_3_ = f32[2,32,640]{2,1,0:T(8,128)S(1)} collective-permute-done((f32[2,32,640]{2,1,0:T(8,128)S(1)}, f32[2,32,640]{2,1,0:T(8,128)S(1)}, u32[]{:S(2)}, u32[]{:S(2)}) %collective-permute-start.16) | collective-permute-done | bytes 163872 | tf_op jit(solution)/shard_map/ppermute | solution.py:322
  121.9 3.4 %place.1 = f32[8,2,32,640]{3,2,1,0:T(8,128)} custom-call(s32[8]{0:T(128)S(1)} %stack.19.dst, f32[2,32,640]{2,1,0:T(8,128)S(1)} %get-tuple-element.25.refs_0_, f32[2,32,640]{2,1,0:T(8,128)S(1)} %collective-permute-done.14.refs_1_, f32[2,32,640]{2,1,0:T(8,128)S(1)} %collective-permute-done.15.refs_2_, f32[2,32,640]{2,1,0:T(8,128)S(1)} %collective-permute-done.16.refs_3_, ...), custom_call_target="tpu_custom_call" | custom-call | tf_op jit(solution)/shard_map/place/pallas_call | solution.py:294
  (48 shorter events, 0.1 us)
Async XLA Ops:
  0.0 4.4 %copy-start.8 = (f32[1,2]{1,0:T(1,128)S(1)}, f32[1,2]{1,0:T(1,128)}, u32[]{:S(2)}) copy-start(f32[1,2]{1,0:T(1,128)} %w_own.3) | copy-start | bytes 28
  0.0 4.9 %copy-start.9 = (bf16[4,32,1280]{2,1,0:T(8,128)(2,1)S(1)}, bf16[4,32,1280]{2,1,0:T(8,128)(2,1)}, u32[]{:S(2)}) copy-start(bf16[4,32,1280]{2,1,0:T(8,128)(2,1)} %param.5) | copy-start | bytes 983044
  4.0 40.9 %collective-permute-start.20 = (bf16[1,2,640,640]{3,2,1,0:T(8,128)(2,1)}, bf16[1,2,640,640]{3,2,1,0:T(8,128)(2,1)S(1)}, u32[]{:S(2)}, u32[]{:S(2)}) collective-permute-start(bf16[1,2,640,640]{3,2,1,0:T(8,128)(2,1)} %get-tuple-element.37), channel_id=1, source_target_pairs={{0,2},{1,3},{2,0},{3,1},{4,6},{5,7},{6,4},{7,5},{8,10},{9,11},{10,... | collective-permute-start | bytes 4915208 | tf_op jit(solution)/shard_map/ppermute | solution.py:322
  4.4 10.5 %collective-permute-start.4 = (f32[1,2]{1,0:T(1,128)S(1)}, f32[1,2]{1,0:T(1,128)S(1)}, u32[]{:S(2)}, u32[]{:S(2)}) collective-permute-start(f32[1,2]{1,0:T(1,128)S(1)} %copy-done.8), channel_id=1, source_target_pairs={{0,2},{1,3},{2,0},{3,1},{4,6},{5,7},{6,4},{7,5},{8,10},{9,11},{10,... | collective-permute-start | bytes 32 | tf_op jit(solution)/shard_map/ppermute | solution.py:322
  4.5 54.8 %collective-permute-start.5 = (bf16[1,2,640,640]{3,2,1,0:T(8,128)(2,1)}, bf16[1,2,640,640]{3,2,1,0:T(8,128)(2,1)S(1)}, u32[]{:S(2)}, u32[]{:S(2)}) collective-permute-start(bf16[1,2,640,640]{3,2,1,0:T(8,128)(2,1)} %get-tuple-element.38), channel_id=1, source_target_pairs={{0,2},{1,3},{2,0},{3,1},{4,6},{5,7},{6,4},{7,5},{8,10},{9,11},{10,... | collective-permute-start | bytes 4915208 | tf_op jit(solution)/shard_map/ppermute | solution.py:322
  5.6 2.7 %collective-permute-start = (bf16[2,32,1280]{2,1,0:T(8,128)(2,1)}, bf16[2,32,1280]{2,1,0:T(8,128)(2,1)}, u32[]{:S(2)}, u32[]{:S(2)}) collective-permute-start(bf16[2,32,1280]{2,1,0:T(8,128)(2,1)} %constant_dynamic-slice_fusion), channel_id=1, source_target_pairs={{0,2},{1,3},{2,0},{3,1},{4,6},{5,7},{6,4},{7,5},{8,10},{9,11},{10,... | collective-permute-start | bytes 491528 | tf_op jit(solution)/shard_map/ppermute | solution.py:322
  9.3 35.5 %copy-start = (bf16[64,1280]{1,0:T(8,128)(2,1)}, bf16[64,1280]{1,0:T(8,128)(2,1)S(1)}, u32[]{:S(2)}) copy-start(bf16[64,1280]{1,0:T(8,128)(2,1)S(1)} %pad_maximum_fusion.1.refs_0_) | copy-start | bytes 491524
  9.3 10.4 %collective-permute-start.17 = (bf16[64,1280]{1,0:T(8,128)(2,1)S(1)}, bf16[64,1280]{1,0:T(8,128)(2,1)}, u32[]{:S(2)}, u32[]{:S(2)}) collective-permute-start(bf16[64,1280]{1,0:T(8,128)(2,1)S(1)} %pad_maximum_fusion.1.refs_0_), channel_id=1, source_target_pairs={{0,8},{1,9},{2,10},{3,11},{4,12},{5,13},{6,14},{7,15},{8,0},{9,1},... | collective-permute-start | bytes 491528 | tf_op jit(solution)/shard_map/ppermute | solution.py:322
  12.3 15.2 %collective-permute-start.18 = (bf16[64,1280]{1,0:T(8,128)(2,1)S(1)}, bf16[64,1280]{1,0:T(8,128)(2,1)}, u32[]{:S(2)}, u32[]{:S(2)}) collective-permute-start(bf16[64,1280]{1,0:T(8,128)(2,1)S(1)} %pad_maximum_fusion.1.refs_0_), channel_id=1, source_target_pairs={{0,16},{1,17},{2,18},{3,19},{4,20},{5,21},{6,22},{7,23},{8,24},{9,... | collective-permute-start | bytes 491528 | tf_op jit(solution)/shard_map/ppermute | solution.py:322
  14.9 12.6 %collective-permute-start.19 = (bf16[64,1280]{1,0:T(8,128)(2,1)S(1)}, bf16[64,1280]{1,0:T(8,128)(2,1)}, u32[]{:S(2)}, u32[]{:S(2)}) collective-permute-start(bf16[64,1280]{1,0:T(8,128)(2,1)S(1)} %pad_maximum_fusion.1.refs_0_), channel_id=1, source_target_pairs={{0,24},{1,25},{2,26},{3,27},{4,28},{5,29},{6,30},{7,31},{8,16},{9,... | collective-permute-start | bytes 491528 | tf_op jit(solution)/shard_map/ppermute | solution.py:322
  19.8 11.7 %collective-permute-start.21 = (bf16[64,1280]{1,0:T(8,128)(2,1)S(1)}, bf16[64,1280]{1,0:T(8,128)(2,1)S(1)}, u32[]{:S(2)}, u32[]{:S(2)}) collective-permute-start(bf16[64,1280]{1,0:T(8,128)(2,1)S(1)} %pad_maximum_fusion.1.refs_0_), channel_id=1, source_target_pairs={{0,4},{1,5},{2,6},{3,7},{4,0},{5,1},{6,2},{7,3},{8,12},{9,13},{10,... | collective-permute-start | bytes 491528 | tf_op jit(solution)/shard_map/ppermute | solution.py:322
  27.5 7.2 %collective-permute-start.1 = (bf16[64,1280]{1,0:T(8,128)(2,1)S(1)}, bf16[64,1280]{1,0:T(8,128)(2,1)S(1)}, u32[]{:S(2)}, u32[]{:S(2)}) collective-permute-start(bf16[64,1280]{1,0:T(8,128)(2,1)S(1)} %pad_maximum_fusion.refs_0_), channel_id=1, source_target_pairs={{0,8},{1,9},{2,10},{3,11},{4,12},{5,13},{6,14},{7,15},{8,0},{9,1},... | collective-permute-start | bytes 491528 | tf_op jit(solution)/shard_map/ppermute | solution.py:322
  27.5 15.8 %collective-permute-start.2 = (bf16[64,1280]{1,0:T(8,128)(2,1)S(1)}, bf16[64,1280]{1,0:T(8,128)(2,1)S(1)}, u32[]{:S(2)}, u32[]{:S(2)}) collective-permute-start(bf16[64,1280]{1,0:T(8,128)(2,1)S(1)} %pad_maximum_fusion.refs_0_), channel_id=1, source_target_pairs={{0,16},{1,17},{2,18},{3,19},{4,20},{5,21},{6,22},{7,23},{8,24},{9,... | collective-permute-start | bytes 491528 | tf_op jit(solution)/shard_map/ppermute | solution.py:322
  31.5 0.7 copy-start.6
  32.1 18.4 %collective-permute-start.3 = (bf16[64,1280]{1,0:T(8,128)(2,1)S(1)}, bf16[64,1280]{1,0:T(8,128)(2,1)}, u32[]{:S(2)}, u32[]{:S(2)}) collective-permute-start(bf16[64,1280]{1,0:T(8,128)(2,1)S(1)} %pad_maximum_fusion.refs_0_), channel_id=1, source_target_pairs={{0,24},{1,25},{2,26},{3,27},{4,28},{5,29},{6,30},{7,31},{8,16},{9,... | collective-permute-start | bytes 491528 | tf_op jit(solution)/shard_map/ppermute | solution.py:322
  34.6 10.2 %copy-start.2 = (bf16[64,1280]{1,0:T(8,128)(2,1)}, bf16[64,1280]{1,0:T(8,128)(2,1)S(1)}, u32[]{:S(2)}) copy-start(bf16[64,1280]{1,0:T(8,128)(2,1)S(1)} %collective-permute-done.1.refs_1_) | copy-start | bytes 491524
  34.6 17.4 %collective-permute-start.22 = (bf16[64,1280]{1,0:T(8,128)(2,1)}, bf16[64,1280]{1,0:T(8,128)(2,1)}, u32[]{:S(2)}, u32[]{:S(2)}) collective-permute-start(bf16[64,1280]{1,0:T(8,128)(2,1)} %collective-permute-done.17.refs_1_), channel_id=1, source_target_pairs={{0,4},{1,5},{2,6},{3,7},{4,0},{5,1},{6,2},{7,3},{8,12},{9,13},{10,... | collective-permute-start | bytes 491528 | tf_op jit(solution)/shard_map/ppermute | solution.py:322
  43.3 1.5 %copy-start.4 = (bf16[64,1280]{1,0:T(8,128)(2,1)}, bf16[64,1280]{1,0:T(8,128)(2,1)S(1)}, u32[]{:S(2)}) copy-start(bf16[64,1280]{1,0:T(8,128)(2,1)S(1)} %collective-permute-done.2.refs_2_) | copy-start | bytes 491524
  43.3 9.3 %collective-permute-start.23 = (bf16[64,1280]{1,0:T(8,128)(2,1)}, bf16[64,1280]{1,0:T(8,128)(2,1)}, u32[]{:S(2)}, u32[]{:S(2)}) collective-permute-start(bf16[64,1280]{1,0:T(8,128)(2,1)} %collective-permute-done.18.refs_2_), channel_id=1, source_target_pairs={{0,4},{1,5},{2,6},{3,7},{4,0},{5,1},{6,2},{7,3},{8,12},{9,13},{10,... | collective-permute-start | bytes 491528 | tf_op jit(solution)/shard_map/ppermute | solution.py:322
  44.9 9.2 %collective-permute-start.24 = (bf16[64,1280]{1,0:T(8,128)(2,1)}, bf16[64,1280]{1,0:T(8,128)(2,1)}, u32[]{:S(2)}, u32[]{:S(2)}) collective-permute-start(bf16[64,1280]{1,0:T(8,128)(2,1)} %collective-permute-done.19.refs_3_), channel_id=1, source_target_pairs={{0,4},{1,5},{2,6},{3,7},{4,0},{5,1},{6,2},{7,3},{8,12},{9,13},{10,... | collective-permute-start | bytes 491528 | tf_op jit(solution)/shard_map/ppermute | solution.py:322
  45.6 6.4 %copy-start.3 = (bf16[64,1280]{1,0:T(8,128)(2,1)S(1)}, bf16[64,1280]{1,0:T(8,128)(2,1)}, u32[]{:S(2)}) copy-start(bf16[64,1280]{1,0:T(8,128)(2,1)} %copy-done.2) | copy-start | bytes 491524
  45.6 7.0 %copy-start.5 = (bf16[64,1280]{1,0:T(8,128)(2,1)S(1)}, bf16[64,1280]{1,0:T(8,128)(2,1)}, u32[]{:S(2)}) copy-start(bf16[64,1280]{1,0:T(8,128)(2,1)} %copy-done.4) | copy-start | bytes 491524
  45.6 9.1 %copy-start.7 = (bf16[64,1280]{1,0:T(8,128)(2,1)S(1)}, bf16[64,1280]{1,0:T(8,128)(2,1)}, u32[]{:S(2)}) copy-start(bf16[64,1280]{1,0:T(8,128)(2,1)} %copy-done.6) | copy-start | bytes 491524
  50.5 15.2 %collective-permute-start.6 = (bf16[64,1280]{1,0:T(8,128)(2,1)S(1)}, bf16[64,1280]{1,0:T(8,128)(2,1)S(1)}, u32[]{:S(2)}, u32[]{:S(2)}) collective-permute-start(bf16[64,1280]{1,0:T(8,128)(2,1)S(1)} %pad_maximum_fusion.refs_0_), channel_id=1, source_target_pairs={{0,4},{1,5},{2,6},{3,7},{4,0},{5,1},{6,2},{7,3},{8,12},{9,13},{10,... | collective-permute-start | bytes 491528 | tf_op jit(solution)/shard_map/ppermute | solution.py:322
  52.0 13.7 %collective-permute-start.7 = (bf16[64,1280]{1,0:T(8,128)(2,1)S(1)}, bf16[64,1280]{1,0:T(8,128)(2,1)S(1)}, u32[]{:S(2)}, u32[]{:S(2)}) collective-permute-start(bf16[64,1280]{1,0:T(8,128)(2,1)S(1)} %copy-done.3), channel_id=1, source_target_pairs={{0,4},{1,5},{2,6},{3,7},{4,0},{5,1},{6,2},{7,3},{8,12},{9,13},{10,... | collective-permute-start | bytes 491528 | tf_op jit(solution)/shard_map/ppermute | solution.py:322
  52.6 13.1 %collective-permute-start.8 = (bf16[64,1280]{1,0:T(8,128)(2,1)S(1)}, bf16[64,1280]{1,0:T(8,128)(2,1)S(1)}, u32[]{:S(2)}, u32[]{:S(2)}) collective-permute-start(bf16[64,1280]{1,0:T(8,128)(2,1)S(1)} %copy-done.5), channel_id=1, source_target_pairs={{0,4},{1,5},{2,6},{3,7},{4,0},{5,1},{6,2},{7,3},{8,12},{9,13},{10,... | collective-permute-start | bytes 491528 | tf_op jit(solution)/shard_map/ppermute | solution.py:322
  54.1 14.2 %collective-permute-start.9 = (bf16[64,1280]{1,0:T(8,128)(2,1)}, bf16[64,1280]{1,0:T(8,128)(2,1)S(1)}, u32[]{:S(2)}, u32[]{:S(2)}) collective-permute-start(bf16[64,1280]{1,0:T(8,128)(2,1)} %collective-permute-done.3.refs_3_), channel_id=1, source_target_pairs={{0,4},{1,5},{2,6},{3,7},{4,0},{5,1},{6,2},{7,3},{8,12},{9,13},{10,... | collective-permute-start | bytes 491528 | tf_op jit(solution)/shard_map/ppermute | solution.py:322
  59.3 24.4 %collective-permute-start.25 = (s16[256,1408]{1,0:T(8,128)(2,1)S(1)}, s16[256,1408]{1,0:T(8,128)(2,1)S(1)}, u32[]{:S(2)}, u32[]{:S(2)}) collective-permute-start(s16[256,1408]{1,0:T(8,128)(2,1)S(1)} %product.7), channel_id=1, source_target_pairs={{0,4},{1,5},{2,6},{3,7},{4,0},{5,1},{6,2},{7,3},{8,12},{9,13},{10,... | collective-permute-start | bytes 2162696 | tf_op jit(solution)/shard_map/ppermute | solution.py:322
  68.3 5.1 %copy-start.1 = (bf16[64,1280]{1,0:T(8,128)(2,1)S(1)}, bf16[64,1280]{1,0:T(8,128)(2,1)}, u32[]{:S(2)}) copy-start(bf16[64,1280]{1,0:T(8,128)(2,1)} %copy-done) | copy-start | bytes 491524
  71.9 23.7 %collective-permute-start.10 = (s16[256,1408]{1,0:T(8,128)(2,1)S(1)}, s16[256,1408]{1,0:T(8,128)(2,1)S(1)}, u32[]{:S(2)}, u32[]{:S(2)}) collective-permute-start(s16[256,1408]{1,0:T(8,128)(2,1)S(1)} %product.5), channel_id=1, source_target_pairs={{0,4},{1,5},{2,6},{3,7},{4,0},{5,1},{6,2},{7,3},{8,12},{9,13},{10,... | collective-permute-start | bytes 2162696 | tf_op jit(solution)/shard_map/ppermute | solution.py:322
  83.7 16.9 %slice-start = ((s8[6553600]{0:T(1024)(128)(4,1)}), s8[4194304]{0:T(1024)(128)(4,1)S(1)}, s32[]{:S(2)}) async-start(s8[6553600]{0:T(1024)(128)(4,1)} %bitcast.21), calls=%async_computation | async-start | bytes 8388608
  84.4 12.0 %collective-permute-start.26 = (s16[64,1408]{1,0:T(8,128)(2,1)S(1)}, s16[64,1408]{1,0:T(8,128)(2,1)S(1)}, u32[]{:S(2)}, u32[]{:S(2)}) collective-permute-start(s16[64,1408]{1,0:T(8,128)(2,1)S(1)} %get-tuple-element.30), channel_id=1, source_target_pairs={{0,8},{1,9},{2,10},{3,11},{4,12},{5,13},{6,14},{7,15},{8,0},{9,1},... | collective-permute-start | bytes 540680 | tf_op jit(solution)/shard_map/ppermute | solution.py:322
  84.4 16.2 %collective-permute-start.27 = (s16[64,1408]{1,0:T(8,128)(2,1)S(1)}, s16[64,1408]{1,0:T(8,128)(2,1)S(1)}, u32[]{:S(2)}, u32[]{:S(2)}) collective-permute-start(s16[64,1408]{1,0:T(8,128)(2,1)S(1)} %get-tuple-element.31), channel_id=1, source_target_pairs={{0,16},{1,17},{2,18},{3,19},{4,20},{5,21},{6,22},{7,23},{8,24},{9,... | collective-permute-start | bytes 540680 | tf_op jit(solution)/shard_map/ppermute | solution.py:322
  86.5 14.1 %slice-start.1 = ((s8[6553600]{0:T(1024)(128)(4,1)}), s8[2359296]{0:T(1024)(128)(4,1)S(1)}, s32[]{:S(2)}) async-start(s8[6553600]{0:T(1024)(128)(4,1)} %bitcast.21), calls=%async_computation.1 | async-start | bytes 4718592
  86.5 14.1 %collective-permute-start.28 = (s16[64,1408]{1,0:T(8,128)(2,1)S(1)}, s16[64,1408]{1,0:T(8,128)(2,1)S(1)}, u32[]{:S(2)}, u32[]{:S(2)}) collective-permute-start(s16[64,1408]{1,0:T(8,128)(2,1)S(1)} %get-tuple-element.32), channel_id=1, source_target_pairs={{0,24},{1,25},{2,26},{3,27},{4,28},{5,29},{6,30},{7,31},{8,16},{9,... | collective-permute-start | bytes 540680 | tf_op jit(solution)/shard_map/ppermute | solution.py:322
  96.2 8.7 %collective-permute-start.11 = (s16[64,1408]{1,0:T(8,128)(2,1)S(1)}, s16[64,1408]{1,0:T(8,128)(2,1)S(1)}, u32[]{:S(2)}, u32[]{:S(2)}) collective-permute-start(s16[64,1408]{1,0:T(8,128)(2,1)S(1)} %get-tuple-element.22), channel_id=1, source_target_pairs={{0,8},{1,9},{2,10},{3,11},{4,12},{5,13},{6,14},{7,15},{8,0},{9,1},... | collective-permute-start | bytes 540680 | tf_op jit(solution)/shard_map/ppermute | solution.py:322
  96.3 13.9 %collective-permute-start.12 = (s16[64,1408]{1,0:T(8,128)(2,1)S(1)}, s16[64,1408]{1,0:T(8,128)(2,1)S(1)}, u32[]{:S(2)}, u32[]{:S(2)}) collective-permute-start(s16[64,1408]{1,0:T(8,128)(2,1)S(1)} %get-tuple-element.23), channel_id=1, source_target_pairs={{0,16},{1,17},{2,18},{3,19},{4,20},{5,21},{6,22},{7,23},{8,24},{9,... | collective-permute-start | bytes 540680 | tf_op jit(solution)/shard_map/ppermute | solution.py:322
  96.4 13.8 %collective-permute-start.13 = (s16[64,1408]{1,0:T(8,128)(2,1)S(1)}, s16[64,1408]{1,0:T(8,128)(2,1)S(1)}, u32[]{:S(2)}, u32[]{:S(2)}) collective-permute-start(s16[64,1408]{1,0:T(8,128)(2,1)S(1)} %get-tuple-element.24), channel_id=1, source_target_pairs={{0,24},{1,25},{2,26},{3,27},{4,28},{5,29},{6,30},{7,31},{8,16},{9,... | collective-permute-start | bytes 540680 | tf_op jit(solution)/shard_map/ppermute | solution.py:322
  102.6 11.1 %collective-permute-start.29 = (f32[2,32,640]{2,1,0:T(8,128)S(1)}, f32[2,32,640]{2,1,0:T(8,128)S(1)}, u32[]{:S(2)}, u32[]{:S(2)}) collective-permute-start(f32[2,32,640]{2,1,0:T(8,128)S(1)} %get-tuple-element.34), channel_id=1, source_target_pairs={{0,2},{1,3},{2,0},{3,1},{4,6},{5,7},{6,4},{7,5},{8,10},{9,11},{10,... | collective-permute-start | bytes 491528 | tf_op jit(solution)/shard_map/ppermute | solution.py:322
  102.7 17.2 %collective-permute-start.30 = (f32[2,32,640]{2,1,0:T(8,128)S(1)}, f32[2,32,640]{2,1,0:T(8,128)S(1)}, u32[]{:S(2)}, u32[]{:S(2)}) collective-permute-start(f32[2,32,640]{2,1,0:T(8,128)S(1)} %get-tuple-element.35), channel_id=1, source_target_pairs={{0,1},{1,0},{2,3},{3,2},{4,5},{5,4},{6,7},{7,6},{8,9},{9,8},{10,11... | collective-permute-start | bytes 491528 | tf_op jit(solution)/shard_map/ppermute | solution.py:322
  104.8 15.0 %collective-permute-start.31 = (f32[2,32,640]{2,1,0:T(8,128)S(1)}, f32[2,32,640]{2,1,0:T(8,128)S(1)}, u32[]{:S(2)}, u32[]{:S(2)}) collective-permute-start(f32[2,32,640]{2,1,0:T(8,128)S(1)} %get-tuple-element.36), channel_id=1, source_target_pairs={{0,3},{1,2},{2,1},{3,0},{4,7},{5,6},{6,5},{7,4},{8,11},{9,10},{10,... | collective-permute-start | bytes 491528 | tf_op jit(solution)/shard_map/ppermute | solution.py:322
  110.1 3.9 %copy-start.10 = (s32[8]{0:T(128)S(1)}, s32[8]{0:T(128)}, u32[]{:S(2)}) copy-start(s32[8]{0:T(128)} %param.9) | copy-start | bytes 100
  112.1 7.8 %collective-permute-start.14 = (f32[2,32,640]{2,1,0:T(8,128)S(1)}, f32[2,32,640]{2,1,0:T(8,128)S(1)}, u32[]{:S(2)}, u32[]{:S(2)}) collective-permute-start(f32[2,32,640]{2,1,0:T(8,128)S(1)} %get-tuple-element.26), channel_id=1, source_target_pairs={{0,2},{1,3},{2,0},{3,1},{4,6},{5,7},{6,4},{7,5},{8,10},{9,11},{10,... | collective-permute-start | bytes 491528 | tf_op jit(solution)/shard_map/ppermute | solution.py:322
  112.2 7.7 %collective-permute-start.15 = (f32[2,32,640]{2,1,0:T(8,128)S(1)}, f32[2,32,640]{2,1,0:T(8,128)S(1)}, u32[]{:S(2)}, u32[]{:S(2)}) collective-permute-start(f32[2,32,640]{2,1,0:T(8,128)S(1)} %get-tuple-element.27), channel_id=1, source_target_pairs={{0,1},{1,0},{2,3},{3,2},{4,5},{5,4},{6,7},{7,6},{8,9},{9,8},{10,11... | collective-permute-start | bytes 491528 | tf_op jit(solution)/shard_map/ppermute | solution.py:322
  113.8 8.1 %collective-permute-start.16 = (f32[2,32,640]{2,1,0:T(8,128)S(1)}, f32[2,32,640]{2,1,0:T(8,128)S(1)}, u32[]{:S(2)}, u32[]{:S(2)}) collective-permute-start(f32[2,32,640]{2,1,0:T(8,128)S(1)} %get-tuple-element.28), channel_id=1, source_target_pairs={{0,3},{1,2},{2,1},{3,0},{4,7},{5,6},{6,5},{7,4},{8,11},{9,10},{10,... | collective-permute-start | bytes 491528 | tf_op jit(solution)/shard_map/ppermute | solution.py:322

commit v2 on v0

v2 whole, which is shorter than its diff:
```python
import functools

import jax
import jax.numpy as jnp
from jax import lax
from jax.experimental import pallas as pl
from jax.experimental.pallas import tpu as pltpu
from jax.sharding import PartitionSpec as P

F32, BF16, I16, I32 = jnp.float32, jnp.bfloat16, jnp.int16, jnp.int32
LANES = 128
TAIL = 16
STEPS = 64.0
TOP = 32000.0
TINY = 1e-30


def params(mib=48):
    return pltpu.CompilerParams(vmem_limit_bytes=mib * 2**20)


def split(x):
    hi = x.astype(BF16)
    return hi, (x - hi.astype(F32)).astype(BF16)


def encode(x):
    top = jnp.maximum(jnp.max(jnp.abs(x), axis=0, keepdims=True), TINY)
    step = jnp.ceil(jnp.log2(top * (1.0 / TOP)) * STEPS)
    code = jnp.round(x * jnp.exp2(step * (-1.0 / STEPS)))
    return code.astype(I32).astype(I16), step


def put_row(tail, row, values):
    at = lax.broadcasted_iota(I32, tail.shape, 0)
    return jnp.where(at == row, values, tail)


def scales(tail):
    return jnp.exp2(tail.astype(I32).astype(F32) * (1.0 / STEPS))


def take_row(table, row):
    at = lax.broadcasted_iota(I32, table.shape, 0)
    return jnp.sum(jnp.where(at == row, table, 0.0), axis=0, keepdims=True)


def message(strips, rows):
    return jax.ShapeDtypeStruct((strips * rows + TAIL, LANES), I16)


def whole(shape):
    return pl.BlockSpec(shape, lambda *_: (0,) * len(shape))


def weighted(w_own, w_got, own, got):
    real = imag = 0.0
    for k in range(own.shape[0]):
        for w, block in ((w_own, own[k, 0]), (w_got, got[k])):
            r, j = block[0].astype(F32), block[1].astype(F32)
            real += w[k, 0] * r - w[k, 1] * j
            imag += w[k, 0] * j + w[k, 1] * r
    return real, imag


def share_kernel(pos, w_own, w_got, own, got, out, tail):
    t = pl.program_id(0)
    size = own.shape[3]
    end = out.shape[0] - TAIL

    @pl.when(t == 0)
    def _():
        tail[...] = jnp.zeros_like(tail)

    for part, value in enumerate(weighted(w_own, w_got, own, got)):
        strip = 2 * t + part
        code, step = encode(value)
        out[pl.ds(pl.multiple_of(strip * size, TAIL), size), :] = code
        tail[...] = put_row(tail[...], strip, step)

    @pl.when(t == pl.num_programs(0) - 1)
    def _():
        out[end:, :] = tail[...].astype(I32).astype(I16)


def own_kernel(pos, w_own, w_got, own, got, out):
    for part, value in enumerate(weighted(w_own, w_got, own, got)):
        out[0, part] = value


def operator(slot, w_own, w_got, inverse, got, first, count, coded):
    terms, _, _, size, _ = inverse.shape
    smem = pl.BlockSpec(memory_space=pltpu.SMEM)
    if coded:
        out_shape = message(2 * count, size)
        out_spec = whole(out_shape.shape)
    else:
        out_shape = jax.ShapeDtypeStruct((count, 2, size, LANES), F32)
        out_spec = pl.BlockSpec((1, 2, size, LANES), lambda t, slot: (t, 0, 0, 0))
    return pl.pallas_call(
        share_kernel if coded else own_kernel,
        out_shape=out_shape,
        grid_spec=pltpu.PrefetchScalarGridSpec(
            num_scalar_prefetch=1,
            grid=(count,),
            in_specs=[
                smem,
                smem,
                pl.BlockSpec(
                    (terms, 1, 2, size, LANES), lambda t, slot: (0, slot[0], 0, 0, t + first)
                ),
                pl.BlockSpec((terms, 2, size, LANES), lambda t, slot: (0, 0, 0, t + first)),
            ],
            out_specs=out_spec,
            scratch_shapes=[pltpu.VMEM((TAIL, LANES), F32)] if coded else [],
        ),
        compiler_params=params(),
        cost_estimate=pl.CostEstimate(
            flops=32 * terms * size * LANES * count,
            bytes_accessed=16 * size * LANES * count,
            transcendentals=0,
        ),
        name="share" if coded else "operator",
    )(slot, w_own, w_got, inverse, got)


def product_kernel(count, tiles, *refs):
    parts, own, got = refs[:count], refs[count], refs[count + 1]
    near, sends = refs[count + 2], refs[count + 3 : 2 * count + 2]
    full, op, tails = refs[2 * count + 2 :]
    rows, width = parts[0].shape
    size = width // 2
    t = pl.program_id(0)

    @pl.when(t == 0)
    def _():
        tails[...] = jnp.zeros_like(tails)
        for i, part in enumerate(parts):
            full[i * rows : (i + 1) * rows, :] = part[...]

    table = scales(got[2 * tiles * size :, :])
    pair = []
    for part in range(2):
        strip = 2 * t + part
        code = got[pl.ds(pl.multiple_of(strip * size, TAIL), size), :]
        pair.append(own[0, part] + code.astype(I32).astype(F32) * take_row(table, strip))
    for level, (r, j) in enumerate(zip(split(pair[0]), split(pair[1]))):
        op[level, :size, :LANES] = r
        op[level, :size, LANES:] = j
        op[level, size:, :LANES] = -j
        op[level, size:, LANES:] = r
    x = full[...]
    acc = jnp.dot(x, op[0], preferred_element_type=F32)
    acc += jnp.dot(x, op[1], preferred_element_type=F32)
    near[0] = acc[:rows]
    for q in range(1, count):
        for part in range(2):
            strip = 2 * t + part
            block = acc[q * rows : (q + 1) * rows, part * LANES : (part + 1) * LANES]
            code, step = encode(block)
            sends[q - 1][pl.ds(pl.multiple_of(strip * rows, TAIL), rows), :] = code
            tails[q - 1] = put_row(tails[q - 1], strip, step)

    @pl.when(t == tiles - 1)
    def _():
        for q in range(1, count):
            sends[q - 1][2 * tiles * rows :, :] = tails[q - 1].astype(I32).astype(I16)


def product(parts, own, got, first, tiles):
    count = len(parts)
    rows, width = parts[0].shape
    size = width // 2
    send = message(2 * tiles, rows)
    return pl.pallas_call(
        functools.partial(product_kernel, count, tiles),
        out_shape=[jax.ShapeDtypeStruct((tiles, rows, 2 * LANES), F32)] + [send] * (count - 1),
        grid=(tiles,),
        in_specs=[whole((rows, width))] * count
        + [
            pl.BlockSpec((1, 2, size, LANES), lambda t: (t + first, 0, 0, 0)),
            whole(got.shape),
        ],
        out_specs=[pl.BlockSpec((1, rows, 2 * LANES), lambda t: (t, 0, 0))]
        + [whole(send.shape)] * (count - 1),
        scratch_shapes=[
            pltpu.VMEM((count * rows, width), BF16),
            pltpu.VMEM((2, width, 2 * LANES), BF16),
            pltpu.VMEM((count - 1, TAIL, LANES), F32),
        ],
        compiler_params=params(),
        cost_estimate=pl.CostEstimate(
            flops=8 * count * rows * width * tiles * LANES,
            bytes_accessed=12 * size * LANES * tiles + 2 * count * rows * width,
            transcendentals=0,
        ),
        name="product",
    )(*parts, own, got)


def add_up(near, got, write):
    base = 0
    for own, parts in zip(near, got):
        tiles, rows, _ = own.shape
        tables = [scales(part[2 * tiles * rows :, :]) for part in parts]
        for t in range(tiles):
            for part in range(2):
                strip = 2 * t + part
                total = own[t, :, part * LANES : (part + 1) * LANES]
                for ref, table in zip(parts, tables):
                    code = ref[strip * rows : (strip + 1) * rows, :]
                    total += code.astype(I32).astype(F32) * table[strip : strip + 1, :]
                write(base + t, part, total)
        base += tiles


def unpack(refs, chunks, count):
    near = refs[:chunks]
    got = [refs[chunks + i * count : chunks + (i + 1) * count] for i in range(chunks)]
    return near, got, refs[chunks * (1 + count) :]


def synthesis_kernel(bands, chunks, count, pos, *refs):
    near, got, rest = unpack(refs, chunks, count)
    table, outs, values = rest[0], rest[1:-1], rest[-1]
    rows = near[0].shape[1]
    band = pl.program_id(0)

    @pl.when(band == 0)
    def _():
        def write(tile, part, total):
            for level, value in enumerate(split(total)):
                values[
                    level, part * rows : (part + 1) * rows, tile * LANES : (tile + 1) * LANES
                ] = value

        add_up(near, got, write)

    grid = jnp.dot(values[0], table[0], preferred_element_type=F32)
    grid += jnp.dot(values[1], table[0], preferred_element_type=F32)
    quarter = rows // 4
    for d in range(bands):

        @pl.when(band == d)
        def _():
            for side in range(4):
                for part in range(2):
                    start = part * rows + side * quarter
                    outs[4 * d + side][part] = grid[start : start + quarter]


def synthesis(pos, near, got, legendre, bands):
    rows = near[0].shape[1]
    size, nlat = legendre.shape[1:]
    band = nlat // bands
    piece = (2, rows // 4, band)
    operands = list(near) + [part for parts in got for part in parts]
    return pl.pallas_call(
        functools.partial(synthesis_kernel, bands, len(near), len(got[0])),
        out_shape=[jax.ShapeDtypeStruct(piece, F32)] * (4 * bands),
        grid_spec=pltpu.PrefetchScalarGridSpec(
            num_scalar_prefetch=1,
            grid=(bands,),
            in_specs=[whole(x.shape) for x in operands]
            + [pl.BlockSpec((1, size, band), lambda b, pos: (pos[0], 0, pos[1] ^ b))],
            out_specs=[whole(piece)] * (4 * bands),
            scratch_shapes=[pltpu.VMEM((2, 2 * rows, size), BF16)],
        ),
        compiler_params=params(),
        cost_estimate=pl.CostEstimate(
            flops=8 * rows * size * nlat,
            bytes_accessed=2 * size * nlat + 8 * rows * nlat,
            transcendentals=0,
        ),
        name="synthesis",
    )(pos, *operands, legendre)


def total_kernel(chunks, count, *refs):
    near, got, (out,) = unpack(refs, chunks, count)

    def write(tile, part, total):
        out[part, :, tile * LANES : (tile + 1) * LANES] = total

    add_up(near, got, write)


def plain_synthesis(pos, near, got, legendre, bands):
    rows = near[0].shape[1]
    size, nlat = legendre.shape[1:]
    total = pl.pallas_call(
        functools.partial(total_kernel, len(near), len(got[0])),
        out_shape=jax.ShapeDtypeStruct((2, rows, size), F32),
        compiler_params=params(),
        name="total",
    )(*near, *[part for parts in got for part in parts])
    table = lax.dynamic_index_in_dim(legendre, pos[0], 0, keepdims=False)
    grid = sum(
        jnp.einsum("pcn,nl->pcl", v, table, preferred_element_type=F32) for v in split(total)
    )
    quarter, band = rows // 4, nlat // bands
    return [
        lax.dynamic_slice(grid, (0, side * quarter, (pos[1] ^ d) * band), (2, quarter, band))
        for d in range(bands)
        for side in range(4)
    ]


def place_kernel(count, dst, *refs):
    pieces, out = refs[:count], refs[count]
    for i in range(count):

        @pl.when(pl.program_id(0) == i)
        def _():
            out[0] = pieces[i][...]


def place(dst, pieces):
    count = len(pieces)
    shape = pieces[0].shape
    return pl.pallas_call(
        functools.partial(place_kernel, count),
        out_shape=jax.ShapeDtypeStruct((count,) + shape, F32),
        grid_spec=pltpu.PrefetchScalarGridSpec(
            num_scalar_prefetch=1,
            grid=(count,),
            in_specs=[whole(shape)] * count,
            out_specs=pl.BlockSpec((1,) + shape, lambda i, dst: (dst[i], 0, 0, 0)),
        ),
        compiler_params=params(),
        name="place",
    )(dst, *pieces)


def shards(mesh, spectral_state, inverse, term_weights, legendre, slot_column):
    terms, waves = mesh.shape["term"], mesh.shape["wave"]
    slots, cols, width = spectral_state.shape
    size = width // 2
    outer = terms // 4
    me, wave = lax.axis_index("term"), lax.axis_index("wave")
    place_of = me % 4
    turn = slots // 4

    def swap(x, term_bits, wave_bits=0):
        pairs = [
            (t * waves + w, (t ^ term_bits) * waves + (w ^ wave_bits))
            for t in range(terms)
            for w in range(waves)
        ]
        return lax.ppermute(x, ("term", "wave"), pairs)

    tiles = size // LANES
    cut = (tiles + 1) // 2
    chunks = [(0, cut), (cut, tiles - cut)] if tiles > 1 else [(0, tiles)]

    pieces = []
    for j in range(turn):
        slot_of = lambda bits: (place_of ^ bits) * turn + j
        state_of = lambda bits: lax.dynamic_index_in_dim(
            spectral_state, slot_of(bits), 0, keepdims=False
        )
        block = jnp.concatenate(
            [state_of(0)] + [swap(state_of(bits), bits) for bits in range(1, 4)], axis=0
        )
        parts = [block] + [swap(block, q * 4) for q in range(1, outer)]

        w_got = swap(term_weights, 1)
        from_core = lambda bits: swap(
            lax.dynamic_index_in_dim(inverse, slot_of(bits ^ 1), 1, keepdims=False), 1
        )
        far, own = from_core(2), from_core(0)
        scalar = lambda x: jnp.reshape(x, (1,)).astype(I32)
        shares = [
            swap(
                operator(scalar(slot_of(2)), term_weights, w_got, inverse, far, *chunk, True), 2
            )
            for chunk in chunks
        ]
        mine = operator(scalar(slot_of(0)), term_weights, w_got, inverse, own, 0, tiles, False)
        near, got = [], []
        for chunk, share in zip(chunks, shares):
            made = product(parts, mine, share, *chunk)
            near.append(made[0])
            got.append([swap(made[q], q * 4) for q in range(1, outer)])
        pos = jnp.stack([slot_of(0), wave]).astype(I32)
        make = synthesis if legendre.shape[2] // waves % LANES == 0 else plain_synthesis
        grid = make(pos, near, got, legendre, waves)
        for d in range(waves):
            for bits in range(4):
                piece = grid[4 * d + bits]
                if d or bits:
                    piece = swap(piece, bits, d)
                pieces.append(((wave ^ d) * slots + slot_of(bits), piece))

    at = jnp.stack([slot for slot, _ in pieces])
    return place(slot_column[at], [piece for _, piece in pieces])


def solution(mesh):
    return jax.shard_map(
        functools.partial(shards, mesh),
        mesh=mesh,
        in_specs=(
            P("wave", "term", None),
            P("term", "wave", None, None, None),
            P("term", None),
            P("wave", None, None),
            P(),
        ),
        out_specs=P(None, None, "term", "wave"),
        check_vma=False,
    )
```

time: 285 us -> 150 us (0.53)
  waiting for transfers between devices: 178 us -> 96.2 us
  local copies, waits for them, and re-layouts: 33.5 us -> 4.68 us
  starting transfers between devices: 0.04 us -> 26.2 us
  Pallas kernels: 0 us -> 21.8 us
  matrix products: 21.6 us -> 0 us
  blocking collectives: 19.1 us -> 0 us
  other arithmetic: 18.3 us -> 0.11 us
  between operations: 13.5 us -> 0.15 us
    reduce_scatter x1 -> x0, waiting for transfers between devices: 118 us -> none  [shards(): lax.psum_scatter(partial_value, 'term', scatter_dimension=2, tiled=True)]
    ppermute x0 -> x24, waiting for transfers between devices: none -> 96.2 us  [swap(): return lax.ppermute(x, ('term', 'wave'), pairs)]
    all_gather x1 -> x0, waiting for transfers between devices: 59.8 us -> none  [shards(): whole = lax.all_gather(spectral_state, 'term', axis=1, tiled=True)]
    ppermute x0 -> x24, starting transfers between devices: none -> 26.2 us  [swap(): return lax.ppermute(x, ('term', 'wave'), pairs)]
    pallas_call x0 -> x7, Pallas kernels: none -> 21.8 us  [the longest x3 8.16 us: operator(): pl.pallas_call(share_kernel if coded else own_kernel, out_shape=out_shape...]
    dot_general x4 -> x0, matrix products: 21.6 us -> none  [the longest x1 7.29 us: shards(): jnp.einsum('srn,ksno->ksro', stacked, inverse[:, :, 1], preferred_element...]
    all_to_all x1 -> x0, blocking collectives: 19.1 us -> none  [shards(): lax.all_to_all(grid, 'wave', split_axis=3, concat_axis=0, tiled=True)]
    unnamed x6 -> x8, local copies, waits for them, and re-layouts: 15.3 us -> 0.02 us
  transfers between devices with their start and end apart: 2 -> 24, of which waited for: 2 -> 12; matrix products, arithmetic and copies ran while one was open for 0% -> 1% of each run, Pallas kernels for 0% -> 10%
where the time goes in v2:
time: 150 us; the launch traced here: 149 us
  waiting for transfers between devices  96.2 us (64%)
  starting transfers between devices  26.2 us (17%)
  Pallas kernels  21.8 us (15%)
  local copies, waits for them, and re-layouts  4.68 us (3%)
    ppermute x24, waiting for transfers between devices, swap(): return lax.ppermute(x, ('term', 'wave'), pairs)  96.2 us
    ppermute x24, starting transfers between devices, swap(): return lax.ppermute(x, ('term', 'wave'), pairs)  26.2 us
    pallas_call x3, Pallas kernels, operator(): pl.pallas_call(share_kernel if coded else own_kernel, out_shape=out_shape...  8.16 us
    pallas_call x2, Pallas kernels, product(): pl.pallas_call(functools.partial(product_kernel, count, tiles), out_shape...  6.6 us
    squeeze x1, local copies, waits for them, and re-layouts, shards(): lax.dynamic_index_in_dim(inverse, slot_of(bits ^ 1), 1, keepdims=False)  3.9 us
    pallas_call x1, Pallas kernels, synthesis(): pl.pallas_call(functools.partial(synthesis_kernel, bands, len(near), len(...  3.66 us
    pallas_call x1, Pallas kernels, place(): pl.pallas_call(functools.partial(place_kernel, count), out_shape=jax.Shap...  3.42 us
  transfers between devices with their start and end apart: 24, of which 12 were waited for; matrix products, arithmetic and copies ran while one was open for 1% of the time, Pallas kernels for 10%

profile of v2, /device:TPU:0, one launch (start us, length us, event | category | flops | bytes accessed | tf_op | source)
XLA Modules:
  0.0 149.2 jit_solution(9121880031204413893)
XLA Ops:
  0.0 0.0 copy-start
  0.0 3.9 %dynamic-slice_bitcast_fusion = (bf16[1,2,640,640]{3,2,1,0:T(8,128)(2,1)}, bf16[1,2,640,640]{3,2,1,0:T(8,128)(2,1)}) fusion(bf16[1,4,2,640,640]{4,3,2,1,0:T(8,128)(2,1)} %own.5, s32[]{:T(128)S(6)} %select_n.38, s32[]{:T(128)S(6)} %select_n.36), kind=kLoop, calls=%fused_computation.1 | loop fusion | bytes 6553608 | tf_op jit(solution)/shard_map/jit(dynamic_index_in_dim)/squeeze | solution.py:369
  3.9 0.5 collective-permute-start.8
  4.4 0.1 collective-permute-start.7
  4.4 0.0 copy-done.2
  4.4 0.5 collective-permute-start.6
  4.9 2.6 %collective-permute-done.6.w_got = f32[1,2]{1,0:T(1,128)S(1)} collective-permute-done((f32[1,2]{1,0:T(1,128)S(1)}, f32[1,2]{1,0:T(1,128)S(1)}, u32[]{:S(2)}, u32[]{:S(2)}) %collective-permute-start.6) | collective-permute-done | bytes 40 | tf_op jit(solution)/shard_map/ppermute | solution.py:350
  7.5 0.2 collective-permute-done.8.got
  7.7 2.7 %share.2 = s16[3856,128]{1,0:T(8,128)(2,1)S(1)} custom-call(s32[1]{0:T(128)} %bitcast.16.pos, f32[1,2]{1,0:T(1,128)S(1)} %copy-done.2, f32[1,2]{1,0:T(1,128)S(1)} %collective-permute-done.6.w_got, bf16[1,4,2,640,640]{4,3,2,1,0:T(8,128)(2,1)} %own.5, bf16[1,2,640,640]{3,2,1,0:T(8,128)(2,1)S(1)} %collective-permute-done.8.got), custom_call_target="tpu_custom_call" | custom-call | flops 7864320 | bytes 3932160 | tf_op jit(solution)/shard_map/share/pallas_call | solution.py:100
  10.4 3.0 %collective-permute-start.9 = (s16[3856,128]{1,0:T(8,128)(2,1)S(1)}, s16[3856,128]{1,0:T(8,128)(2,1)S(1)}, u32[]{:S(2)}, u32[]{:S(2)}) collective-permute-start(s16[3856,128]{1,0:T(8,128)(2,1)S(1)} %share.2), channel_id=1, source_target_pairs={{0,4},{1,5},{2,6},{3,7},{4,0},{5,1},{6,2},{7,3},{8,12},{9,13},{10,... | collective-permute-start | bytes 2961416 | tf_op jit(solution)/shard_map/ppermute | solution.py:350
  13.4 0.0 copy-done.3
  13.4 0.1 collective-permute-start
  13.5 1.7 %share.3 = s16[2576,128]{1,0:T(8,128)(2,1)S(1)} custom-call(s32[1]{0:T(128)} %bitcast.16.pos, f32[1,2]{1,0:T(1,128)S(1)} %copy-done.2, f32[1,2]{1,0:T(1,128)S(1)} %collective-permute-done.6.w_got, bf16[1,4,2,640,640]{4,3,2,1,0:T(8,128)(2,1)} %own.5, bf16[1,2,640,640]{3,2,1,0:T(8,128)(2,1)S(1)} %collective-permute-done.8.got), custom_call_target="tpu_custom_call" | custom-call | flops 5242880 | bytes 2621440 | tf_op jit(solution)/shard_map/share/pallas_call | solution.py:100
  15.2 0.2 collective-permute-start.10
  15.4 1.7 %collective-permute-start.2 = (bf16[32,1280]{1,0:T(8,128)(2,1)S(1)}, bf16[32,1280]{1,0:T(8,128)(2,1)S(1)}, u32[]{:S(2)}, u32[]{:S(2)}) collective-permute-start(bf16[32,1280]{1,0:T(8,128)(2,1)S(1)} %get-tuple-element.41), channel_id=1, source_target_pairs={{0,6},{1,7},{2,4},{3,5},{4,2},{5,3},{6,0},{7,1},{8,14},{9,15},{10,... | collective-permute-start | bytes 245768 | tf_op jit(solution)/shard_map/ppermute | solution.py:350
  17.1 0.0 collective-permute-done
  17.1 0.4 collective-permute-start.1
  17.5 34.0 %collective-permute-done.2 = bf16[32,1280]{1,0:T(8,128)(2,1)S(1)} collective-permute-done((bf16[32,1280]{1,0:T(8,128)(2,1)S(1)}, bf16[32,1280]{1,0:T(8,128)(2,1)S(1)}, u32[]{:S(2)}, u32[]{:S(2)}) %collective-permute-start.2) | collective-permute-done | bytes 81952 | tf_op jit(solution)/shard_map/ppermute | solution.py:350
  51.5 1.7 %collective-permute-done.1 = bf16[32,1280]{1,0:T(8,128)(2,1)S(1)} collective-permute-done((bf16[32,1280]{1,0:T(8,128)(2,1)S(1)}, bf16[32,1280]{1,0:T(8,128)(2,1)S(1)}, u32[]{:S(2)}, u32[]{:S(2)}) %collective-permute-start.1) | collective-permute-done | bytes 81952 | tf_op jit(solution)/shard_map/ppermute | solution.py:350
  53.2 3.9 %collective-permute-start.5 = (bf16[128,1280]{1,0:T(8,128)(2,1)S(1)}, bf16[128,1280]{1,0:T(8,128)(2,1)S(1)}, u32[]{:S(2)}, u32[]{:S(2)}) collective-permute-start(bf16[128,1280]{1,0:T(8,128)(2,1)S(1)} %pad_maximum_fusion.refs_0_), channel_id=1, source_target_pairs={{0,24},{1,25},{2,26},{3,27},{4,28},{5,29},{6,30},{7,31},{8,16},{9,... | collective-permute-start | bytes 983048 | tf_op jit(solution)/shard_map/ppermute | solution.py:350
  57.1 0.0 collective-permute-start.4
  57.1 0.0 collective-permute-done.7.got
  57.1 0.6 collective-permute-start.3
  57.7 3.7 %operator.1.refs_4_ = f32[5,2,640,128]{3,2,1,0:T(8,128)S(1)} custom-call(s32[1]{0:T(128)} %bitcast.9.pos, f32[1,2]{1,0:T(1,128)S(1)} %copy-done.2, f32[1,2]{1,0:T(1,128)S(1)} %collective-permute-done.6.w_got, bf16[1,4,2,640,640]{4,3,2,1,0:T(8,128)(2,1)} %own.5, bf16[1,2,640,640]{3,2,1,0:T(8,128)(2,1)S(1)} %collective-permute-done.7.got), custom_call_target="tpu_custom_call" | custom-call | flops 13107200 | bytes 6553600 | tf_op jit(solution)/shard_map/operator/pallas_call | solution.py:100
  61.5 0.0 copy-start.1
  61.5 4.3 %collective-permute-done.5.refs_3_ = bf16[128,1280]{1,0:T(8,128)(2,1)S(1)} collective-permute-done((bf16[128,1280]{1,0:T(8,128)(2,1)S(1)}, bf16[128,1280]{1,0:T(8,128)(2,1)S(1)}, u32[]{:S(2)}, u32[]{:S(2)}) %collective-permute-start.5) | collective-permute-done | bytes 327712 | tf_op jit(solution)/shard_map/ppermute | solution.py:350
  65.8 18.7 %collective-permute-done.4.refs_2_ = bf16[128,1280]{1,0:T(8,128)(2,1)S(1)} collective-permute-done((bf16[128,1280]{1,0:T(8,128)(2,1)S(1)}, bf16[128,1280]{1,0:T(8,128)(2,1)S(1)}, u32[]{:S(2)}, u32[]{:S(2)}) %collective-permute-start.4) | collective-permute-done | bytes 327712 | tf_op jit(solution)/shard_map/ppermute | solution.py:350
  84.5 0.0 collective-permute-done.3.refs_1_
  84.5 0.0 collective-permute-done.10.refs_5_
  84.5 2.2 %product.3 = (f32[2,128,256]{2,1,0:T(8,128)S(1)}, s16[528,128]{1,0:T(8,128)(2,1)S(1)}, s16[528,128]{1,0:T(8,128)(2,1)S(1)}, s16[528,128]{1,0:T(8,128)(2,1)S(1)}) custom-call(bf16[128,1280]{1,0:T(8,128)(2,1)S(1)} %pad_maximum_fusion.refs_0_, bf16[128,1280]{1,0:T(8,128)(2,1)S(1)} %collective-permute-done.3.refs_1_, ...), custom_call_target="tpu_custom_call" | custom-call | flops 1342177280 | bytes 3276800 | tf_op jit(solution)/shard_map/product/pallas_call | solution.py:175
  86.7 0.1 collective-permute-start.14
  86.8 0.0 collective-permute-done.9.refs_5_
  86.8 4.4 %product.2 = (f32[3,128,256]{2,1,0:T(8,128)S(1)}, s16[784,128]{1,0:T(8,128)(2,1)S(1)}, s16[784,128]{1,0:T(8,128)(2,1)S(1)}, s16[784,128]{1,0:T(8,128)(2,1)S(1)}) custom-call(bf16[128,1280]{1,0:T(8,128)(2,1)S(1)} %pad_maximum_fusion.refs_0_, bf16[128,1280]{1,0:T(8,128)(2,1)S(1)} %collective-permute-done.3.refs_1_, ...), custom_call_target="tpu_custom_call" | custom-call | flops 2013265920 | bytes 4259840 | tf_op jit(solution)/shard_map/product/pallas_call | solution.py:175
  91.2 2.1 %collective-permute-start.11 = (s16[784,128]{1,0:T(8,128)(2,1)S(1)}, s16[784,128]{1,0:T(8,128)(2,1)S(1)}, u32[]{:S(2)}, u32[]{:S(2)}) collective-permute-start(s16[784,128]{1,0:T(8,128)(2,1)S(1)} %get-tuple-element.23), channel_id=1, source_target_pairs={{0,8},{1,9},{2,10},{3,11},{4,12},{5,13},{6,14},{7,15},{8,0},{9,1},... | collective-permute-start | bytes 602120 | tf_op jit(solution)/shard_map/ppermute | solution.py:350
  93.3 1.1 collective-permute-start.12
  94.3 1.4 collective-permute-start.13
  95.7 2.0 %collective-permute-start.15 = (s16[528,128]{1,0:T(8,128)(2,1)S(1)}, s16[528,128]{1,0:T(8,128)(2,1)S(1)}, u32[]{:S(2)}, u32[]{:S(2)}) collective-permute-start(s16[528,128]{1,0:T(8,128)(2,1)S(1)} %get-tuple-element.27), channel_id=1, source_target_pairs={{0,16},{1,17},{2,18},{3,19},{4,20},{5,21},{6,22},{7,23},{8,24},{9,... | collective-permute-start | bytes 405512 | tf_op jit(solution)/shard_map/ppermute | solution.py:350
  97.8 0.0 collective-permute-done.14.refs_5_
  97.8 1.4 collective-permute-start.16
  99.1 0.1 pad_add_fusion.pos
  99.2 23.4 %collective-permute-done.15.refs_6_ = s16[528,128]{1,0:T(8,128)(2,1)S(1)} collective-permute-done((s16[528,128]{1,0:T(8,128)(2,1)S(1)}, s16[528,128]{1,0:T(8,128)(2,1)S(1)}, u32[]{:S(2)}, u32[]{:S(2)}) %collective-permute-start.15) | collective-permute-done | bytes 135200 | tf_op jit(solution)/shard_map/ppermute | solution.py:350
  122.6 0.0 collective-permute-done.16.refs_7_
  122.6 0.0 collective-permute-done.11.refs_2_
  122.6 0.0 collective-permute-done.12.refs_3_
  122.7 0.0 collective-permute-done.13.refs_4_
  122.7 3.7 %synthesis.1 = (f32[2,32,640]{2,1,0:T(8,128)S(1)}, f32[2,32,640]{2,1,0:T(8,128)S(1)}, f32[2,32,640]{2,1,0:T(8,128)S(1)}, f32[2,32,640]{2,1,0:T(8,128)S(1)}, f32[...) custom-call(s32[2]{0:T(128)S(1)} %pad_add_fusion.pos, ...), custom_call_target="tpu_custom_call" | custom-call | flops 838860800 | bytes 2949120 | tf_op jit(solution)/shard_map/synthesis/pallas_call | solution.py:258
  126.3 0.1 collective-permute-start.17
  126.4 1.6 %collective-permute-start.18 = (f32[2,32,640]{2,1,0:T(8,128)S(1)}, f32[2,32,640]{2,1,0:T(8,128)S(1)}, u32[]{:S(2)}, u32[]{:S(2)}) collective-permute-start(f32[2,32,640]{2,1,0:T(8,128)S(1)} %get-tuple-element.31), channel_id=1, source_target_pairs={{0,4},{1,5},{2,6},{3,7},{4,0},{5,1},{6,2},{7,3},{8,12},{9,13},{10,... | collective-permute-start | bytes 491528 | tf_op jit(solution)/shard_map/ppermute | solution.py:350
  128.0 0.1 stack.44
  128.1 0.3 collective-permute-start.19
  128.4 1.5 %collective-permute-start.20 = (f32[2,32,640]{2,1,0:T(8,128)S(1)}, f32[2,32,640]{2,1,0:T(8,128)S(1)}, u32[]{:S(2)}, u32[]{:S(2)}) collective-permute-start(f32[2,32,640]{2,1,0:T(8,128)S(1)} %get-tuple-element.33), channel_id=1, source_target_pairs={{0,1},{1,0},{2,3},{3,2},{4,5},{5,4},{6,7},{7,6},{8,9},{9,8},{10,11... | collective-permute-start | bytes 491528 | tf_op jit(solution)/shard_map/ppermute | solution.py:350
  129.9 0.2 collective-permute-start.21
  130.1 0.0 collective-permute-done.17.refs_1_
  130.1 2.5 %collective-permute-start.22 = (f32[2,32,640]{2,1,0:T(8,128)S(1)}, f32[2,32,640]{2,1,0:T(8,128)S(1)}, u32[]{:S(2)}, u32[]{:S(2)}) collective-permute-start(f32[2,32,640]{2,1,0:T(8,128)S(1)} %get-tuple-element.35), channel_id=1, source_target_pairs={{0,5},{1,4},{2,7},{3,6},{4,1},{5,0},{6,3},{7,2},{8,13},{9,12},{10,... | collective-permute-start | bytes 491528 | tf_op jit(solution)/shard_map/ppermute | solution.py:350
  132.6 0.9 collective-permute-done.18.refs_2_
  133.5 1.3 collective-permute-start.23
  134.8 0.0 copy-done
  134.8 0.6 gather_fusion
  135.4 0.6 collective-permute-done.19.refs_3_
  136.1 0.0 collective-permute-done.20.refs_4_
  136.1 1.9 %collective-permute-done.21.refs_5_ = f32[2,32,640]{2,1,0:T(8,128)S(1)} collective-permute-done((f32[2,32,640]{2,1,0:T(8,128)S(1)}, f32[2,32,640]{2,1,0:T(8,128)S(1)}, u32[]{:S(2)}, u32[]{:S(2)}) %collective-permute-start.21) | collective-permute-done | bytes 163872 | tf_op jit(solution)/shard_map/ppermute | solution.py:350
  138.0 5.5 %collective-permute-done.22.refs_6_ = f32[2,32,640]{2,1,0:T(8,128)S(1)} collective-permute-done((f32[2,32,640]{2,1,0:T(8,128)S(1)}, f32[2,32,640]{2,1,0:T(8,128)S(1)}, u32[]{:S(2)}, u32[]{:S(2)}) %collective-permute-start.22) | collective-permute-done | bytes 163872 | tf_op jit(solution)/shard_map/ppermute | solution.py:350
  143.4 2.4 %collective-permute-done.23.refs_7_ = f32[2,32,640]{2,1,0:T(8,128)S(1)} collective-permute-done((f32[2,32,640]{2,1,0:T(8,128)S(1)}, f32[2,32,640]{2,1,0:T(8,128)S(1)}, u32[]{:S(2)}, u32[]{:S(2)}) %collective-permute-start.23) | collective-permute-done | bytes 163872 | tf_op jit(solution)/shard_map/ppermute | solution.py:350
  145.8 3.4 %place.1 = f32[8,2,32,640]{3,2,1,0:T(8,128)} custom-call(s32[8]{0:T(128)S(1)} %gather_fusion, f32[2,32,640]{2,1,0:T(8,128)S(1)} %get-tuple-element.29.refs_0_, f32[2,32,640]{2,1,0:T(8,128)S(1)} %collective-permute-done.17.refs_1_, f32[2,32,640]{2,1,0:T(8,128)S(1)} %collective-permute-done.18.refs_2_, f32[2,32,640]{2,1,0:T(8,128)S(1)} %collective-permute-done.19.refs_3_, ...), custom_call_target="tpu_custom_call" | custom-call | tf_op jit(solution)/shard_map/place/pallas_call | solution.py:321
  (7 shorter events, 0.1 us)
Async XLA Ops:
  0.0 134.8 %copy-start = (s32[8]{0:T(128)S(1)}, s32[8]{0:T(128)}, u32[]{:S(2)}) copy-start(s32[8]{0:T(128)} %param.9) | copy-start | bytes 100
  0.0 4.4 %copy-start.2 = (f32[1,2]{1,0:T(1,128)S(1)}, f32[1,2]{1,0:T(1,128)}, u32[]{:S(2)}) copy-start(f32[1,2]{1,0:T(1,128)} %w_own.5) | copy-start | bytes 28
  3.9 3.8 %collective-permute-start.8 = (bf16[1,2,640,640]{3,2,1,0:T(8,128)(2,1)}, bf16[1,2,640,640]{3,2,1,0:T(8,128)(2,1)S(1)}, u32[]{:S(2)}, u32[]{:S(2)}) collective-permute-start(bf16[1,2,640,640]{3,2,1,0:T(8,128)(2,1)} %get-tuple-element.37), channel_id=1, source_target_pairs={{0,2},{1,3},{2,0},{3,1},{4,6},{5,7},{6,4},{7,5},{8,10},{9,11},{10,... | collective-permute-start | bytes 4915208 | tf_op jit(solution)/shard_map/ppermute | solution.py:350
  4.4 52.7 %collective-permute-start.7 = (bf16[1,2,640,640]{3,2,1,0:T(8,128)(2,1)}, bf16[1,2,640,640]{3,2,1,0:T(8,128)(2,1)S(1)}, u32[]{:S(2)}, u32[]{:S(2)}) collective-permute-start(bf16[1,2,640,640]{3,2,1,0:T(8,128)(2,1)} %get-tuple-element.38), channel_id=1, source_target_pairs={{0,2},{1,3},{2,0},{3,1},{4,6},{5,7},{6,4},{7,5},{8,10},{9,11},{10,... | collective-permute-start | bytes 4915208 | tf_op jit(solution)/shard_map/ppermute | solution.py:350
  4.4 3.1 %collective-permute-start.6 = (f32[1,2]{1,0:T(1,128)S(1)}, f32[1,2]{1,0:T(1,128)S(1)}, u32[]{:S(2)}, u32[]{:S(2)}) collective-permute-start(f32[1,2]{1,0:T(1,128)S(1)} %copy-done.2), channel_id=1, source_target_pairs={{0,2},{1,3},{2,0},{3,1},{4,6},{5,7},{6,4},{7,5},{8,10},{9,11},{10,... | collective-permute-start | bytes 32 | tf_op jit(solution)/shard_map/ppermute | solution.py:350
  7.7 5.7 %copy-start.3 = (bf16[4,32,1280]{2,1,0:T(8,128)(2,1)S(1)}, bf16[4,32,1280]{2,1,0:T(8,128)(2,1)}, u32[]{:S(2)}) copy-start(bf16[4,32,1280]{2,1,0:T(8,128)(2,1)} %param.5) | copy-start | bytes 983044
  10.4 76.4 %collective-permute-start.9 = (s16[3856,128]{1,0:T(8,128)(2,1)S(1)}, s16[3856,128]{1,0:T(8,128)(2,1)S(1)}, u32[]{:S(2)}, u32[]{:S(2)}) collective-permute-start(s16[3856,128]{1,0:T(8,128)(2,1)S(1)} %share.2), channel_id=1, source_target_pairs={{0,4},{1,5},{2,6},{3,7},{4,0},{5,1},{6,2},{7,3},{8,12},{9,13},{10,... | collective-permute-start | bytes 2961416 | tf_op jit(solution)/shard_map/ppermute | solution.py:350
  13.4 3.7 %collective-permute-start = (bf16[32,1280]{1,0:T(8,128)(2,1)S(1)}, bf16[32,1280]{1,0:T(8,128)(2,1)S(1)}, u32[]{:S(2)}, u32[]{:S(2)}) collective-permute-start(bf16[32,1280]{1,0:T(8,128)(2,1)S(1)} %get-tuple-element.40), channel_id=1, source_target_pairs={{0,2},{1,3},{2,0},{3,1},{4,6},{5,7},{6,4},{7,5},{8,10},{9,11},{10,... | collective-permute-start | bytes 245768 | tf_op jit(solution)/shard_map/ppermute | solution.py:350
  15.2 69.3 %collective-permute-start.10 = (s16[2576,128]{1,0:T(8,128)(2,1)S(1)}, s16[2576,128]{1,0:T(8,128)(2,1)S(1)}, u32[]{:S(2)}, u32[]{:S(2)}) collective-permute-start(s16[2576,128]{1,0:T(8,128)(2,1)S(1)} %share.3), channel_id=1, source_target_pairs={{0,4},{1,5},{2,6},{3,7},{4,0},{5,1},{6,2},{7,3},{8,12},{9,13},{10,... | collective-permute-start | bytes 1978376 | tf_op jit(solution)/shard_map/ppermute | solution.py:350
  15.4 36.0 %collective-permute-start.2 = (bf16[32,1280]{1,0:T(8,128)(2,1)S(1)}, bf16[32,1280]{1,0:T(8,128)(2,1)S(1)}, u32[]{:S(2)}, u32[]{:S(2)}) collective-permute-start(bf16[32,1280]{1,0:T(8,128)(2,1)S(1)} %get-tuple-element.41), channel_id=1, source_target_pairs={{0,6},{1,7},{2,4},{3,5},{4,2},{5,3},{6,0},{7,1},{8,14},{9,15},{10,... | collective-permute-start | bytes 245768 | tf_op jit(solution)/shard_map/ppermute | solution.py:350
  17.1 36.1 %collective-permute-start.1 = (bf16[32,1280]{1,0:T(8,128)(2,1)S(1)}, bf16[32,1280]{1,0:T(8,128)(2,1)S(1)}, u32[]{:S(2)}, u32[]{:S(2)}) collective-permute-start(bf16[32,1280]{1,0:T(8,128)(2,1)S(1)} %get-tuple-element.42), channel_id=1, source_target_pairs={{0,4},{1,5},{2,6},{3,7},{4,0},{5,1},{6,2},{7,3},{8,12},{9,13},{10,... | collective-permute-start | bytes 245768 | tf_op jit(solution)/shard_map/ppermute | solution.py:350
  53.2 12.6 %collective-permute-start.5 = (bf16[128,1280]{1,0:T(8,128)(2,1)S(1)}, bf16[128,1280]{1,0:T(8,128)(2,1)S(1)}, u32[]{:S(2)}, u32[]{:S(2)}) collective-permute-start(bf16[128,1280]{1,0:T(8,128)(2,1)S(1)} %pad_maximum_fusion.refs_0_), channel_id=1, source_target_pairs={{0,24},{1,25},{2,26},{3,27},{4,28},{5,29},{6,30},{7,31},{8,16},{9,... | collective-permute-start | bytes 983048 | tf_op jit(solution)/shard_map/ppermute | solution.py:350
  57.1 27.4 %collective-permute-start.4 = (bf16[128,1280]{1,0:T(8,128)(2,1)S(1)}, bf16[128,1280]{1,0:T(8,128)(2,1)S(1)}, u32[]{:S(2)}, u32[]{:S(2)}) collective-permute-start(bf16[128,1280]{1,0:T(8,128)(2,1)S(1)} %pad_maximum_fusion.refs_0_), channel_id=1, source_target_pairs={{0,16},{1,17},{2,18},{3,19},{4,20},{5,21},{6,22},{7,23},{8,24},{9,... | collective-permute-start | bytes 983048 | tf_op jit(solution)/shard_map/ppermute | solution.py:350
  57.1 27.4 %collective-permute-start.3 = (bf16[128,1280]{1,0:T(8,128)(2,1)S(1)}, bf16[128,1280]{1,0:T(8,128)(2,1)S(1)}, u32[]{:S(2)}, u32[]{:S(2)}) collective-permute-start(bf16[128,1280]{1,0:T(8,128)(2,1)S(1)} %pad_maximum_fusion.refs_0_), channel_id=1, source_target_pairs={{0,8},{1,9},{2,10},{3,11},{4,12},{5,13},{6,14},{7,15},{8,0},{9,1},... | collective-permute-start | bytes 983048 | tf_op jit(solution)/shard_map/ppermute | solution.py:350
  61.5 25.2 %copy-start.1 = (f32[5,2,640,128]{3,2,1,0:T(8,128)}, f32[5,2,640,128]{3,2,1,0:T(8,128)S(1)}, u32[]{:S(2)}) copy-start(f32[5,2,640,128]{3,2,1,0:T(8,128)S(1)} %operator.1.refs_4_) | copy-start | bytes 9830404
  86.7 11.1 %collective-permute-start.14 = (s16[528,128]{1,0:T(8,128)(2,1)S(1)}, s16[528,128]{1,0:T(8,128)(2,1)S(1)}, u32[]{:S(2)}, u32[]{:S(2)}) collective-permute-start(s16[528,128]{1,0:T(8,128)(2,1)S(1)} %get-tuple-element.26), channel_id=1, source_target_pairs={{0,8},{1,9},{2,10},{3,11},{4,12},{5,13},{6,14},{7,15},{8,0},{9,1},... | collective-permute-start | bytes 405512 | tf_op jit(solution)/shard_map/ppermute | solution.py:350
  91.2 31.5 %collective-permute-start.11 = (s16[784,128]{1,0:T(8,128)(2,1)S(1)}, s16[784,128]{1,0:T(8,128)(2,1)S(1)}, u32[]{:S(2)}, u32[]{:S(2)}) collective-permute-start(s16[784,128]{1,0:T(8,128)(2,1)S(1)} %get-tuple-element.23), channel_id=1, source_target_pairs={{0,8},{1,9},{2,10},{3,11},{4,12},{5,13},{6,14},{7,15},{8,0},{9,1},... | collective-permute-start | bytes 602120 | tf_op jit(solution)/shard_map/ppermute | solution.py:350
  93.3 29.4 %collective-permute-start.12 = (s16[784,128]{1,0:T(8,128)(2,1)S(1)}, s16[784,128]{1,0:T(8,128)(2,1)S(1)}, u32[]{:S(2)}, u32[]{:S(2)}) collective-permute-start(s16[784,128]{1,0:T(8,128)(2,1)S(1)} %get-tuple-element.24), channel_id=1, source_target_pairs={{0,16},{1,17},{2,18},{3,19},{4,20},{5,21},{6,22},{7,23},{8,24},{9,... | collective-permute-start | bytes 602120 | tf_op jit(solution)/shard_map/ppermute | solution.py:350
  94.3 28.3 %collective-permute-start.13 = (s16[784,128]{1,0:T(8,128)(2,1)S(1)}, s16[784,128]{1,0:T(8,128)(2,1)S(1)}, u32[]{:S(2)}, u32[]{:S(2)}) collective-permute-start(s16[784,128]{1,0:T(8,128)(2,1)S(1)} %get-tuple-element.25), channel_id=1, source_target_pairs={{0,24},{1,25},{2,26},{3,27},{4,28},{5,29},{6,30},{7,31},{8,16},{9,... | collective-permute-start | bytes 602120 | tf_op jit(solution)/shard_map/ppermute | solution.py:350
  95.7 26.9 %collective-permute-start.15 = (s16[528,128]{1,0:T(8,128)(2,1)S(1)}, s16[528,128]{1,0:T(8,128)(2,1)S(1)}, u32[]{:S(2)}, u32[]{:S(2)}) collective-permute-start(s16[528,128]{1,0:T(8,128)(2,1)S(1)} %get-tuple-element.27), channel_id=1, source_target_pairs={{0,16},{1,17},{2,18},{3,19},{4,20},{5,21},{6,22},{7,23},{8,24},{9,... | collective-permute-start | bytes 405512 | tf_op jit(solution)/shard_map/ppermute | solution.py:350
  97.8 24.9 %collective-permute-start.16 = (s16[528,128]{1,0:T(8,128)(2,1)S(1)}, s16[528,128]{1,0:T(8,128)(2,1)S(1)}, u32[]{:S(2)}, u32[]{:S(2)}) collective-permute-start(s16[528,128]{1,0:T(8,128)(2,1)S(1)} %get-tuple-element.28), channel_id=1, source_target_pairs={{0,24},{1,25},{2,26},{3,27},{4,28},{5,29},{6,30},{7,31},{8,16},{9,... | collective-permute-start | bytes 405512 | tf_op jit(solution)/shard_map/ppermute | solution.py:350
  126.3 3.8 %collective-permute-start.17 = (f32[2,32,640]{2,1,0:T(8,128)S(1)}, f32[2,32,640]{2,1,0:T(8,128)S(1)}, u32[]{:S(2)}, u32[]{:S(2)}) collective-permute-start(f32[2,32,640]{2,1,0:T(8,128)S(1)} %get-tuple-element.30), channel_id=1, source_target_pairs={{0,2},{1,3},{2,0},{3,1},{4,6},{5,7},{6,4},{7,5},{8,10},{9,11},{10,... | collective-permute-start | bytes 491528 | tf_op jit(solution)/shard_map/ppermute | solution.py:350
  126.4 7.1 %collective-permute-start.18 = (f32[2,32,640]{2,1,0:T(8,128)S(1)}, f32[2,32,640]{2,1,0:T(8,128)S(1)}, u32[]{:S(2)}, u32[]{:S(2)}) collective-permute-start(f32[2,32,640]{2,1,0:T(8,128)S(1)} %get-tuple-element.31), channel_id=1, source_target_pairs={{0,4},{1,5},{2,6},{3,7},{4,0},{5,1},{6,2},{7,3},{8,12},{9,13},{10,... | collective-permute-start | bytes 491528 | tf_op jit(solution)/shard_map/ppermute | solution.py:350
  128.1 8.0 %collective-permute-start.19 = (f32[2,32,640]{2,1,0:T(8,128)S(1)}, f32[2,32,640]{2,1,0:T(8,128)S(1)}, u32[]{:S(2)}, u32[]{:S(2)}) collective-permute-start(f32[2,32,640]{2,1,0:T(8,128)S(1)} %get-tuple-element.32), channel_id=1, source_target_pairs={{0,6},{1,7},{2,4},{3,5},{4,2},{5,3},{6,0},{7,1},{8,14},{9,15},{10,... | collective-permute-start | bytes 491528 | tf_op jit(solution)/shard_map/ppermute | solution.py:350
  128.4 7.7 %collective-permute-start.20 = (f32[2,32,640]{2,1,0:T(8,128)S(1)}, f32[2,32,640]{2,1,0:T(8,128)S(1)}, u32[]{:S(2)}, u32[]{:S(2)}) collective-permute-start(f32[2,32,640]{2,1,0:T(8,128)S(1)} %get-tuple-element.33), channel_id=1, source_target_pairs={{0,1},{1,0},{2,3},{3,2},{4,5},{5,4},{6,7},{7,6},{8,9},{9,8},{10,11... | collective-permute-start | bytes 491528 | tf_op jit(solution)/shard_map/ppermute | solution.py:350
  129.9 8.0 %collective-permute-start.21 = (f32[2,32,640]{2,1,0:T(8,128)S(1)}, f32[2,32,640]{2,1,0:T(8,128)S(1)}, u32[]{:S(2)}, u32[]{:S(2)}) collective-permute-start(f32[2,32,640]{2,1,0:T(8,128)S(1)} %get-tuple-element.34), channel_id=1, source_target_pairs={{0,3},{1,2},{2,1},{3,0},{4,7},{5,6},{6,5},{7,4},{8,11},{9,10},{10,... | collective-permute-start | bytes 491528 | tf_op jit(solution)/shard_map/ppermute | solution.py:350
  130.1 13.3 %collective-permute-start.22 = (f32[2,32,640]{2,1,0:T(8,128)S(1)}, f32[2,32,640]{2,1,0:T(8,128)S(1)}, u32[]{:S(2)}, u32[]{:S(2)}) collective-permute-start(f32[2,32,640]{2,1,0:T(8,128)S(1)} %get-tuple-element.35), channel_id=1, source_target_pairs={{0,5},{1,4},{2,7},{3,6},{4,1},{5,0},{6,3},{7,2},{8,13},{9,12},{10,... | collective-permute-start | bytes 491528 | tf_op jit(solution)/shard_map/ppermute | solution.py:350
  133.5 12.3 %collective-permute-start.23 = (f32[2,32,640]{2,1,0:T(8,128)S(1)}, f32[2,32,640]{2,1,0:T(8,128)S(1)}, u32[]{:S(2)}, u32[]{:S(2)}) collective-permute-start(f32[2,32,640]{2,1,0:T(8,128)S(1)} %get-tuple-element.36), channel_id=1, source_target_pairs={{0,7},{1,6},{2,5},{3,4},{4,3},{5,2},{6,1},{7,0},{8,15},{9,14},{10,... | collective-permute-start | bytes 491528 | tf_op jit(solution)/shard_map/ppermute | solution.py:350

commit v3 on v2

--- a/solution.py
+++ b/solution.py
@@ -38,11 +38,6 @@
 
 def scales(tail):
     return jnp.exp2(tail.astype(I32).astype(F32) * (1.0 / STEPS))
-
-
-def take_row(table, row):
-    at = lax.broadcasted_iota(I32, table.shape, 0)
-    return jnp.sum(jnp.where(at == row, table, 0.0), axis=0, keepdims=True)
 
 
 def message(strips, rows):
@@ -63,7 +58,8 @@
     return real, imag
 
 
-def share_kernel(pos, w_own, w_got, own, got, out, tail):
+def share_kernel(after, where, w_own, w_got, own, got, *refs):
+    out, tail = refs[after:]
     t = pl.program_id(0)
     size = own.shape[3]
     end = out.shape[0] - TAIL
@@ -83,12 +79,12 @@
         out[end:, :] = tail[...].astype(I32).astype(I16)
 
 
-def own_kernel(pos, w_own, w_got, own, got, out):
+def own_kernel(where, w_own, w_got, own, got, out):
     for part, value in enumerate(weighted(w_own, w_got, own, got)):
         out[0, part] = value
 
 
-def operator(slot, w_own, w_got, inverse, got, first, count, coded):
+def operator(where, bits, w_own, w_got, inverse, got, first, count, coded, after=()):
     terms, _, _, size, _ = inverse.shape
     smem = pl.BlockSpec(memory_space=pltpu.SMEM)
     if coded:
@@ -96,9 +92,9 @@
         out_spec = whole(out_shape.shape)
     else:
         out_shape = jax.ShapeDtypeStruct((count, 2, size, LANES), F32)
-        out_spec = pl.BlockSpec((1, 2, size, LANES), lambda t, slot: (t, 0, 0, 0))
+        out_spec = pl.BlockSpec((1, 2, size, LANES), lambda t, where: (t, 0, 0, 0))
     return pl.pallas_call(
-        share_kernel if coded else own_kernel,
+        functools.partial(share_kernel, len(after)) if coded else own_kernel,
         out_shape=out_shape,
         grid_spec=pltpu.PrefetchScalarGridSpec(
             num_scalar_prefetch=1,
@@ -107,10 +103,12 @@
                 smem,
                 smem,
                 pl.BlockSpec(
-                    (terms, 1, 2, size, LANES), lambda t, slot: (0, slot[0], 0, 0, t + first)
+                    (terms, 1, 2, size, LANES),
+                    lambda t, where: (0, where[bits], 0, 0, t + first),
                 ),
-                pl.BlockSpec((terms, 2, size, LANES), lambda t, slot: (0, 0, 0, t + first)),
-            ],
+                pl.BlockSpec((terms, 2, size, LANES), lambda t, where: (0, 0, 0, t + first)),
+            ]
+            + [pl.BlockSpec(memory_space=pl.ANY)] * len(after),
             out_specs=out_spec,
             scratch_shapes=[pltpu.VMEM((TAIL, LANES), F32)] if coded else [],
         ),
@@ -121,13 +119,14 @@
             transcendentals=0,
         ),
         name="share" if coded else "operator",
-    )(slot, w_own, w_got, inverse, got)
-
-
-def product_kernel(count, tiles, *refs):
-    parts, own, got = refs[:count], refs[count], refs[count + 1]
-    near, sends = refs[count + 2], refs[count + 3 : 2 * count + 2]
-    full, op, tails = refs[2 * count + 2 :]
+    )(where, w_own, w_got, inverse, got, *after)
+
+
+def product_kernel(count, tiles, after, *refs):
+    parts, own, got = refs[:count], refs[count], refs[count + 1 : count + 1 + tiles]
+    refs = refs[count + 1 + tiles + after :]
+    near, sends = refs[0], refs[1:count]
+    full, op, tails = refs[count:]
     rows, width = parts[0].shape
     size = width // 2
     t = pl.program_id(0)
@@ -138,17 +137,23 @@
         for i, part in enumerate(parts):
             full[i * rows : (i + 1) * rows, :] = part[...]
 
-    table = scales(got[2 * tiles * size :, :])
-    pair = []
-    for part in range(2):
-        strip = 2 * t + part
-        code = got[pl.ds(pl.multiple_of(strip * size, TAIL), size), :]
-        pair.append(own[0, part] + code.astype(I32).astype(F32) * take_row(table, strip))
-    for level, (r, j) in enumerate(zip(split(pair[0]), split(pair[1]))):
-        op[level, :size, :LANES] = r
-        op[level, :size, LANES:] = j
-        op[level, size:, :LANES] = -j
-        op[level, size:, LANES:] = r
+    for i in range(tiles):
+
+        @pl.when(t == i)
+        def _():
+            table = scales(got[i][2 * size :, :])
+            real, imag = (
+                own[0, part]
+                + got[i][part * size : (part + 1) * size, :].astype(I32).astype(F32)
+                * table[part : part + 1, :]
+                for part in range(2)
+            )
+            for level, (r, j) in enumerate(zip(split(real), split(imag))):
+                op[level, :size, :LANES] = r
+                op[level, :size, LANES:] = j
+                op[level, size:, :LANES] = -j
+                op[level, size:, LANES:] = r
+
     x = full[...]
     acc = jnp.dot(x, op[0], preferred_element_type=F32)
     acc += jnp.dot(x, op[1], preferred_element_type=F32)
@@ -167,20 +172,21 @@
             sends[q - 1][2 * tiles * rows :, :] = tails[q - 1].astype(I32).astype(I16)
 
 
-def product(parts, own, got, first, tiles):
-    count = len(parts)
+def product(parts, own, got, first, after):
+    count, tiles = len(parts), len(got)
     rows, width = parts[0].shape
     size = width // 2
     send = message(2 * tiles, rows)
     return pl.pallas_call(
-        functools.partial(product_kernel, count, tiles),
+        functools.partial(product_kernel, count, tiles, len(after)),
         out_shape=[jax.ShapeDtypeStruct((tiles, rows, 2 * LANES), F32)] + [send] * (count - 1),
         grid=(tiles,),
         in_specs=[whole((rows, width))] * count
         + [
             pl.BlockSpec((1, 2, size, LANES), lambda t: (t + first, 0, 0, 0)),
-            whole(got.shape),
-        ],
+        ]
+        + [whole(x.shape) for x in got]
+        + [pl.BlockSpec(memory_space=pl.ANY)] * len(after),
         out_specs=[pl.BlockSpec((1, rows, 2 * LANES), lambda t: (t, 0, 0))]
         + [whole(send.shape)] * (count - 1),
         scratch_shapes=[
@@ -195,7 +201,7 @@
             transcendentals=0,
         ),
         name="product",
-    )(*parts, own, got)
+    )(*parts, own, *got, *after)
 
 
 def add_up(near, got, write):
@@ -220,7 +226,7 @@
     return near, got, refs[chunks * (1 + count) :]
 
 
-def synthesis_kernel(bands, chunks, count, pos, *refs):
+def synthesis_kernel(bands, chunks, count, where, *refs):
     near, got, rest = unpack(refs, chunks, count)
     table, outs, values = rest[0], rest[1:-1], rest[-1]
     rows = near[0].shape[1]
@@ -244,26 +250,41 @@
         @pl.when(band == d)
         def _():
             for side in range(4):
+                out = outs[4 * d + side]
+                if len(out.shape) == 3:
+                    for part in range(2):
+                        start = part * rows + side * quarter
+                        out[part] = grid[start : start + quarter]
+                    continue
+                tail = jnp.zeros((TAIL, LANES), F32)
                 for part in range(2):
                     start = part * rows + side * quarter
-                    outs[4 * d + side][part] = grid[start : start + quarter]
-
-
-def synthesis(pos, near, got, legendre, bands):
+                    for k in range(grid.shape[1] // LANES):
+                        strip = 2 * k + part
+                        code, step = encode(
+                            grid[start : start + quarter, k * LANES : (k + 1) * LANES]
+                        )
+                        out[strip * quarter : (strip + 1) * quarter, :] = code
+                        tail = put_row(tail, strip, step)
+                out[out.shape[0] - TAIL :, :] = tail.astype(I32).astype(I16)
+
+
+def synthesis(where, near, got, legendre, bands):
     rows = near[0].shape[1]
     size, nlat = legendre.shape[1:]
     band = nlat // bands
-    piece = (2, rows // 4, band)
+    send = message(2 * band // LANES, rows // 4)
+    outs = [jax.ShapeDtypeStruct((2, rows // 4, band), F32)] + [send] * (4 * bands - 1)
     operands = list(near) + [part for parts in got for part in parts]
     return pl.pallas_call(
         functools.partial(synthesis_kernel, bands, len(near), len(got[0])),
-        out_shape=[jax.ShapeDtypeStruct(piece, F32)] * (4 * bands),
+        out_shape=outs,
         grid_spec=pltpu.PrefetchScalarGridSpec(
             num_scalar_prefetch=1,
             grid=(bands,),
             in_specs=[whole(x.shape) for x in operands]
-            + [pl.BlockSpec((1, size, band), lambda b, pos: (pos[0], 0, pos[1] ^ b))],
-            out_specs=[whole(piece)] * (4 * bands),
+            + [pl.BlockSpec((1, size, band), lambda b, where: (where[0], 0, where[4] ^ b))],
+            out_specs=[whole(out.shape) for out in outs],
             scratch_shapes=[pltpu.VMEM((2, 2 * rows, size), BF16)],
         ),
         compiler_params=params(),
@@ -273,7 +294,7 @@
             transcendentals=0,
         ),
         name="synthesis",
-    )(pos, *operands, legendre)
+    )(where, *operands, legendre)
 
 
 def total_kernel(chunks, count, *refs):
@@ -285,7 +306,7 @@
     add_up(near, got, write)
 
 
-def plain_synthesis(pos, near, got, legendre, bands):
+def plain_synthesis(where, near, got, legendre, bands):
     rows = near[0].shape[1]
     size, nlat = legendre.shape[1:]
     total = pl.pallas_call(
@@ -294,42 +315,85 @@
         compiler_params=params(),
         name="total",
     )(*near, *[part for parts in got for part in parts])
-    table = lax.dynamic_index_in_dim(legendre, pos[0], 0, keepdims=False)
+    table = lax.dynamic_index_in_dim(legendre, where[0], 0, keepdims=False)
     grid = sum(
         jnp.einsum("pcn,nl->pcl", v, table, preferred_element_type=F32) for v in split(total)
     )
     quarter, band = rows // 4, nlat // bands
     return [
-        lax.dynamic_slice(grid, (0, side * quarter, (pos[1] ^ d) * band), (2, quarter, band))
+        lax.dynamic_slice(grid, (0, side * quarter, (where[4] ^ d) * band), (2, quarter, band))
         for d in range(bands)
         for side in range(4)
     ]
 
 
-def place_kernel(count, dst, *refs):
+def place_kernel(count, where, column, *refs):
     pieces, out = refs[:count], refs[count]
+    _, _, rows, lanes = out.shape
     for i in range(count):
 
         @pl.when(pl.program_id(0) == i)
         def _():
-            out[0] = pieces[i][...]
-
-
-def place(dst, pieces):
+            piece = pieces[i]
+            if len(piece.shape) == 3:
+                out[0] = piece[...]
+                return
+            strips = 2 * lanes // LANES
+            table = scales(piece[strips * rows :, :])
+            for strip in range(strips):
+                code = piece[strip * rows : (strip + 1) * rows, :]
+                at = strip // 2 * LANES
+                out[0, strip % 2, :, at : at + LANES] = (
+                    code.astype(I32).astype(F32) * table[strip : strip + 1, :]
+                )
+
+
+def place(where, column, slots, pieces):
     count = len(pieces)
     shape = pieces[0].shape
     return pl.pallas_call(
         functools.partial(place_kernel, count),
         out_shape=jax.ShapeDtypeStruct((count,) + shape, F32),
         grid_spec=pltpu.PrefetchScalarGridSpec(
+            num_scalar_prefetch=2,
+            grid=(count,),
+            in_specs=[whole(piece.shape) for piece in pieces],
+            out_specs=pl.BlockSpec(
+                (1,) + shape,
+                lambda i, where, column: (
+                    column[(where[4] ^ (i // 4)) * slots + where[i % 4]],
+                    0,
+                    0,
+                    0,
+                ),
+            ),
+        ),
+        compiler_params=params(),
+        name="place",
+    )(where, column, *pieces)
+
+
+def pick_kernel(where, *refs):
+    count = len(refs) // 2
+    for i in range(count):
+        refs[count + i][...] = refs[i][0]
+
+
+def pick(where, state):
+    shape = state.shape[1:]
+    block = lambda i: pl.BlockSpec((1,) + shape, lambda _, where: (where[i], 0, 0))
+    return pl.pallas_call(
+        pick_kernel,
+        out_shape=[jax.ShapeDtypeStruct(shape, state.dtype)] * 4,
+        grid_spec=pltpu.PrefetchScalarGridSpec(
             num_scalar_prefetch=1,
-            grid=(count,),
-            in_specs=[whole(shape)] * count,
-            out_specs=pl.BlockSpec((1,) + shape, lambda i, dst: (dst[i], 0, 0, 0)),
-        ),
-        compiler_params=params(),
-        name="place",
-    )(dst, *pieces)
+            grid=(1,),
+            in_specs=[block(i) for i in range(4)],
+            out_specs=[whole(shape)] * 4,
+        ),
+        compiler_params=params(),
+        name="pick",
+    )(where, *[state] * 4)
 
 
 def shards(mesh, spectral_state, inverse, term_weights, legendre, slot_column):
@@ -339,7 +403,6 @@
     outer = terms // 4
     me, wave = lax.axis_index("term"), lax.axis_index("wave")
     place_of = me % 4
-    turn = slots // 4
 
     def swap(x, term_bits, wave_bits=0):
         pairs = [
@@ -353,47 +416,39 @@
     cut = (tiles + 1) // 2
     chunks = [(0, cut), (cut, tiles - cut)] if tiles > 1 else [(0, tiles)]
 
-    pieces = []
-    for j in range(turn):
-        slot_of = lambda bits: (place_of ^ bits) * turn + j
-        state_of = lambda bits: lax.dynamic_index_in_dim(
-            spectral_state, slot_of(bits), 0, keepdims=False
-        )
-        block = jnp.concatenate(
-            [state_of(0)] + [swap(state_of(bits), bits) for bits in range(1, 4)], axis=0
-        )
-        parts = [block] + [swap(block, q * 4) for q in range(1, outer)]
-
-        w_got = swap(term_weights, 1)
-        from_core = lambda bits: swap(
-            lax.dynamic_index_in_dim(inverse, slot_of(bits ^ 1), 1, keepdims=False), 1
-        )
-        far, own = from_core(2), from_core(0)
-        scalar = lambda x: jnp.reshape(x, (1,)).astype(I32)
-        shares = [
-            swap(
-                operator(scalar(slot_of(2)), term_weights, w_got, inverse, far, *chunk, True), 2
-            )
-            for chunk in chunks
-        ]
-        mine = operator(scalar(slot_of(0)), term_weights, w_got, inverse, own, 0, tiles, False)
-        near, got = [], []
-        for chunk, share in zip(chunks, shares):
-            made = product(parts, mine, share, *chunk)
-            near.append(made[0])
-            got.append([swap(made[q], q * 4) for q in range(1, outer)])
-        pos = jnp.stack([slot_of(0), wave]).astype(I32)
-        make = synthesis if legendre.shape[2] // waves % LANES == 0 else plain_synthesis
-        grid = make(pos, near, got, legendre, waves)
-        for d in range(waves):
-            for bits in range(4):
-                piece = grid[4 * d + bits]
-                if d or bits:
-                    piece = swap(piece, bits, d)
-                pieces.append(((wave ^ d) * slots + slot_of(bits), piece))
-
-    at = jnp.stack([slot for slot, _ in pieces])
-    return place(slot_column[at], [piece for _, piece in pieces])
+    assert slots == 4
+    where = jnp.stack([place_of ^ bits for bits in range(4)] + [wave]).astype(I32)
+    states = pick(where, spectral_state)
+    block = jnp.concatenate(
+        [states[0]] + [swap(states[bits], bits) for bits in range(1, 4)], axis=0
+    )
+    parts = [block] + [swap(block, q * 4) for q in range(1, outer)]
+
+    w_got = swap(term_weights, 1)
+    far, own = (
+        swap(lax.dynamic_index_in_dim(inverse, place_of ^ bits, 1, keepdims=False), 1)
+        for bits in (3, 1)
+    )
+    mine = operator(where, 0, term_weights, w_got, inverse, own, 0, tiles, False)
+    shares = []
+    for t in range(tiles):
+        after = (block,) if t < tiles - 1 else (*parts[1:], mine)
+        share = operator(where, 2, term_weights, w_got, inverse, far, t, 1, True, after)
+        shares.append(swap(share, 2))
+    near, got = [], []
+    for first, count in chunks:
+        after = [near[-1], got[-1][0]] if near else []
+        made = product(parts, mine, shares[first : first + count], first, after)
+        near.append(made[0])
+        got.append([swap(made[q], q * 4) for q in range(1, outer)])
+    make = synthesis if legendre.shape[2] // waves % LANES == 0 else plain_synthesis
+    grid = make(where, near, got, legendre, waves)
+    pieces = [
+        swap(grid[4 * d + bits], bits, d) if d or bits else grid[0]
+        for d in range(waves)
+        for bits in range(4)
+    ]
+    return place(where, slot_column, slots, pieces)
 
 
 def solution(mesh):

time: 150 us -> 114 us (0.76)
  waiting for transfers between devices: 96.2 us -> 44.1 us
  Pallas kernels: 21.8 us -> 30.1 us
  starting transfers between devices: 26.2 us -> 33.8 us
    ppermute x24 -> x27, waiting for transfers between devices: 96.2 us -> 44.1 us  [swap(): return lax.ppermute(x, ('term', 'wave'), pairs)]
    pallas_call x5 -> x9, Pallas kernels: 14.8 us -> 22.6 us  [the longest x6 13.8 us: operator(): pl.pallas_call(functools.partial(share_kernel, len(after)) if coded else...]
    ppermute x24 -> x27, starting transfers between devices: 26.2 us -> 33.8 us  [swap(): return lax.ppermute(x, ('term', 'wave'), pairs)]
    unnamed x8 -> x11, local copies, waits for them, and re-layouts: 0.02 us -> 1.71 us
    squeeze x2 -> x1, local copies, waits for them, and re-layouts: 3.92 us -> 3.94 us  [shards(): lax.dynamic_index_in_dim(inverse, place_of ^ bits, 1, keepdims=False)]
  transfers between devices with their start and end apart: 24 -> 27, of which waited for: 12 -> 12; matrix products, arithmetic and copies ran while one was open for 1% -> 0% of each run, Pallas kernels for 10% -> 20%
where the time goes in v3:
time: 114 us
  waiting for transfers between devices  44.1 us (39%)
  starting transfers between devices  33.8 us (30%)
  Pallas kernels  30.1 us (26%)
  local copies, waits for them, and re-layouts  5.73 us (5%)
    ppermute x27, waiting for transfers between devices, swap(): return lax.ppermute(x, ('term', 'wave'), pairs)  44.1 us
    ppermute x27, starting transfers between devices, swap(): return lax.ppermute(x, ('term', 'wave'), pairs)  33.8 us
    pallas_call x6, Pallas kernels, operator(): pl.pallas_call(functools.partial(share_kernel, len(after)) if coded else...  13.8 us
    pallas_call x2, Pallas kernels, product(): pl.pallas_call(functools.partial(product_kernel, count, tiles, len(after)...  8.27 us
    squeeze x1, local copies, waits for them, and re-layouts, shards(): lax.dynamic_index_in_dim(inverse, place_of ^ bits, 1, keepdims=False)  3.94 us
    pallas_call x1, Pallas kernels, synthesis(): pl.pallas_call(functools.partial(synthesis_kernel, bands, len(near), len(...  3.89 us
    pallas_call x1, Pallas kernels, place(): pl.pallas_call(functools.partial(place_kernel, count), out_shape=jax.Shap...  3.58 us
  transfers between devices with their start and end apart: 27, of which 12 were waited for; matrix products, arithmetic and copies ran while one was open for 0% of the time, Pallas kernels for 20%

profile of v3, /device:TPU:0, one launch (start us, length us, event | category | flops | bytes accessed | tf_op | source)
XLA Modules:
  0.0 113.9 jit_solution(8668482342349561980)
XLA Ops:
  0.0 3.9 %dynamic-slice_bitcast_fusion = (bf16[1,2,640,640]{3,2,1,0:T(8,128)(2,1)}, bf16[1,2,640,640]{3,2,1,0:T(8,128)(2,1)}) fusion(bf16[1,4,2,640,640]{4,3,2,1,0:T(8,128)(2,1)} %own.11, s32[]{:T(128)S(6)} %select_n.16, s32[]{:T(128)S(6)} %select_n.15), kind=kLoop, calls=%fused_computation | loop fusion | bytes 6553608 | tf_op jit(solution)/shard_map/jit(dynamic_index_in_dim)/squeeze | solution.py:429
  3.9 0.5 collective-permute-start.8
  4.4 0.1 collective-permute-start.7
  4.5 0.1 stack.23.where
  4.5 0.6 pick.1
  5.1 0.5 collective-permute-start
  5.6 2.6 %collective-permute-start.1 = (bf16[32,1280]{1,0:T(8,128)(2,1)S(1)}, bf16[32,1280]{1,0:T(8,128)(2,1)S(1)}, u32[]{:S(2)}, u32[]{:S(2)}) collective-permute-start(bf16[32,1280]{1,0:T(8,128)(2,1)S(1)} %get-tuple-element.27), channel_id=1, source_target_pairs={{0,4},{1,5},{2,6},{3,7},{4,0},{5,1},{6,2},{7,3},{8,12},{9,13},{10,... | collective-permute-start | bytes 245768 | tf_op jit(solution)/shard_map/ppermute | solution.py:413
  8.2 0.1 collective-permute-start.2
  8.3 1.2 %collective-permute-done = bf16[32,1280]{1,0:T(8,128)(2,1)S(1)} collective-permute-done((bf16[32,1280]{1,0:T(8,128)(2,1)S(1)}, bf16[32,1280]{1,0:T(8,128)(2,1)S(1)}, u32[]{:S(2)}, u32[]{:S(2)}) %collective-permute-start) | collective-permute-done | bytes 81952 | tf_op jit(solution)/shard_map/ppermute | solution.py:413
  9.5 1.7 %collective-permute-done.1 = bf16[32,1280]{1,0:T(8,128)(2,1)S(1)} collective-permute-done((bf16[32,1280]{1,0:T(8,128)(2,1)S(1)}, bf16[32,1280]{1,0:T(8,128)(2,1)S(1)}, u32[]{:S(2)}, u32[]{:S(2)}) %collective-permute-start.1) | collective-permute-done | bytes 81952 | tf_op jit(solution)/shard_map/ppermute | solution.py:413
  11.3 1.4 %collective-permute-done.2 = bf16[32,1280]{1,0:T(8,128)(2,1)S(1)} collective-permute-done((bf16[32,1280]{1,0:T(8,128)(2,1)S(1)}, bf16[32,1280]{1,0:T(8,128)(2,1)S(1)}, u32[]{:S(2)}, u32[]{:S(2)}) %collective-permute-start.2) | collective-permute-done | bytes 81952 | tf_op jit(solution)/shard_map/ppermute | solution.py:413
  12.7 1.8 %collective-permute-start.3 = (bf16[128,1280]{1,0:T(8,128)(2,1)S(1)}, bf16[128,1280]{1,0:T(8,128)(2,1)S(1)}, u32[]{:S(2)}, u32[]{:S(2)}) collective-permute-start(bf16[128,1280]{1,0:T(8,128)(2,1)S(1)} %constant_dynamic-update-slice_fusion.refs_0_), channel_id=1, source_target_pairs={{0,8},{1,9},{2,10},{3,11},{4,12},{5,13},{6,14},{7,15},{8,0},{9,1},... | collective-permute-start | bytes 983048 | tf_op jit(solution)/shard_map/ppermute | solution.py:413
  14.5 0.0 collective-permute-start.6
  14.5 1.1 collective-permute-done.6.w_got
  15.7 0.0 collective-permute-done.8.got
  15.7 1.8 %share.5 = s16[1296,128]{1,0:T(8,128)(2,1)S(1)} custom-call(s32[5]{0:T(128)S(1)} %stack.23.where, f32[1,2]{1,0:T(1,128)S(1)} %copy-done.2, f32[1,2]{1,0:T(1,128)S(1)} %collective-permute-done.6.w_got, bf16[1,4,2,640,640]{4,3,2,1,0:T(8,128)(2,1)} %own.11, bf16[1,2,640,640]{3,2,1,0:T(8,128)(2,1)S(1)} %collective-permute-done.8.got, ...), custom_call_target="tpu_custom_call" | custom-call | flops 2621440 | bytes 1310720 | tf_op jit(solution)/shard_map/share/pallas_call | solution.py:96
  17.5 1.4 %collective-permute-start.9 = (s16[1296,128]{1,0:T(8,128)(2,1)S(1)}, s16[1296,128]{1,0:T(8,128)(2,1)S(1)}, u32[]{:S(2)}, u32[]{:S(2)}) collective-permute-start(s16[1296,128]{1,0:T(8,128)(2,1)S(1)} %share.5), channel_id=1, source_target_pairs={{0,4},{1,5},{2,6},{3,7},{4,0},{5,1},{6,2},{7,3},{8,12},{9,13},{10,... | collective-permute-start | bytes 995336 | tf_op jit(solution)/shard_map/ppermute | solution.py:413
  18.9 1.8 %share.6 = s16[1296,128]{1,0:T(8,128)(2,1)S(1)} custom-call(s32[5]{0:T(128)S(1)} %stack.23.where, f32[1,2]{1,0:T(1,128)S(1)} %copy-done.2, f32[1,2]{1,0:T(1,128)S(1)} %collective-permute-done.6.w_got, bf16[1,4,2,640,640]{4,3,2,1,0:T(8,128)(2,1)} %own.11, bf16[1,2,640,640]{3,2,1,0:T(8,128)(2,1)S(1)} %collective-permute-done.8.got, ...), custom_call_target="tpu_custom_call" | custom-call | flops 2621440 | bytes 1310720 | tf_op jit(solution)/shard_map/share/pallas_call | solution.py:96
  20.8 0.7 collective-permute-start.10
  21.5 1.8 %share.7 = s16[1296,128]{1,0:T(8,128)(2,1)S(1)} custom-call(s32[5]{0:T(128)S(1)} %stack.23.where, f32[1,2]{1,0:T(1,128)S(1)} %copy-done.2, f32[1,2]{1,0:T(1,128)S(1)} %collective-permute-done.6.w_got, bf16[1,4,2,640,640]{4,3,2,1,0:T(8,128)(2,1)} %own.11, bf16[1,2,640,640]{3,2,1,0:T(8,128)(2,1)S(1)} %collective-permute-done.8.got, ...), custom_call_target="tpu_custom_call" | custom-call | flops 2621440 | bytes 1310720 | tf_op jit(solution)/shard_map/share/pallas_call | solution.py:96
  23.4 1.4 %collective-permute-start.11 = (s16[1296,128]{1,0:T(8,128)(2,1)S(1)}, s16[1296,128]{1,0:T(8,128)(2,1)S(1)}, u32[]{:S(2)}, u32[]{:S(2)}) collective-permute-start(s16[1296,128]{1,0:T(8,128)(2,1)S(1)} %share.7), channel_id=1, source_target_pairs={{0,4},{1,5},{2,6},{3,7},{4,0},{5,1},{6,2},{7,3},{8,12},{9,13},{10,... | collective-permute-start | bytes 995336 | tf_op jit(solution)/shard_map/ppermute | solution.py:413
  24.8 0.0 collective-permute-done.3.refs_1_.refs_0_
  24.8 2.6 %collective-permute-start.4 = (bf16[128,1280]{1,0:T(8,128)(2,1)S(1)}, bf16[128,1280]{1,0:T(8,128)(2,1)S(1)}, u32[]{:S(2)}, u32[]{:S(2)}) collective-permute-start(bf16[128,1280]{1,0:T(8,128)(2,1)S(1)} %constant_dynamic-update-slice_fusion.refs_0_), channel_id=1, source_target_pairs={{0,16},{1,17},{2,18},{3,19},{4,20},{5,21},{6,22},{7,23},{8,24},{9,... | collective-permute-start | bytes 983048 | tf_op jit(solution)/shard_map/ppermute | solution.py:413
  27.4 0.0 collective-permute-done.7.got
  27.4 0.2 collective-permute-start.5
  27.6 1.8 %share.8 = s16[1296,128]{1,0:T(8,128)(2,1)S(1)} custom-call(s32[5]{0:T(128)S(1)} %stack.23.where, f32[1,2]{1,0:T(1,128)S(1)} %copy-done.2, f32[1,2]{1,0:T(1,128)S(1)} %collective-permute-done.6.w_got, bf16[1,4,2,640,640]{4,3,2,1,0:T(8,128)(2,1)} %own.11, bf16[1,2,640,640]{3,2,1,0:T(8,128)(2,1)S(1)} %collective-permute-done.8.got, ...), custom_call_target="tpu_custom_call" | custom-call | flops 2621440 | bytes 1310720 | tf_op jit(solution)/shard_map/share/pallas_call | solution.py:96
  29.5 4.6 %operator.1.refs_4_.refs_3_ = f32[5,2,640,128]{3,2,1,0:T(8,128)S(1)} custom-call(s32[5]{0:T(128)S(1)} %stack.23.where, f32[1,2]{1,0:T(1,128)S(1)} %copy-done.2, f32[1,2]{1,0:T(1,128)S(1)} %collective-permute-done.6.w_got, bf16[1,4,2,640,640]{4,3,2,1,0:T(8,128)(2,1)} %own.11, bf16[1,2,640,640]{3,2,1,0:T(8,128)(2,1)} %collective-permute-done.7.got), custom_call_target="tpu_custom_call" | custom-call | flops 13107200 | bytes 6553600 | tf_op jit(solution)/shard_map/operator/pallas_call | solution.py:96
  34.1 1.7 %copy-done = f32[5,2,640,128]{3,2,1,0:T(8,128)} copy-done((f32[5,2,640,128]{3,2,1,0:T(8,128)}, f32[5,2,640,128]{3,2,1,0:T(8,128)S(1)}, u32[]{:S(2)}) %copy-start) | copy-done | bytes 3276824
  35.8 12.9 %collective-permute-done.4.refs_2_.refs_1_ = bf16[128,1280]{1,0:T(8,128)(2,1)S(1)} collective-permute-done((bf16[128,1280]{1,0:T(8,128)(2,1)S(1)}, bf16[128,1280]{1,0:T(8,128)(2,1)S(1)}, u32[]{:S(2)}, u32[]{:S(2)}) %collective-permute-start.4) | collective-permute-done | bytes 327712 | tf_op jit(solution)/shard_map/ppermute | solution.py:413
  48.7 0.6 collective-permute-start.12
  49.3 0.0 collective-permute-done.5.refs_3_.refs_2_
  49.4 1.8 %share.9 = s16[1296,128]{1,0:T(8,128)(2,1)S(1)} custom-call(s32[5]{0:T(128)S(1)} %stack.23.where, f32[1,2]{1,0:T(1,128)S(1)} %copy-done.2, f32[1,2]{1,0:T(1,128)S(1)} %collective-permute-done.6.w_got, bf16[1,4,2,640,640]{4,3,2,1,0:T(8,128)(2,1)} %own.11, bf16[1,2,640,640]{3,2,1,0:T(8,128)(2,1)S(1)} %collective-permute-done.8.got, ...), custom_call_target="tpu_custom_call" | custom-call | flops 2621440 | bytes 1310720 | tf_op jit(solution)/shard_map/share/pallas_call | solution.py:96
  51.2 1.4 %collective-permute-start.13 = (s16[1296,128]{1,0:T(8,128)(2,1)S(1)}, s16[1296,128]{1,0:T(8,128)(2,1)S(1)}, u32[]{:S(2)}, u32[]{:S(2)}) collective-permute-start(s16[1296,128]{1,0:T(8,128)(2,1)S(1)} %share.9), channel_id=1, source_target_pairs={{0,4},{1,5},{2,6},{3,7},{4,0},{5,1},{6,2},{7,3},{8,12},{9,13},{10,... | collective-permute-start | bytes 995336 | tf_op jit(solution)/shard_map/ppermute | solution.py:413
  52.6 0.0 collective-permute-done.9.refs_5_
  52.6 0.0 collective-permute-done.10.refs_6_
  52.6 0.0 collective-permute-done.11.refs_7_
  52.7 4.7 %product.2 = (f32[3,128,256]{2,1,0:T(8,128)S(1)}, s16[784,128]{1,0:T(8,128)(2,1)S(1)}, s16[784,128]{1,0:T(8,128)(2,1)S(1)}, s16[784,128]{1,0:T(8,128)(2,1)S(1)}) custom-call(bf16[128,1280]{1,0:T(8,128)(2,1)S(1)} %constant_dynamic-update-slice_fusion.refs_0_, bf16[128,1280]{1,0:T(8,128)(2,1)S(1)} %collective-permute-done.3.refs_1_.refs_0_, ...), custom_call_target="tpu_custom_call" | custom-call | flops 2013265920 | bytes 4259840 | tf_op jit(solution)/shard_map/product/pallas_call | solution.py:180
  57.4 6.2 %collective-permute-start.14 = (s16[784,128]{1,0:T(8,128)(2,1)S(1)}, s16[784,128]{1,0:T(8,128)(2,1)S(1)}, u32[]{:S(2)}, u32[]{:S(2)}) collective-permute-start(s16[784,128]{1,0:T(8,128)(2,1)S(1)} %get-tuple-element.30), channel_id=1, source_target_pairs={{0,8},{1,9},{2,10},{3,11},{4,12},{5,13},{6,14},{7,15},{8,0},{9,1},... | collective-permute-start | bytes 602120 | tf_op jit(solution)/shard_map/ppermute | solution.py:413
  63.6 1.2 %collective-permute-start.15 = (s16[784,128]{1,0:T(8,128)(2,1)S(1)}, s16[784,128]{1,0:T(8,128)(2,1)S(1)}, u32[]{:S(2)}, u32[]{:S(2)}) collective-permute-start(s16[784,128]{1,0:T(8,128)(2,1)S(1)} %get-tuple-element.32), channel_id=1, source_target_pairs={{0,16},{1,17},{2,18},{3,19},{4,20},{5,21},{6,22},{7,23},{8,24},{9,... | collective-permute-start | bytes 602120 | tf_op jit(solution)/shard_map/ppermute | solution.py:413
  64.8 1.4 %collective-permute-start.16 = (s16[784,128]{1,0:T(8,128)(2,1)S(1)}, s16[784,128]{1,0:T(8,128)(2,1)S(1)}, u32[]{:S(2)}, u32[]{:S(2)}) collective-permute-start(s16[784,128]{1,0:T(8,128)(2,1)S(1)} %get-tuple-element.33), channel_id=1, source_target_pairs={{0,24},{1,25},{2,26},{3,27},{4,28},{5,29},{6,30},{7,31},{8,16},{9,... | collective-permute-start | bytes 602120 | tf_op jit(solution)/shard_map/ppermute | solution.py:413
  66.2 0.0 collective-permute-done.12.refs_5_
  66.2 0.0 collective-permute-done.13.refs_6_
  66.2 4.9 %collective-permute-done.14.refs_8_.refs_2_ = s16[784,128]{1,0:T(8,128)(2,1)S(1)} collective-permute-done((s16[784,128]{1,0:T(8,128)(2,1)S(1)}, s16[784,128]{1,0:T(8,128)(2,1)S(1)}, u32[]{:S(2)}, u32[]{:S(2)}) %collective-permute-start.14) | collective-permute-done | bytes 200736 | tf_op jit(solution)/shard_map/ppermute | solution.py:413
  71.1 3.5 %product.3 = (f32[2,128,256]{2,1,0:T(8,128)S(1)}, s16[528,128]{1,0:T(8,128)(2,1)S(1)}, s16[528,128]{1,0:T(8,128)(2,1)S(1)}, s16[528,128]{1,0:T(8,128)(2,1)S(1)}) custom-call(bf16[128,1280]{1,0:T(8,128)(2,1)S(1)} %constant_dynamic-update-slice_fusion.refs_0_, bf16[128,1280]{1,0:T(8,128)(2,1)S(1)} %collective-permute-done.3.refs_1_.refs_0_, ...), custom_call_target="tpu_custom_call" | custom-call | flops 1342177280 | bytes 3276800 | tf_op jit(solution)/shard_map/product/pallas_call | solution.py:180
  74.6 0.4 collective-permute-start.17
  75.1 1.7 %collective-permute-start.18 = (s16[528,128]{1,0:T(8,128)(2,1)S(1)}, s16[528,128]{1,0:T(8,128)(2,1)S(1)}, u32[]{:S(2)}, u32[]{:S(2)}) collective-permute-start(s16[528,128]{1,0:T(8,128)(2,1)S(1)} %get-tuple-element.35), channel_id=1, source_target_pairs={{0,16},{1,17},{2,18},{3,19},{4,20},{5,21},{6,22},{7,23},{8,24},{9,... | collective-permute-start | bytes 405512 | tf_op jit(solution)/shard_map/ppermute | solution.py:413
  76.8 2.3 %collective-permute-start.19 = (s16[528,128]{1,0:T(8,128)(2,1)S(1)}, s16[528,128]{1,0:T(8,128)(2,1)S(1)}, u32[]{:S(2)}, u32[]{:S(2)}) collective-permute-start(s16[528,128]{1,0:T(8,128)(2,1)S(1)} %get-tuple-element.36), channel_id=1, source_target_pairs={{0,24},{1,25},{2,26},{3,27},{4,28},{5,29},{6,30},{7,31},{8,16},{9,... | collective-permute-start | bytes 405512 | tf_op jit(solution)/shard_map/ppermute | solution.py:413
  79.1 3.4 %collective-permute-done.15.refs_3_ = s16[784,128]{1,0:T(8,128)(2,1)S(1)} collective-permute-done((s16[784,128]{1,0:T(8,128)(2,1)S(1)}, s16[784,128]{1,0:T(8,128)(2,1)S(1)}, u32[]{:S(2)}, u32[]{:S(2)}) %collective-permute-start.15) | collective-permute-done | bytes 200736 | tf_op jit(solution)/shard_map/ppermute | solution.py:413
  82.5 11.2 %collective-permute-done.18.refs_6_ = s16[528,128]{1,0:T(8,128)(2,1)S(1)} collective-permute-done((s16[528,128]{1,0:T(8,128)(2,1)S(1)}, s16[528,128]{1,0:T(8,128)(2,1)S(1)}, u32[]{:S(2)}, u32[]{:S(2)}) %collective-permute-start.18) | collective-permute-done | bytes 135200 | tf_op jit(solution)/shard_map/ppermute | solution.py:413
  93.6 3.9 %synthesis.1 = (f32[2,32,640]{2,1,0:T(8,128)S(1)}, s16[336,128]{1,0:T(8,128)(2,1)S(1)}, s16[336,128]{1,0:T(8,128)(2,1)S(1)}, s16[336,128]{1,0:T(8,128)(2,1)S(1)}...) custom-call(s32[5]{0:T(128)S(1)} %stack.23.where, ...), custom_call_target="tpu_custom_call" | custom-call | flops 838860800 | bytes 2949120 | tf_op jit(solution)/shard_map/synthesis/pallas_call | solution.py:279
  97.5 0.1 collective-permute-start.20
  97.6 1.4 %collective-permute-start.21 = (s16[336,128]{1,0:T(8,128)(2,1)S(1)}, s16[336,128]{1,0:T(8,128)(2,1)S(1)}, u32[]{:S(2)}, u32[]{:S(2)}) collective-permute-start(s16[336,128]{1,0:T(8,128)(2,1)S(1)} %get-tuple-element.39), channel_id=1, source_target_pairs={{0,4},{1,5},{2,6},{3,7},{4,0},{5,1},{6,2},{7,3},{8,12},{9,13},{10,... | collective-permute-start | bytes 258056 | tf_op jit(solution)/shard_map/ppermute | solution.py:413
  99.1 0.4 collective-permute-start.22
  99.5 1.5 %collective-permute-start.23 = (s16[336,128]{1,0:T(8,128)(2,1)S(1)}, s16[336,128]{1,0:T(8,128)(2,1)S(1)}, u32[]{:S(2)}, u32[]{:S(2)}) collective-permute-start(s16[336,128]{1,0:T(8,128)(2,1)S(1)} %get-tuple-element.41), channel_id=1, source_target_pairs={{0,1},{1,0},{2,3},{3,2},{4,5},{5,4},{6,7},{7,6},{8,9},{9,8},{10,11... | collective-permute-start | bytes 258056 | tf_op jit(solution)/shard_map/ppermute | solution.py:413
  101.0 0.2 collective-permute-start.24
  101.2 2.3 %collective-permute-start.25 = (s16[336,128]{1,0:T(8,128)(2,1)S(1)}, s16[336,128]{1,0:T(8,128)(2,1)S(1)}, u32[]{:S(2)}, u32[]{:S(2)}) collective-permute-start(s16[336,128]{1,0:T(8,128)(2,1)S(1)} %get-tuple-element.43), channel_id=1, source_target_pairs={{0,5},{1,4},{2,7},{3,6},{4,1},{5,0},{6,3},{7,2},{8,13},{9,12},{10,... | collective-permute-start | bytes 258056 | tf_op jit(solution)/shard_map/ppermute | solution.py:413
  103.5 0.0 collective-permute-done.21.refs_2_
  103.5 0.6 collective-permute-start.26
  104.1 0.0 collective-permute-done.22.refs_3_
  104.1 0.4 collective-permute-done.23.refs_4_
  104.6 1.2 %collective-permute-done.24.refs_5_ = s16[336,128]{1,0:T(8,128)(2,1)S(1)} collective-permute-done((s16[336,128]{1,0:T(8,128)(2,1)S(1)}, s16[336,128]{1,0:T(8,128)(2,1)S(1)}, u32[]{:S(2)}, u32[]{:S(2)}) %collective-permute-start.24) | collective-permute-done | bytes 86048 | tf_op jit(solution)/shard_map/ppermute | solution.py:413
  105.8 3.3 %collective-permute-done.25.refs_6_ = s16[336,128]{1,0:T(8,128)(2,1)S(1)} collective-permute-done((s16[336,128]{1,0:T(8,128)(2,1)S(1)}, s16[336,128]{1,0:T(8,128)(2,1)S(1)}, u32[]{:S(2)}, u32[]{:S(2)}) %collective-permute-start.25) | collective-permute-done | bytes 86048 | tf_op jit(solution)/shard_map/ppermute | solution.py:413
  109.1 1.2 %collective-permute-done.26.refs_7_ = s16[336,128]{1,0:T(8,128)(2,1)S(1)} collective-permute-done((s16[336,128]{1,0:T(8,128)(2,1)S(1)}, s16[336,128]{1,0:T(8,128)(2,1)S(1)}, u32[]{:S(2)}, u32[]{:S(2)}) %collective-permute-start.26) | collective-permute-done | bytes 86048 | tf_op jit(solution)/shard_map/ppermute | solution.py:413
  110.3 3.6 %place.1 = f32[8,2,32,640]{3,2,1,0:T(8,128)} custom-call(s32[5]{0:T(128)S(1)} %stack.23.where, s32[8]{0:T(128)S(1)} %copy-done.3, f32[2,32,640]{2,1,0:T(8,128)S(1)} %get-tuple-element.37.refs_0_, s16[336,128]{1,0:T(8,128)(2,1)S(1)} %collective-permute-done.20.refs_1_, s16[336,128]{1,0:T(8,128)(2,1)S(1)} %collective-permute-done.21.refs_2_, ...), custom_call_target="tpu_custom_call" | custom-call | tf_op jit(solution)/shard_map/place/pallas_call | solution.py:354
  (15 shorter events, 0.0 us)
Async XLA Ops:
  0.0 4.5 %copy-start.1 = (bf16[4,32,1280]{2,1,0:T(8,128)(2,1)S(1)}, bf16[4,32,1280]{2,1,0:T(8,128)(2,1)}, u32[]{:S(2)}) copy-start(bf16[4,32,1280]{2,1,0:T(8,128)(2,1)} %refs_3_.1) | copy-start | bytes 983044
  3.9 10.6 %copy-start.2 = (f32[1,2]{1,0:T(1,128)S(1)}, f32[1,2]{1,0:T(1,128)}, u32[]{:S(2)}) copy-start(f32[1,2]{1,0:T(1,128)} %w_own.11) | copy-start | bytes 28
  3.9 11.7 %collective-permute-start.8 = (bf16[1,2,640,640]{3,2,1,0:T(8,128)(2,1)}, bf16[1,2,640,640]{3,2,1,0:T(8,128)(2,1)S(1)}, u32[]{:S(2)}, u32[]{:S(2)}) collective-permute-start(bf16[1,2,640,640]{3,2,1,0:T(8,128)(2,1)} %get-tuple-element.45), channel_id=1, source_target_pairs={{0,2},{1,3},{2,0},{3,1},{4,6},{5,7},{6,4},{7,5},{8,10},{9,11},{10,... | collective-permute-start | bytes 4915208 | tf_op jit(solution)/shard_map/ppermute | solution.py:413
  4.4 23.0 %collective-permute-start.7 = (bf16[1,2,640,640]{3,2,1,0:T(8,128)(2,1)}, bf16[1,2,640,640]{3,2,1,0:T(8,128)(2,1)}, u32[]{:S(2)}, u32[]{:S(2)}) collective-permute-start(bf16[1,2,640,640]{3,2,1,0:T(8,128)(2,1)} %get-tuple-element.46), channel_id=1, source_target_pairs={{0,2},{1,3},{2,0},{3,1},{4,6},{5,7},{6,4},{7,5},{8,10},{9,11},{10,... | collective-permute-start | bytes 4915208 | tf_op jit(solution)/shard_map/ppermute | solution.py:413
  5.1 4.4 %collective-permute-start = (bf16[32,1280]{1,0:T(8,128)(2,1)S(1)}, bf16[32,1280]{1,0:T(8,128)(2,1)S(1)}, u32[]{:S(2)}, u32[]{:S(2)}) collective-permute-start(bf16[32,1280]{1,0:T(8,128)(2,1)S(1)} %get-tuple-element.26), channel_id=1, source_target_pairs={{0,2},{1,3},{2,0},{3,1},{4,6},{5,7},{6,4},{7,5},{8,10},{9,11},{10,... | collective-permute-start | bytes 245768 | tf_op jit(solution)/shard_map/ppermute | solution.py:413
  5.6 5.6 %collective-permute-start.1 = (bf16[32,1280]{1,0:T(8,128)(2,1)S(1)}, bf16[32,1280]{1,0:T(8,128)(2,1)S(1)}, u32[]{:S(2)}, u32[]{:S(2)}) collective-permute-start(bf16[32,1280]{1,0:T(8,128)(2,1)S(1)} %get-tuple-element.27), channel_id=1, source_target_pairs={{0,4},{1,5},{2,6},{3,7},{4,0},{5,1},{6,2},{7,3},{8,12},{9,13},{10,... | collective-permute-start | bytes 245768 | tf_op jit(solution)/shard_map/ppermute | solution.py:413
  8.2 4.5 %collective-permute-start.2 = (bf16[32,1280]{1,0:T(8,128)(2,1)S(1)}, bf16[32,1280]{1,0:T(8,128)(2,1)S(1)}, u32[]{:S(2)}, u32[]{:S(2)}) collective-permute-start(bf16[32,1280]{1,0:T(8,128)(2,1)S(1)} %get-tuple-element.28), channel_id=1, source_target_pairs={{0,6},{1,7},{2,4},{3,5},{4,2},{5,3},{6,0},{7,1},{8,14},{9,15},{10,... | collective-permute-start | bytes 245768 | tf_op jit(solution)/shard_map/ppermute | solution.py:413
  12.7 12.1 %collective-permute-start.3 = (bf16[128,1280]{1,0:T(8,128)(2,1)S(1)}, bf16[128,1280]{1,0:T(8,128)(2,1)S(1)}, u32[]{:S(2)}, u32[]{:S(2)}) collective-permute-start(bf16[128,1280]{1,0:T(8,128)(2,1)S(1)} %constant_dynamic-update-slice_fusion.refs_0_), channel_id=1, source_target_pairs={{0,8},{1,9},{2,10},{3,11},{4,12},{5,13},{6,14},{7,15},{8,0},{9,1},... | collective-permute-start | bytes 983048 | tf_op jit(solution)/shard_map/ppermute | solution.py:413
  14.5 1.1 collective-permute-start.6
  17.5 35.1 %collective-permute-start.9 = (s16[1296,128]{1,0:T(8,128)(2,1)S(1)}, s16[1296,128]{1,0:T(8,128)(2,1)S(1)}, u32[]{:S(2)}, u32[]{:S(2)}) collective-permute-start(s16[1296,128]{1,0:T(8,128)(2,1)S(1)} %share.5), channel_id=1, source_target_pairs={{0,4},{1,5},{2,6},{3,7},{4,0},{5,1},{6,2},{7,3},{8,12},{9,13},{10,... | collective-permute-start | bytes 995336 | tf_op jit(solution)/shard_map/ppermute | solution.py:413
  20.8 31.9 %collective-permute-start.10 = (s16[1296,128]{1,0:T(8,128)(2,1)S(1)}, s16[1296,128]{1,0:T(8,128)(2,1)S(1)}, u32[]{:S(2)}, u32[]{:S(2)}) collective-permute-start(s16[1296,128]{1,0:T(8,128)(2,1)S(1)} %share.6), channel_id=1, source_target_pairs={{0,4},{1,5},{2,6},{3,7},{4,0},{5,1},{6,2},{7,3},{8,12},{9,13},{10,... | collective-permute-start | bytes 995336 | tf_op jit(solution)/shard_map/ppermute | solution.py:413
  23.4 29.3 %collective-permute-start.11 = (s16[1296,128]{1,0:T(8,128)(2,1)S(1)}, s16[1296,128]{1,0:T(8,128)(2,1)S(1)}, u32[]{:S(2)}, u32[]{:S(2)}) collective-permute-start(s16[1296,128]{1,0:T(8,128)(2,1)S(1)} %share.7), channel_id=1, source_target_pairs={{0,4},{1,5},{2,6},{3,7},{4,0},{5,1},{6,2},{7,3},{8,12},{9,13},{10,... | collective-permute-start | bytes 995336 | tf_op jit(solution)/shard_map/ppermute | solution.py:413
  24.8 23.9 %collective-permute-start.4 = (bf16[128,1280]{1,0:T(8,128)(2,1)S(1)}, bf16[128,1280]{1,0:T(8,128)(2,1)S(1)}, u32[]{:S(2)}, u32[]{:S(2)}) collective-permute-start(bf16[128,1280]{1,0:T(8,128)(2,1)S(1)} %constant_dynamic-update-slice_fusion.refs_0_), channel_id=1, source_target_pairs={{0,16},{1,17},{2,18},{3,19},{4,20},{5,21},{6,22},{7,23},{8,24},{9,... | collective-permute-start | bytes 983048 | tf_op jit(solution)/shard_map/ppermute | solution.py:413
  27.4 22.0 %collective-permute-start.5 = (bf16[128,1280]{1,0:T(8,128)(2,1)S(1)}, bf16[128,1280]{1,0:T(8,128)(2,1)S(1)}, u32[]{:S(2)}, u32[]{:S(2)}) collective-permute-start(bf16[128,1280]{1,0:T(8,128)(2,1)S(1)} %constant_dynamic-update-slice_fusion.refs_0_), channel_id=1, source_target_pairs={{0,24},{1,25},{2,26},{3,27},{4,28},{5,29},{6,30},{7,31},{8,16},{9,... | collective-permute-start | bytes 983048 | tf_op jit(solution)/shard_map/ppermute | solution.py:413
  34.1 1.7 %copy-start = (f32[5,2,640,128]{3,2,1,0:T(8,128)}, f32[5,2,640,128]{3,2,1,0:T(8,128)S(1)}, u32[]{:S(2)}) copy-start(f32[5,2,640,128]{3,2,1,0:T(8,128)S(1)} %operator.1.refs_4_.refs_3_) | copy-start | bytes 9830404
  48.7 17.5 %collective-permute-start.12 = (s16[1296,128]{1,0:T(8,128)(2,1)S(1)}, s16[1296,128]{1,0:T(8,128)(2,1)S(1)}, u32[]{:S(2)}, u32[]{:S(2)}) collective-permute-start(s16[1296,128]{1,0:T(8,128)(2,1)S(1)} %share.8), channel_id=1, source_target_pairs={{0,4},{1,5},{2,6},{3,7},{4,0},{5,1},{6,2},{7,3},{8,12},{9,13},{10,... | collective-permute-start | bytes 995336 | tf_op jit(solution)/shard_map/ppermute | solution.py:413
  51.2 15.0 %collective-permute-start.13 = (s16[1296,128]{1,0:T(8,128)(2,1)S(1)}, s16[1296,128]{1,0:T(8,128)(2,1)S(1)}, u32[]{:S(2)}, u32[]{:S(2)}) collective-permute-start(s16[1296,128]{1,0:T(8,128)(2,1)S(1)} %share.9), channel_id=1, source_target_pairs={{0,4},{1,5},{2,6},{3,7},{4,0},{5,1},{6,2},{7,3},{8,12},{9,13},{10,... | collective-permute-start | bytes 995336 | tf_op jit(solution)/shard_map/ppermute | solution.py:413
  57.4 13.7 %collective-permute-start.14 = (s16[784,128]{1,0:T(8,128)(2,1)S(1)}, s16[784,128]{1,0:T(8,128)(2,1)S(1)}, u32[]{:S(2)}, u32[]{:S(2)}) collective-permute-start(s16[784,128]{1,0:T(8,128)(2,1)S(1)} %get-tuple-element.30), channel_id=1, source_target_pairs={{0,8},{1,9},{2,10},{3,11},{4,12},{5,13},{6,14},{7,15},{8,0},{9,1},... | collective-permute-start | bytes 602120 | tf_op jit(solution)/shard_map/ppermute | solution.py:413
  63.6 18.9 %collective-permute-start.15 = (s16[784,128]{1,0:T(8,128)(2,1)S(1)}, s16[784,128]{1,0:T(8,128)(2,1)S(1)}, u32[]{:S(2)}, u32[]{:S(2)}) collective-permute-start(s16[784,128]{1,0:T(8,128)(2,1)S(1)} %get-tuple-element.32), channel_id=1, source_target_pairs={{0,16},{1,17},{2,18},{3,19},{4,20},{5,21},{6,22},{7,23},{8,24},{9,... | collective-permute-start | bytes 602120 | tf_op jit(solution)/shard_map/ppermute | solution.py:413
  64.8 17.7 %collective-permute-start.16 = (s16[784,128]{1,0:T(8,128)(2,1)S(1)}, s16[784,128]{1,0:T(8,128)(2,1)S(1)}, u32[]{:S(2)}, u32[]{:S(2)}) collective-permute-start(s16[784,128]{1,0:T(8,128)(2,1)S(1)} %get-tuple-element.33), channel_id=1, source_target_pairs={{0,24},{1,25},{2,26},{3,27},{4,28},{5,29},{6,30},{7,31},{8,16},{9,... | collective-permute-start | bytes 602120 | tf_op jit(solution)/shard_map/ppermute | solution.py:413
  74.6 7.8 %collective-permute-start.17 = (s16[528,128]{1,0:T(8,128)(2,1)S(1)}, s16[528,128]{1,0:T(8,128)(2,1)S(1)}, u32[]{:S(2)}, u32[]{:S(2)}) collective-permute-start(s16[528,128]{1,0:T(8,128)(2,1)S(1)} %get-tuple-element.34), channel_id=1, source_target_pairs={{0,8},{1,9},{2,10},{3,11},{4,12},{5,13},{6,14},{7,15},{8,0},{9,1},... | collective-permute-start | bytes 405512 | tf_op jit(solution)/shard_map/ppermute | solution.py:413
  75.1 18.6 %collective-permute-start.18 = (s16[528,128]{1,0:T(8,128)(2,1)S(1)}, s16[528,128]{1,0:T(8,128)(2,1)S(1)}, u32[]{:S(2)}, u32[]{:S(2)}) collective-permute-start(s16[528,128]{1,0:T(8,128)(2,1)S(1)} %get-tuple-element.35), channel_id=1, source_target_pairs={{0,16},{1,17},{2,18},{3,19},{4,20},{5,21},{6,22},{7,23},{8,24},{9,... | collective-permute-start | bytes 405512 | tf_op jit(solution)/shard_map/ppermute | solution.py:413
  76.8 16.8 %collective-permute-start.19 = (s16[528,128]{1,0:T(8,128)(2,1)S(1)}, s16[528,128]{1,0:T(8,128)(2,1)S(1)}, u32[]{:S(2)}, u32[]{:S(2)}) collective-permute-start(s16[528,128]{1,0:T(8,128)(2,1)S(1)} %get-tuple-element.36), channel_id=1, source_target_pairs={{0,24},{1,25},{2,26},{3,27},{4,28},{5,29},{6,30},{7,31},{8,16},{9,... | collective-permute-start | bytes 405512 | tf_op jit(solution)/shard_map/ppermute | solution.py:413
  93.6 16.7 %copy-start.3 = (s32[8]{0:T(128)S(1)}, s32[8]{0:T(128)}, u32[]{:S(2)}) copy-start(s32[8]{0:T(128)} %column.1) | copy-start | bytes 100
  97.5 3.6 %collective-permute-start.20 = (s16[336,128]{1,0:T(8,128)(2,1)S(1)}, s16[336,128]{1,0:T(8,128)(2,1)S(1)}, u32[]{:S(2)}, u32[]{:S(2)}) collective-permute-start(s16[336,128]{1,0:T(8,128)(2,1)S(1)} %get-tuple-element.38), channel_id=1, source_target_pairs={{0,2},{1,3},{2,0},{3,1},{4,6},{5,7},{6,4},{7,5},{8,10},{9,11},{10,... | collective-permute-start | bytes 258056 | tf_op jit(solution)/shard_map/ppermute | solution.py:413
  97.6 5.9 %collective-permute-start.21 = (s16[336,128]{1,0:T(8,128)(2,1)S(1)}, s16[336,128]{1,0:T(8,128)(2,1)S(1)}, u32[]{:S(2)}, u32[]{:S(2)}) collective-permute-start(s16[336,128]{1,0:T(8,128)(2,1)S(1)} %get-tuple-element.39), channel_id=1, source_target_pairs={{0,4},{1,5},{2,6},{3,7},{4,0},{5,1},{6,2},{7,3},{8,12},{9,13},{10,... | collective-permute-start | bytes 258056 | tf_op jit(solution)/shard_map/ppermute | solution.py:413
  99.1 5.1 %collective-permute-start.22 = (s16[336,128]{1,0:T(8,128)(2,1)S(1)}, s16[336,128]{1,0:T(8,128)(2,1)S(1)}, u32[]{:S(2)}, u32[]{:S(2)}) collective-permute-start(s16[336,128]{1,0:T(8,128)(2,1)S(1)} %get-tuple-element.40), channel_id=1, source_target_pairs={{0,6},{1,7},{2,4},{3,5},{4,2},{5,3},{6,0},{7,1},{8,14},{9,15},{10,... | collective-permute-start | bytes 258056 | tf_op jit(solution)/shard_map/ppermute | solution.py:413
  99.5 5.1 %collective-permute-start.23 = (s16[336,128]{1,0:T(8,128)(2,1)S(1)}, s16[336,128]{1,0:T(8,128)(2,1)S(1)}, u32[]{:S(2)}, u32[]{:S(2)}) collective-permute-start(s16[336,128]{1,0:T(8,128)(2,1)S(1)} %get-tuple-element.41), channel_id=1, source_target_pairs={{0,1},{1,0},{2,3},{3,2},{4,5},{5,4},{6,7},{7,6},{8,9},{9,8},{10,11... | collective-permute-start | bytes 258056 | tf_op jit(solution)/shard_map/ppermute | solution.py:413
  101.0 4.8 %collective-permute-start.24 = (s16[336,128]{1,0:T(8,128)(2,1)S(1)}, s16[336,128]{1,0:T(8,128)(2,1)S(1)}, u32[]{:S(2)}, u32[]{:S(2)}) collective-permute-start(s16[336,128]{1,0:T(8,128)(2,1)S(1)} %get-tuple-element.42), channel_id=1, source_target_pairs={{0,3},{1,2},{2,1},{3,0},{4,7},{5,6},{6,5},{7,4},{8,11},{9,10},{10,... | collective-permute-start | bytes 258056 | tf_op jit(solution)/shard_map/ppermute | solution.py:413
  101.2 7.9 %collective-permute-start.25 = (s16[336,128]{1,0:T(8,128)(2,1)S(1)}, s16[336,128]{1,0:T(8,128)(2,1)S(1)}, u32[]{:S(2)}, u32[]{:S(2)}) collective-permute-start(s16[336,128]{1,0:T(8,128)(2,1)S(1)} %get-tuple-element.43), channel_id=1, source_target_pairs={{0,5},{1,4},{2,7},{3,6},{4,1},{5,0},{6,3},{7,2},{8,13},{9,12},{10,... | collective-permute-start | bytes 258056 | tf_op jit(solution)/shard_map/ppermute | solution.py:413
  103.5 6.8 %collective-permute-start.26 = (s16[336,128]{1,0:T(8,128)(2,1)S(1)}, s16[336,128]{1,0:T(8,128)(2,1)S(1)}, u32[]{:S(2)}, u32[]{:S(2)}) collective-permute-start(s16[336,128]{1,0:T(8,128)(2,1)S(1)} %get-tuple-element.44), channel_id=1, source_target_pairs={{0,7},{1,6},{2,5},{3,4},{4,3},{5,2},{6,1},{7,0},{8,15},{9,14},{10,... | collective-permute-start | bytes 258056 | tf_op jit(solution)/shard_map/ppermute | solution.py:413

commit v4 on v3

--- a/solution.py
+++ b/solution.py
@@ -123,8 +123,8 @@
 
 
 def product_kernel(count, tiles, after, *refs):
-    parts, own, got = refs[:count], refs[count], refs[count + 1 : count + 1 + tiles]
-    refs = refs[count + 1 + tiles + after :]
+    parts, own, got = refs[:count], refs[count], refs[count + 1]
+    refs = refs[count + 2 + after :]
     near, sends = refs[0], refs[1:count]
     full, op, tails = refs[count:]
     rows, width = parts[0].shape
@@ -141,12 +141,12 @@
 
         @pl.when(t == i)
         def _():
-            table = scales(got[i][2 * size :, :])
+            table = scales(got[2 * tiles * size :, :])
             real, imag = (
-                own[0, part]
-                + got[i][part * size : (part + 1) * size, :].astype(I32).astype(F32)
-                * table[part : part + 1, :]
-                for part in range(2)
+                own[0, strip % 2]
+                + got[strip * size : (strip + 1) * size, :].astype(I32).astype(F32)
+                * table[strip : strip + 1, :]
+                for strip in (2 * i, 2 * i + 1)
             )
             for level, (r, j) in enumerate(zip(split(real), split(imag))):
                 op[level, :size, :LANES] = r
@@ -172,8 +172,8 @@
             sends[q - 1][2 * tiles * rows :, :] = tails[q - 1].astype(I32).astype(I16)
 
 
-def product(parts, own, got, first, after):
-    count, tiles = len(parts), len(got)
+def product(parts, own, got, first, tiles, after):
+    count = len(parts)
     rows, width = parts[0].shape
     size = width // 2
     send = message(2 * tiles, rows)
@@ -185,7 +185,7 @@
         + [
             pl.BlockSpec((1, 2, size, LANES), lambda t: (t + first, 0, 0, 0)),
         ]
-        + [whole(x.shape) for x in got]
+        + [whole(got.shape)]
         + [pl.BlockSpec(memory_space=pl.ANY)] * len(after),
         out_specs=[pl.BlockSpec((1, rows, 2 * LANES), lambda t: (t, 0, 0))]
         + [whole(send.shape)] * (count - 1),
@@ -201,7 +201,7 @@
             transcendentals=0,
         ),
         name="product",
-    )(*parts, own, *got, *after)
+    )(*parts, own, got, *after)
 
 
 def add_up(near, got, write):
@@ -430,15 +430,15 @@
         for bits in (3, 1)
     )
     mine = operator(where, 0, term_weights, w_got, inverse, own, 0, tiles, False)
-    shares = []
-    for t in range(tiles):
-        after = (block,) if t < tiles - 1 else (*parts[1:], mine)
-        share = operator(where, 2, term_weights, w_got, inverse, far, t, 1, True, after)
-        shares.append(swap(share, 2))
+    behind = [(block,), (mine,)]
+    shares = [
+        swap(operator(where, 2, term_weights, w_got, inverse, far, *chunk, True, after), 2)
+        for chunk, after in zip(chunks, behind)
+    ]
     near, got = [], []
-    for first, count in chunks:
+    for chunk, share in zip(chunks, shares):
         after = [near[-1], got[-1][0]] if near else []
-        made = product(parts, mine, shares[first : first + count], first, after)
+        made = product(parts, mine, share, *chunk, after)
         near.append(made[0])
         got.append([swap(made[q], q * 4) for q in range(1, outer)])
     make = synthesis if legendre.shape[2] // waves % LANES == 0 else plain_synthesis

time: 114 us -> 105 us (0.921)
  starting transfers between devices: 33.8 us -> 29.7 us
  Pallas kernels: 30.1 us -> 26.7 us
  local copies, waits for them, and re-layouts: 5.73 us -> 4.05 us
    ppermute x27 -> x24, starting transfers between devices: 33.8 us -> 29.7 us  [swap(): return lax.ppermute(x, ('term', 'wave'), pairs)]
    pallas_call x6 -> x3, Pallas kernels: 13.8 us -> 10.4 us  [operator(): pl.pallas_call(functools.partial(share_kernel, len(after)) if coded else...]
    unnamed x11, local copies, waits for them, and re-layouts: 1.71 us -> 0.03 us
    ppermute x27 -> x24, waiting for transfers between devices: 44.1 us -> 44 us  [swap(): return lax.ppermute(x, ('term', 'wave'), pairs)]
  transfers between devices with their start and end apart: 27 -> 24, of which waited for: 12 -> 14; matrix products, arithmetic and copies ran while one was open for 0% -> 0% of each run, Pallas kernels for 20% -> 18%
where the time goes in v4:
time: 105 us
  waiting for transfers between devices  44 us (42%)
  starting transfers between devices  29.7 us (28%)
  Pallas kernels  26.7 us (25%)
  local copies, waits for them, and re-layouts  4.05 us (4%)
    ppermute x24, waiting for transfers between devices, swap(): return lax.ppermute(x, ('term', 'wave'), pairs)  44 us
    ppermute x24, starting transfers between devices, swap(): return lax.ppermute(x, ('term', 'wave'), pairs)  29.7 us
    pallas_call x3, Pallas kernels, operator(): pl.pallas_call(functools.partial(share_kernel, len(after)) if coded else...  10.4 us
    pallas_call x2, Pallas kernels, product(): pl.pallas_call(functools.partial(product_kernel, count, tiles, len(after)...  8.25 us
    squeeze x1, local copies, waits for them, and re-layouts, shards(): lax.dynamic_index_in_dim(inverse, place_of ^ bits, 1, keepdims=False)  3.92 us
    pallas_call x1, Pallas kernels, synthesis(): pl.pallas_call(functools.partial(synthesis_kernel, bands, len(near), len(...  3.89 us
    pallas_call x1, Pallas kernels, place(): pl.pallas_call(functools.partial(place_kernel, count), out_shape=jax.Shap...  3.58 us
  transfers between devices with their start and end apart: 24, of which 14 were waited for; matrix products, arithmetic and copies ran while one was open for 0% of the time, Pallas kernels for 18%

profile of v4, /device:TPU:0, one launch (start us, length us, event | category | flops | bytes accessed | tf_op | source)
XLA Modules:
  0.0 104.6 jit_solution(10815237703814164355)
XLA Ops:
  0.0 0.0 copy-start.1
  0.0 3.9 %dynamic-slice_bitcast_fusion = (bf16[1,2,640,640]{3,2,1,0:T(8,128)(2,1)}, bf16[1,2,640,640]{3,2,1,0:T(8,128)(2,1)}) fusion(bf16[1,4,2,640,640]{4,3,2,1,0:T(8,128)(2,1)} %own.5, s32[]{:T(128)S(6)} %select_n.16, s32[]{:T(128)S(6)} %select_n.15), kind=kLoop, calls=%fused_computation | loop fusion | bytes 6553608 | tf_op jit(solution)/shard_map/jit(dynamic_index_in_dim)/squeeze | solution.py:429
  3.9 0.5 collective-permute-start.8
  4.4 0.1 collective-permute-start.7
  4.4 0.1 stack.23.where
  4.5 0.0 copy-done.1
  4.5 0.6 pick.1
  5.1 0.5 collective-permute-start
  5.6 2.6 %collective-permute-start.1 = (bf16[32,1280]{1,0:T(8,128)(2,1)S(1)}, bf16[32,1280]{1,0:T(8,128)(2,1)S(1)}, u32[]{:S(2)}, u32[]{:S(2)}) collective-permute-start(bf16[32,1280]{1,0:T(8,128)(2,1)S(1)} %get-tuple-element.27), channel_id=1, source_target_pairs={{0,4},{1,5},{2,6},{3,7},{4,0},{5,1},{6,2},{7,3},{8,12},{9,13},{10,... | collective-permute-start | bytes 245768 | tf_op jit(solution)/shard_map/ppermute | solution.py:413
  8.2 0.1 collective-permute-start.2
  8.3 1.2 %collective-permute-done = bf16[32,1280]{1,0:T(8,128)(2,1)S(1)} collective-permute-done((bf16[32,1280]{1,0:T(8,128)(2,1)S(1)}, bf16[32,1280]{1,0:T(8,128)(2,1)S(1)}, u32[]{:S(2)}, u32[]{:S(2)}) %collective-permute-start) | collective-permute-done | bytes 81952 | tf_op jit(solution)/shard_map/ppermute | solution.py:413
  9.5 0.0 copy-done.2
  9.5 0.4 collective-permute-start.6
  9.9 1.4 %collective-permute-done.1 = bf16[32,1280]{1,0:T(8,128)(2,1)S(1)} collective-permute-done((bf16[32,1280]{1,0:T(8,128)(2,1)S(1)}, bf16[32,1280]{1,0:T(8,128)(2,1)S(1)}, u32[]{:S(2)}, u32[]{:S(2)}) %collective-permute-start.1) | collective-permute-done | bytes 81952 | tf_op jit(solution)/shard_map/ppermute | solution.py:413
  11.3 1.4 %collective-permute-done.2 = bf16[32,1280]{1,0:T(8,128)(2,1)S(1)} collective-permute-done((bf16[32,1280]{1,0:T(8,128)(2,1)S(1)}, bf16[32,1280]{1,0:T(8,128)(2,1)S(1)}, u32[]{:S(2)}, u32[]{:S(2)}) %collective-permute-start.2) | collective-permute-done | bytes 81952 | tf_op jit(solution)/shard_map/ppermute | solution.py:413
  12.7 0.0 collective-permute-done.6.w_got
  12.7 0.0 collective-permute-done.8.got
  12.7 3.2 %share.2 = s16[3856,128]{1,0:T(8,128)(2,1)S(1)} custom-call(s32[5]{0:T(128)S(1)} %stack.23.where, f32[1,2]{1,0:T(1,128)S(1)} %copy-done.2, f32[1,2]{1,0:T(1,128)S(1)} %collective-permute-done.6.w_got, bf16[1,4,2,640,640]{4,3,2,1,0:T(8,128)(2,1)} %own.5, bf16[1,2,640,640]{3,2,1,0:T(8,128)(2,1)S(1)} %collective-permute-done.8.got, ...), custom_call_target="tpu_custom_call" | custom-call | flops 7864320 | bytes 3932160 | tf_op jit(solution)/shard_map/share/pallas_call | solution.py:96
  16.0 1.7 %collective-permute-start.9 = (s16[3856,128]{1,0:T(8,128)(2,1)S(1)}, s16[3856,128]{1,0:T(8,128)(2,1)S(1)}, u32[]{:S(2)}, u32[]{:S(2)}) collective-permute-start(s16[3856,128]{1,0:T(8,128)(2,1)S(1)} %share.2), channel_id=1, source_target_pairs={{0,4},{1,5},{2,6},{3,7},{4,0},{5,1},{6,2},{7,3},{8,12},{9,13},{10,... | collective-permute-start | bytes 2961416 | tf_op jit(solution)/shard_map/ppermute | solution.py:413
  17.6 1.6 %collective-permute-start.3 = (bf16[128,1280]{1,0:T(8,128)(2,1)S(1)}, bf16[128,1280]{1,0:T(8,128)(2,1)S(1)}, u32[]{:S(2)}, u32[]{:S(2)}) collective-permute-start(bf16[128,1280]{1,0:T(8,128)(2,1)S(1)} %constant_dynamic-update-slice_fusion.refs_0_), channel_id=1, source_target_pairs={{0,8},{1,9},{2,10},{3,11},{4,12},{5,13},{6,14},{7,15},{8,0},{9,1},... | collective-permute-start | bytes 983048 | tf_op jit(solution)/shard_map/ppermute | solution.py:413
  19.2 2.6 %collective-permute-start.4 = (bf16[128,1280]{1,0:T(8,128)(2,1)S(1)}, bf16[128,1280]{1,0:T(8,128)(2,1)S(1)}, u32[]{:S(2)}, u32[]{:S(2)}) collective-permute-start(bf16[128,1280]{1,0:T(8,128)(2,1)S(1)} %constant_dynamic-update-slice_fusion.refs_0_), channel_id=1, source_target_pairs={{0,16},{1,17},{2,18},{3,19},{4,20},{5,21},{6,22},{7,23},{8,24},{9,... | collective-permute-start | bytes 983048 | tf_op jit(solution)/shard_map/ppermute | solution.py:413
  21.8 0.2 collective-permute-start.5
  22.0 0.0 collective-permute-done.7.got
  22.0 4.6 %operator.1.refs_4_.refs_0_ = f32[5,2,640,128]{3,2,1,0:T(8,128)S(1)} custom-call(s32[5]{0:T(128)S(1)} %stack.23.where, f32[1,2]{1,0:T(1,128)S(1)} %copy-done.2, f32[1,2]{1,0:T(1,128)S(1)} %collective-permute-done.6.w_got, bf16[1,4,2,640,640]{4,3,2,1,0:T(8,128)(2,1)} %own.5, bf16[1,2,640,640]{3,2,1,0:T(8,128)(2,1)} %collective-permute-done.7.got), custom_call_target="tpu_custom_call" | custom-call | flops 13107200 | bytes 6553600 | tf_op jit(solution)/shard_map/operator/pallas_call | solution.py:96
  26.6 0.0 copy-start
  26.6 2.5 %share.3 = s16[2576,128]{1,0:T(8,128)(2,1)S(1)} custom-call(s32[5]{0:T(128)S(1)} %stack.23.where, f32[1,2]{1,0:T(1,128)S(1)} %copy-done.2, f32[1,2]{1,0:T(1,128)S(1)} %collective-permute-done.6.w_got, bf16[1,4,2,640,640]{4,3,2,1,0:T(8,128)(2,1)} %own.5, bf16[1,2,640,640]{3,2,1,0:T(8,128)(2,1)S(1)} %collective-permute-done.8.got, ...), custom_call_target="tpu_custom_call" | custom-call | flops 5242880 | bytes 2621440 | tf_op jit(solution)/shard_map/share/pallas_call | solution.py:96
  29.2 0.0 copy-done
  29.2 0.5 collective-permute-start.10
  29.7 3.9 %collective-permute-done.3.refs_1_ = bf16[128,1280]{1,0:T(8,128)(2,1)S(1)} collective-permute-done((bf16[128,1280]{1,0:T(8,128)(2,1)S(1)}, bf16[128,1280]{1,0:T(8,128)(2,1)S(1)}, u32[]{:S(2)}, u32[]{:S(2)}) %collective-permute-start.3) | collective-permute-done | bytes 327712 | tf_op jit(solution)/shard_map/ppermute | solution.py:413
  33.6 11.2 %collective-permute-done.4.refs_2_ = bf16[128,1280]{1,0:T(8,128)(2,1)S(1)} collective-permute-done((bf16[128,1280]{1,0:T(8,128)(2,1)S(1)}, bf16[128,1280]{1,0:T(8,128)(2,1)S(1)}, u32[]{:S(2)}, u32[]{:S(2)}) %collective-permute-start.4) | collective-permute-done | bytes 327712 | tf_op jit(solution)/shard_map/ppermute | solution.py:413
  44.8 0.0 collective-permute-done.5.refs_3_
  44.8 0.0 collective-permute-done.9.refs_5_
  44.8 4.7 %product.2 = (f32[3,128,256]{2,1,0:T(8,128)S(1)}, s16[784,128]{1,0:T(8,128)(2,1)S(1)}, s16[784,128]{1,0:T(8,128)(2,1)S(1)}, s16[784,128]{1,0:T(8,128)(2,1)S(1)}) custom-call(bf16[128,1280]{1,0:T(8,128)(2,1)S(1)} %constant_dynamic-update-slice_fusion.refs_0_, bf16[128,1280]{1,0:T(8,128)(2,1)S(1)} %collective-permute-done.3.refs_1_, ...), custom_call_target="tpu_custom_call" | custom-call | flops 2013265920 | bytes 4259840 | tf_op jit(solution)/shard_map/product/pallas_call | solution.py:180
  49.5 6.4 %collective-permute-start.11 = (s16[784,128]{1,0:T(8,128)(2,1)S(1)}, s16[784,128]{1,0:T(8,128)(2,1)S(1)}, u32[]{:S(2)}, u32[]{:S(2)}) collective-permute-start(s16[784,128]{1,0:T(8,128)(2,1)S(1)} %get-tuple-element.30), channel_id=1, source_target_pairs={{0,8},{1,9},{2,10},{3,11},{4,12},{5,13},{6,14},{7,15},{8,0},{9,1},... | collective-permute-start | bytes 602120 | tf_op jit(solution)/shard_map/ppermute | solution.py:413
  55.9 1.1 %collective-permute-start.12 = (s16[784,128]{1,0:T(8,128)(2,1)S(1)}, s16[784,128]{1,0:T(8,128)(2,1)S(1)}, u32[]{:S(2)}, u32[]{:S(2)}) collective-permute-start(s16[784,128]{1,0:T(8,128)(2,1)S(1)} %get-tuple-element.32), channel_id=1, source_target_pairs={{0,16},{1,17},{2,18},{3,19},{4,20},{5,21},{6,22},{7,23},{8,24},{9,... | collective-permute-start | bytes 602120 | tf_op jit(solution)/shard_map/ppermute | solution.py:413
  57.0 1.4 %collective-permute-start.13 = (s16[784,128]{1,0:T(8,128)(2,1)S(1)}, s16[784,128]{1,0:T(8,128)(2,1)S(1)}, u32[]{:S(2)}, u32[]{:S(2)}) collective-permute-start(s16[784,128]{1,0:T(8,128)(2,1)S(1)} %get-tuple-element.33), channel_id=1, source_target_pairs={{0,24},{1,25},{2,26},{3,27},{4,28},{5,29},{6,30},{7,31},{8,16},{9,... | collective-permute-start | bytes 602120 | tf_op jit(solution)/shard_map/ppermute | solution.py:413
  58.4 0.0 collective-permute-done.10.refs_5_
  58.4 4.2 %collective-permute-done.11.refs_7_.refs_2_ = s16[784,128]{1,0:T(8,128)(2,1)S(1)} collective-permute-done((s16[784,128]{1,0:T(8,128)(2,1)S(1)}, s16[784,128]{1,0:T(8,128)(2,1)S(1)}, u32[]{:S(2)}, u32[]{:S(2)}) %collective-permute-start.11) | collective-permute-done | bytes 200736 | tf_op jit(solution)/shard_map/ppermute | solution.py:413
  62.6 3.5 %product.3 = (f32[2,128,256]{2,1,0:T(8,128)S(1)}, s16[528,128]{1,0:T(8,128)(2,1)S(1)}, s16[528,128]{1,0:T(8,128)(2,1)S(1)}, s16[528,128]{1,0:T(8,128)(2,1)S(1)}) custom-call(bf16[128,1280]{1,0:T(8,128)(2,1)S(1)} %constant_dynamic-update-slice_fusion.refs_0_, bf16[128,1280]{1,0:T(8,128)(2,1)S(1)} %collective-permute-done.3.refs_1_, ...), custom_call_target="tpu_custom_call" | custom-call | flops 1342177280 | bytes 3276800 | tf_op jit(solution)/shard_map/product/pallas_call | solution.py:180
  66.2 1.3 %collective-permute-start.14 = (s16[528,128]{1,0:T(8,128)(2,1)S(1)}, s16[528,128]{1,0:T(8,128)(2,1)S(1)}, u32[]{:S(2)}, u32[]{:S(2)}) collective-permute-start(s16[528,128]{1,0:T(8,128)(2,1)S(1)} %get-tuple-element.34), channel_id=1, source_target_pairs={{0,8},{1,9},{2,10},{3,11},{4,12},{5,13},{6,14},{7,15},{8,0},{9,1},... | collective-permute-start | bytes 405512 | tf_op jit(solution)/shard_map/ppermute | solution.py:413
  67.4 1.8 %collective-permute-start.15 = (s16[528,128]{1,0:T(8,128)(2,1)S(1)}, s16[528,128]{1,0:T(8,128)(2,1)S(1)}, u32[]{:S(2)}, u32[]{:S(2)}) collective-permute-start(s16[528,128]{1,0:T(8,128)(2,1)S(1)} %get-tuple-element.35), channel_id=1, source_target_pairs={{0,16},{1,17},{2,18},{3,19},{4,20},{5,21},{6,22},{7,23},{8,24},{9,... | collective-permute-start | bytes 405512 | tf_op jit(solution)/shard_map/ppermute | solution.py:413
  69.2 1.4 %collective-permute-start.16 = (s16[528,128]{1,0:T(8,128)(2,1)S(1)}, s16[528,128]{1,0:T(8,128)(2,1)S(1)}, u32[]{:S(2)}, u32[]{:S(2)}) collective-permute-start(s16[528,128]{1,0:T(8,128)(2,1)S(1)} %get-tuple-element.36), channel_id=1, source_target_pairs={{0,24},{1,25},{2,26},{3,27},{4,28},{5,29},{6,30},{7,31},{8,16},{9,... | collective-permute-start | bytes 405512 | tf_op jit(solution)/shard_map/ppermute | solution.py:413
  70.6 4.2 %collective-permute-done.12.refs_3_ = s16[784,128]{1,0:T(8,128)(2,1)S(1)} collective-permute-done((s16[784,128]{1,0:T(8,128)(2,1)S(1)}, s16[784,128]{1,0:T(8,128)(2,1)S(1)}, u32[]{:S(2)}, u32[]{:S(2)}) %collective-permute-start.12) | collective-permute-done | bytes 200736 | tf_op jit(solution)/shard_map/ppermute | solution.py:413
  74.8 0.0 collective-permute-done.13.refs_4_
  74.8 0.0 collective-permute-done.14.refs_5_
  74.8 10.6 %collective-permute-done.15.refs_6_ = s16[528,128]{1,0:T(8,128)(2,1)S(1)} collective-permute-done((s16[528,128]{1,0:T(8,128)(2,1)S(1)}, s16[528,128]{1,0:T(8,128)(2,1)S(1)}, u32[]{:S(2)}, u32[]{:S(2)}) %collective-permute-start.15) | collective-permute-done | bytes 135200 | tf_op jit(solution)/shard_map/ppermute | solution.py:413
  85.4 0.0 collective-permute-done.16.refs_7_
  85.4 3.9 %synthesis.1 = (f32[2,32,640]{2,1,0:T(8,128)S(1)}, s16[336,128]{1,0:T(8,128)(2,1)S(1)}, s16[336,128]{1,0:T(8,128)(2,1)S(1)}, s16[336,128]{1,0:T(8,128)(2,1)S(1)}...) custom-call(s32[5]{0:T(128)S(1)} %stack.23.where, ...), custom_call_target="tpu_custom_call" | custom-call | flops 838860800 | bytes 2949120 | tf_op jit(solution)/shard_map/synthesis/pallas_call | solution.py:279
  89.3 0.1 collective-permute-start.17
  89.4 0.4 collective-permute-start.18
  89.8 1.5 %collective-permute-start.19 = (s16[336,128]{1,0:T(8,128)(2,1)S(1)}, s16[336,128]{1,0:T(8,128)(2,1)S(1)}, u32[]{:S(2)}, u32[]{:S(2)}) collective-permute-start(s16[336,128]{1,0:T(8,128)(2,1)S(1)} %get-tuple-element.40), channel_id=1, source_target_pairs={{0,6},{1,7},{2,4},{3,5},{4,2},{5,3},{6,0},{7,1},{8,14},{9,15},{10,... | collective-permute-start | bytes 258056 | tf_op jit(solution)/shard_map/ppermute | solution.py:413
  91.2 1.5 %collective-permute-start.20 = (s16[336,128]{1,0:T(8,128)(2,1)S(1)}, s16[336,128]{1,0:T(8,128)(2,1)S(1)}, u32[]{:S(2)}, u32[]{:S(2)}) collective-permute-start(s16[336,128]{1,0:T(8,128)(2,1)S(1)} %get-tuple-element.41), channel_id=1, source_target_pairs={{0,1},{1,0},{2,3},{3,2},{4,5},{5,4},{6,7},{7,6},{8,9},{9,8},{10,11... | collective-permute-start | bytes 258056 | tf_op jit(solution)/shard_map/ppermute | solution.py:413
  92.7 0.2 collective-permute-start.21
  92.9 0.0 collective-permute-done.17.refs_1_
  92.9 1.3 %collective-permute-start.22 = (s16[336,128]{1,0:T(8,128)(2,1)S(1)}, s16[336,128]{1,0:T(8,128)(2,1)S(1)}, u32[]{:S(2)}, u32[]{:S(2)}) collective-permute-start(s16[336,128]{1,0:T(8,128)(2,1)S(1)} %get-tuple-element.43), channel_id=1, source_target_pairs={{0,5},{1,4},{2,7},{3,6},{4,1},{5,0},{6,3},{7,2},{8,13},{9,12},{10,... | collective-permute-start | bytes 258056 | tf_op jit(solution)/shard_map/ppermute | solution.py:413
  94.2 0.6 collective-permute-done.18.refs_2_
  94.8 0.9 collective-permute-start.23
  95.6 0.1 collective-permute-done.19.refs_3_
  95.7 0.6 collective-permute-done.20.refs_4_
  96.3 1.2 %collective-permute-done.21.refs_5_ = s16[336,128]{1,0:T(8,128)(2,1)S(1)} collective-permute-done((s16[336,128]{1,0:T(8,128)(2,1)S(1)}, s16[336,128]{1,0:T(8,128)(2,1)S(1)}, u32[]{:S(2)}, u32[]{:S(2)}) %collective-permute-start.21) | collective-permute-done | bytes 86048 | tf_op jit(solution)/shard_map/ppermute | solution.py:413
  97.5 2.2 %collective-permute-done.22.refs_6_ = s16[336,128]{1,0:T(8,128)(2,1)S(1)} collective-permute-done((s16[336,128]{1,0:T(8,128)(2,1)S(1)}, s16[336,128]{1,0:T(8,128)(2,1)S(1)}, u32[]{:S(2)}, u32[]{:S(2)}) %collective-permute-start.22) | collective-permute-done | bytes 86048 | tf_op jit(solution)/shard_map/ppermute | solution.py:413
  99.8 1.2 %collective-permute-done.23.refs_7_ = s16[336,128]{1,0:T(8,128)(2,1)S(1)} collective-permute-done((s16[336,128]{1,0:T(8,128)(2,1)S(1)}, s16[336,128]{1,0:T(8,128)(2,1)S(1)}, u32[]{:S(2)}, u32[]{:S(2)}) %collective-permute-start.23) | collective-permute-done | bytes 86048 | tf_op jit(solution)/shard_map/ppermute | solution.py:413
  101.0 0.0 copy-done.3
  101.0 3.6 %place.1 = f32[8,2,32,640]{3,2,1,0:T(8,128)} custom-call(s32[5]{0:T(128)S(1)} %stack.23.where, s32[8]{0:T(128)S(1)} %copy-done.3, f32[2,32,640]{2,1,0:T(8,128)S(1)} %get-tuple-element.37.refs_0_, s16[336,128]{1,0:T(8,128)(2,1)S(1)} %collective-permute-done.17.refs_1_, s16[336,128]{1,0:T(8,128)(2,1)S(1)} %collective-permute-done.18.refs_2_, ...), custom_call_target="tpu_custom_call" | custom-call | tf_op jit(solution)/shard_map/place/pallas_call | solution.py:354
  (6 shorter events, 0.0 us)
Async XLA Ops:
  0.0 4.5 %copy-start.1 = (bf16[4,32,1280]{2,1,0:T(8,128)(2,1)S(1)}, bf16[4,32,1280]{2,1,0:T(8,128)(2,1)}, u32[]{:S(2)}) copy-start(bf16[4,32,1280]{2,1,0:T(8,128)(2,1)} %refs_3_.1) | copy-start | bytes 983044
  0.0 9.5 %copy-start.2 = (f32[1,2]{1,0:T(1,128)S(1)}, f32[1,2]{1,0:T(1,128)}, u32[]{:S(2)}) copy-start(f32[1,2]{1,0:T(1,128)} %w_own.5) | copy-start | bytes 28
  3.9 8.8 %collective-permute-start.8 = (bf16[1,2,640,640]{3,2,1,0:T(8,128)(2,1)}, bf16[1,2,640,640]{3,2,1,0:T(8,128)(2,1)S(1)}, u32[]{:S(2)}, u32[]{:S(2)}) collective-permute-start(bf16[1,2,640,640]{3,2,1,0:T(8,128)(2,1)} %get-tuple-element.45), channel_id=1, source_target_pairs={{0,2},{1,3},{2,0},{3,1},{4,6},{5,7},{6,4},{7,5},{8,10},{9,11},{10,... | collective-permute-start | bytes 4915208 | tf_op jit(solution)/shard_map/ppermute | solution.py:413
  4.4 17.6 %collective-permute-start.7 = (bf16[1,2,640,640]{3,2,1,0:T(8,128)(2,1)}, bf16[1,2,640,640]{3,2,1,0:T(8,128)(2,1)}, u32[]{:S(2)}, u32[]{:S(2)}) collective-permute-start(bf16[1,2,640,640]{3,2,1,0:T(8,128)(2,1)} %get-tuple-element.46), channel_id=1, source_target_pairs={{0,2},{1,3},{2,0},{3,1},{4,6},{5,7},{6,4},{7,5},{8,10},{9,11},{10,... | collective-permute-start | bytes 4915208 | tf_op jit(solution)/shard_map/ppermute | solution.py:413
  5.1 4.4 %collective-permute-start = (bf16[32,1280]{1,0:T(8,128)(2,1)S(1)}, bf16[32,1280]{1,0:T(8,128)(2,1)S(1)}, u32[]{:S(2)}, u32[]{:S(2)}) collective-permute-start(bf16[32,1280]{1,0:T(8,128)(2,1)S(1)} %get-tuple-element.26), channel_id=1, source_target_pairs={{0,2},{1,3},{2,0},{3,1},{4,6},{5,7},{6,4},{7,5},{8,10},{9,11},{10,... | collective-permute-start | bytes 245768 | tf_op jit(solution)/shard_map/ppermute | solution.py:413
  5.6 5.6 %collective-permute-start.1 = (bf16[32,1280]{1,0:T(8,128)(2,1)S(1)}, bf16[32,1280]{1,0:T(8,128)(2,1)S(1)}, u32[]{:S(2)}, u32[]{:S(2)}) collective-permute-start(bf16[32,1280]{1,0:T(8,128)(2,1)S(1)} %get-tuple-element.27), channel_id=1, source_target_pairs={{0,4},{1,5},{2,6},{3,7},{4,0},{5,1},{6,2},{7,3},{8,12},{9,13},{10,... | collective-permute-start | bytes 245768 | tf_op jit(solution)/shard_map/ppermute | solution.py:413
  8.2 4.5 %collective-permute-start.2 = (bf16[32,1280]{1,0:T(8,128)(2,1)S(1)}, bf16[32,1280]{1,0:T(8,128)(2,1)S(1)}, u32[]{:S(2)}, u32[]{:S(2)}) collective-permute-start(bf16[32,1280]{1,0:T(8,128)(2,1)S(1)} %get-tuple-element.28), channel_id=1, source_target_pairs={{0,6},{1,7},{2,4},{3,5},{4,2},{5,3},{6,0},{7,1},{8,14},{9,15},{10,... | collective-permute-start | bytes 245768 | tf_op jit(solution)/shard_map/ppermute | solution.py:413
  9.5 3.2 %collective-permute-start.6 = (f32[1,2]{1,0:T(1,128)S(1)}, f32[1,2]{1,0:T(1,128)S(1)}, u32[]{:S(2)}, u32[]{:S(2)}) collective-permute-start(f32[1,2]{1,0:T(1,128)S(1)} %copy-done.2), channel_id=1, source_target_pairs={{0,2},{1,3},{2,0},{3,1},{4,6},{5,7},{6,4},{7,5},{8,10},{9,11},{10,... | collective-permute-start | bytes 32 | tf_op jit(solution)/shard_map/ppermute | solution.py:413
  16.0 28.8 %collective-permute-start.9 = (s16[3856,128]{1,0:T(8,128)(2,1)S(1)}, s16[3856,128]{1,0:T(8,128)(2,1)S(1)}, u32[]{:S(2)}, u32[]{:S(2)}) collective-permute-start(s16[3856,128]{1,0:T(8,128)(2,1)S(1)} %share.2), channel_id=1, source_target_pairs={{0,4},{1,5},{2,6},{3,7},{4,0},{5,1},{6,2},{7,3},{8,12},{9,13},{10,... | collective-permute-start | bytes 2961416 | tf_op jit(solution)/shard_map/ppermute | solution.py:413
  17.6 16.0 %collective-permute-start.3 = (bf16[128,1280]{1,0:T(8,128)(2,1)S(1)}, bf16[128,1280]{1,0:T(8,128)(2,1)S(1)}, u32[]{:S(2)}, u32[]{:S(2)}) collective-permute-start(bf16[128,1280]{1,0:T(8,128)(2,1)S(1)} %constant_dynamic-update-slice_fusion.refs_0_), channel_id=1, source_target_pairs={{0,8},{1,9},{2,10},{3,11},{4,12},{5,13},{6,14},{7,15},{8,0},{9,1},... | collective-permute-start | bytes 983048 | tf_op jit(solution)/shard_map/ppermute | solution.py:413
  19.2 25.6 %collective-permute-start.4 = (bf16[128,1280]{1,0:T(8,128)(2,1)S(1)}, bf16[128,1280]{1,0:T(8,128)(2,1)S(1)}, u32[]{:S(2)}, u32[]{:S(2)}) collective-permute-start(bf16[128,1280]{1,0:T(8,128)(2,1)S(1)} %constant_dynamic-update-slice_fusion.refs_0_), channel_id=1, source_target_pairs={{0,16},{1,17},{2,18},{3,19},{4,20},{5,21},{6,22},{7,23},{8,24},{9,... | collective-permute-start | bytes 983048 | tf_op jit(solution)/shard_map/ppermute | solution.py:413
  21.8 23.0 %collective-permute-start.5 = (bf16[128,1280]{1,0:T(8,128)(2,1)S(1)}, bf16[128,1280]{1,0:T(8,128)(2,1)S(1)}, u32[]{:S(2)}, u32[]{:S(2)}) collective-permute-start(bf16[128,1280]{1,0:T(8,128)(2,1)S(1)} %constant_dynamic-update-slice_fusion.refs_0_), channel_id=1, source_target_pairs={{0,24},{1,25},{2,26},{3,27},{4,28},{5,29},{6,30},{7,31},{8,16},{9,... | collective-permute-start | bytes 983048 | tf_op jit(solution)/shard_map/ppermute | solution.py:413
  26.6 2.6 %copy-start = (f32[5,2,640,128]{3,2,1,0:T(8,128)}, f32[5,2,640,128]{3,2,1,0:T(8,128)S(1)}, u32[]{:S(2)}) copy-start(f32[5,2,640,128]{3,2,1,0:T(8,128)S(1)} %operator.1.refs_4_.refs_0_) | copy-start | bytes 9830404
  29.2 29.2 %collective-permute-start.10 = (s16[2576,128]{1,0:T(8,128)(2,1)S(1)}, s16[2576,128]{1,0:T(8,128)(2,1)S(1)}, u32[]{:S(2)}, u32[]{:S(2)}) collective-permute-start(s16[2576,128]{1,0:T(8,128)(2,1)S(1)} %share.3), channel_id=1, source_target_pairs={{0,4},{1,5},{2,6},{3,7},{4,0},{5,1},{6,2},{7,3},{8,12},{9,13},{10,... | collective-permute-start | bytes 1978376 | tf_op jit(solution)/shard_map/ppermute | solution.py:413
  49.5 13.1 %collective-permute-start.11 = (s16[784,128]{1,0:T(8,128)(2,1)S(1)}, s16[784,128]{1,0:T(8,128)(2,1)S(1)}, u32[]{:S(2)}, u32[]{:S(2)}) collective-permute-start(s16[784,128]{1,0:T(8,128)(2,1)S(1)} %get-tuple-element.30), channel_id=1, source_target_pairs={{0,8},{1,9},{2,10},{3,11},{4,12},{5,13},{6,14},{7,15},{8,0},{9,1},... | collective-permute-start | bytes 602120 | tf_op jit(solution)/shard_map/ppermute | solution.py:413
  55.9 18.9 %collective-permute-start.12 = (s16[784,128]{1,0:T(8,128)(2,1)S(1)}, s16[784,128]{1,0:T(8,128)(2,1)S(1)}, u32[]{:S(2)}, u32[]{:S(2)}) collective-permute-start(s16[784,128]{1,0:T(8,128)(2,1)S(1)} %get-tuple-element.32), channel_id=1, source_target_pairs={{0,16},{1,17},{2,18},{3,19},{4,20},{5,21},{6,22},{7,23},{8,24},{9,... | collective-permute-start | bytes 602120 | tf_op jit(solution)/shard_map/ppermute | solution.py:413
  57.0 17.8 %collective-permute-start.13 = (s16[784,128]{1,0:T(8,128)(2,1)S(1)}, s16[784,128]{1,0:T(8,128)(2,1)S(1)}, u32[]{:S(2)}, u32[]{:S(2)}) collective-permute-start(s16[784,128]{1,0:T(8,128)(2,1)S(1)} %get-tuple-element.33), channel_id=1, source_target_pairs={{0,24},{1,25},{2,26},{3,27},{4,28},{5,29},{6,30},{7,31},{8,16},{9,... | collective-permute-start | bytes 602120 | tf_op jit(solution)/shard_map/ppermute | solution.py:413
  66.2 8.6 %collective-permute-start.14 = (s16[528,128]{1,0:T(8,128)(2,1)S(1)}, s16[528,128]{1,0:T(8,128)(2,1)S(1)}, u32[]{:S(2)}, u32[]{:S(2)}) collective-permute-start(s16[528,128]{1,0:T(8,128)(2,1)S(1)} %get-tuple-element.34), channel_id=1, source_target_pairs={{0,8},{1,9},{2,10},{3,11},{4,12},{5,13},{6,14},{7,15},{8,0},{9,1},... | collective-permute-start | bytes 405512 | tf_op jit(solution)/shard_map/ppermute | solution.py:413
  67.4 17.9 %collective-permute-start.15 = (s16[528,128]{1,0:T(8,128)(2,1)S(1)}, s16[528,128]{1,0:T(8,128)(2,1)S(1)}, u32[]{:S(2)}, u32[]{:S(2)}) collective-permute-start(s16[528,128]{1,0:T(8,128)(2,1)S(1)} %get-tuple-element.35), channel_id=1, source_target_pairs={{0,16},{1,17},{2,18},{3,19},{4,20},{5,21},{6,22},{7,23},{8,24},{9,... | collective-permute-start | bytes 405512 | tf_op jit(solution)/shard_map/ppermute | solution.py:413
  69.2 16.1 %collective-permute-start.16 = (s16[528,128]{1,0:T(8,128)(2,1)S(1)}, s16[528,128]{1,0:T(8,128)(2,1)S(1)}, u32[]{:S(2)}, u32[]{:S(2)}) collective-permute-start(s16[528,128]{1,0:T(8,128)(2,1)S(1)} %get-tuple-element.36), channel_id=1, source_target_pairs={{0,24},{1,25},{2,26},{3,27},{4,28},{5,29},{6,30},{7,31},{8,16},{9,... | collective-permute-start | bytes 405512 | tf_op jit(solution)/shard_map/ppermute | solution.py:413
  85.4 15.6 %copy-start.3 = (s32[8]{0:T(128)S(1)}, s32[8]{0:T(128)}, u32[]{:S(2)}) copy-start(s32[8]{0:T(128)} %column.1) | copy-start | bytes 100
  89.3 3.6 %collective-permute-start.17 = (s16[336,128]{1,0:T(8,128)(2,1)S(1)}, s16[336,128]{1,0:T(8,128)(2,1)S(1)}, u32[]{:S(2)}, u32[]{:S(2)}) collective-permute-start(s16[336,128]{1,0:T(8,128)(2,1)S(1)} %get-tuple-element.38), channel_id=1, source_target_pairs={{0,2},{1,3},{2,0},{3,1},{4,6},{5,7},{6,4},{7,5},{8,10},{9,11},{10,... | collective-permute-start | bytes 258056 | tf_op jit(solution)/shard_map/ppermute | solution.py:413
  89.4 5.4 %collective-permute-start.18 = (s16[336,128]{1,0:T(8,128)(2,1)S(1)}, s16[336,128]{1,0:T(8,128)(2,1)S(1)}, u32[]{:S(2)}, u32[]{:S(2)}) collective-permute-start(s16[336,128]{1,0:T(8,128)(2,1)S(1)} %get-tuple-element.39), channel_id=1, source_target_pairs={{0,4},{1,5},{2,6},{3,7},{4,0},{5,1},{6,2},{7,3},{8,12},{9,13},{10,... | collective-permute-start | bytes 258056 | tf_op jit(solution)/shard_map/ppermute | solution.py:413
  89.8 5.9 %collective-permute-start.19 = (s16[336,128]{1,0:T(8,128)(2,1)S(1)}, s16[336,128]{1,0:T(8,128)(2,1)S(1)}, u32[]{:S(2)}, u32[]{:S(2)}) collective-permute-start(s16[336,128]{1,0:T(8,128)(2,1)S(1)} %get-tuple-element.40), channel_id=1, source_target_pairs={{0,6},{1,7},{2,4},{3,5},{4,2},{5,3},{6,0},{7,1},{8,14},{9,15},{10,... | collective-permute-start | bytes 258056 | tf_op jit(solution)/shard_map/ppermute | solution.py:413
  91.2 5.1 %collective-permute-start.20 = (s16[336,128]{1,0:T(8,128)(2,1)S(1)}, s16[336,128]{1,0:T(8,128)(2,1)S(1)}, u32[]{:S(2)}, u32[]{:S(2)}) collective-permute-start(s16[336,128]{1,0:T(8,128)(2,1)S(1)} %get-tuple-element.41), channel_id=1, source_target_pairs={{0,1},{1,0},{2,3},{3,2},{4,5},{5,4},{6,7},{7,6},{8,9},{9,8},{10,11... | collective-permute-start | bytes 258056 | tf_op jit(solution)/shard_map/ppermute | solution.py:413
  92.7 4.8 %collective-permute-start.21 = (s16[336,128]{1,0:T(8,128)(2,1)S(1)}, s16[336,128]{1,0:T(8,128)(2,1)S(1)}, u32[]{:S(2)}, u32[]{:S(2)}) collective-permute-start(s16[336,128]{1,0:T(8,128)(2,1)S(1)} %get-tuple-element.42), channel_id=1, source_target_pairs={{0,3},{1,2},{2,1},{3,0},{4,7},{5,6},{6,5},{7,4},{8,11},{9,10},{10,... | collective-permute-start | bytes 258056 | tf_op jit(solution)/shard_map/ppermute | solution.py:413
  92.9 6.8 %collective-permute-start.22 = (s16[336,128]{1,0:T(8,128)(2,1)S(1)}, s16[336,128]{1,0:T(8,128)(2,1)S(1)}, u32[]{:S(2)}, u32[]{:S(2)}) collective-permute-start(s16[336,128]{1,0:T(8,128)(2,1)S(1)} %get-tuple-element.43), channel_id=1, source_target_pairs={{0,5},{1,4},{2,7},{3,6},{4,1},{5,0},{6,3},{7,2},{8,13},{9,12},{10,... | collective-permute-start | bytes 258056 | tf_op jit(solution)/shard_map/ppermute | solution.py:413
  94.8 6.2 %collective-permute-start.23 = (s16[336,128]{1,0:T(8,128)(2,1)S(1)}, s16[336,128]{1,0:T(8,128)(2,1)S(1)}, u32[]{:S(2)}, u32[]{:S(2)}) collective-permute-start(s16[336,128]{1,0:T(8,128)(2,1)S(1)} %get-tuple-element.44), channel_id=1, source_target_pairs={{0,7},{1,6},{2,5},{3,4},{4,3},{5,2},{6,1},{7,0},{8,15},{9,14},{10,... | collective-permute-start | bytes 258056 | tf_op jit(solution)/shard_map/ppermute | solution.py:413

commit v5 on v4

--- a/solution.py
+++ b/solution.py
@@ -122,9 +122,10 @@
     )(where, w_own, w_got, inverse, got, *after)
 
 
-def product_kernel(count, tiles, after, *refs):
-    parts, own, got = refs[:count], refs[count], refs[count + 1]
-    refs = refs[count + 2 + after :]
+def product_kernel(pieces, count, held, after, *refs):
+    tiles = sum(held)
+    parts, own, got = refs[:pieces], refs[pieces], refs[pieces + 1 : pieces + 1 + len(held)]
+    refs = refs[pieces + 1 + len(held) + after :]
     near, sends = refs[0], refs[1:count]
     full, op, tails = refs[count:]
     rows, width = parts[0].shape
@@ -134,17 +135,20 @@
     @pl.when(t == 0)
     def _():
         tails[...] = jnp.zeros_like(tails)
-        for i, part in enumerate(parts):
-            full[i * rows : (i + 1) * rows, :] = part[...]
-
-    for i in range(tiles):
-
-        @pl.when(t == i)
+        start = 0
+        for part in parts:
+            full[start : start + part.shape[0], :] = part[...]
+            start += part.shape[0]
+
+    sources = [(ref, i) for ref, n in zip(got, held) for i in range(n)]
+    for at, (ref, i) in enumerate(sources):
+
+        @pl.when(t == at)
         def _():
-            table = scales(got[2 * tiles * size :, :])
+            table = scales(ref[ref.shape[0] - TAIL :, :])
             real, imag = (
                 own[0, strip % 2]
-                + got[strip * size : (strip + 1) * size, :].astype(I32).astype(F32)
+                + ref[strip * size : (strip + 1) * size, :].astype(I32).astype(F32)
                 * table[strip : strip + 1, :]
                 for strip in (2 * i, 2 * i + 1)
             )
@@ -172,20 +176,21 @@
             sends[q - 1][2 * tiles * rows :, :] = tails[q - 1].astype(I32).astype(I16)
 
 
-def product(parts, own, got, first, tiles, after):
-    count = len(parts)
+def product(parts, own, got, first, held, after):
+    tiles = sum(held)
     rows, width = parts[0].shape
+    count = sum(part.shape[0] for part in parts) // rows
     size = width // 2
     send = message(2 * tiles, rows)
     return pl.pallas_call(
-        functools.partial(product_kernel, count, tiles, len(after)),
+        functools.partial(product_kernel, len(parts), count, held, len(after)),
         out_shape=[jax.ShapeDtypeStruct((tiles, rows, 2 * LANES), F32)] + [send] * (count - 1),
         grid=(tiles,),
-        in_specs=[whole((rows, width))] * count
+        in_specs=[whole(part.shape) for part in parts]
         + [
             pl.BlockSpec((1, 2, size, LANES), lambda t: (t + first, 0, 0, 0)),
         ]
-        + [whole(got.shape)]
+        + [whole(x.shape) for x in got]
         + [pl.BlockSpec(memory_space=pl.ANY)] * len(after),
         out_specs=[pl.BlockSpec((1, rows, 2 * LANES), lambda t: (t, 0, 0))]
         + [whole(send.shape)] * (count - 1),
@@ -201,7 +206,7 @@
             transcendentals=0,
         ),
         name="product",
-    )(*parts, own, got, *after)
+    )(*parts, own, *got, *after)
 
 
 def add_up(near, got, write):
@@ -413,34 +418,39 @@
         return lax.ppermute(x, ("term", "wave"), pairs)
 
     tiles = size // LANES
-    cut = (tiles + 1) // 2
-    chunks = [(0, cut), (cut, tiles - cut)] if tiles > 1 else [(0, tiles)]
-
     assert slots == 4
     where = jnp.stack([place_of ^ bits for bits in range(4)] + [wave]).astype(I32)
     states = pick(where, spectral_state)
-    block = jnp.concatenate(
-        [states[0]] + [swap(states[bits], bits) for bits in range(1, 4)], axis=0
-    )
-    parts = [block] + [swap(block, q * 4) for q in range(1, outer)]
+    received = [swap(states[bits], bits) for bits in range(1, 4)]
+    turned, received[0] = lax.optimization_barrier((place_of, received[0]))
+    block = jnp.concatenate([states[0]] + received, axis=0)
+    steps = [q for q in range(1, outer) if q != 2] + [2]
+    parts = [block] + [swap(block, q * 4) for q in steps[:-1]]
+    half = block.shape[0] // 2
+    parts += [swap(parts[1][:half], 3 * 4), swap(parts[2][half:], 1 * 4)]
 
     w_got = swap(term_weights, 1)
     far, own = (
-        swap(lax.dynamic_index_in_dim(inverse, place_of ^ bits, 1, keepdims=False), 1)
+        swap(lax.dynamic_index_in_dim(inverse, turned ^ bits, 1, keepdims=False), 1)
         for bits in (3, 1)
     )
     mine = operator(where, 0, term_weights, w_got, inverse, own, 0, tiles, False)
-    behind = [(block,), (mine,)]
-    shares = [
-        swap(operator(where, 2, term_weights, w_got, inverse, far, *chunk, True, after), 2)
-        for chunk, after in zip(chunks, behind)
-    ]
-    near, got = [], []
-    for chunk, share in zip(chunks, shares):
+    groups = ((2, 1), (2,))
+    shares, near, got = [], [], []
+    first = 0
+    for group in groups:
+        start, messages = first, []
+        for n in group:
+            after = (block,) if not shares else (shares[-1], mine)
+            shares.append(
+                operator(where, 2, term_weights, w_got, inverse, far, first, n, True, after)
+            )
+            messages.append(swap(shares[-1], 2))
+            first += n
         after = [near[-1], got[-1][0]] if near else []
-        made = product(parts, mine, share, *chunk, after)
+        made = product(parts, mine, messages, start, group, after)
         near.append(made[0])
-        got.append([swap(made[q], q * 4) for q in range(1, outer)])
+        got.append([swap(send, q * 4) for send, q in zip(made[1:], steps)])
     make = synthesis if legendre.shape[2] // waves % LANES == 0 else plain_synthesis
     grid = make(where, near, got, legendre, waves)
     pieces = [

time: 105 us -> 99.6 us (0.949)
  waiting for transfers between devices: 44 us -> 36.8 us
  starting transfers between devices: 29.7 us -> 31.7 us
    ppermute x24 -> x26, waiting for transfers between devices: 44 us -> 36.8 us  [swap(): return lax.ppermute(x, ('term', 'wave'), pairs)]
    ppermute x24 -> x26, starting transfers between devices: 29.7 us -> 31.7 us  [swap(): return lax.ppermute(x, ('term', 'wave'), pairs)]
    squeeze x1, local copies, waits for them, and re-layouts: 3.92 us -> 2.22 us  [shards(): lax.dynamic_index_in_dim(inverse, turned ^ bits, 1, keepdims=False)]
    pallas_call x3 -> x4, Pallas kernels: 10.4 us -> 10.9 us  [operator(): pl.pallas_call(functools.partial(share_kernel, len(after)) if coded else...]
  transfers between devices with their start and end apart: 24 -> 26, of which waited for: 14 -> 15; matrix products, arithmetic and copies ran while one was open for 0% -> 0% of each run, Pallas kernels for 18% -> 19%
where the time goes in v5:
time: 99.6 us; the launch traced here: 99.3 us
  waiting for transfers between devices  36.8 us (37%)
  starting transfers between devices  31.7 us (32%)
  Pallas kernels  27.2 us (27%)
  local copies, waits for them, and re-layouts  3.34 us (3%)
    ppermute x26, waiting for transfers between devices, swap(): return lax.ppermute(x, ('term', 'wave'), pairs)  36.8 us
    ppermute x26, starting transfers between devices, swap(): return lax.ppermute(x, ('term', 'wave'), pairs)  31.7 us
    pallas_call x4, Pallas kernels, operator(): pl.pallas_call(functools.partial(share_kernel, len(after)) if coded else...  10.9 us
    pallas_call x2, Pallas kernels, product(): pl.pallas_call(functools.partial(product_kernel, len(parts), count, held,...  8.27 us
    pallas_call x1, Pallas kernels, synthesis(): pl.pallas_call(functools.partial(synthesis_kernel, bands, len(near), len(...  3.89 us
    pallas_call x1, Pallas kernels, place(): pl.pallas_call(functools.partial(place_kernel, count), out_shape=jax.Shap...  3.58 us
    squeeze x1, local copies, waits for them, and re-layouts, shards(): lax.dynamic_index_in_dim(inverse, turned ^ bits, 1, keepdims=False)  2.22 us
  transfers between devices with their start and end apart: 26, of which 15 were waited for; matrix products, arithmetic and copies ran while one was open for 0% of the time, Pallas kernels for 19%

profile of v5, /device:TPU:0, one launch (start us, length us, event | category | flops | bytes accessed | tf_op | source)
XLA Modules:
  0.0 99.3 jit_solution(7168547686585699771)
XLA Ops:
  0.0 0.1 stack.23.where
  0.1 1.0 copy-done.1
  1.1 0.6 pick.1
  1.6 0.5 collective-permute-start
  2.2 0.9 collective-permute-done
  3.1 2.2 %dynamic-slice_bitcast_fusion = (bf16[1,2,640,640]{3,2,1,0:T(8,128)(2,1)S(1)}, bf16[1,2,640,640]{3,2,1,0:T(8,128)(2,1)S(1)}) fusion(bf16[1,4,2,640,640]{4,3,2,1,0:T(8,128)(2,1)} %own.7, s32[]{:T(128)S(6)} %select_n.16, s32[]{:T(128)S(6)} %select_n.15), kind=kLoop, calls=%fused_computation | loop fusion | bytes 6553608 | tf_op jit(solution)/shard_map/jit(dynamic_index_in_dim)/squeeze | solution.py:434
  5.3 0.4 collective-permute-start.9
  5.7 0.2 collective-permute-start.8
  5.9 0.4 collective-permute-start.7
  6.2 2.7 %collective-permute-start.1 = (bf16[32,1280]{1,0:T(8,128)(2,1)S(1)}, bf16[32,1280]{1,0:T(8,128)(2,1)S(1)}, u32[]{:S(2)}, u32[]{:S(2)}) collective-permute-start(bf16[32,1280]{1,0:T(8,128)(2,1)S(1)} %get-tuple-element.30), channel_id=1, source_target_pairs={{0,4},{1,5},{2,6},{3,7},{4,0},{5,1},{6,2},{7,3},{8,12},{9,13},{10,... | collective-permute-start | bytes 245768 | tf_op jit(solution)/shard_map/ppermute | solution.py:418
  8.9 0.0 collective-permute-start.2
  8.9 2.9 %collective-permute-done.1 = bf16[32,1280]{1,0:T(8,128)(2,1)S(1)} collective-permute-done((bf16[32,1280]{1,0:T(8,128)(2,1)S(1)}, bf16[32,1280]{1,0:T(8,128)(2,1)S(1)}, u32[]{:S(2)}, u32[]{:S(2)}) %collective-permute-start.1) | collective-permute-done | bytes 81952 | tf_op jit(solution)/shard_map/ppermute | solution.py:418
  11.9 1.5 %collective-permute-done.2 = bf16[32,1280]{1,0:T(8,128)(2,1)S(1)} collective-permute-done((bf16[32,1280]{1,0:T(8,128)(2,1)S(1)}, bf16[32,1280]{1,0:T(8,128)(2,1)S(1)}, u32[]{:S(2)}, u32[]{:S(2)}) %collective-permute-start.2) | collective-permute-done | bytes 81952 | tf_op jit(solution)/shard_map/ppermute | solution.py:418
  13.4 0.0 collective-permute-done.7.w_got
  13.4 0.0 collective-permute-done.9.got
  13.4 2.3 %share.3.refs_0_ = s16[2576,128]{1,0:T(8,128)(2,1)S(1)} custom-call(s32[5]{0:T(128)S(1)} %stack.23.where, f32[1,2]{1,0:T(1,128)S(1)} %copy-done.2, f32[1,2]{1,0:T(1,128)S(1)} %collective-permute-done.7.w_got, bf16[1,4,2,640,640]{4,3,2,1,0:T(8,128)(2,1)} %own.7, bf16[1,2,640,640]{3,2,1,0:T(8,128)(2,1)S(1)} %collective-permute-done.9.got, ...), custom_call_target="tpu_custom_call" | custom-call | flops 5242880 | bytes 2621440 | tf_op jit(solution)/shard_map/share/pallas_call | solution.py:96
  15.7 1.4 %collective-permute-start.10 = (s16[2576,128]{1,0:T(8,128)(2,1)S(1)}, s16[2576,128]{1,0:T(8,128)(2,1)S(1)}, u32[]{:S(2)}, u32[]{:S(2)}) collective-permute-start(s16[2576,128]{1,0:T(8,128)(2,1)S(1)} %share.3.refs_0_), channel_id=1, source_target_pairs={{0,4},{1,5},{2,6},{3,7},{4,0},{5,1},{6,2},{7,3},{8,12},{9,13},{10,... | collective-permute-start | bytes 1978376 | tf_op jit(solution)/shard_map/ppermute | solution.py:418
  17.1 1.6 %collective-permute-start.3 = (bf16[128,1280]{1,0:T(8,128)(2,1)S(1)}, bf16[128,1280]{1,0:T(8,128)(2,1)S(1)}, u32[]{:S(2)}, u32[]{:S(2)}) collective-permute-start(bf16[128,1280]{1,0:T(8,128)(2,1)S(1)} %constant_dynamic-update-slice_fusion.refs_0_), channel_id=1, source_target_pairs={{0,8},{1,9},{2,10},{3,11},{4,12},{5,13},{6,14},{7,15},{8,0},{9,1},... | collective-permute-start | bytes 983048 | tf_op jit(solution)/shard_map/ppermute | solution.py:418
  18.8 2.5 %collective-permute-start.4 = (bf16[128,1280]{1,0:T(8,128)(2,1)S(1)}, bf16[128,1280]{1,0:T(8,128)(2,1)S(1)}, u32[]{:S(2)}, u32[]{:S(2)}) collective-permute-start(bf16[128,1280]{1,0:T(8,128)(2,1)S(1)} %constant_dynamic-update-slice_fusion.refs_0_), channel_id=1, source_target_pairs={{0,24},{1,25},{2,26},{3,27},{4,28},{5,29},{6,30},{7,31},{8,16},{9,... | collective-permute-start | bytes 983048 | tf_op jit(solution)/shard_map/ppermute | solution.py:418
  21.2 0.0 collective-permute-done.8.got
  21.2 4.3 %operator.1.refs_1_.refs_5_ = f32[5,2,640,128]{3,2,1,0:T(8,128)S(1)} custom-call(s32[5]{0:T(128)S(1)} %stack.23.where, f32[1,2]{1,0:T(1,128)S(1)} %copy-done.2, f32[1,2]{1,0:T(1,128)S(1)} %collective-permute-done.7.w_got, bf16[1,4,2,640,640]{4,3,2,1,0:T(8,128)(2,1)} %own.7, bf16[1,2,640,640]{3,2,1,0:T(8,128)(2,1)S(1)} %collective-permute-done.8.got), custom_call_target="tpu_custom_call" | custom-call | flops 13107200 | bytes 6553600 | tf_op jit(solution)/shard_map/operator/pallas_call | solution.py:96
  25.5 2.1 %share.4.refs_0_ = s16[1296,128]{1,0:T(8,128)(2,1)S(1)} custom-call(s32[5]{0:T(128)S(1)} %stack.23.where, f32[1,2]{1,0:T(1,128)S(1)} %copy-done.2, f32[1,2]{1,0:T(1,128)S(1)} %collective-permute-done.7.w_got, bf16[1,4,2,640,640]{4,3,2,1,0:T(8,128)(2,1)} %own.7, bf16[1,2,640,640]{3,2,1,0:T(8,128)(2,1)S(1)} %collective-permute-done.9.got, ...), custom_call_target="tpu_custom_call" | custom-call | flops 2621440 | bytes 1310720 | tf_op jit(solution)/shard_map/share/pallas_call | solution.py:96
  27.7 0.9 collective-permute-start.11
  28.6 2.3 %share.5 = s16[2576,128]{1,0:T(8,128)(2,1)S(1)} custom-call(s32[5]{0:T(128)S(1)} %stack.23.where, f32[1,2]{1,0:T(1,128)S(1)} %copy-done.2, f32[1,2]{1,0:T(1,128)S(1)} %collective-permute-done.7.w_got, bf16[1,4,2,640,640]{4,3,2,1,0:T(8,128)(2,1)} %own.7, bf16[1,2,640,640]{3,2,1,0:T(8,128)(2,1)S(1)} %collective-permute-done.9.got, ...), custom_call_target="tpu_custom_call" | custom-call | flops 5242880 | bytes 2621440 | tf_op jit(solution)/shard_map/share/pallas_call | solution.py:96
  30.8 1.3 %collective-permute-start.12 = (s16[2576,128]{1,0:T(8,128)(2,1)S(1)}, s16[2576,128]{1,0:T(8,128)(2,1)S(1)}, u32[]{:S(2)}, u32[]{:S(2)}) collective-permute-start(s16[2576,128]{1,0:T(8,128)(2,1)S(1)} %share.5), channel_id=1, source_target_pairs={{0,4},{1,5},{2,6},{3,7},{4,0},{5,1},{6,2},{7,3},{8,12},{9,13},{10,... | collective-permute-start | bytes 1978376 | tf_op jit(solution)/shard_map/ppermute | solution.py:418
  32.1 0.0 collective-permute-done.3.refs_1_
  32.1 7.2 %collective-permute-start.5 = (bf16[64,1280]{1,0:T(8,128)(2,1)S(1)}, bf16[64,1280]{1,0:T(8,128)(2,1)S(1)}, u32[]{:S(2)}, u32[]{:S(2)}) collective-permute-start(bf16[64,1280]{1,0:T(8,128)(2,1)S(1)} %slice.8), channel_id=1, source_target_pairs={{0,24},{1,25},{2,26},{3,27},{4,28},{5,29},{6,30},{7,31},{8,16},{9,... | collective-permute-start | bytes 491528 | tf_op jit(solution)/shard_map/ppermute | solution.py:418
  39.3 0.0 collective-permute-done.4.refs_2_
  39.4 0.1 collective-permute-start.6
  39.4 4.8 %collective-permute-done.5.refs_3_ = bf16[64,1280]{1,0:T(8,128)(2,1)S(1)} collective-permute-done((bf16[64,1280]{1,0:T(8,128)(2,1)S(1)}, bf16[64,1280]{1,0:T(8,128)(2,1)S(1)}, u32[]{:S(2)}, u32[]{:S(2)}) %collective-permute-start.5) | collective-permute-done | bytes 163872 | tf_op jit(solution)/shard_map/ppermute | solution.py:418
  44.2 1.2 %collective-permute-done.6.refs_4_ = bf16[64,1280]{1,0:T(8,128)(2,1)S(1)} collective-permute-done((bf16[64,1280]{1,0:T(8,128)(2,1)S(1)}, bf16[64,1280]{1,0:T(8,128)(2,1)S(1)}, u32[]{:S(2)}, u32[]{:S(2)}) %collective-permute-start.6) | collective-permute-done | bytes 163872 | tf_op jit(solution)/shard_map/ppermute | solution.py:418
  45.4 0.0 collective-permute-done.11.refs_7_
  45.4 0.0 collective-permute-done.10.refs_6_
  45.4 4.7 %product.2 = (f32[3,128,256]{2,1,0:T(8,128)S(1)}, s16[784,128]{1,0:T(8,128)(2,1)S(1)}, s16[784,128]{1,0:T(8,128)(2,1)S(1)}, s16[784,128]{1,0:T(8,128)(2,1)S(1)}) custom-call(bf16[128,1280]{1,0:T(8,128)(2,1)S(1)} %constant_dynamic-update-slice_fusion.refs_0_, bf16[128,1280]{1,0:T(8,128)(2,1)S(1)} %collective-permute-done.3.refs_1_, ...), custom_call_target="tpu_custom_call" | custom-call | flops 2013265920 | bytes 4259840 | tf_op jit(solution)/shard_map/product/pallas_call | solution.py:185
  50.2 1.0 %collective-permute-start.13 = (s16[784,128]{1,0:T(8,128)(2,1)S(1)}, s16[784,128]{1,0:T(8,128)(2,1)S(1)}, u32[]{:S(2)}, u32[]{:S(2)}) collective-permute-start(s16[784,128]{1,0:T(8,128)(2,1)S(1)} %get-tuple-element.34), channel_id=1, source_target_pairs={{0,8},{1,9},{2,10},{3,11},{4,12},{5,13},{6,14},{7,15},{8,0},{9,1},... | collective-permute-start | bytes 602120 | tf_op jit(solution)/shard_map/ppermute | solution.py:418
  51.2 1.5 %collective-permute-start.14 = (s16[784,128]{1,0:T(8,128)(2,1)S(1)}, s16[784,128]{1,0:T(8,128)(2,1)S(1)}, u32[]{:S(2)}, u32[]{:S(2)}) collective-permute-start(s16[784,128]{1,0:T(8,128)(2,1)S(1)} %get-tuple-element.36), channel_id=1, source_target_pairs={{0,24},{1,25},{2,26},{3,27},{4,28},{5,29},{6,30},{7,31},{8,16},{9,... | collective-permute-start | bytes 602120 | tf_op jit(solution)/shard_map/ppermute | solution.py:418
  52.7 1.1 %collective-permute-start.15 = (s16[784,128]{1,0:T(8,128)(2,1)S(1)}, s16[784,128]{1,0:T(8,128)(2,1)S(1)}, u32[]{:S(2)}, u32[]{:S(2)}) collective-permute-start(s16[784,128]{1,0:T(8,128)(2,1)S(1)} %get-tuple-element.37), channel_id=1, source_target_pairs={{0,16},{1,17},{2,18},{3,19},{4,20},{5,21},{6,22},{7,23},{8,24},{9,... | collective-permute-start | bytes 602120 | tf_op jit(solution)/shard_map/ppermute | solution.py:418
  53.7 0.1 collective-permute-done.12.refs_6_
  53.9 5.8 %collective-permute-done.13.refs_8_.refs_2_ = s16[784,128]{1,0:T(8,128)(2,1)S(1)} collective-permute-done((s16[784,128]{1,0:T(8,128)(2,1)S(1)}, s16[784,128]{1,0:T(8,128)(2,1)S(1)}, u32[]{:S(2)}, u32[]{:S(2)}) %collective-permute-start.13) | collective-permute-done | bytes 200736 | tf_op jit(solution)/shard_map/ppermute | solution.py:418
  59.7 3.5 %product.3 = (f32[2,128,256]{2,1,0:T(8,128)S(1)}, s16[528,128]{1,0:T(8,128)(2,1)S(1)}, s16[528,128]{1,0:T(8,128)(2,1)S(1)}, s16[528,128]{1,0:T(8,128)(2,1)S(1)}) custom-call(bf16[128,1280]{1,0:T(8,128)(2,1)S(1)} %constant_dynamic-update-slice_fusion.refs_0_, bf16[128,1280]{1,0:T(8,128)(2,1)S(1)} %collective-permute-done.3.refs_1_, ...), custom_call_target="tpu_custom_call" | custom-call | flops 1342177280 | bytes 3276800 | tf_op jit(solution)/shard_map/product/pallas_call | solution.py:185
  63.2 0.1 collective-permute-start.16
  63.3 0.9 collective-permute-start.17
  64.2 2.6 %collective-permute-start.18 = (s16[528,128]{1,0:T(8,128)(2,1)S(1)}, s16[528,128]{1,0:T(8,128)(2,1)S(1)}, u32[]{:S(2)}, u32[]{:S(2)}) collective-permute-start(s16[528,128]{1,0:T(8,128)(2,1)S(1)} %get-tuple-element.40), channel_id=1, source_target_pairs={{0,16},{1,17},{2,18},{3,19},{4,20},{5,21},{6,22},{7,23},{8,24},{9,... | collective-permute-start | bytes 405512 | tf_op jit(solution)/shard_map/ppermute | solution.py:418
  66.8 0.0 collective-permute-done.14.refs_3_
  66.8 10.2 %collective-permute-done.15.refs_4_ = s16[784,128]{1,0:T(8,128)(2,1)S(1)} collective-permute-done((s16[784,128]{1,0:T(8,128)(2,1)S(1)}, s16[784,128]{1,0:T(8,128)(2,1)S(1)}, u32[]{:S(2)}, u32[]{:S(2)}) %collective-permute-start.15) | collective-permute-done | bytes 200736 | tf_op jit(solution)/shard_map/ppermute | solution.py:418
  77.0 0.0 collective-permute-done.16.refs_5_
  77.0 0.0 collective-permute-done.17.refs_6_
  77.0 3.1 %collective-permute-done.18.refs_7_ = s16[528,128]{1,0:T(8,128)(2,1)S(1)} collective-permute-done((s16[528,128]{1,0:T(8,128)(2,1)S(1)}, s16[528,128]{1,0:T(8,128)(2,1)S(1)}, u32[]{:S(2)}, u32[]{:S(2)}) %collective-permute-start.18) | collective-permute-done | bytes 135200 | tf_op jit(solution)/shard_map/ppermute | solution.py:418
  80.1 3.9 %synthesis.1 = (f32[2,32,640]{2,1,0:T(8,128)S(1)}, s16[336,128]{1,0:T(8,128)(2,1)S(1)}, s16[336,128]{1,0:T(8,128)(2,1)S(1)}, s16[336,128]{1,0:T(8,128)(2,1)S(1)}...) custom-call(s32[5]{0:T(128)S(1)} %stack.23.where, ...), custom_call_target="tpu_custom_call" | custom-call | flops 838860800 | bytes 2949120 | tf_op jit(solution)/shard_map/synthesis/pallas_call | solution.py:284
  84.0 0.1 collective-permute-start.19
  84.1 0.1 collective-permute-start.20
  84.2 1.8 %collective-permute-start.21 = (s16[336,128]{1,0:T(8,128)(2,1)S(1)}, s16[336,128]{1,0:T(8,128)(2,1)S(1)}, u32[]{:S(2)}, u32[]{:S(2)}) collective-permute-start(s16[336,128]{1,0:T(8,128)(2,1)S(1)} %get-tuple-element.44), channel_id=1, source_target_pairs={{0,6},{1,7},{2,4},{3,5},{4,2},{5,3},{6,0},{7,1},{8,14},{9,15},{10,... | collective-permute-start | bytes 258056 | tf_op jit(solution)/shard_map/ppermute | solution.py:418
  85.9 1.5 %collective-permute-start.22 = (s16[336,128]{1,0:T(8,128)(2,1)S(1)}, s16[336,128]{1,0:T(8,128)(2,1)S(1)}, u32[]{:S(2)}, u32[]{:S(2)}) collective-permute-start(s16[336,128]{1,0:T(8,128)(2,1)S(1)} %get-tuple-element.45), channel_id=1, source_target_pairs={{0,1},{1,0},{2,3},{3,2},{4,5},{5,4},{6,7},{7,6},{8,9},{9,8},{10,11... | collective-permute-start | bytes 258056 | tf_op jit(solution)/shard_map/ppermute | solution.py:418
  87.4 0.2 collective-permute-start.23
  87.6 0.0 collective-permute-done.19.refs_1_
  87.6 1.0 %collective-permute-start.24 = (s16[336,128]{1,0:T(8,128)(2,1)S(1)}, s16[336,128]{1,0:T(8,128)(2,1)S(1)}, u32[]{:S(2)}, u32[]{:S(2)}) collective-permute-start(s16[336,128]{1,0:T(8,128)(2,1)S(1)} %get-tuple-element.47), channel_id=1, source_target_pairs={{0,5},{1,4},{2,7},{3,6},{4,1},{5,0},{6,3},{7,2},{8,13},{9,12},{10,... | collective-permute-start | bytes 258056 | tf_op jit(solution)/shard_map/ppermute | solution.py:418
  88.7 0.8 collective-permute-done.20.refs_2_
  89.5 0.9 collective-permute-start.25
  90.3 0.1 collective-permute-done.21.refs_3_
  90.4 0.6 collective-permute-done.22.refs_4_
  91.0 1.2 %collective-permute-done.23.refs_5_ = s16[336,128]{1,0:T(8,128)(2,1)S(1)} collective-permute-done((s16[336,128]{1,0:T(8,128)(2,1)S(1)}, s16[336,128]{1,0:T(8,128)(2,1)S(1)}, u32[]{:S(2)}, u32[]{:S(2)}) %collective-permute-start.23) | collective-permute-done | bytes 86048 | tf_op jit(solution)/shard_map/ppermute | solution.py:418
  92.2 1.8 %collective-permute-done.24.refs_6_ = s16[336,128]{1,0:T(8,128)(2,1)S(1)} collective-permute-done((s16[336,128]{1,0:T(8,128)(2,1)S(1)}, s16[336,128]{1,0:T(8,128)(2,1)S(1)}, u32[]{:S(2)}, u32[]{:S(2)}) %collective-permute-start.24) | collective-permute-done | bytes 86048 | tf_op jit(solution)/shard_map/ppermute | solution.py:418
  94.0 1.7 %collective-permute-done.25.refs_7_ = s16[336,128]{1,0:T(8,128)(2,1)S(1)} collective-permute-done((s16[336,128]{1,0:T(8,128)(2,1)S(1)}, s16[336,128]{1,0:T(8,128)(2,1)S(1)}, u32[]{:S(2)}, u32[]{:S(2)}) %collective-permute-start.25) | collective-permute-done | bytes 86048 | tf_op jit(solution)/shard_map/ppermute | solution.py:418
  95.7 3.6 %place.1 = f32[8,2,32,640]{3,2,1,0:T(8,128)} custom-call(s32[5]{0:T(128)S(1)} %stack.23.where, s32[8]{0:T(128)S(1)} %copy-done.3, f32[2,32,640]{2,1,0:T(8,128)S(1)} %get-tuple-element.41.refs_0_, s16[336,128]{1,0:T(8,128)(2,1)S(1)} %collective-permute-done.19.refs_1_, s16[336,128]{1,0:T(8,128)(2,1)S(1)} %collective-permute-done.20.refs_2_, ...), custom_call_target="tpu_custom_call" | custom-call | tf_op jit(solution)/shard_map/place/pallas_call | solution.py:359
  (13 shorter events, 0.1 us)
Async XLA Ops:
  0.1 1.0 copy-start.1
  1.6 1.4 %collective-permute-start = (bf16[32,1280]{1,0:T(8,128)(2,1)S(1)}, bf16[32,1280]{1,0:T(8,128)(2,1)S(1)}, u32[]{:S(2)}, u32[]{:S(2)}) collective-permute-start(bf16[32,1280]{1,0:T(8,128)(2,1)S(1)} %get-tuple-element.28), channel_id=1, source_target_pairs={{0,2},{1,3},{2,0},{3,1},{4,6},{5,7},{6,4},{7,5},{8,10},{9,11},{10,... | collective-permute-start | bytes 245768 | tf_op jit(solution)/shard_map/ppermute | solution.py:418
  3.1 2.8 %copy-start.2 = (f32[1,2]{1,0:T(1,128)S(1)}, f32[1,2]{1,0:T(1,128)}, u32[]{:S(2)}) copy-start(f32[1,2]{1,0:T(1,128)} %w_own.7) | copy-start | bytes 28
  5.3 8.1 %collective-permute-start.9 = (bf16[1,2,640,640]{3,2,1,0:T(8,128)(2,1)S(1)}, bf16[1,2,640,640]{3,2,1,0:T(8,128)(2,1)S(1)}, u32[]{:S(2)}, u32[]{:S(2)}) collective-permute-start(bf16[1,2,640,640]{3,2,1,0:T(8,128)(2,1)S(1)} %get-tuple-element.49), channel_id=1, source_target_pairs={{0,2},{1,3},{2,0},{3,1},{4,6},{5,7},{6,4},{7,5},{8,10},{9,11},{10,... | collective-permute-start | bytes 4915208 | tf_op jit(solution)/shard_map/ppermute | solution.py:418
  5.7 15.5 %collective-permute-start.8 = (bf16[1,2,640,640]{3,2,1,0:T(8,128)(2,1)S(1)}, bf16[1,2,640,640]{3,2,1,0:T(8,128)(2,1)S(1)}, u32[]{:S(2)}, u32[]{:S(2)}) collective-permute-start(bf16[1,2,640,640]{3,2,1,0:T(8,128)(2,1)S(1)} %get-tuple-element.50), channel_id=1, source_target_pairs={{0,2},{1,3},{2,0},{3,1},{4,6},{5,7},{6,4},{7,5},{8,10},{9,11},{10,... | collective-permute-start | bytes 4915208 | tf_op jit(solution)/shard_map/ppermute | solution.py:418
  5.9 7.6 %collective-permute-start.7 = (f32[1,2]{1,0:T(1,128)S(1)}, f32[1,2]{1,0:T(1,128)S(1)}, u32[]{:S(2)}, u32[]{:S(2)}) collective-permute-start(f32[1,2]{1,0:T(1,128)S(1)} %copy-done.2), channel_id=1, source_target_pairs={{0,2},{1,3},{2,0},{3,1},{4,6},{5,7},{6,4},{7,5},{8,10},{9,11},{10,... | collective-permute-start | bytes 32 | tf_op jit(solution)/shard_map/ppermute | solution.py:418
  6.2 5.6 %collective-permute-start.1 = (bf16[32,1280]{1,0:T(8,128)(2,1)S(1)}, bf16[32,1280]{1,0:T(8,128)(2,1)S(1)}, u32[]{:S(2)}, u32[]{:S(2)}) collective-permute-start(bf16[32,1280]{1,0:T(8,128)(2,1)S(1)} %get-tuple-element.30), channel_id=1, source_target_pairs={{0,4},{1,5},{2,6},{3,7},{4,0},{5,1},{6,2},{7,3},{8,12},{9,13},{10,... | collective-permute-start | bytes 245768 | tf_op jit(solution)/shard_map/ppermute | solution.py:418
  8.9 4.5 %collective-permute-start.2 = (bf16[32,1280]{1,0:T(8,128)(2,1)S(1)}, bf16[32,1280]{1,0:T(8,128)(2,1)S(1)}, u32[]{:S(2)}, u32[]{:S(2)}) collective-permute-start(bf16[32,1280]{1,0:T(8,128)(2,1)S(1)} %get-tuple-element.31), channel_id=1, source_target_pairs={{0,6},{1,7},{2,4},{3,5},{4,2},{5,3},{6,0},{7,1},{8,14},{9,15},{10,... | collective-permute-start | bytes 245768 | tf_op jit(solution)/shard_map/ppermute | solution.py:418
  15.7 29.7 %collective-permute-start.10 = (s16[2576,128]{1,0:T(8,128)(2,1)S(1)}, s16[2576,128]{1,0:T(8,128)(2,1)S(1)}, u32[]{:S(2)}, u32[]{:S(2)}) collective-permute-start(s16[2576,128]{1,0:T(8,128)(2,1)S(1)} %share.3.refs_0_), channel_id=1, source_target_pairs={{0,4},{1,5},{2,6},{3,7},{4,0},{5,1},{6,2},{7,3},{8,12},{9,13},{10,... | collective-permute-start | bytes 1978376 | tf_op jit(solution)/shard_map/ppermute | solution.py:418
  17.1 14.9 %collective-permute-start.3 = (bf16[128,1280]{1,0:T(8,128)(2,1)S(1)}, bf16[128,1280]{1,0:T(8,128)(2,1)S(1)}, u32[]{:S(2)}, u32[]{:S(2)}) collective-permute-start(bf16[128,1280]{1,0:T(8,128)(2,1)S(1)} %constant_dynamic-update-slice_fusion.refs_0_), channel_id=1, source_target_pairs={{0,8},{1,9},{2,10},{3,11},{4,12},{5,13},{6,14},{7,15},{8,0},{9,1},... | collective-permute-start | bytes 983048 | tf_op jit(solution)/shard_map/ppermute | solution.py:418
  18.8 20.6 %collective-permute-start.4 = (bf16[128,1280]{1,0:T(8,128)(2,1)S(1)}, bf16[128,1280]{1,0:T(8,128)(2,1)S(1)}, u32[]{:S(2)}, u32[]{:S(2)}) collective-permute-start(bf16[128,1280]{1,0:T(8,128)(2,1)S(1)} %constant_dynamic-update-slice_fusion.refs_0_), channel_id=1, source_target_pairs={{0,24},{1,25},{2,26},{3,27},{4,28},{5,29},{6,30},{7,31},{8,16},{9,... | collective-permute-start | bytes 983048 | tf_op jit(solution)/shard_map/ppermute | solution.py:418
  25.5 3.0 %copy-start = (f32[5,2,640,128]{3,2,1,0:T(8,128)}, f32[5,2,640,128]{3,2,1,0:T(8,128)S(1)}, u32[]{:S(2)}) copy-start(f32[5,2,640,128]{3,2,1,0:T(8,128)S(1)} %operator.1.refs_1_.refs_5_) | copy-start | bytes 9830404
  27.7 17.8 %collective-permute-start.11 = (s16[1296,128]{1,0:T(8,128)(2,1)S(1)}, s16[1296,128]{1,0:T(8,128)(2,1)S(1)}, u32[]{:S(2)}, u32[]{:S(2)}) collective-permute-start(s16[1296,128]{1,0:T(8,128)(2,1)S(1)} %share.4.refs_0_), channel_id=1, source_target_pairs={{0,4},{1,5},{2,6},{3,7},{4,0},{5,1},{6,2},{7,3},{8,12},{9,13},{10,... | collective-permute-start | bytes 995336 | tf_op jit(solution)/shard_map/ppermute | solution.py:418
  30.8 23.0 %collective-permute-start.12 = (s16[2576,128]{1,0:T(8,128)(2,1)S(1)}, s16[2576,128]{1,0:T(8,128)(2,1)S(1)}, u32[]{:S(2)}, u32[]{:S(2)}) collective-permute-start(s16[2576,128]{1,0:T(8,128)(2,1)S(1)} %share.5), channel_id=1, source_target_pairs={{0,4},{1,5},{2,6},{3,7},{4,0},{5,1},{6,2},{7,3},{8,12},{9,13},{10,... | collective-permute-start | bytes 1978376 | tf_op jit(solution)/shard_map/ppermute | solution.py:418
  32.1 12.1 %collective-permute-start.5 = (bf16[64,1280]{1,0:T(8,128)(2,1)S(1)}, bf16[64,1280]{1,0:T(8,128)(2,1)S(1)}, u32[]{:S(2)}, u32[]{:S(2)}) collective-permute-start(bf16[64,1280]{1,0:T(8,128)(2,1)S(1)} %slice.8), channel_id=1, source_target_pairs={{0,24},{1,25},{2,26},{3,27},{4,28},{5,29},{6,30},{7,31},{8,16},{9,... | collective-permute-start | bytes 491528 | tf_op jit(solution)/shard_map/ppermute | solution.py:418
  39.4 6.1 %collective-permute-start.6 = (bf16[64,1280]{1,0:T(8,128)(2,1)S(1)}, bf16[64,1280]{1,0:T(8,128)(2,1)S(1)}, u32[]{:S(2)}, u32[]{:S(2)}) collective-permute-start(bf16[64,1280]{1,0:T(8,128)(2,1)S(1)} %slice.9), channel_id=1, source_target_pairs={{0,8},{1,9},{2,10},{3,11},{4,12},{5,13},{6,14},{7,15},{8,0},{9,1},... | collective-permute-start | bytes 491528 | tf_op jit(solution)/shard_map/ppermute | solution.py:418
  50.2 9.5 %collective-permute-start.13 = (s16[784,128]{1,0:T(8,128)(2,1)S(1)}, s16[784,128]{1,0:T(8,128)(2,1)S(1)}, u32[]{:S(2)}, u32[]{:S(2)}) collective-permute-start(s16[784,128]{1,0:T(8,128)(2,1)S(1)} %get-tuple-element.34), channel_id=1, source_target_pairs={{0,8},{1,9},{2,10},{3,11},{4,12},{5,13},{6,14},{7,15},{8,0},{9,1},... | collective-permute-start | bytes 602120 | tf_op jit(solution)/shard_map/ppermute | solution.py:418
  51.2 15.6 %collective-permute-start.14 = (s16[784,128]{1,0:T(8,128)(2,1)S(1)}, s16[784,128]{1,0:T(8,128)(2,1)S(1)}, u32[]{:S(2)}, u32[]{:S(2)}) collective-permute-start(s16[784,128]{1,0:T(8,128)(2,1)S(1)} %get-tuple-element.36), channel_id=1, source_target_pairs={{0,24},{1,25},{2,26},{3,27},{4,28},{5,29},{6,30},{7,31},{8,16},{9,... | collective-permute-start | bytes 602120 | tf_op jit(solution)/shard_map/ppermute | solution.py:418
  52.7 24.3 %collective-permute-start.15 = (s16[784,128]{1,0:T(8,128)(2,1)S(1)}, s16[784,128]{1,0:T(8,128)(2,1)S(1)}, u32[]{:S(2)}, u32[]{:S(2)}) collective-permute-start(s16[784,128]{1,0:T(8,128)(2,1)S(1)} %get-tuple-element.37), channel_id=1, source_target_pairs={{0,16},{1,17},{2,18},{3,19},{4,20},{5,21},{6,22},{7,23},{8,24},{9,... | collective-permute-start | bytes 602120 | tf_op jit(solution)/shard_map/ppermute | solution.py:418
  63.2 13.8 %collective-permute-start.16 = (s16[528,128]{1,0:T(8,128)(2,1)S(1)}, s16[528,128]{1,0:T(8,128)(2,1)S(1)}, u32[]{:S(2)}, u32[]{:S(2)}) collective-permute-start(s16[528,128]{1,0:T(8,128)(2,1)S(1)} %get-tuple-element.38), channel_id=1, source_target_pairs={{0,8},{1,9},{2,10},{3,11},{4,12},{5,13},{6,14},{7,15},{8,0},{9,1},... | collective-permute-start | bytes 405512 | tf_op jit(solution)/shard_map/ppermute | solution.py:418
  63.3 13.7 %collective-permute-start.17 = (s16[528,128]{1,0:T(8,128)(2,1)S(1)}, s16[528,128]{1,0:T(8,128)(2,1)S(1)}, u32[]{:S(2)}, u32[]{:S(2)}) collective-permute-start(s16[528,128]{1,0:T(8,128)(2,1)S(1)} %get-tuple-element.39), channel_id=1, source_target_pairs={{0,24},{1,25},{2,26},{3,27},{4,28},{5,29},{6,30},{7,31},{8,16},{9,... | collective-permute-start | bytes 405512 | tf_op jit(solution)/shard_map/ppermute | solution.py:418
  64.2 15.9 %collective-permute-start.18 = (s16[528,128]{1,0:T(8,128)(2,1)S(1)}, s16[528,128]{1,0:T(8,128)(2,1)S(1)}, u32[]{:S(2)}, u32[]{:S(2)}) collective-permute-start(s16[528,128]{1,0:T(8,128)(2,1)S(1)} %get-tuple-element.40), channel_id=1, source_target_pairs={{0,16},{1,17},{2,18},{3,19},{4,20},{5,21},{6,22},{7,23},{8,24},{9,... | collective-permute-start | bytes 405512 | tf_op jit(solution)/shard_map/ppermute | solution.py:418
  80.1 15.6 %copy-start.3 = (s32[8]{0:T(128)S(1)}, s32[8]{0:T(128)}, u32[]{:S(2)}) copy-start(s32[8]{0:T(128)} %column.1) | copy-start | bytes 100
  84.0 3.6 %collective-permute-start.19 = (s16[336,128]{1,0:T(8,128)(2,1)S(1)}, s16[336,128]{1,0:T(8,128)(2,1)S(1)}, u32[]{:S(2)}, u32[]{:S(2)}) collective-permute-start(s16[336,128]{1,0:T(8,128)(2,1)S(1)} %get-tuple-element.42), channel_id=1, source_target_pairs={{0,2},{1,3},{2,0},{3,1},{4,6},{5,7},{6,4},{7,5},{8,10},{9,11},{10,... | collective-permute-start | bytes 258056 | tf_op jit(solution)/shard_map/ppermute | solution.py:418
  84.1 5.4 %collective-permute-start.20 = (s16[336,128]{1,0:T(8,128)(2,1)S(1)}, s16[336,128]{1,0:T(8,128)(2,1)S(1)}, u32[]{:S(2)}, u32[]{:S(2)}) collective-permute-start(s16[336,128]{1,0:T(8,128)(2,1)S(1)} %get-tuple-element.43), channel_id=1, source_target_pairs={{0,4},{1,5},{2,6},{3,7},{4,0},{5,1},{6,2},{7,3},{8,12},{9,13},{10,... | collective-permute-start | bytes 258056 | tf_op jit(solution)/shard_map/ppermute | solution.py:418
  84.2 6.3 %collective-permute-start.21 = (s16[336,128]{1,0:T(8,128)(2,1)S(1)}, s16[336,128]{1,0:T(8,128)(2,1)S(1)}, u32[]{:S(2)}, u32[]{:S(2)}) collective-permute-start(s16[336,128]{1,0:T(8,128)(2,1)S(1)} %get-tuple-element.44), channel_id=1, source_target_pairs={{0,6},{1,7},{2,4},{3,5},{4,2},{5,3},{6,0},{7,1},{8,14},{9,15},{10,... | collective-permute-start | bytes 258056 | tf_op jit(solution)/shard_map/ppermute | solution.py:418
  85.9 5.1 %collective-permute-start.22 = (s16[336,128]{1,0:T(8,128)(2,1)S(1)}, s16[336,128]{1,0:T(8,128)(2,1)S(1)}, u32[]{:S(2)}, u32[]{:S(2)}) collective-permute-start(s16[336,128]{1,0:T(8,128)(2,1)S(1)} %get-tuple-element.45), channel_id=1, source_target_pairs={{0,1},{1,0},{2,3},{3,2},{4,5},{5,4},{6,7},{7,6},{8,9},{9,8},{10,11... | collective-permute-start | bytes 258056 | tf_op jit(solution)/shard_map/ppermute | solution.py:418
  87.4 4.8 %collective-permute-start.23 = (s16[336,128]{1,0:T(8,128)(2,1)S(1)}, s16[336,128]{1,0:T(8,128)(2,1)S(1)}, u32[]{:S(2)}, u32[]{:S(2)}) collective-permute-start(s16[336,128]{1,0:T(8,128)(2,1)S(1)} %get-tuple-element.46), channel_id=1, source_target_pairs={{0,3},{1,2},{2,1},{3,0},{4,7},{5,6},{6,5},{7,4},{8,11},{9,10},{10,... | collective-permute-start | bytes 258056 | tf_op jit(solution)/shard_map/ppermute | solution.py:418
  87.6 6.4 %collective-permute-start.24 = (s16[336,128]{1,0:T(8,128)(2,1)S(1)}, s16[336,128]{1,0:T(8,128)(2,1)S(1)}, u32[]{:S(2)}, u32[]{:S(2)}) collective-permute-start(s16[336,128]{1,0:T(8,128)(2,1)S(1)} %get-tuple-element.47), channel_id=1, source_target_pairs={{0,5},{1,4},{2,7},{3,6},{4,1},{5,0},{6,3},{7,2},{8,13},{9,12},{10,... | collective-permute-start | bytes 258056 | tf_op jit(solution)/shard_map/ppermute | solution.py:418
  89.5 6.2 %collective-permute-start.25 = (s16[336,128]{1,0:T(8,128)(2,1)S(1)}, s16[336,128]{1,0:T(8,128)(2,1)S(1)}, u32[]{:S(2)}, u32[]{:S(2)}) collective-permute-start(s16[336,128]{1,0:T(8,128)(2,1)S(1)} %get-tuple-element.48), channel_id=1, source_target_pairs={{0,7},{1,6},{2,5},{3,4},{4,3},{5,2},{6,1},{7,0},{8,15},{9,14},{10,... | collective-permute-start | bytes 258056 | tf_op jit(solution)/shard_map/ppermute | solution.py:418

commit v6 on v5

v6 whole, which is shorter than its diff:
```python
import functools

import jax
import jax.numpy as jnp
from jax import lax
from jax.experimental import pallas as pl
from jax.experimental.pallas import tpu as pltpu
from jax.sharding import PartitionSpec as P

F32, BF16, I16, I32 = jnp.float32, jnp.bfloat16, jnp.int16, jnp.int32
LANES = 128
TAIL = 16
STEPS = 64.0
TOP = 32000.0
TINY = 1e-30


def params(mib=8):
    return pltpu.CompilerParams(vmem_limit_bytes=mib * 2**20)


def split(x):
    hi = x.astype(BF16)
    return hi, (x - hi.astype(F32)).astype(BF16)


def encode(x):
    top = jnp.maximum(jnp.max(jnp.abs(x), axis=0, keepdims=True), TINY)
    step = jnp.ceil(jnp.log2(top * (1.0 / TOP)) * STEPS)
    code = jnp.round(x * jnp.exp2(step * (-1.0 / STEPS)))
    return code.astype(I32).astype(I16), step


def put_row(tail, row, values):
    at = lax.broadcasted_iota(I32, tail.shape, 0)
    return jnp.where(at == row, values, tail)


def scales(tail):
    return jnp.exp2(tail.astype(I32).astype(F32) * (1.0 / STEPS))


def message(strips, rows):
    return jax.ShapeDtypeStruct((strips * rows + TAIL, LANES), I16)


def whole(shape):
    return pl.BlockSpec(memory_space=pltpu.VMEM)


def weighted(w_own, w_got, own, got):
    real = imag = 0.0
    for k in range(own.shape[0]):
        for w, block in ((w_own, own[k, 0]), (w_got, got[k])):
            r, j = block[0].astype(F32), block[1].astype(F32)
            real += w[k, 0] * r - w[k, 1] * j
            imag += w[k, 0] * j + w[k, 1] * r
    return real, imag


def share_kernel(after, where, w_own, w_got, own, got, *refs):
    out, tail = refs[after:]
    t = pl.program_id(0)
    size = own.shape[3]
    end = out.shape[0] - TAIL

    @pl.when(t == 0)
    def _():
        tail[...] = jnp.zeros_like(tail)

    for part, value in enumerate(weighted(w_own, w_got, own, got)):
        strip = 2 * t + part
        code, step = encode(value)
        out[pl.ds(pl.multiple_of(strip * size, TAIL), size), :] = code
        tail[...] = put_row(tail[...], strip, step)

    @pl.when(t == pl.num_programs(0) - 1)
    def _():
        out[end:, :] = tail[...].astype(I32).astype(I16)


def own_kernel(where, w_own, w_got, own, got, out):
    for part, value in enumerate(weighted(w_own, w_got, own, got)):
        out[0, part] = value


def share(where, w_own, w_got, inverse, got, first, count, after):
    terms, _, _, size, _ = inverse.shape
    smem = pl.BlockSpec(memory_space=pltpu.SMEM)
    out = message(2 * count, size)
    return pl.pallas_call(
        functools.partial(share_kernel, len(after)),
        out_shape=out,
        grid_spec=pltpu.PrefetchScalarGridSpec(
            num_scalar_prefetch=1,
            grid=(count,),
            in_specs=[smem, smem]
            + operator_specs(terms, size, 2, first)
            + [pl.BlockSpec(memory_space=pl.ANY)] * len(after),
            out_specs=whole(out.shape),
            scratch_shapes=[pltpu.VMEM((TAIL, LANES), F32)],
        ),
        compiler_params=params(),
        cost_estimate=pl.CostEstimate(
            flops=32 * terms * size * LANES * count,
            bytes_accessed=16 * size * LANES * count,
            transcendentals=0,
        ),
        name="share",
    )(where, w_own, w_got, inverse, got, *after)


def operator_specs(terms, size, bits, first):
    return [
        pl.BlockSpec(
            (terms, 1, 2, size, LANES), lambda t, where: (0, where[bits], 0, 0, t + first)
        ),
        pl.BlockSpec((terms, 2, size, LANES), lambda t, where: (0, 0, 0, t + first)),
    ]


def operator(where, w_own, w_got, inverse, got):
    terms, _, _, size, _ = inverse.shape
    tiles = size // LANES
    smem = pl.BlockSpec(memory_space=pltpu.SMEM)
    return pl.pallas_call(
        own_kernel,
        out_shape=jax.ShapeDtypeStruct((tiles, 2, size, LANES), F32),
        grid_spec=pltpu.PrefetchScalarGridSpec(
            num_scalar_prefetch=1,
            grid=(tiles,),
            in_specs=[smem, smem] + operator_specs(terms, size, 0, 0),
            out_specs=pl.BlockSpec((1, 2, size, LANES), lambda t, where: (t, 0, 0, 0)),
        ),
        compiler_params=params(),
        cost_estimate=pl.CostEstimate(
            flops=32 * terms * size * size,
            bytes_accessed=16 * size * size,
            transcendentals=0,
        ),
        name="operator",
    )(where, w_own, w_got, inverse, got)


def table_kernel(where, legendre, after, out):
    out[...] = legendre[0]


def slot_table(where, legendre, after):
    _, size, nlat = legendre.shape
    return pl.pallas_call(
        table_kernel,
        out_shape=jax.ShapeDtypeStruct((size, nlat), legendre.dtype),
        grid_spec=pltpu.PrefetchScalarGridSpec(
            num_scalar_prefetch=1,
            grid=(size // LANES,),
            in_specs=[
                pl.BlockSpec((1, LANES, nlat), lambda i, where: (where[0], i, 0)),
                pl.BlockSpec(memory_space=pl.ANY),
            ],
            out_specs=pl.BlockSpec((LANES, nlat), lambda i, where: (i, 0)),
        ),
        compiler_params=params(),
        name="table",
    )(where, legendre, after)


def build_kernel(first, held, own, *refs):
    got, op = refs[: len(held)], refs[len(held)]
    size = own.shape[2]
    sources = [(ref, i) for ref, n in zip(got, held) for i in range(n)]
    for t, (ref, i) in enumerate(sources):
        table = scales(ref[ref.shape[0] - TAIL :, :])
        real, imag = (
            own[first + t, strip % 2]
            + ref[strip * size : (strip + 1) * size, :].astype(I32).astype(F32)
            * table[strip : strip + 1, :]
            for strip in (2 * i, 2 * i + 1)
        )
        for level, (r, j) in enumerate(zip(split(real), split(imag))):
            op[t, level, :size, :LANES] = r
            op[t, level, :size, LANES:] = j
            op[t, level, size:, :LANES] = -j
            op[t, level, size:, LANES:] = r


def build(own, got, first, held):
    size = own.shape[2]
    out = jax.ShapeDtypeStruct((sum(held), 2, 2 * size, 2 * LANES), BF16)
    return pl.pallas_call(
        functools.partial(build_kernel, first, held),
        out_shape=out,
        in_specs=[whole(x.shape) for x in (own, *got)],
        out_specs=whole(out.shape),
        compiler_params=params(),
        cost_estimate=pl.CostEstimate(
            flops=8 * out.size, bytes_accessed=4 * out.size, transcendentals=0
        ),
        name="build",
    )(own, *got)


def product_kernel(pieces, count, after, *refs):
    parts, op = refs[:pieces], refs[pieces]
    refs = refs[pieces + 1 + after :]
    near, sends, full = refs[0], refs[1:count], refs[count]
    tiles = op.shape[0]
    rows = parts[0].shape[0]
    start = 0
    for part in parts:
        full[start : start + part.shape[0], :] = part[...]
        start += part.shape[0]
    tails = [jnp.zeros((TAIL, LANES), F32)] * (count - 1)
    for t in range(tiles):
        x = full[...]
        acc = jnp.dot(x, op[t, 0], preferred_element_type=F32)
        acc += jnp.dot(x, op[t, 1], preferred_element_type=F32)
        near[t] = acc[:rows]
        for q in range(1, count):
            for part in range(2):
                strip = 2 * t + part
                block = acc[q * rows : (q + 1) * rows, part * LANES : (part + 1) * LANES]
                code, step = encode(block)
                sends[q - 1][strip * rows : (strip + 1) * rows, :] = code
                tails[q - 1] = put_row(tails[q - 1], strip, step)
    for send, tail in zip(sends, tails):
        send[2 * tiles * rows :, :] = tail.astype(I32).astype(I16)


def product(parts, op, after):
    tiles = op.shape[0]
    rows, width = parts[0].shape
    count = sum(part.shape[0] for part in parts) // rows
    send = message(2 * tiles, rows)
    return pl.pallas_call(
        functools.partial(product_kernel, len(parts), count, len(after)),
        out_shape=[jax.ShapeDtypeStruct((tiles, rows, 2 * LANES), F32)] + [send] * (count - 1),
        in_specs=[whole(x.shape) for x in (*parts, op)]
        + [pl.BlockSpec(memory_space=pl.ANY)] * len(after),
        out_specs=[whole(send.shape)] * count,
        scratch_shapes=[pltpu.VMEM((count * rows, width), BF16)],
        compiler_params=params(),
        cost_estimate=pl.CostEstimate(
            flops=8 * count * rows * width * tiles * LANES,
            bytes_accessed=2 * op.size + 2 * count * rows * width,
            transcendentals=0,
        ),
        name="product",
    )(*parts, op, *after)


def add_up(near, got, write):
    base = 0
    for own, parts in zip(near, got):
        tiles, rows, _ = own.shape
        tables = [scales(part[2 * tiles * rows :, :]) for part in parts]
        for t in range(tiles):
            for part in range(2):
                strip = 2 * t + part
                total = own[t, :, part * LANES : (part + 1) * LANES]
                for ref, table in zip(parts, tables):
                    code = ref[strip * rows : (strip + 1) * rows, :]
                    total += code.astype(I32).astype(F32) * table[strip : strip + 1, :]
                write(base + t, part, total)
        base += tiles


def unpack(refs, chunks, count):
    near = refs[:chunks]
    got = [refs[chunks + i * count : chunks + (i + 1) * count] for i in range(chunks)]
    return near, got, refs[chunks * (1 + count) :]


def synthesis_kernel(bands, chunks, count, where, *refs):
    near, got, rest = unpack(refs, chunks, count)
    table, outs, values = rest[0], rest[1:-1], rest[-1]
    rows = near[0].shape[1]
    quarter = rows // 4
    band = table.shape[1] // bands

    def write(tile, part, total):
        for level, value in enumerate(split(total)):
            values[
                level, part * rows : (part + 1) * rows, tile * LANES : (tile + 1) * LANES
            ] = value

    add_up(near, got, write)
    for d in reversed(range(bands)):
        start = pl.multiple_of((where[4] ^ d) * band, LANES)
        columns = table[:, pl.ds(start, band)]
        grid = jnp.dot(values[0], columns, preferred_element_type=F32)
        grid += jnp.dot(values[1], columns, preferred_element_type=F32)
        for side in range(4):
            out = outs[4 * d + side]
            if len(out.shape) == 3:
                for part in range(2):
                    start = part * rows + side * quarter
                    out[part] = grid[start : start + quarter]
                continue
            tail = jnp.zeros((TAIL, LANES), F32)
            for part in range(2):
                start = part * rows + side * quarter
                for k in range(band // LANES):
                    strip = 2 * k + part
                    code, step = encode(
                        grid[start : start + quarter, k * LANES : (k + 1) * LANES]
                    )
                    out[strip * quarter : (strip + 1) * quarter, :] = code
                    tail = put_row(tail, strip, step)
            out[out.shape[0] - TAIL :, :] = tail.astype(I32).astype(I16)


def synthesis(where, near, got, table, bands):
    rows = near[0].shape[1]
    size, nlat = table.shape
    band = nlat // bands
    send = message(2 * band // LANES, rows // 4)
    outs = [jax.ShapeDtypeStruct((2, rows // 4, band), F32)] + [send] * (4 * bands - 1)
    operands = [*near, *[part for parts in got for part in parts], table]
    return pl.pallas_call(
        functools.partial(synthesis_kernel, bands, len(near), len(got[0])),
        out_shape=outs,
        in_specs=[pl.BlockSpec(memory_space=pltpu.SMEM)] + [whole(x.shape) for x in operands],
        out_specs=[whole(out.shape) for out in outs],
        scratch_shapes=[pltpu.VMEM((2, 2 * rows, size), BF16)],
        compiler_params=params(),
        cost_estimate=pl.CostEstimate(
            flops=8 * rows * size * nlat,
            bytes_accessed=2 * size * nlat + 8 * rows * nlat,
            transcendentals=0,
        ),
        name="synthesis",
    )(where, *operands)


def total_kernel(chunks, count, *refs):
    near, got, (out,) = unpack(refs, chunks, count)

    def write(tile, part, total):
        out[part, :, tile * LANES : (tile + 1) * LANES] = total

    add_up(near, got, write)


def plain_synthesis(where, near, got, table, bands):
    rows = near[0].shape[1]
    size, nlat = table.shape
    total = pl.pallas_call(
        functools.partial(total_kernel, len(near), len(got[0])),
        out_shape=jax.ShapeDtypeStruct((2, rows, size), F32),
        compiler_params=params(),
        name="total",
    )(*near, *[part for parts in got for part in parts])
    grid = sum(
        jnp.einsum("pcn,nl->pcl", v, table, preferred_element_type=F32) for v in split(total)
    )
    quarter, band = rows // 4, nlat // bands
    return [
        lax.dynamic_slice(grid, (0, side * quarter, (where[4] ^ d) * band), (2, quarter, band))
        for d in range(bands)
        for side in range(4)
    ]


def place_kernel(count, slots, where, column, *refs):
    pieces, out, full, sems = refs[:count], refs[count], refs[count + 1], refs[count + 2]
    _, _, rows, lanes = full.shape
    copies = []
    for i, piece in enumerate(pieces):
        if len(piece.shape) == 3:
            full[i] = piece[...]
        else:
            strips = 2 * lanes // LANES
            table = scales(piece[strips * rows :, :])
            for strip in range(strips):
                code = piece[strip * rows : (strip + 1) * rows, :]
                at = strip // 2 * LANES
                full[i, strip % 2, :, at : at + LANES] = (
                    code.astype(I32).astype(F32) * table[strip : strip + 1, :]
                )
        slot = column[(where[4] ^ (i // 4)) * slots + where[i % 4]]
        copies.append(pltpu.make_async_copy(full.at[i], out.at[slot], sems.at[i]))
        copies[-1].start()
    for copy in copies:
        copy.wait()


def place(where, column, slots, pieces):
    count = len(pieces)
    shape = (count,) + pieces[0].shape
    smem = pl.BlockSpec(memory_space=pltpu.SMEM)
    return pl.pallas_call(
        functools.partial(place_kernel, count, slots),
        out_shape=jax.ShapeDtypeStruct(shape, F32),
        in_specs=[smem, smem] + [whole(piece.shape) for piece in pieces],
        out_specs=pl.BlockSpec(memory_space=pl.ANY),
        scratch_shapes=[pltpu.VMEM(shape, F32), pltpu.SemaphoreType.DMA((count,))],
        compiler_params=params(),
        name="place",
    )(where, column, *pieces)


def pick_kernel(where, *refs):
    count = len(refs) // 2
    for i in range(count):
        refs[count + i][...] = refs[i][0]


def pick(where, state):
    shape = state.shape[1:]
    block = lambda i: pl.BlockSpec((1,) + shape, lambda _, where: (where[i], 0, 0))
    return pl.pallas_call(
        pick_kernel,
        out_shape=[jax.ShapeDtypeStruct(shape, state.dtype)] * 4,
        grid_spec=pltpu.PrefetchScalarGridSpec(
            num_scalar_prefetch=1,
            grid=(1,),
            in_specs=[block(i) for i in range(4)],
            out_specs=[whole(shape)] * 4,
        ),
        compiler_params=params(),
        name="pick",
    )(where, *[state] * 4)


def shards(mesh, spectral_state, inverse, term_weights, legendre, slot_column):
    terms, waves = mesh.shape["term"], mesh.shape["wave"]
    slots, cols, width = spectral_state.shape
    size = width // 2
    outer = terms // 4
    me, wave = lax.axis_index("term"), lax.axis_index("wave")
    place_of = me % 4

    def swap(x, term_bits, wave_bits=0):
        pairs = [
            (t * waves + w, (t ^ term_bits) * waves + (w ^ wave_bits))
            for t in range(terms)
            for w in range(waves)
        ]
        return lax.ppermute(x, ("term", "wave"), pairs)

    tiles = size // LANES
    assert slots == 4
    where = jnp.stack([place_of ^ bits for bits in range(4)] + [wave]).astype(I32)
    states = pick(where, spectral_state)
    received = [swap(states[bits], bits) for bits in range(1, 4)]
    turned, received[0] = lax.optimization_barrier((place_of, received[0]))
    block = jnp.concatenate([states[0]] + received, axis=0)
    steps = [q for q in range(1, outer) if q != 2] + [2]
    parts = [block] + [swap(block, q * 4) for q in steps[:-1]]
    half = block.shape[0] // 2
    parts += [swap(parts[1][:half], 3 * 4), swap(parts[2][half:], 1 * 4)]

    w_got = swap(term_weights, 1)
    far, own = (
        swap(lax.dynamic_index_in_dim(inverse, turned ^ bits, 1, keepdims=False), 1)
        for bits in (3, 1)
    )
    mine = operator(where, term_weights, w_got, inverse, own)
    groups = ((2, 1), (2,))
    shares, near, got = [], [], []
    first = 0
    for group in groups:
        start, messages = first, []
        for n in group:
            after = (block,) if not shares else (shares[-1], mine)
            shares.append(
                share(where, term_weights, w_got, inverse, far, first, n, after)
            )
            messages.append(swap(shares[-1], 2))
            first += n
        after = [near[-1], got[-1][0]] if near else []
        made = product(parts, build(mine, messages, start, group), after)
        near.append(made[0])
        got.append([swap(send, q * 4) for send, q in zip(made[1:], steps)])
    make = synthesis if legendre.shape[2] // waves % LANES == 0 else plain_synthesis
    table = slot_table(where, legendre, near[-1])
    grid = make(where, near, got, table, waves)
    pieces = [
        swap(grid[4 * d + bits], bits, d) if d or bits else grid[0]
        for d in range(waves)
        for bits in range(4)
    ]
    return place(where, slot_column, slots, pieces)


def solution(mesh):
    return jax.shard_map(
        functools.partial(shards, mesh),
        mesh=mesh,
        in_specs=(
            P("wave", "term", None),
            P("term", "wave", None, None, None),
            P("term", None),
            P("wave", None, None),
            P(),
        ),
        out_specs=P(None, None, "term", "wave"),
        check_vma=False,
    )
```

time: 99.6 us -> 93.1 us (0.935)
  Pallas kernels: 27.2 us -> 18.5 us
  starting transfers between devices: 31.7 us -> 34.1 us
    pallas_call x7 -> x10, Pallas kernels: 22.8 us -> 15.8 us  [the longest x3 5.27 us: share(): pl.pallas_call(functools.partial(share_kernel, len(after)), out_shape=out...]
    ppermute x26, starting transfers between devices: 31.7 us -> 34.1 us  [swap(): return lax.ppermute(x, ('term', 'wave'), pairs)]
    pallas_call x1, Pallas kernels: 3.89 us -> 2.17 us  [synthesis(): pl.pallas_call(functools.partial(synthesis_kernel, bands, len(near), len(...]
  transfers between devices with their start and end apart: 26 -> 26, of which waited for: 15 -> 16; matrix products, arithmetic and copies ran while one was open for 0% -> 0% of each run, Pallas kernels for 19% -> 15%
where the time goes in v6:
time: 93.1 us; the launch traced here: 93 us
  waiting for transfers between devices  36.6 us (39%)
  starting transfers between devices  34.1 us (37%)
  Pallas kernels  18.5 us (20%)
  local copies, waits for them, and re-layouts  3.48 us (4%)
    ppermute x26, waiting for transfers between devices, swap(): return lax.ppermute(x, ('term', 'wave'), pairs)  36.6 us
    ppermute x26, starting transfers between devices, swap(): return lax.ppermute(x, ('term', 'wave'), pairs)  34.1 us
    pallas_call x3, Pallas kernels, share(): pl.pallas_call(functools.partial(share_kernel, len(after)), out_shape=out...  5.27 us
    pallas_call x2, Pallas kernels, product(): pl.pallas_call(functools.partial(product_kernel, len(parts), count, len(a...  3.91 us
    pallas_call x1, Pallas kernels, operator(): pl.pallas_call(own_kernel, out_shape=jax.ShapeDtypeStruct((tiles, 2, size...  2.91 us
    squeeze x1, local copies, waits for them, and re-layouts, shards(): lax.dynamic_index_in_dim(inverse, turned ^ bits, 1, keepdims=False)  2.36 us
    pallas_call x1, Pallas kernels, synthesis(): pl.pallas_call(functools.partial(synthesis_kernel, bands, len(near), len(...  2.17 us
  transfers between devices with their start and end apart: 26, of which 16 were waited for; matrix products, arithmetic and copies ran while one was open for 0% of the time, Pallas kernels for 15%

profile of v6, /device:TPU:0, one launch (start us, length us, event | category | flops | bytes accessed | tf_op | source)
XLA Modules:
  0.0 93.0 jit_solution(12155200081940808280)
XLA Ops:
  0.0 0.1 stack.23.where
  0.1 1.0 %copy-done.1 = bf16[4,32,1280]{2,1,0:T(8,128)(2,1)S(1)} copy-done((bf16[4,32,1280]{2,1,0:T(8,128)(2,1)S(1)}, bf16[4,32,1280]{2,1,0:T(8,128)(2,1)}, u32[]{:S(2)}) %copy-start.1) | copy-done | bytes 327704
  1.1 0.6 pick.1
  1.6 0.5 collective-permute-start
  2.2 0.9 collective-permute-done
  3.1 2.4 %dynamic-slice_bitcast_fusion = (bf16[1,2,640,640]{3,2,1,0:T(8,128)(2,1)S(1)}, bf16[1,2,640,640]{3,2,1,0:T(8,128)(2,1)S(1)}) fusion(bf16[1,4,2,640,640]{4,3,2,1,0:T(8,128)(2,1)} %own.7, s32[]{:T(128)S(6)} %select_n.16, s32[]{:T(128)S(6)} %select_n.15), kind=kLoop, calls=%fused_computation | loop fusion | bytes 6553608 | tf_op jit(solution)/shard_map/jit(dynamic_index_in_dim)/squeeze | solution.py:456
  5.4 0.4 collective-permute-start.9
  5.9 0.2 collective-permute-start.8
  6.0 0.4 collective-permute-start.7
  6.4 2.7 %collective-permute-start.1 = (bf16[32,1280]{1,0:T(8,128)(2,1)S(1)}, bf16[32,1280]{1,0:T(8,128)(2,1)S(1)}, u32[]{:S(2)}, u32[]{:S(2)}) collective-permute-start(bf16[32,1280]{1,0:T(8,128)(2,1)S(1)} %get-tuple-element.30), channel_id=1, source_target_pairs={{0,4},{1,5},{2,6},{3,7},{4,0},{5,1},{6,2},{7,3},{8,12},{9,13},{10,... | collective-permute-start | bytes 245768 | tf_op jit(solution)/shard_map/ppermute | solution.py:440
  9.1 0.0 collective-permute-start.2
  9.1 2.9 %collective-permute-done.1 = bf16[32,1280]{1,0:T(8,128)(2,1)S(1)} collective-permute-done((bf16[32,1280]{1,0:T(8,128)(2,1)S(1)}, bf16[32,1280]{1,0:T(8,128)(2,1)S(1)}, u32[]{:S(2)}, u32[]{:S(2)}) %collective-permute-start.1) | collective-permute-done | bytes 81952 | tf_op jit(solution)/shard_map/ppermute | solution.py:440
  12.0 1.5 %collective-permute-done.2 = bf16[32,1280]{1,0:T(8,128)(2,1)S(1)} collective-permute-done((bf16[32,1280]{1,0:T(8,128)(2,1)S(1)}, bf16[32,1280]{1,0:T(8,128)(2,1)S(1)}, u32[]{:S(2)}, u32[]{:S(2)}) %collective-permute-start.2) | collective-permute-done | bytes 81952 | tf_op jit(solution)/shard_map/ppermute | solution.py:440
  13.6 0.0 collective-permute-done.7.w_got
  13.6 0.0 collective-permute-done.9.got
  13.6 1.9 %share.3.refs_0_ = s16[2576,128]{1,0:T(8,128)(2,1)S(1)} custom-call(s32[5]{0:T(128)S(1)} %stack.23.where, f32[1,2]{1,0:T(1,128)S(1)} %copy-done.2, f32[1,2]{1,0:T(1,128)S(1)} %collective-permute-done.7.w_got, bf16[1,4,2,640,640]{4,3,2,1,0:T(8,128)(2,1)S(1)} %copy-done, bf16[1,2,640,640]{3,2,1,0:T(8,128)(2,1)S(1)} %collective-permute-done.9.got, ...), custom_call_target="tpu_custom_call" | custom-call | flops 5242880 | bytes 2621440 | tf_op jit(solution)/shard_map/share/pallas_call | solution.py:91
  15.5 1.4 %collective-permute-start.10 = (s16[2576,128]{1,0:T(8,128)(2,1)S(1)}, s16[2576,128]{1,0:T(8,128)(2,1)S(1)}, u32[]{:S(2)}, u32[]{:S(2)}) collective-permute-start(s16[2576,128]{1,0:T(8,128)(2,1)S(1)} %share.3.refs_0_), channel_id=1, source_target_pairs={{0,4},{1,5},{2,6},{3,7},{4,0},{5,1},{6,2},{7,3},{8,12},{9,13},{10,... | collective-permute-start | bytes 1978376 | tf_op jit(solution)/shard_map/ppermute | solution.py:440
  17.0 1.6 %collective-permute-start.3 = (bf16[128,1280]{1,0:T(8,128)(2,1)S(1)}, bf16[128,1280]{1,0:T(8,128)(2,1)S(1)}, u32[]{:S(2)}, u32[]{:S(2)}) collective-permute-start(bf16[128,1280]{1,0:T(8,128)(2,1)S(1)} %constant_dynamic-update-slice_fusion.refs_0_), channel_id=1, source_target_pairs={{0,8},{1,9},{2,10},{3,11},{4,12},{5,13},{6,14},{7,15},{8,0},{9,1},... | collective-permute-start | bytes 983048 | tf_op jit(solution)/shard_map/ppermute | solution.py:440
  18.6 2.5 %collective-permute-start.4 = (bf16[128,1280]{1,0:T(8,128)(2,1)S(1)}, bf16[128,1280]{1,0:T(8,128)(2,1)S(1)}, u32[]{:S(2)}, u32[]{:S(2)}) collective-permute-start(bf16[128,1280]{1,0:T(8,128)(2,1)S(1)} %constant_dynamic-update-slice_fusion.refs_0_), channel_id=1, source_target_pairs={{0,24},{1,25},{2,26},{3,27},{4,28},{5,29},{6,30},{7,31},{8,16},{9,... | collective-permute-start | bytes 983048 | tf_op jit(solution)/shard_map/ppermute | solution.py:440
  21.1 0.0 collective-permute-done.8.got
  21.1 2.9 %operator.1.refs_1_.own = f32[5,2,640,128]{3,2,1,0:T(8,128)S(1)} custom-call(s32[5]{0:T(128)S(1)} %stack.23.where, f32[1,2]{1,0:T(1,128)S(1)} %copy-done.2, f32[1,2]{1,0:T(1,128)S(1)} %collective-permute-done.7.w_got, bf16[1,4,2,640,640]{4,3,2,1,0:T(8,128)(2,1)S(1)} %copy-done, bf16[1,2,640,640]{3,2,1,0:T(8,128)(2,1)S(1)} %collective-permute-done.8.got), custom_call_target="tpu_custom_call" | custom-call | flops 13107200 | bytes 6553600 | tf_op jit(solution)/shard_map/operator/pallas_call | solution.py:126
  24.0 1.4 %share.4.refs_0_ = s16[1296,128]{1,0:T(8,128)(2,1)S(1)} custom-call(s32[5]{0:T(128)S(1)} %stack.23.where, f32[1,2]{1,0:T(1,128)S(1)} %copy-done.2, f32[1,2]{1,0:T(1,128)S(1)} %collective-permute-done.7.w_got, bf16[1,4,2,640,640]{4,3,2,1,0:T(8,128)(2,1)S(1)} %copy-done, bf16[1,2,640,640]{3,2,1,0:T(8,128)(2,1)S(1)} %collective-permute-done.9.got, ...), custom_call_target="tpu_custom_call" | custom-call | flops 2621440 | bytes 1310720 | tf_op jit(solution)/shard_map/share/pallas_call | solution.py:91
  25.4 0.9 collective-permute-start.11
  26.3 1.9 %share.5 = s16[2576,128]{1,0:T(8,128)(2,1)S(1)} custom-call(s32[5]{0:T(128)S(1)} %stack.23.where, f32[1,2]{1,0:T(1,128)S(1)} %copy-done.2, f32[1,2]{1,0:T(1,128)S(1)} %collective-permute-done.7.w_got, bf16[1,4,2,640,640]{4,3,2,1,0:T(8,128)(2,1)S(1)} %copy-done, bf16[1,2,640,640]{3,2,1,0:T(8,128)(2,1)S(1)} %collective-permute-done.9.got, ...), custom_call_target="tpu_custom_call" | custom-call | flops 5242880 | bytes 2621440 | tf_op jit(solution)/shard_map/share/pallas_call | solution.py:91
  28.2 1.3 %collective-permute-start.12 = (s16[2576,128]{1,0:T(8,128)(2,1)S(1)}, s16[2576,128]{1,0:T(8,128)(2,1)S(1)}, u32[]{:S(2)}, u32[]{:S(2)}) collective-permute-start(s16[2576,128]{1,0:T(8,128)(2,1)S(1)} %share.5), channel_id=1, source_target_pairs={{0,4},{1,5},{2,6},{3,7},{4,0},{5,1},{6,2},{7,3},{8,12},{9,13},{10,... | collective-permute-start | bytes 1978376 | tf_op jit(solution)/shard_map/ppermute | solution.py:440
  29.5 9.7 %collective-permute-start.5 = (bf16[64,1280]{1,0:T(8,128)(2,1)S(1)}, bf16[64,1280]{1,0:T(8,128)(2,1)S(1)}, u32[]{:S(2)}, u32[]{:S(2)}) collective-permute-start(bf16[64,1280]{1,0:T(8,128)(2,1)S(1)} %slice.8), channel_id=1, source_target_pairs={{0,24},{1,25},{2,26},{3,27},{4,28},{5,29},{6,30},{7,31},{8,16},{9,... | collective-permute-start | bytes 491528 | tf_op jit(solution)/shard_map/ppermute | solution.py:440
  39.2 0.1 collective-permute-start.6
  39.3 1.1 %collective-permute-done.11.refs_1_ = s16[1296,128]{1,0:T(8,128)(2,1)S(1)} collective-permute-done((s16[1296,128]{1,0:T(8,128)(2,1)S(1)}, s16[1296,128]{1,0:T(8,128)(2,1)S(1)}, u32[]{:S(2)}, u32[]{:S(2)}) %collective-permute-start.11) | collective-permute-done | bytes 331808 | tf_op jit(solution)/shard_map/ppermute | solution.py:440
  40.4 0.8 build.2.refs_5_
  41.2 2.8 %collective-permute-done.5.refs_3_ = bf16[64,1280]{1,0:T(8,128)(2,1)S(1)} collective-permute-done((bf16[64,1280]{1,0:T(8,128)(2,1)S(1)}, bf16[64,1280]{1,0:T(8,128)(2,1)S(1)}, u32[]{:S(2)}, u32[]{:S(2)}) %collective-permute-start.5) | collective-permute-done | bytes 163872 | tf_op jit(solution)/shard_map/ppermute | solution.py:440
  44.0 1.2 %collective-permute-done.6.refs_4_ = bf16[64,1280]{1,0:T(8,128)(2,1)S(1)} collective-permute-done((bf16[64,1280]{1,0:T(8,128)(2,1)S(1)}, bf16[64,1280]{1,0:T(8,128)(2,1)S(1)}, u32[]{:S(2)}, u32[]{:S(2)}) %collective-permute-start.6) | collective-permute-done | bytes 163872 | tf_op jit(solution)/shard_map/ppermute | solution.py:440
  45.3 2.3 %product.2 = (f32[3,128,256]{2,1,0:T(8,128)S(1)}, s16[784,128]{1,0:T(8,128)(2,1)S(1)}, s16[784,128]{1,0:T(8,128)(2,1)S(1)}, s16[784,128]{1,0:T(8,128)(2,1)S(1)}) custom-call(bf16[128,1280]{1,0:T(8,128)(2,1)S(1)} %constant_dynamic-update-slice_fusion.refs_0_, bf16[128,1280]{1,0:T(8,128)(2,1)S(1)} %collective-permute-done.3.refs_1_, ...), custom_call_target="tpu_custom_call" | custom-call | flops 2013265920 | bytes 5242880 | tf_op jit(solution)/shard_map/product/pallas_call | solution.py:235
  47.6 1.0 %collective-permute-start.13 = (s16[784,128]{1,0:T(8,128)(2,1)S(1)}, s16[784,128]{1,0:T(8,128)(2,1)S(1)}, u32[]{:S(2)}, u32[]{:S(2)}) collective-permute-start(s16[784,128]{1,0:T(8,128)(2,1)S(1)} %get-tuple-element.34), channel_id=1, source_target_pairs={{0,8},{1,9},{2,10},{3,11},{4,12},{5,13},{6,14},{7,15},{8,0},{9,1},... | collective-permute-start | bytes 602120 | tf_op jit(solution)/shard_map/ppermute | solution.py:440
  48.6 1.5 %collective-permute-start.14 = (s16[784,128]{1,0:T(8,128)(2,1)S(1)}, s16[784,128]{1,0:T(8,128)(2,1)S(1)}, u32[]{:S(2)}, u32[]{:S(2)}) collective-permute-start(s16[784,128]{1,0:T(8,128)(2,1)S(1)} %get-tuple-element.36), channel_id=1, source_target_pairs={{0,24},{1,25},{2,26},{3,27},{4,28},{5,29},{6,30},{7,31},{8,16},{9,... | collective-permute-start | bytes 602120 | tf_op jit(solution)/shard_map/ppermute | solution.py:440
  50.1 1.1 %collective-permute-start.15 = (s16[784,128]{1,0:T(8,128)(2,1)S(1)}, s16[784,128]{1,0:T(8,128)(2,1)S(1)}, u32[]{:S(2)}, u32[]{:S(2)}) collective-permute-start(s16[784,128]{1,0:T(8,128)(2,1)S(1)} %get-tuple-element.37), channel_id=1, source_target_pairs={{0,16},{1,17},{2,18},{3,19},{4,20},{5,21},{6,22},{7,23},{8,24},{9,... | collective-permute-start | bytes 602120 | tf_op jit(solution)/shard_map/ppermute | solution.py:440
  51.1 2.6 %collective-permute-done.12.refs_0_ = s16[2576,128]{1,0:T(8,128)(2,1)S(1)} collective-permute-done((s16[2576,128]{1,0:T(8,128)(2,1)S(1)}, s16[2576,128]{1,0:T(8,128)(2,1)S(1)}, u32[]{:S(2)}, u32[]{:S(2)}) %collective-permute-start.12) | collective-permute-done | bytes 659488 | tf_op jit(solution)/shard_map/ppermute | solution.py:440
  53.7 0.5 build.3.refs_5_
  54.2 2.8 %collective-permute-done.13.refs_7_.refs_2_ = s16[784,128]{1,0:T(8,128)(2,1)S(1)} collective-permute-done((s16[784,128]{1,0:T(8,128)(2,1)S(1)}, s16[784,128]{1,0:T(8,128)(2,1)S(1)}, u32[]{:S(2)}, u32[]{:S(2)}) %collective-permute-start.13) | collective-permute-done | bytes 200736 | tf_op jit(solution)/shard_map/ppermute | solution.py:440
  57.0 1.6 %product.3 = (f32[2,128,256]{2,1,0:T(8,128)S(1)}, s16[528,128]{1,0:T(8,128)(2,1)S(1)}, s16[528,128]{1,0:T(8,128)(2,1)S(1)}, s16[528,128]{1,0:T(8,128)(2,1)S(1)}) custom-call(bf16[128,1280]{1,0:T(8,128)(2,1)S(1)} %constant_dynamic-update-slice_fusion.refs_0_, bf16[128,1280]{1,0:T(8,128)(2,1)S(1)} %collective-permute-done.3.refs_1_, ...), custom_call_target="tpu_custom_call" | custom-call | flops 1342177280 | bytes 3932160 | tf_op jit(solution)/shard_map/product/pallas_call | solution.py:235
  58.6 0.1 collective-permute-start.16
  58.7 1.5 %collective-permute-start.17 = (s16[528,128]{1,0:T(8,128)(2,1)S(1)}, s16[528,128]{1,0:T(8,128)(2,1)S(1)}, u32[]{:S(2)}, u32[]{:S(2)}) collective-permute-start(s16[528,128]{1,0:T(8,128)(2,1)S(1)} %get-tuple-element.39), channel_id=1, source_target_pairs={{0,24},{1,25},{2,26},{3,27},{4,28},{5,29},{6,30},{7,31},{8,16},{9,... | collective-permute-start | bytes 405512 | tf_op jit(solution)/shard_map/ppermute | solution.py:440
  60.2 2.0 %collective-permute-start.18 = (s16[528,128]{1,0:T(8,128)(2,1)S(1)}, s16[528,128]{1,0:T(8,128)(2,1)S(1)}, u32[]{:S(2)}, u32[]{:S(2)}) collective-permute-start(s16[528,128]{1,0:T(8,128)(2,1)S(1)} %get-tuple-element.40), channel_id=1, source_target_pairs={{0,16},{1,17},{2,18},{3,19},{4,20},{5,21},{6,22},{7,23},{8,24},{9,... | collective-permute-start | bytes 405512 | tf_op jit(solution)/shard_map/ppermute | solution.py:440
  62.2 0.8 table.1.refs_8_
  63.0 0.0 copy-start.3
  63.0 0.0 collective-permute-done.14.refs_3_
  63.0 11.4 %collective-permute-done.15.refs_4_ = s16[784,128]{1,0:T(8,128)(2,1)S(1)} collective-permute-done((s16[784,128]{1,0:T(8,128)(2,1)S(1)}, s16[784,128]{1,0:T(8,128)(2,1)S(1)}, u32[]{:S(2)}, u32[]{:S(2)}) %collective-permute-start.15) | collective-permute-done | bytes 200736 | tf_op jit(solution)/shard_map/ppermute | solution.py:440
  74.4 0.0 collective-permute-done.16.refs_5_
  74.4 0.0 collective-permute-done.17.refs_6_
  74.4 3.1 %collective-permute-done.18.refs_7_ = s16[528,128]{1,0:T(8,128)(2,1)S(1)} collective-permute-done((s16[528,128]{1,0:T(8,128)(2,1)S(1)}, s16[528,128]{1,0:T(8,128)(2,1)S(1)}, u32[]{:S(2)}, u32[]{:S(2)}) %collective-permute-start.18) | collective-permute-done | bytes 135200 | tf_op jit(solution)/shard_map/ppermute | solution.py:440
  77.5 2.2 %synthesis.1 = (f32[2,32,640]{2,1,0:T(8,128)S(1)}, s16[336,128]{1,0:T(8,128)(2,1)S(1)}, s16[336,128]{1,0:T(8,128)(2,1)S(1)}, s16[336,128]{1,0:T(8,128)(2,1)S(1)}...) custom-call(s32[5]{0:T(128)S(1)} %stack.23.where, ...), custom_call_target="tpu_custom_call" | custom-call | flops 838860800 | bytes 2949120 | tf_op jit(solution)/shard_map/synthesis/pallas_call | solution.py:320
  79.7 0.1 collective-permute-start.19
  79.8 0.1 collective-permute-start.20
  79.8 1.8 %collective-permute-start.21 = (s16[336,128]{1,0:T(8,128)(2,1)S(1)}, s16[336,128]{1,0:T(8,128)(2,1)S(1)}, u32[]{:S(2)}, u32[]{:S(2)}) collective-permute-start(s16[336,128]{1,0:T(8,128)(2,1)S(1)} %get-tuple-element.44), channel_id=1, source_target_pairs={{0,6},{1,7},{2,4},{3,5},{4,2},{5,3},{6,0},{7,1},{8,14},{9,15},{10,... | collective-permute-start | bytes 258056 | tf_op jit(solution)/shard_map/ppermute | solution.py:440
  81.6 1.5 %collective-permute-start.22 = (s16[336,128]{1,0:T(8,128)(2,1)S(1)}, s16[336,128]{1,0:T(8,128)(2,1)S(1)}, u32[]{:S(2)}, u32[]{:S(2)}) collective-permute-start(s16[336,128]{1,0:T(8,128)(2,1)S(1)} %get-tuple-element.45), channel_id=1, source_target_pairs={{0,1},{1,0},{2,3},{3,2},{4,5},{5,4},{6,7},{7,6},{8,9},{9,8},{10,11... | collective-permute-start | bytes 258056 | tf_op jit(solution)/shard_map/ppermute | solution.py:440
  83.1 0.2 collective-permute-start.23
  83.3 1.0 %collective-permute-start.24 = (s16[336,128]{1,0:T(8,128)(2,1)S(1)}, s16[336,128]{1,0:T(8,128)(2,1)S(1)}, u32[]{:S(2)}, u32[]{:S(2)}) collective-permute-start(s16[336,128]{1,0:T(8,128)(2,1)S(1)} %get-tuple-element.47), channel_id=1, source_target_pairs={{0,5},{1,4},{2,7},{3,6},{4,1},{5,0},{6,3},{7,2},{8,13},{9,12},{10,... | collective-permute-start | bytes 258056 | tf_op jit(solution)/shard_map/ppermute | solution.py:440
  84.3 0.8 collective-permute-done.20.refs_2_
  85.2 0.9 collective-permute-start.25
  86.0 0.1 collective-permute-done.21.refs_3_
  86.1 0.6 collective-permute-done.22.refs_4_
  86.7 1.2 %collective-permute-done.23.refs_5_ = s16[336,128]{1,0:T(8,128)(2,1)S(1)} collective-permute-done((s16[336,128]{1,0:T(8,128)(2,1)S(1)}, s16[336,128]{1,0:T(8,128)(2,1)S(1)}, u32[]{:S(2)}, u32[]{:S(2)}) %collective-permute-start.23) | collective-permute-done | bytes 86048 | tf_op jit(solution)/shard_map/ppermute | solution.py:440
  87.9 1.8 %collective-permute-done.24.refs_6_ = s16[336,128]{1,0:T(8,128)(2,1)S(1)} collective-permute-done((s16[336,128]{1,0:T(8,128)(2,1)S(1)}, s16[336,128]{1,0:T(8,128)(2,1)S(1)}, u32[]{:S(2)}, u32[]{:S(2)}) %collective-permute-start.24) | collective-permute-done | bytes 86048 | tf_op jit(solution)/shard_map/ppermute | solution.py:440
  89.7 1.6 %collective-permute-done.25.refs_7_ = s16[336,128]{1,0:T(8,128)(2,1)S(1)} collective-permute-done((s16[336,128]{1,0:T(8,128)(2,1)S(1)}, s16[336,128]{1,0:T(8,128)(2,1)S(1)}, u32[]{:S(2)}, u32[]{:S(2)}) %collective-permute-start.25) | collective-permute-done | bytes 86048 | tf_op jit(solution)/shard_map/ppermute | solution.py:440
  91.3 1.7 %place.1 = f32[8,2,32,640]{3,2,1,0:T(8,128)} custom-call(s32[5]{0:T(128)S(1)} %stack.23.where, s32[8]{0:T(128)S(1)} %copy-done.3, f32[2,32,640]{2,1,0:T(8,128)S(1)} %get-tuple-element.41.refs_0_, s16[336,128]{1,0:T(8,128)(2,1)S(1)} %collective-permute-done.19.refs_1_, s16[336,128]{1,0:T(8,128)(2,1)S(1)} %collective-permute-done.20.refs_2_, ...), custom_call_target="tpu_custom_call" | custom-call | tf_op jit(solution)/shard_map/place/pallas_call | solution.py:392
  (21 shorter events, 0.1 us)
Async XLA Ops:
  0.1 1.0 %copy-start.1 = (bf16[4,32,1280]{2,1,0:T(8,128)(2,1)S(1)}, bf16[4,32,1280]{2,1,0:T(8,128)(2,1)}, u32[]{:S(2)}) copy-start(bf16[4,32,1280]{2,1,0:T(8,128)(2,1)} %refs_3_.1) | copy-start | bytes 983044
  1.6 1.4 %collective-permute-start = (bf16[32,1280]{1,0:T(8,128)(2,1)S(1)}, bf16[32,1280]{1,0:T(8,128)(2,1)S(1)}, u32[]{:S(2)}, u32[]{:S(2)}) collective-permute-start(bf16[32,1280]{1,0:T(8,128)(2,1)S(1)} %get-tuple-element.28), channel_id=1, source_target_pairs={{0,2},{1,3},{2,0},{3,1},{4,6},{5,7},{6,4},{7,5},{8,10},{9,11},{10,... | collective-permute-start | bytes 245768 | tf_op jit(solution)/shard_map/ppermute | solution.py:440
  3.1 2.9 %copy-start.2 = (f32[1,2]{1,0:T(1,128)S(1)}, f32[1,2]{1,0:T(1,128)}, u32[]{:S(2)}) copy-start(f32[1,2]{1,0:T(1,128)} %w_own.7) | copy-start | bytes 28
  3.1 10.5 %copy-start = (bf16[1,4,2,640,640]{4,3,2,1,0:T(8,128)(2,1)S(1)}, bf16[1,4,2,640,640]{4,3,2,1,0:T(8,128)(2,1)}, u32[]{:S(2)}) copy-start(bf16[1,4,2,640,640]{4,3,2,1,0:T(8,128)(2,1)} %own.7) | copy-start | bytes 19660804
  5.4 8.1 %collective-permute-start.9 = (bf16[1,2,640,640]{3,2,1,0:T(8,128)(2,1)S(1)}, bf16[1,2,640,640]{3,2,1,0:T(8,128)(2,1)S(1)}, u32[]{:S(2)}, u32[]{:S(2)}) collective-permute-start(bf16[1,2,640,640]{3,2,1,0:T(8,128)(2,1)S(1)} %get-tuple-element.49), channel_id=1, source_target_pairs={{0,2},{1,3},{2,0},{3,1},{4,6},{5,7},{6,4},{7,5},{8,10},{9,11},{10,... | collective-permute-start | bytes 4915208 | tf_op jit(solution)/shard_map/ppermute | solution.py:440
  5.9 15.2 %collective-permute-start.8 = (bf16[1,2,640,640]{3,2,1,0:T(8,128)(2,1)S(1)}, bf16[1,2,640,640]{3,2,1,0:T(8,128)(2,1)S(1)}, u32[]{:S(2)}, u32[]{:S(2)}) collective-permute-start(bf16[1,2,640,640]{3,2,1,0:T(8,128)(2,1)S(1)} %get-tuple-element.50), channel_id=1, source_target_pairs={{0,2},{1,3},{2,0},{3,1},{4,6},{5,7},{6,4},{7,5},{8,10},{9,11},{10,... | collective-permute-start | bytes 4915208 | tf_op jit(solution)/shard_map/ppermute | solution.py:440
  6.0 7.6 %collective-permute-start.7 = (f32[1,2]{1,0:T(1,128)S(1)}, f32[1,2]{1,0:T(1,128)S(1)}, u32[]{:S(2)}, u32[]{:S(2)}) collective-permute-start(f32[1,2]{1,0:T(1,128)S(1)} %copy-done.2), channel_id=1, source_target_pairs={{0,2},{1,3},{2,0},{3,1},{4,6},{5,7},{6,4},{7,5},{8,10},{9,11},{10,... | collective-permute-start | bytes 32 | tf_op jit(solution)/shard_map/ppermute | solution.py:440
  6.4 5.6 %collective-permute-start.1 = (bf16[32,1280]{1,0:T(8,128)(2,1)S(1)}, bf16[32,1280]{1,0:T(8,128)(2,1)S(1)}, u32[]{:S(2)}, u32[]{:S(2)}) collective-permute-start(bf16[32,1280]{1,0:T(8,128)(2,1)S(1)} %get-tuple-element.30), channel_id=1, source_target_pairs={{0,4},{1,5},{2,6},{3,7},{4,0},{5,1},{6,2},{7,3},{8,12},{9,13},{10,... | collective-permute-start | bytes 245768 | tf_op jit(solution)/shard_map/ppermute | solution.py:440
  9.1 4.5 %collective-permute-start.2 = (bf16[32,1280]{1,0:T(8,128)(2,1)S(1)}, bf16[32,1280]{1,0:T(8,128)(2,1)S(1)}, u32[]{:S(2)}, u32[]{:S(2)}) collective-permute-start(bf16[32,1280]{1,0:T(8,128)(2,1)S(1)} %get-tuple-element.31), channel_id=1, source_target_pairs={{0,6},{1,7},{2,4},{3,5},{4,2},{5,3},{6,0},{7,1},{8,14},{9,15},{10,... | collective-permute-start | bytes 245768 | tf_op jit(solution)/shard_map/ppermute | solution.py:440
  15.5 24.8 %collective-permute-start.10 = (s16[2576,128]{1,0:T(8,128)(2,1)S(1)}, s16[2576,128]{1,0:T(8,128)(2,1)S(1)}, u32[]{:S(2)}, u32[]{:S(2)}) collective-permute-start(s16[2576,128]{1,0:T(8,128)(2,1)S(1)} %share.3.refs_0_), channel_id=1, source_target_pairs={{0,4},{1,5},{2,6},{3,7},{4,0},{5,1},{6,2},{7,3},{8,12},{9,13},{10,... | collective-permute-start | bytes 1978376 | tf_op jit(solution)/shard_map/ppermute | solution.py:440
  17.0 12.5 %collective-permute-start.3 = (bf16[128,1280]{1,0:T(8,128)(2,1)S(1)}, bf16[128,1280]{1,0:T(8,128)(2,1)S(1)}, u32[]{:S(2)}, u32[]{:S(2)}) collective-permute-start(bf16[128,1280]{1,0:T(8,128)(2,1)S(1)} %constant_dynamic-update-slice_fusion.refs_0_), channel_id=1, source_target_pairs={{0,8},{1,9},{2,10},{3,11},{4,12},{5,13},{6,14},{7,15},{8,0},{9,1},... | collective-permute-start | bytes 983048 | tf_op jit(solution)/shard_map/ppermute | solution.py:440
  18.6 20.6 %collective-permute-start.4 = (bf16[128,1280]{1,0:T(8,128)(2,1)S(1)}, bf16[128,1280]{1,0:T(8,128)(2,1)S(1)}, u32[]{:S(2)}, u32[]{:S(2)}) collective-permute-start(bf16[128,1280]{1,0:T(8,128)(2,1)S(1)} %constant_dynamic-update-slice_fusion.refs_0_), channel_id=1, source_target_pairs={{0,24},{1,25},{2,26},{3,27},{4,28},{5,29},{6,30},{7,31},{8,16},{9,... | collective-permute-start | bytes 983048 | tf_op jit(solution)/shard_map/ppermute | solution.py:440
  25.4 15.0 %collective-permute-start.11 = (s16[1296,128]{1,0:T(8,128)(2,1)S(1)}, s16[1296,128]{1,0:T(8,128)(2,1)S(1)}, u32[]{:S(2)}, u32[]{:S(2)}) collective-permute-start(s16[1296,128]{1,0:T(8,128)(2,1)S(1)} %share.4.refs_0_), channel_id=1, source_target_pairs={{0,4},{1,5},{2,6},{3,7},{4,0},{5,1},{6,2},{7,3},{8,12},{9,13},{10,... | collective-permute-start | bytes 995336 | tf_op jit(solution)/shard_map/ppermute | solution.py:440
  28.2 25.5 %collective-permute-start.12 = (s16[2576,128]{1,0:T(8,128)(2,1)S(1)}, s16[2576,128]{1,0:T(8,128)(2,1)S(1)}, u32[]{:S(2)}, u32[]{:S(2)}) collective-permute-start(s16[2576,128]{1,0:T(8,128)(2,1)S(1)} %share.5), channel_id=1, source_target_pairs={{0,4},{1,5},{2,6},{3,7},{4,0},{5,1},{6,2},{7,3},{8,12},{9,13},{10,... | collective-permute-start | bytes 1978376 | tf_op jit(solution)/shard_map/ppermute | solution.py:440
  29.5 14.5 %collective-permute-start.5 = (bf16[64,1280]{1,0:T(8,128)(2,1)S(1)}, bf16[64,1280]{1,0:T(8,128)(2,1)S(1)}, u32[]{:S(2)}, u32[]{:S(2)}) collective-permute-start(bf16[64,1280]{1,0:T(8,128)(2,1)S(1)} %slice.8), channel_id=1, source_target_pairs={{0,24},{1,25},{2,26},{3,27},{4,28},{5,29},{6,30},{7,31},{8,16},{9,... | collective-permute-start | bytes 491528 | tf_op jit(solution)/shard_map/ppermute | solution.py:440
  39.2 6.1 %collective-permute-start.6 = (bf16[64,1280]{1,0:T(8,128)(2,1)S(1)}, bf16[64,1280]{1,0:T(8,128)(2,1)S(1)}, u32[]{:S(2)}, u32[]{:S(2)}) collective-permute-start(bf16[64,1280]{1,0:T(8,128)(2,1)S(1)} %slice.9), channel_id=1, source_target_pairs={{0,8},{1,9},{2,10},{3,11},{4,12},{5,13},{6,14},{7,15},{8,0},{9,1},... | collective-permute-start | bytes 491528 | tf_op jit(solution)/shard_map/ppermute | solution.py:440
  45.3 16.9 %slice-start = ((s8[6553600]{0:T(1024)(128)(4,1)}), s8[4194304]{0:T(1024)(128)(4,1)S(1)}, s32[]{:S(2)}) async-start(s8[6553600]{0:T(1024)(128)(4,1)} %bitcast.9), calls=%async_computation | async-start | bytes 8388608
  47.6 9.4 %collective-permute-start.13 = (s16[784,128]{1,0:T(8,128)(2,1)S(1)}, s16[784,128]{1,0:T(8,128)(2,1)S(1)}, u32[]{:S(2)}, u32[]{:S(2)}) collective-permute-start(s16[784,128]{1,0:T(8,128)(2,1)S(1)} %get-tuple-element.34), channel_id=1, source_target_pairs={{0,8},{1,9},{2,10},{3,11},{4,12},{5,13},{6,14},{7,15},{8,0},{9,1},... | collective-permute-start | bytes 602120 | tf_op jit(solution)/shard_map/ppermute | solution.py:440
  48.6 14.4 %collective-permute-start.14 = (s16[784,128]{1,0:T(8,128)(2,1)S(1)}, s16[784,128]{1,0:T(8,128)(2,1)S(1)}, u32[]{:S(2)}, u32[]{:S(2)}) collective-permute-start(s16[784,128]{1,0:T(8,128)(2,1)S(1)} %get-tuple-element.36), channel_id=1, source_target_pairs={{0,24},{1,25},{2,26},{3,27},{4,28},{5,29},{6,30},{7,31},{8,16},{9,... | collective-permute-start | bytes 602120 | tf_op jit(solution)/shard_map/ppermute | solution.py:440
  50.1 12.1 %slice-start.1 = ((s8[6553600]{0:T(1024)(128)(4,1)}), s8[2359296]{0:T(1024)(128)(4,1)S(1)}, s32[]{:S(2)}) async-start(s8[6553600]{0:T(1024)(128)(4,1)} %bitcast.9), calls=%async_computation.1 | async-start | bytes 4718592
  50.1 24.3 %collective-permute-start.15 = (s16[784,128]{1,0:T(8,128)(2,1)S(1)}, s16[784,128]{1,0:T(8,128)(2,1)S(1)}, u32[]{:S(2)}, u32[]{:S(2)}) collective-permute-start(s16[784,128]{1,0:T(8,128)(2,1)S(1)} %get-tuple-element.37), channel_id=1, source_target_pairs={{0,16},{1,17},{2,18},{3,19},{4,20},{5,21},{6,22},{7,23},{8,24},{9,... | collective-permute-start | bytes 602120 | tf_op jit(solution)/shard_map/ppermute | solution.py:440
  58.6 15.8 %collective-permute-start.16 = (s16[528,128]{1,0:T(8,128)(2,1)S(1)}, s16[528,128]{1,0:T(8,128)(2,1)S(1)}, u32[]{:S(2)}, u32[]{:S(2)}) collective-permute-start(s16[528,128]{1,0:T(8,128)(2,1)S(1)} %get-tuple-element.38), channel_id=1, source_target_pairs={{0,8},{1,9},{2,10},{3,11},{4,12},{5,13},{6,14},{7,15},{8,0},{9,1},... | collective-permute-start | bytes 405512 | tf_op jit(solution)/shard_map/ppermute | solution.py:440
  58.7 15.7 %collective-permute-start.17 = (s16[528,128]{1,0:T(8,128)(2,1)S(1)}, s16[528,128]{1,0:T(8,128)(2,1)S(1)}, u32[]{:S(2)}, u32[]{:S(2)}) collective-permute-start(s16[528,128]{1,0:T(8,128)(2,1)S(1)} %get-tuple-element.39), channel_id=1, source_target_pairs={{0,24},{1,25},{2,26},{3,27},{4,28},{5,29},{6,30},{7,31},{8,16},{9,... | collective-permute-start | bytes 405512 | tf_op jit(solution)/shard_map/ppermute | solution.py:440
  60.2 17.3 %collective-permute-start.18 = (s16[528,128]{1,0:T(8,128)(2,1)S(1)}, s16[528,128]{1,0:T(8,128)(2,1)S(1)}, u32[]{:S(2)}, u32[]{:S(2)}) collective-permute-start(s16[528,128]{1,0:T(8,128)(2,1)S(1)} %get-tuple-element.40), channel_id=1, source_target_pairs={{0,16},{1,17},{2,18},{3,19},{4,20},{5,21},{6,22},{7,23},{8,24},{9,... | collective-permute-start | bytes 405512 | tf_op jit(solution)/shard_map/ppermute | solution.py:440
  63.0 28.4 %copy-start.3 = (s32[8]{0:T(128)S(1)}, s32[8]{0:T(128)}, u32[]{:S(2)}) copy-start(s32[8]{0:T(128)} %column.1) | copy-start | bytes 100
  79.7 3.6 %collective-permute-start.19 = (s16[336,128]{1,0:T(8,128)(2,1)S(1)}, s16[336,128]{1,0:T(8,128)(2,1)S(1)}, u32[]{:S(2)}, u32[]{:S(2)}) collective-permute-start(s16[336,128]{1,0:T(8,128)(2,1)S(1)} %get-tuple-element.42), channel_id=1, source_target_pairs={{0,2},{1,3},{2,0},{3,1},{4,6},{5,7},{6,4},{7,5},{8,10},{9,11},{10,... | collective-permute-start | bytes 258056 | tf_op jit(solution)/shard_map/ppermute | solution.py:440
  79.8 5.4 %collective-permute-start.20 = (s16[336,128]{1,0:T(8,128)(2,1)S(1)}, s16[336,128]{1,0:T(8,128)(2,1)S(1)}, u32[]{:S(2)}, u32[]{:S(2)}) collective-permute-start(s16[336,128]{1,0:T(8,128)(2,1)S(1)} %get-tuple-element.43), channel_id=1, source_target_pairs={{0,4},{1,5},{2,6},{3,7},{4,0},{5,1},{6,2},{7,3},{8,12},{9,13},{10,... | collective-permute-start | bytes 258056 | tf_op jit(solution)/shard_map/ppermute | solution.py:440
  79.8 6.3 %collective-permute-start.21 = (s16[336,128]{1,0:T(8,128)(2,1)S(1)}, s16[336,128]{1,0:T(8,128)(2,1)S(1)}, u32[]{:S(2)}, u32[]{:S(2)}) collective-permute-start(s16[336,128]{1,0:T(8,128)(2,1)S(1)} %get-tuple-element.44), channel_id=1, source_target_pairs={{0,6},{1,7},{2,4},{3,5},{4,2},{5,3},{6,0},{7,1},{8,14},{9,15},{10,... | collective-permute-start | bytes 258056 | tf_op jit(solution)/shard_map/ppermute | solution.py:440
  81.6 5.1 %collective-permute-start.22 = (s16[336,128]{1,0:T(8,128)(2,1)S(1)}, s16[336,128]{1,0:T(8,128)(2,1)S(1)}, u32[]{:S(2)}, u32[]{:S(2)}) collective-permute-start(s16[336,128]{1,0:T(8,128)(2,1)S(1)} %get-tuple-element.45), channel_id=1, source_target_pairs={{0,1},{1,0},{2,3},{3,2},{4,5},{5,4},{6,7},{7,6},{8,9},{9,8},{10,11... | collective-permute-start | bytes 258056 | tf_op jit(solution)/shard_map/ppermute | solution.py:440
  83.1 4.8 %collective-permute-start.23 = (s16[336,128]{1,0:T(8,128)(2,1)S(1)}, s16[336,128]{1,0:T(8,128)(2,1)S(1)}, u32[]{:S(2)}, u32[]{:S(2)}) collective-permute-start(s16[336,128]{1,0:T(8,128)(2,1)S(1)} %get-tuple-element.46), channel_id=1, source_target_pairs={{0,3},{1,2},{2,1},{3,0},{4,7},{5,6},{6,5},{7,4},{8,11},{9,10},{10,... | collective-permute-start | bytes 258056 | tf_op jit(solution)/shard_map/ppermute | solution.py:440
  83.3 6.4 %collective-permute-start.24 = (s16[336,128]{1,0:T(8,128)(2,1)S(1)}, s16[336,128]{1,0:T(8,128)(2,1)S(1)}, u32[]{:S(2)}, u32[]{:S(2)}) collective-permute-start(s16[336,128]{1,0:T(8,128)(2,1)S(1)} %get-tuple-element.47), channel_id=1, source_target_pairs={{0,5},{1,4},{2,7},{3,6},{4,1},{5,0},{6,3},{7,2},{8,13},{9,12},{10,... | collective-permute-start | bytes 258056 | tf_op jit(solution)/shard_map/ppermute | solution.py:440
  85.2 6.2 %collective-permute-start.25 = (s16[336,128]{1,0:T(8,128)(2,1)S(1)}, s16[336,128]{1,0:T(8,128)(2,1)S(1)}, u32[]{:S(2)}, u32[]{:S(2)}) collective-permute-start(s16[336,128]{1,0:T(8,128)(2,1)S(1)} %get-tuple-element.48), channel_id=1, source_target_pairs={{0,7},{1,6},{2,5},{3,4},{4,3},{5,2},{6,1},{7,0},{8,15},{9,14},{10,... | collective-permute-start | bytes 258056 | tf_op jit(solution)/shard_map/ppermute | solution.py:440

commit v7 on v6

--- a/solution.py
+++ b/solution.py
@@ -200,41 +200,42 @@
     )(own, *got)
 
 
-def product_kernel(pieces, count, after, *refs):
+def product_kernel(pieces, kept, after, *refs):
     parts, op = refs[:pieces], refs[pieces]
     refs = refs[pieces + 1 + after :]
-    near, sends, full = refs[0], refs[1:count], refs[count]
+    outs, full = refs[:pieces], refs[pieces]
     tiles = op.shape[0]
     rows = parts[0].shape[0]
-    start = 0
-    for part in parts:
-        full[start : start + part.shape[0], :] = part[...]
-        start += part.shape[0]
-    tails = [jnp.zeros((TAIL, LANES), F32)] * (count - 1)
+    for i, part in enumerate(parts):
+        full[i * rows : (i + 1) * rows, :] = part[...]
+    tails = {q: jnp.zeros((TAIL, LANES), F32) for q in range(pieces) if q not in kept}
     for t in range(tiles):
         x = full[...]
         acc = jnp.dot(x, op[t, 0], preferred_element_type=F32)
         acc += jnp.dot(x, op[t, 1], preferred_element_type=F32)
-        near[t] = acc[:rows]
-        for q in range(1, count):
+        for q in range(pieces):
+            block = acc[q * rows : (q + 1) * rows]
+            if q in kept:
+                outs[q][t] = block
+                continue
             for part in range(2):
                 strip = 2 * t + part
-                block = acc[q * rows : (q + 1) * rows, part * LANES : (part + 1) * LANES]
-                code, step = encode(block)
-                sends[q - 1][strip * rows : (strip + 1) * rows, :] = code
-                tails[q - 1] = put_row(tails[q - 1], strip, step)
-    for send, tail in zip(sends, tails):
-        send[2 * tiles * rows :, :] = tail.astype(I32).astype(I16)
-
-
-def product(parts, op, after):
+                code, step = encode(block[:, part * LANES : (part + 1) * LANES])
+                outs[q][strip * rows : (strip + 1) * rows, :] = code
+                tails[q] = put_row(tails[q], strip, step)
+    for q, tail in tails.items():
+        outs[q][2 * tiles * rows :, :] = tail.astype(I32).astype(I16)
+
+
+def product(parts, op, kept, after):
     tiles = op.shape[0]
     rows, width = parts[0].shape
-    count = sum(part.shape[0] for part in parts) // rows
+    count = len(parts)
+    plain = jax.ShapeDtypeStruct((tiles, rows, 2 * LANES), F32)
     send = message(2 * tiles, rows)
     return pl.pallas_call(
-        functools.partial(product_kernel, len(parts), count, len(after)),
-        out_shape=[jax.ShapeDtypeStruct((tiles, rows, 2 * LANES), F32)] + [send] * (count - 1),
+        functools.partial(product_kernel, count, kept, len(after)),
+        out_shape=[plain if q in kept else send for q in range(count)],
         in_specs=[whole(x.shape) for x in (*parts, op)]
         + [pl.BlockSpec(memory_space=pl.ANY)] * len(after),
         out_specs=[whole(send.shape)] * count,
@@ -247,6 +248,38 @@
         ),
         name="product",
     )(*parts, op, *after)
+
+
+def fold_kernel(own, got, *refs):
+    out = refs[-1]
+    tail = jnp.zeros((TAIL, LANES), F32)
+    sums = {}
+
+    def write(tile, part, total):
+        sums[2 * tile + part] = total
+
+    add_up([own], [[got]], write)
+    rows = own.shape[1]
+    for strip, total in sums.items():
+        code, step = encode(total)
+        out[strip * rows : (strip + 1) * rows, :] = code
+        tail = put_row(tail, strip, step)
+    out[out.shape[0] - TAIL :, :] = tail.astype(I32).astype(I16)
+
+
+def fold(own, got, after):
+    return pl.pallas_call(
+        fold_kernel,
+        out_shape=jax.ShapeDtypeStruct(got.shape, got.dtype),
+        in_specs=[whole(own.shape), whole(got.shape)]
+        + [pl.BlockSpec(memory_space=pl.ANY)] * len(after),
+        out_specs=whole(got.shape),
+        compiler_params=params(),
+        cost_estimate=pl.CostEstimate(
+            flops=12 * own.size, bytes_accessed=8 * own.size, transcendentals=0
+        ),
+        name="fold",
+    )(own, got, *after)
 
 
 def add_up(near, got, write):
@@ -265,14 +298,16 @@
         base += tiles
 
 
-def unpack(refs, chunks, count):
-    near = refs[:chunks]
-    got = [refs[chunks + i * count : chunks + (i + 1) * count] for i in range(chunks)]
-    return near, got, refs[chunks * (1 + count) :]
-
-
-def synthesis_kernel(bands, chunks, count, where, *refs):
-    near, got, rest = unpack(refs, chunks, count)
+def unpack(refs, counts):
+    near, refs, got = refs[: len(counts)], refs[len(counts) :], []
+    for count in counts:
+        got.append(refs[:count])
+        refs = refs[count:]
+    return near, got, refs
+
+
+def synthesis_kernel(bands, counts, where, *refs):
+    near, got, rest = unpack(refs, counts)
     table, outs, values = rest[0], rest[1:-1], rest[-1]
     rows = near[0].shape[1]
     quarter = rows // 4
@@ -318,7 +353,7 @@
     outs = [jax.ShapeDtypeStruct((2, rows // 4, band), F32)] + [send] * (4 * bands - 1)
     operands = [*near, *[part for parts in got for part in parts], table]
     return pl.pallas_call(
-        functools.partial(synthesis_kernel, bands, len(near), len(got[0])),
+        functools.partial(synthesis_kernel, bands, [len(parts) for parts in got]),
         out_shape=outs,
         in_specs=[pl.BlockSpec(memory_space=pltpu.SMEM)] + [whole(x.shape) for x in operands],
         out_specs=[whole(out.shape) for out in outs],
@@ -333,8 +368,8 @@
     )(where, *operands)
 
 
-def total_kernel(chunks, count, *refs):
-    near, got, (out,) = unpack(refs, chunks, count)
+def total_kernel(counts, *refs):
+    near, got, (out,) = unpack(refs, counts)
 
     def write(tile, part, total):
         out[part, :, tile * LANES : (tile + 1) * LANES] = total
@@ -346,7 +381,7 @@
     rows = near[0].shape[1]
     size, nlat = table.shape
     total = pl.pallas_call(
-        functools.partial(total_kernel, len(near), len(got[0])),
+        functools.partial(total_kernel, [len(parts) for parts in got]),
         out_shape=jax.ShapeDtypeStruct((2, rows, size), F32),
         compiler_params=params(),
         name="total",
@@ -362,7 +397,7 @@
     ]
 
 
-def place_kernel(count, slots, where, column, *refs):
+def place_kernel(count, slots, order, where, column, *refs):
     pieces, out, full, sems = refs[:count], refs[count], refs[count + 1], refs[count + 2]
     _, _, rows, lanes = full.shape
     copies = []
@@ -378,19 +413,20 @@
                 full[i, strip % 2, :, at : at + LANES] = (
                     code.astype(I32).astype(F32) * table[strip : strip + 1, :]
                 )
-        slot = column[(where[4] ^ (i // 4)) * slots + where[i % 4]]
+        d, bits = order[i]
+        slot = column[(where[4] ^ d) * slots + where[bits]]
         copies.append(pltpu.make_async_copy(full.at[i], out.at[slot], sems.at[i]))
         copies[-1].start()
     for copy in copies:
         copy.wait()
 
 
-def place(where, column, slots, pieces):
+def place(where, column, slots, order, pieces):
     count = len(pieces)
-    shape = (count,) + pieces[0].shape
+    shape = (count,) + pieces[order.index((0, 0))].shape
     smem = pl.BlockSpec(memory_space=pltpu.SMEM)
     return pl.pallas_call(
-        functools.partial(place_kernel, count, slots),
+        functools.partial(place_kernel, count, slots, order),
         out_shape=jax.ShapeDtypeStruct(shape, F32),
         in_specs=[smem, smem] + [whole(piece.shape) for piece in pieces],
         out_specs=pl.BlockSpec(memory_space=pl.ANY),
@@ -446,10 +482,9 @@
     received = [swap(states[bits], bits) for bits in range(1, 4)]
     turned, received[0] = lax.optimization_barrier((place_of, received[0]))
     block = jnp.concatenate([states[0]] + received, axis=0)
-    steps = [q for q in range(1, outer) if q != 2] + [2]
+    steps = [3, 1] + list(range(4, outer)) + [2]
     parts = [block] + [swap(block, q * 4) for q in steps[:-1]]
-    half = block.shape[0] // 2
-    parts += [swap(parts[1][:half], 3 * 4), swap(parts[2][half:], 1 * 4)]
+    parts.append(swap(parts[1], 1 * 4))
 
     w_got = swap(term_weights, 1)
     far, own = (
@@ -463,25 +498,31 @@
     for group in groups:
         start, messages = first, []
         for n in group:
-            after = (block,) if not shares else (shares[-1], mine)
+            after = () if not shares else (shares[-1], mine)
             shares.append(
                 share(where, term_weights, w_got, inverse, far, first, n, after)
             )
             messages.append(swap(shares[-1], 2))
             first += n
         after = [near[-1], got[-1][0]] if near else []
-        made = product(parts, build(mine, messages, start, group), after)
+        op = build(mine, messages, start, group)
+        if group is not groups[-1]:
+            made = product(parts, op, (0,), after)
+            sends = made[1:]
+        else:
+            made = product(parts, op, (0, 1), after)
+            sends = [fold(made[1], swap(made[-1], 1 * 4), got[-1][1:] if got else []), *made[2:-1]]
         near.append(made[0])
-        got.append([swap(send, q * 4) for send, q in zip(made[1:], steps)])
+        got.append([swap(send, q * 4) for send, q in zip(sends, steps)])
     make = synthesis if legendre.shape[2] // waves % LANES == 0 else plain_synthesis
     table = slot_table(where, legendre, near[-1])
     grid = make(where, near, got, table, waves)
+    order = [(d, bits) for d in reversed(range(waves)) for bits in (2, 3, 0, 1)]
+    order.append(order.pop(order.index((0, 0))))
     pieces = [
-        swap(grid[4 * d + bits], bits, d) if d or bits else grid[0]
-        for d in range(waves)
-        for bits in range(4)
+        swap(grid[4 * d + bits], bits, d) if d or bits else grid[0] for d, bits in order
     ]
-    return place(where, slot_column, slots, pieces)
+    return place(where, slot_column, slots, order, pieces)
 
 
 def solution(mesh):

time: 93.1 us -> 88.3 us (0.948)
  waiting for transfers between devices: 36.6 us -> 30.6 us
  starting transfers between devices: 34.1 us -> 35.3 us
    ppermute x26 -> x25, waiting for transfers between devices: 36.6 us -> 30.6 us  [swap(): return lax.ppermute(x, ('term', 'wave'), pairs)]
    ppermute x26 -> x25, starting transfers between devices: 34.1 us -> 35.3 us  [swap(): return lax.ppermute(x, ('term', 'wave'), pairs)]
    pallas_call x4 -> x5, Pallas kernels: 7.75 us -> 7.79 us  [the longest x2 3.88 us: product(): pl.pallas_call(functools.partial(product_kernel, count, kept, len(after))...]
  transfers between devices with their start and end apart: 26 -> 25, of which waited for: 16 -> 15; matrix products, arithmetic and copies ran while one was open for 0% -> 0% of each run, Pallas kernels for 15% -> 16%
where the time goes in v7:
time: 88.3 us; the launch traced here: 88.2 us
  starting transfers between devices  35.3 us (40%)
  waiting for transfers between devices  30.6 us (35%)
  Pallas kernels  18.6 us (21%)
  local copies, waits for them, and re-layouts  3.46 us (4%)
    ppermute x25, starting transfers between devices, swap(): return lax.ppermute(x, ('term', 'wave'), pairs)  35.3 us
    ppermute x25, waiting for transfers between devices, swap(): return lax.ppermute(x, ('term', 'wave'), pairs)  30.6 us
    pallas_call x3, Pallas kernels, share(): pl.pallas_call(functools.partial(share_kernel, len(after)), out_shape=out...  5.27 us
    pallas_call x2, Pallas kernels, product(): pl.pallas_call(functools.partial(product_kernel, count, kept, len(after))...  3.88 us
    pallas_call x1, Pallas kernels, operator(): pl.pallas_call(own_kernel, out_shape=jax.ShapeDtypeStruct((tiles, 2, size...  2.91 us
    squeeze x1, local copies, waits for them, and re-layouts, shards(): lax.dynamic_index_in_dim(inverse, turned ^ bits, 1, keepdims=False)  2.36 us
    pallas_call x1, Pallas kernels, synthesis(): pl.pallas_call(functools.partial(synthesis_kernel, bands, [len(parts) for...  2.13 us
  transfers between devices with their start and end apart: 25, of which 15 were waited for; matrix products, arithmetic and copies ran while one was open for 0% of the time, Pallas kernels for 16%

profile of v7, /device:TPU:0, one launch (start us, length us, event | category | flops | bytes accessed | tf_op | source)
XLA Modules:
  0.0 88.2 jit_solution(1202727308121306487)
XLA Ops:
  0.0 0.1 stack.23.where
  0.1 1.0 %copy-done.1 = bf16[4,32,1280]{2,1,0:T(8,128)(2,1)S(1)} copy-done((bf16[4,32,1280]{2,1,0:T(8,128)(2,1)S(1)}, bf16[4,32,1280]{2,1,0:T(8,128)(2,1)}, u32[]{:S(2)}) %copy-start.1) | copy-done | bytes 327704
  1.1 0.6 pick.1
  1.6 0.5 collective-permute-start
  2.2 0.9 %collective-permute-done = bf16[32,1280]{1,0:T(8,128)(2,1)S(1)} collective-permute-done((bf16[32,1280]{1,0:T(8,128)(2,1)S(1)}, bf16[32,1280]{1,0:T(8,128)(2,1)S(1)}, u32[]{:S(2)}, u32[]{:S(2)}) %collective-permute-start) | collective-permute-done | bytes 81952 | tf_op jit(solution)/shard_map/ppermute | solution.py:476
  3.1 2.4 %dynamic-slice_bitcast_fusion = (bf16[1,2,640,640]{3,2,1,0:T(8,128)(2,1)S(1)}, bf16[1,2,640,640]{3,2,1,0:T(8,128)(2,1)S(1)}) fusion(bf16[1,4,2,640,640]{4,3,2,1,0:T(8,128)(2,1)} %own.7, s32[]{:T(128)S(6)} %select_n.16, s32[]{:T(128)S(6)} %select_n.15), kind=kLoop, calls=%fused_computation | loop fusion | bytes 6553608 | tf_op jit(solution)/shard_map/jit(dynamic_index_in_dim)/squeeze | solution.py:491
  5.4 0.4 collective-permute-start.8
  5.9 0.2 collective-permute-start.7
  6.0 0.4 collective-permute-start.6
  6.4 2.7 %collective-permute-start.1 = (bf16[32,1280]{1,0:T(8,128)(2,1)S(1)}, bf16[32,1280]{1,0:T(8,128)(2,1)S(1)}, u32[]{:S(2)}, u32[]{:S(2)}) collective-permute-start(bf16[32,1280]{1,0:T(8,128)(2,1)S(1)} %get-tuple-element.30), channel_id=1, source_target_pairs={{0,4},{1,5},{2,6},{3,7},{4,0},{5,1},{6,2},{7,3},{8,12},{9,13},{10,... | collective-permute-start | bytes 245768 | tf_op jit(solution)/shard_map/ppermute | solution.py:476
  9.1 0.0 collective-permute-start.2
  9.1 2.9 %collective-permute-done.1 = bf16[32,1280]{1,0:T(8,128)(2,1)S(1)} collective-permute-done((bf16[32,1280]{1,0:T(8,128)(2,1)S(1)}, bf16[32,1280]{1,0:T(8,128)(2,1)S(1)}, u32[]{:S(2)}, u32[]{:S(2)}) %collective-permute-start.1) | collective-permute-done | bytes 81952 | tf_op jit(solution)/shard_map/ppermute | solution.py:476
  12.0 0.0 collective-permute-done.6.w_got
  12.0 0.0 collective-permute-done.8.got
  12.0 1.9 %share.3.refs_0_ = s16[2576,128]{1,0:T(8,128)(2,1)S(1)} custom-call(s32[5]{0:T(128)S(1)} %stack.23.where, f32[1,2]{1,0:T(1,128)S(1)} %copy-done.2, f32[1,2]{1,0:T(1,128)S(1)} %collective-permute-done.6.w_got, bf16[1,4,2,640,640]{4,3,2,1,0:T(8,128)(2,1)S(1)} %copy-done, bf16[1,2,640,640]{3,2,1,0:T(8,128)(2,1)S(1)} %collective-permute-done.8.got), custom_call_target="tpu_custom_call" | custom-call | flops 5242880 | bytes 2621440 | tf_op jit(solution)/shard_map/share/pallas_call | solution.py:91
  14.0 2.4 %collective-permute-start.9 = (s16[2576,128]{1,0:T(8,128)(2,1)S(1)}, s16[2576,128]{1,0:T(8,128)(2,1)S(1)}, u32[]{:S(2)}, u32[]{:S(2)}) collective-permute-start(s16[2576,128]{1,0:T(8,128)(2,1)S(1)} %share.3.refs_0_), channel_id=1, source_target_pairs={{0,4},{1,5},{2,6},{3,7},{4,0},{5,1},{6,2},{7,3},{8,12},{9,13},{10,... | collective-permute-start | bytes 1978376 | tf_op jit(solution)/shard_map/ppermute | solution.py:476
  16.4 0.0 collective-permute-done.2
  16.4 3.7 %collective-permute-start.3 = (bf16[128,1280]{1,0:T(8,128)(2,1)S(1)}, bf16[128,1280]{1,0:T(8,128)(2,1)S(1)}, u32[]{:S(2)}, u32[]{:S(2)}) collective-permute-start(bf16[128,1280]{1,0:T(8,128)(2,1)S(1)} %constant_dynamic-update-slice_fusion.refs_0_), channel_id=1, source_target_pairs={{0,24},{1,25},{2,26},{3,27},{4,28},{5,29},{6,30},{7,31},{8,16},{9,... | collective-permute-start | bytes 983048 | tf_op jit(solution)/shard_map/ppermute | solution.py:476
  20.0 0.0 collective-permute-done.7.got
  20.0 2.9 %operator.1.refs_1_.own = f32[5,2,640,128]{3,2,1,0:T(8,128)S(1)} custom-call(s32[5]{0:T(128)S(1)} %stack.23.where, f32[1,2]{1,0:T(1,128)S(1)} %copy-done.2, f32[1,2]{1,0:T(1,128)S(1)} %collective-permute-done.6.w_got, bf16[1,4,2,640,640]{4,3,2,1,0:T(8,128)(2,1)S(1)} %copy-done, bf16[1,2,640,640]{3,2,1,0:T(8,128)(2,1)S(1)} %collective-permute-done.7.got), custom_call_target="tpu_custom_call" | custom-call | flops 13107200 | bytes 6553600 | tf_op jit(solution)/shard_map/operator/pallas_call | solution.py:126
  23.0 1.4 %share.4.refs_0_ = s16[1296,128]{1,0:T(8,128)(2,1)S(1)} custom-call(s32[5]{0:T(128)S(1)} %stack.23.where, f32[1,2]{1,0:T(1,128)S(1)} %copy-done.2, f32[1,2]{1,0:T(1,128)S(1)} %collective-permute-done.6.w_got, bf16[1,4,2,640,640]{4,3,2,1,0:T(8,128)(2,1)S(1)} %copy-done, bf16[1,2,640,640]{3,2,1,0:T(8,128)(2,1)S(1)} %collective-permute-done.8.got, ...), custom_call_target="tpu_custom_call" | custom-call | flops 2621440 | bytes 1310720 | tf_op jit(solution)/shard_map/share/pallas_call | solution.py:91
  24.4 0.5 collective-permute-start.10
  24.8 4.0 %collective-permute-done.3.refs_1_ = bf16[128,1280]{1,0:T(8,128)(2,1)S(1)} collective-permute-done((bf16[128,1280]{1,0:T(8,128)(2,1)S(1)}, bf16[128,1280]{1,0:T(8,128)(2,1)S(1)}, u32[]{:S(2)}, u32[]{:S(2)}) %collective-permute-start.3) | collective-permute-done | bytes 327712 | tf_op jit(solution)/shard_map/ppermute | solution.py:476
  28.8 5.6 %collective-permute-start.5 = (bf16[128,1280]{1,0:T(8,128)(2,1)S(1)}, bf16[128,1280]{1,0:T(8,128)(2,1)S(1)}, u32[]{:S(2)}, u32[]{:S(2)}) collective-permute-start(bf16[128,1280]{1,0:T(8,128)(2,1)S(1)} %collective-permute-done.3.refs_1_), channel_id=1, source_target_pairs={{0,8},{1,9},{2,10},{3,11},{4,12},{5,13},{6,14},{7,15},{8,0},{9,1},... | collective-permute-start | bytes 983048 | tf_op jit(solution)/shard_map/ppermute | solution.py:476
  34.4 1.9 %share.5 = s16[2576,128]{1,0:T(8,128)(2,1)S(1)} custom-call(s32[5]{0:T(128)S(1)} %stack.23.where, f32[1,2]{1,0:T(1,128)S(1)} %copy-done.2, f32[1,2]{1,0:T(1,128)S(1)} %collective-permute-done.6.w_got, bf16[1,4,2,640,640]{4,3,2,1,0:T(8,128)(2,1)S(1)} %copy-done, bf16[1,2,640,640]{3,2,1,0:T(8,128)(2,1)S(1)} %collective-permute-done.8.got, ...), custom_call_target="tpu_custom_call" | custom-call | flops 5242880 | bytes 2621440 | tf_op jit(solution)/shard_map/share/pallas_call | solution.py:91
  36.4 0.6 collective-permute-start.11
  36.9 2.2 %collective-permute-done.10.refs_1_ = s16[1296,128]{1,0:T(8,128)(2,1)S(1)} collective-permute-done((s16[1296,128]{1,0:T(8,128)(2,1)S(1)}, s16[1296,128]{1,0:T(8,128)(2,1)S(1)}, u32[]{:S(2)}, u32[]{:S(2)}) %collective-permute-start.10) | collective-permute-done | bytes 331808 | tf_op jit(solution)/shard_map/ppermute | solution.py:476
  39.1 0.8 build.2.refs_4_
  39.9 0.0 collective-permute-done.4.refs_2_
  39.9 1.9 %collective-permute-done.5.refs_3_ = bf16[128,1280]{1,0:T(8,128)(2,1)S(1)} collective-permute-done((bf16[128,1280]{1,0:T(8,128)(2,1)S(1)}, bf16[128,1280]{1,0:T(8,128)(2,1)S(1)}, u32[]{:S(2)}, u32[]{:S(2)}) %collective-permute-start.5) | collective-permute-done | bytes 327712 | tf_op jit(solution)/shard_map/ppermute | solution.py:476
  41.8 2.3 %product.2 = (f32[3,128,256]{2,1,0:T(8,128)S(1)}, s16[784,128]{1,0:T(8,128)(2,1)S(1)}, s16[784,128]{1,0:T(8,128)(2,1)S(1)}, s16[784,128]{1,0:T(8,128)(2,1)S(1)}) custom-call(bf16[128,1280]{1,0:T(8,128)(2,1)S(1)} %constant_dynamic-update-slice_fusion.refs_0_, bf16[128,1280]{1,0:T(8,128)(2,1)S(1)} %collective-permute-done.3.refs_1_, ...), custom_call_target="tpu_custom_call" | custom-call | flops 2013265920 | bytes 5242880 | tf_op jit(solution)/shard_map/product/pallas_call | solution.py:236
  44.1 3.6 %collective-permute-start.12 = (s16[784,128]{1,0:T(8,128)(2,1)S(1)}, s16[784,128]{1,0:T(8,128)(2,1)S(1)}, u32[]{:S(2)}, u32[]{:S(2)}) collective-permute-start(s16[784,128]{1,0:T(8,128)(2,1)S(1)} %get-tuple-element.34), channel_id=1, source_target_pairs={{0,24},{1,25},{2,26},{3,27},{4,28},{5,29},{6,30},{7,31},{8,16},{9,... | collective-permute-start | bytes 602120 | tf_op jit(solution)/shard_map/ppermute | solution.py:476
  47.7 0.0 collective-permute-start.13
  47.7 0.9 collective-permute-start.14
  48.6 4.0 %collective-permute-done.11.refs_0_ = s16[2576,128]{1,0:T(8,128)(2,1)S(1)} collective-permute-done((s16[2576,128]{1,0:T(8,128)(2,1)S(1)}, s16[2576,128]{1,0:T(8,128)(2,1)S(1)}, u32[]{:S(2)}, u32[]{:S(2)}) %collective-permute-start.11) | collective-permute-done | bytes 659488 | tf_op jit(solution)/shard_map/ppermute | solution.py:476
  52.6 0.5 build.3.refs_4_
  53.1 0.8 collective-permute-done.12.refs_6_.refs_2_
  53.9 1.6 %product.3 = (f32[2,128,256]{2,1,0:T(8,128)S(1)}, f32[2,128,256]{2,1,0:T(8,128)S(1)}, s16[528,128]{1,0:T(8,128)(2,1)S(1)}, s16[528,128]{1,0:T(8,128)(2,1)S(1)}) custom-call(bf16[128,1280]{1,0:T(8,128)(2,1)S(1)} %constant_dynamic-update-slice_fusion.refs_0_, bf16[128,1280]{1,0:T(8,128)(2,1)S(1)} %collective-permute-done.3.refs_1_, ...), custom_call_target="tpu_custom_call" | custom-call | flops 1342177280 | bytes 3932160 | tf_op jit(solution)/shard_map/product/pallas_call | solution.py:236
  55.5 7.5 %collective-permute-start.15 = (s16[528,128]{1,0:T(8,128)(2,1)S(1)}, s16[528,128]{1,0:T(8,128)(2,1)S(1)}, u32[]{:S(2)}, u32[]{:S(2)}) collective-permute-start(s16[528,128]{1,0:T(8,128)(2,1)S(1)} %get-tuple-element.39), channel_id=1, source_target_pairs={{0,8},{1,9},{2,10},{3,11},{4,12},{5,13},{6,14},{7,15},{8,0},{9,1},... | collective-permute-start | bytes 405512 | tf_op jit(solution)/shard_map/ppermute | solution.py:476
  63.0 0.1 collective-permute-start.17
  63.1 0.0 collective-permute-done.13.refs_0_.refs_3_
  63.1 0.9 %collective-permute-done.14.refs_1_.refs_4_ = s16[784,128]{1,0:T(8,128)(2,1)S(1)} collective-permute-done((s16[784,128]{1,0:T(8,128)(2,1)S(1)}, s16[784,128]{1,0:T(8,128)(2,1)S(1)}, u32[]{:S(2)}, u32[]{:S(2)}) %collective-permute-start.14) | collective-permute-done | bytes 200736 | tf_op jit(solution)/shard_map/ppermute | solution.py:476
  64.0 2.4 %collective-permute-done.15.got = s16[528,128]{1,0:T(8,128)(2,1)S(1)} collective-permute-done((s16[528,128]{1,0:T(8,128)(2,1)S(1)}, s16[528,128]{1,0:T(8,128)(2,1)S(1)}, u32[]{:S(2)}, u32[]{:S(2)}) %collective-permute-start.15) | collective-permute-done | bytes 135200 | tf_op jit(solution)/shard_map/ppermute | solution.py:476
  66.4 0.1 fold.1
  66.5 1.0 %collective-permute-start.16 = (s16[528,128]{1,0:T(8,128)(2,1)S(1)}, s16[528,128]{1,0:T(8,128)(2,1)S(1)}, u32[]{:S(2)}, u32[]{:S(2)}) collective-permute-start(s16[528,128]{1,0:T(8,128)(2,1)S(1)} %fold.1), channel_id=1, source_target_pairs={{0,24},{1,25},{2,26},{3,27},{4,28},{5,29},{6,30},{7,31},{8,16},{9,... | collective-permute-start | bytes 405512 | tf_op jit(solution)/shard_map/ppermute | solution.py:476
  67.5 0.8 table.1.refs_7_
  68.2 0.0 copy-start.3
  68.3 1.2 %collective-permute-done.17.refs_6_ = s16[528,128]{1,0:T(8,128)(2,1)S(1)} collective-permute-done((s16[528,128]{1,0:T(8,128)(2,1)S(1)}, s16[528,128]{1,0:T(8,128)(2,1)S(1)}, u32[]{:S(2)}, u32[]{:S(2)}) %collective-permute-start.17) | collective-permute-done | bytes 135200 | tf_op jit(solution)/shard_map/ppermute | solution.py:476
  69.5 4.0 %collective-permute-done.16.refs_5_ = s16[528,128]{1,0:T(8,128)(2,1)S(1)} collective-permute-done((s16[528,128]{1,0:T(8,128)(2,1)S(1)}, s16[528,128]{1,0:T(8,128)(2,1)S(1)}, u32[]{:S(2)}, u32[]{:S(2)}) %collective-permute-start.16) | collective-permute-done | bytes 135200 | tf_op jit(solution)/shard_map/ppermute | solution.py:476
  73.5 2.1 %synthesis.1 = (f32[2,32,640]{2,1,0:T(8,128)S(1)}, s16[336,128]{1,0:T(8,128)(2,1)S(1)}, s16[336,128]{1,0:T(8,128)(2,1)S(1)}, s16[336,128]{1,0:T(8,128)(2,1)S(1)}...) custom-call(s32[5]{0:T(128)S(1)} %stack.23.where, ...), custom_call_target="tpu_custom_call" | custom-call | flops 838860800 | bytes 2949120 | tf_op jit(solution)/shard_map/synthesis/pallas_call | solution.py:355
  75.6 1.1 %collective-permute-start.18 = (s16[336,128]{1,0:T(8,128)(2,1)S(1)}, s16[336,128]{1,0:T(8,128)(2,1)S(1)}, u32[]{:S(2)}, u32[]{:S(2)}) collective-permute-start(s16[336,128]{1,0:T(8,128)(2,1)S(1)} %get-tuple-element.41), channel_id=1, source_target_pairs={{0,5},{1,4},{2,7},{3,6},{4,1},{5,0},{6,3},{7,2},{8,13},{9,12},{10,... | collective-permute-start | bytes 258056 | tf_op jit(solution)/shard_map/ppermute | solution.py:476
  76.7 0.0 collective-permute-start.19
  76.7 0.6 collective-permute-start.20
  77.3 2.8 %collective-permute-start.21 = (s16[336,128]{1,0:T(8,128)(2,1)S(1)}, s16[336,128]{1,0:T(8,128)(2,1)S(1)}, u32[]{:S(2)}, u32[]{:S(2)}) collective-permute-start(s16[336,128]{1,0:T(8,128)(2,1)S(1)} %get-tuple-element.44), channel_id=1, source_target_pairs={{0,3},{1,2},{2,1},{3,0},{4,7},{5,6},{6,5},{7,4},{8,11},{9,10},{10,... | collective-permute-start | bytes 258056 | tf_op jit(solution)/shard_map/ppermute | solution.py:476
  80.1 0.1 collective-permute-start.22
  80.2 1.5 %collective-permute-done.18.refs_0_ = s16[336,128]{1,0:T(8,128)(2,1)S(1)} collective-permute-done((s16[336,128]{1,0:T(8,128)(2,1)S(1)}, s16[336,128]{1,0:T(8,128)(2,1)S(1)}, u32[]{:S(2)}, u32[]{:S(2)}) %collective-permute-start.18) | collective-permute-done | bytes 86048 | tf_op jit(solution)/shard_map/ppermute | solution.py:476
  81.6 0.7 collective-permute-done.19.refs_1_
  82.3 1.0 %collective-permute-start.24 = (s16[336,128]{1,0:T(8,128)(2,1)S(1)}, s16[336,128]{1,0:T(8,128)(2,1)S(1)}, u32[]{:S(2)}, u32[]{:S(2)}) collective-permute-start(s16[336,128]{1,0:T(8,128)(2,1)S(1)} %get-tuple-element.47), channel_id=1, source_target_pairs={{0,2},{1,3},{2,0},{3,1},{4,6},{5,7},{6,4},{7,5},{8,10},{9,11},{10,... | collective-permute-start | bytes 258056 | tf_op jit(solution)/shard_map/ppermute | solution.py:476
  83.3 0.0 collective-permute-done.20.refs_2_
  83.3 1.9 %collective-permute-done.21.refs_3_ = s16[336,128]{1,0:T(8,128)(2,1)S(1)} collective-permute-done((s16[336,128]{1,0:T(8,128)(2,1)S(1)}, s16[336,128]{1,0:T(8,128)(2,1)S(1)}, u32[]{:S(2)}, u32[]{:S(2)}) %collective-permute-start.21) | collective-permute-done | bytes 86048 | tf_op jit(solution)/shard_map/ppermute | solution.py:476
  85.2 0.0 collective-permute-done.22.refs_4_
  85.2 1.3 %collective-permute-done.23.refs_5_ = s16[336,128]{1,0:T(8,128)(2,1)S(1)} collective-permute-done((s16[336,128]{1,0:T(8,128)(2,1)S(1)}, s16[336,128]{1,0:T(8,128)(2,1)S(1)}, u32[]{:S(2)}, u32[]{:S(2)}) %collective-permute-start.23) | collective-permute-done | bytes 86048 | tf_op jit(solution)/shard_map/ppermute | solution.py:476
  86.5 0.0 collective-permute-done.24.refs_6_
  86.5 1.7 %place.1 = f32[8,2,32,640]{3,2,1,0:T(8,128)} custom-call(s32[5]{0:T(128)S(1)} %stack.23.where, s32[8]{0:T(128)S(1)} %copy-done.3, s16[336,128]{1,0:T(8,128)(2,1)S(1)} %collective-permute-done.18.refs_0_, s16[336,128]{1,0:T(8,128)(2,1)S(1)} %collective-permute-done.19.refs_1_, s16[336,128]{1,0:T(8,128)(2,1)S(1)} %collective-permute-done.20.refs_2_, ...), custom_call_target="tpu_custom_call" | custom-call | tf_op jit(solution)/shard_map/place/pallas_call | solution.py:428
  (18 shorter events, 0.1 us)
Async XLA Ops:
  0.1 1.0 %copy-start.1 = (bf16[4,32,1280]{2,1,0:T(8,128)(2,1)S(1)}, bf16[4,32,1280]{2,1,0:T(8,128)(2,1)}, u32[]{:S(2)}) copy-start(bf16[4,32,1280]{2,1,0:T(8,128)(2,1)} %refs_3_.1) | copy-start | bytes 983044
  1.6 1.4 %collective-permute-start = (bf16[32,1280]{1,0:T(8,128)(2,1)S(1)}, bf16[32,1280]{1,0:T(8,128)(2,1)S(1)}, u32[]{:S(2)}, u32[]{:S(2)}) collective-permute-start(bf16[32,1280]{1,0:T(8,128)(2,1)S(1)} %get-tuple-element.28), channel_id=1, source_target_pairs={{0,2},{1,3},{2,0},{3,1},{4,6},{5,7},{6,4},{7,5},{8,10},{9,11},{10,... | collective-permute-start | bytes 245768 | tf_op jit(solution)/shard_map/ppermute | solution.py:476
  3.1 2.9 %copy-start.2 = (f32[1,2]{1,0:T(1,128)S(1)}, f32[1,2]{1,0:T(1,128)}, u32[]{:S(2)}) copy-start(f32[1,2]{1,0:T(1,128)} %w_own.7) | copy-start | bytes 28
  3.1 9.0 %copy-start = (bf16[1,4,2,640,640]{4,3,2,1,0:T(8,128)(2,1)S(1)}, bf16[1,4,2,640,640]{4,3,2,1,0:T(8,128)(2,1)}, u32[]{:S(2)}) copy-start(bf16[1,4,2,640,640]{4,3,2,1,0:T(8,128)(2,1)} %own.7) | copy-start | bytes 19660804
  5.4 6.6 %collective-permute-start.8 = (bf16[1,2,640,640]{3,2,1,0:T(8,128)(2,1)S(1)}, bf16[1,2,640,640]{3,2,1,0:T(8,128)(2,1)S(1)}, u32[]{:S(2)}, u32[]{:S(2)}) collective-permute-start(bf16[1,2,640,640]{3,2,1,0:T(8,128)(2,1)S(1)} %get-tuple-element.49), channel_id=1, source_target_pairs={{0,2},{1,3},{2,0},{3,1},{4,6},{5,7},{6,4},{7,5},{8,10},{9,11},{10,... | collective-permute-start | bytes 4915208 | tf_op jit(solution)/shard_map/ppermute | solution.py:476
  5.9 14.2 %collective-permute-start.7 = (bf16[1,2,640,640]{3,2,1,0:T(8,128)(2,1)S(1)}, bf16[1,2,640,640]{3,2,1,0:T(8,128)(2,1)S(1)}, u32[]{:S(2)}, u32[]{:S(2)}) collective-permute-start(bf16[1,2,640,640]{3,2,1,0:T(8,128)(2,1)S(1)} %get-tuple-element.50), channel_id=1, source_target_pairs={{0,2},{1,3},{2,0},{3,1},{4,6},{5,7},{6,4},{7,5},{8,10},{9,11},{10,... | collective-permute-start | bytes 4915208 | tf_op jit(solution)/shard_map/ppermute | solution.py:476
  6.0 6.0 %collective-permute-start.6 = (f32[1,2]{1,0:T(1,128)S(1)}, f32[1,2]{1,0:T(1,128)S(1)}, u32[]{:S(2)}, u32[]{:S(2)}) collective-permute-start(f32[1,2]{1,0:T(1,128)S(1)} %copy-done.2), channel_id=1, source_target_pairs={{0,2},{1,3},{2,0},{3,1},{4,6},{5,7},{6,4},{7,5},{8,10},{9,11},{10,... | collective-permute-start | bytes 32 | tf_op jit(solution)/shard_map/ppermute | solution.py:476
  6.4 5.6 %collective-permute-start.1 = (bf16[32,1280]{1,0:T(8,128)(2,1)S(1)}, bf16[32,1280]{1,0:T(8,128)(2,1)S(1)}, u32[]{:S(2)}, u32[]{:S(2)}) collective-permute-start(bf16[32,1280]{1,0:T(8,128)(2,1)S(1)} %get-tuple-element.30), channel_id=1, source_target_pairs={{0,4},{1,5},{2,6},{3,7},{4,0},{5,1},{6,2},{7,3},{8,12},{9,13},{10,... | collective-permute-start | bytes 245768 | tf_op jit(solution)/shard_map/ppermute | solution.py:476
  9.1 7.3 %collective-permute-start.2 = (bf16[32,1280]{1,0:T(8,128)(2,1)S(1)}, bf16[32,1280]{1,0:T(8,128)(2,1)S(1)}, u32[]{:S(2)}, u32[]{:S(2)}) collective-permute-start(bf16[32,1280]{1,0:T(8,128)(2,1)S(1)} %get-tuple-element.31), channel_id=1, source_target_pairs={{0,6},{1,7},{2,4},{3,5},{4,2},{5,3},{6,0},{7,1},{8,14},{9,15},{10,... | collective-permute-start | bytes 245768 | tf_op jit(solution)/shard_map/ppermute | solution.py:476
  14.0 25.1 %collective-permute-start.9 = (s16[2576,128]{1,0:T(8,128)(2,1)S(1)}, s16[2576,128]{1,0:T(8,128)(2,1)S(1)}, u32[]{:S(2)}, u32[]{:S(2)}) collective-permute-start(s16[2576,128]{1,0:T(8,128)(2,1)S(1)} %share.3.refs_0_), channel_id=1, source_target_pairs={{0,4},{1,5},{2,6},{3,7},{4,0},{5,1},{6,2},{7,3},{8,12},{9,13},{10,... | collective-permute-start | bytes 1978376 | tf_op jit(solution)/shard_map/ppermute | solution.py:476
  16.4 12.5 %collective-permute-start.3 = (bf16[128,1280]{1,0:T(8,128)(2,1)S(1)}, bf16[128,1280]{1,0:T(8,128)(2,1)S(1)}, u32[]{:S(2)}, u32[]{:S(2)}) collective-permute-start(bf16[128,1280]{1,0:T(8,128)(2,1)S(1)} %constant_dynamic-update-slice_fusion.refs_0_), channel_id=1, source_target_pairs={{0,24},{1,25},{2,26},{3,27},{4,28},{5,29},{6,30},{7,31},{8,16},{9,... | collective-permute-start | bytes 983048 | tf_op jit(solution)/shard_map/ppermute | solution.py:476
  24.4 14.7 %collective-permute-start.10 = (s16[1296,128]{1,0:T(8,128)(2,1)S(1)}, s16[1296,128]{1,0:T(8,128)(2,1)S(1)}, u32[]{:S(2)}, u32[]{:S(2)}) collective-permute-start(s16[1296,128]{1,0:T(8,128)(2,1)S(1)} %share.4.refs_0_), channel_id=1, source_target_pairs={{0,4},{1,5},{2,6},{3,7},{4,0},{5,1},{6,2},{7,3},{8,12},{9,13},{10,... | collective-permute-start | bytes 995336 | tf_op jit(solution)/shard_map/ppermute | solution.py:476
  24.8 15.1 %collective-permute-start.4 = (bf16[128,1280]{1,0:T(8,128)(2,1)S(1)}, bf16[128,1280]{1,0:T(8,128)(2,1)S(1)}, u32[]{:S(2)}, u32[]{:S(2)}) collective-permute-start(bf16[128,1280]{1,0:T(8,128)(2,1)S(1)} %constant_dynamic-update-slice_fusion.refs_0_), channel_id=1, source_target_pairs={{0,8},{1,9},{2,10},{3,11},{4,12},{5,13},{6,14},{7,15},{8,0},{9,1},... | collective-permute-start | bytes 983048 | tf_op jit(solution)/shard_map/ppermute | solution.py:476
  28.8 13.0 %collective-permute-start.5 = (bf16[128,1280]{1,0:T(8,128)(2,1)S(1)}, bf16[128,1280]{1,0:T(8,128)(2,1)S(1)}, u32[]{:S(2)}, u32[]{:S(2)}) collective-permute-start(bf16[128,1280]{1,0:T(8,128)(2,1)S(1)} %collective-permute-done.3.refs_1_), channel_id=1, source_target_pairs={{0,8},{1,9},{2,10},{3,11},{4,12},{5,13},{6,14},{7,15},{8,0},{9,1},... | collective-permute-start | bytes 983048 | tf_op jit(solution)/shard_map/ppermute | solution.py:476
  36.4 16.3 %collective-permute-start.11 = (s16[2576,128]{1,0:T(8,128)(2,1)S(1)}, s16[2576,128]{1,0:T(8,128)(2,1)S(1)}, u32[]{:S(2)}, u32[]{:S(2)}) collective-permute-start(s16[2576,128]{1,0:T(8,128)(2,1)S(1)} %share.5), channel_id=1, source_target_pairs={{0,4},{1,5},{2,6},{3,7},{4,0},{5,1},{6,2},{7,3},{8,12},{9,13},{10,... | collective-permute-start | bytes 1978376 | tf_op jit(solution)/shard_map/ppermute | solution.py:476
  44.1 9.8 %collective-permute-start.12 = (s16[784,128]{1,0:T(8,128)(2,1)S(1)}, s16[784,128]{1,0:T(8,128)(2,1)S(1)}, u32[]{:S(2)}, u32[]{:S(2)}) collective-permute-start(s16[784,128]{1,0:T(8,128)(2,1)S(1)} %get-tuple-element.34), channel_id=1, source_target_pairs={{0,24},{1,25},{2,26},{3,27},{4,28},{5,29},{6,30},{7,31},{8,16},{9,... | collective-permute-start | bytes 602120 | tf_op jit(solution)/shard_map/ppermute | solution.py:476
  47.7 15.4 %collective-permute-start.13 = (s16[784,128]{1,0:T(8,128)(2,1)S(1)}, s16[784,128]{1,0:T(8,128)(2,1)S(1)}, u32[]{:S(2)}, u32[]{:S(2)}) collective-permute-start(s16[784,128]{1,0:T(8,128)(2,1)S(1)} %get-tuple-element.36), channel_id=1, source_target_pairs={{0,8},{1,9},{2,10},{3,11},{4,12},{5,13},{6,14},{7,15},{8,0},{9,1},... | collective-permute-start | bytes 602120 | tf_op jit(solution)/shard_map/ppermute | solution.py:476
  47.7 19.7 %slice-start = ((s8[6553600]{0:T(1024)(128)(4,1)}), s8[4194304]{0:T(1024)(128)(4,1)S(1)}, s32[]{:S(2)}) async-start(s8[6553600]{0:T(1024)(128)(4,1)} %bitcast.9), calls=%async_computation | async-start | bytes 8388608
  47.7 19.7 %slice-start.1 = ((s8[6553600]{0:T(1024)(128)(4,1)}), s8[2359296]{0:T(1024)(128)(4,1)S(1)}, s32[]{:S(2)}) async-start(s8[6553600]{0:T(1024)(128)(4,1)} %bitcast.9), calls=%async_computation.1 | async-start | bytes 4718592
  47.7 16.3 %collective-permute-start.14 = (s16[784,128]{1,0:T(8,128)(2,1)S(1)}, s16[784,128]{1,0:T(8,128)(2,1)S(1)}, u32[]{:S(2)}, u32[]{:S(2)}) collective-permute-start(s16[784,128]{1,0:T(8,128)(2,1)S(1)} %get-tuple-element.37), channel_id=1, source_target_pairs={{0,16},{1,17},{2,18},{3,19},{4,20},{5,21},{6,22},{7,23},{8,24},{9,... | collective-permute-start | bytes 602120 | tf_op jit(solution)/shard_map/ppermute | solution.py:476
  55.5 10.9 %collective-permute-start.15 = (s16[528,128]{1,0:T(8,128)(2,1)S(1)}, s16[528,128]{1,0:T(8,128)(2,1)S(1)}, u32[]{:S(2)}, u32[]{:S(2)}) collective-permute-start(s16[528,128]{1,0:T(8,128)(2,1)S(1)} %get-tuple-element.39), channel_id=1, source_target_pairs={{0,8},{1,9},{2,10},{3,11},{4,12},{5,13},{6,14},{7,15},{8,0},{9,1},... | collective-permute-start | bytes 405512 | tf_op jit(solution)/shard_map/ppermute | solution.py:476
  63.0 6.5 %collective-permute-start.17 = (s16[528,128]{1,0:T(8,128)(2,1)S(1)}, s16[528,128]{1,0:T(8,128)(2,1)S(1)}, u32[]{:S(2)}, u32[]{:S(2)}) collective-permute-start(s16[528,128]{1,0:T(8,128)(2,1)S(1)} %get-tuple-element.40), channel_id=1, source_target_pairs={{0,8},{1,9},{2,10},{3,11},{4,12},{5,13},{6,14},{7,15},{8,0},{9,1},... | collective-permute-start | bytes 405512 | tf_op jit(solution)/shard_map/ppermute | solution.py:476
  66.5 7.0 %collective-permute-start.16 = (s16[528,128]{1,0:T(8,128)(2,1)S(1)}, s16[528,128]{1,0:T(8,128)(2,1)S(1)}, u32[]{:S(2)}, u32[]{:S(2)}) collective-permute-start(s16[528,128]{1,0:T(8,128)(2,1)S(1)} %fold.1), channel_id=1, source_target_pairs={{0,24},{1,25},{2,26},{3,27},{4,28},{5,29},{6,30},{7,31},{8,16},{9,... | collective-permute-start | bytes 405512 | tf_op jit(solution)/shard_map/ppermute | solution.py:476
  68.2 18.2 %copy-start.3 = (s32[8]{0:T(128)S(1)}, s32[8]{0:T(128)}, u32[]{:S(2)}) copy-start(s32[8]{0:T(128)} %column.1) | copy-start | bytes 100
  75.6 6.0 %collective-permute-start.18 = (s16[336,128]{1,0:T(8,128)(2,1)S(1)}, s16[336,128]{1,0:T(8,128)(2,1)S(1)}, u32[]{:S(2)}, u32[]{:S(2)}) collective-permute-start(s16[336,128]{1,0:T(8,128)(2,1)S(1)} %get-tuple-element.41), channel_id=1, source_target_pairs={{0,5},{1,4},{2,7},{3,6},{4,1},{5,0},{6,3},{7,2},{8,13},{9,12},{10,... | collective-permute-start | bytes 258056 | tf_op jit(solution)/shard_map/ppermute | solution.py:476
  76.7 5.6 %collective-permute-start.19 = (s16[336,128]{1,0:T(8,128)(2,1)S(1)}, s16[336,128]{1,0:T(8,128)(2,1)S(1)}, u32[]{:S(2)}, u32[]{:S(2)}) collective-permute-start(s16[336,128]{1,0:T(8,128)(2,1)S(1)} %get-tuple-element.42), channel_id=1, source_target_pairs={{0,7},{1,6},{2,5},{3,4},{4,3},{5,2},{6,1},{7,0},{8,15},{9,14},{10,... | collective-permute-start | bytes 258056 | tf_op jit(solution)/shard_map/ppermute | solution.py:476
  76.7 6.6 %collective-permute-start.20 = (s16[336,128]{1,0:T(8,128)(2,1)S(1)}, s16[336,128]{1,0:T(8,128)(2,1)S(1)}, u32[]{:S(2)}, u32[]{:S(2)}) collective-permute-start(s16[336,128]{1,0:T(8,128)(2,1)S(1)} %get-tuple-element.43), channel_id=1, source_target_pairs={{0,1},{1,0},{2,3},{3,2},{4,5},{5,4},{6,7},{7,6},{8,9},{9,8},{10,11... | collective-permute-start | bytes 258056 | tf_op jit(solution)/shard_map/ppermute | solution.py:476
  77.3 7.9 %collective-permute-start.21 = (s16[336,128]{1,0:T(8,128)(2,1)S(1)}, s16[336,128]{1,0:T(8,128)(2,1)S(1)}, u32[]{:S(2)}, u32[]{:S(2)}) collective-permute-start(s16[336,128]{1,0:T(8,128)(2,1)S(1)} %get-tuple-element.44), channel_id=1, source_target_pairs={{0,3},{1,2},{2,1},{3,0},{4,7},{5,6},{6,5},{7,4},{8,11},{9,10},{10,... | collective-permute-start | bytes 258056 | tf_op jit(solution)/shard_map/ppermute | solution.py:476
  80.1 5.1 %collective-permute-start.22 = (s16[336,128]{1,0:T(8,128)(2,1)S(1)}, s16[336,128]{1,0:T(8,128)(2,1)S(1)}, u32[]{:S(2)}, u32[]{:S(2)}) collective-permute-start(s16[336,128]{1,0:T(8,128)(2,1)S(1)} %get-tuple-element.45), channel_id=1, source_target_pairs={{0,4},{1,5},{2,6},{3,7},{4,0},{5,1},{6,2},{7,3},{8,12},{9,13},{10,... | collective-permute-start | bytes 258056 | tf_op jit(solution)/shard_map/ppermute | solution.py:476
  81.6 4.8 %collective-permute-start.23 = (s16[336,128]{1,0:T(8,128)(2,1)S(1)}, s16[336,128]{1,0:T(8,128)(2,1)S(1)}, u32[]{:S(2)}, u32[]{:S(2)}) collective-permute-start(s16[336,128]{1,0:T(8,128)(2,1)S(1)} %get-tuple-element.46), channel_id=1, source_target_pairs={{0,6},{1,7},{2,4},{3,5},{4,2},{5,3},{6,0},{7,1},{8,14},{9,15},{10,... | collective-permute-start | bytes 258056 | tf_op jit(solution)/shard_map/ppermute | solution.py:476
  82.3 4.2 %collective-permute-start.24 = (s16[336,128]{1,0:T(8,128)(2,1)S(1)}, s16[336,128]{1,0:T(8,128)(2,1)S(1)}, u32[]{:S(2)}, u32[]{:S(2)}) collective-permute-start(s16[336,128]{1,0:T(8,128)(2,1)S(1)} %get-tuple-element.47), channel_id=1, source_target_pairs={{0,2},{1,3},{2,0},{3,1},{4,6},{5,7},{6,4},{7,5},{8,10},{9,11},{10,... | collective-permute-start | bytes 258056 | tf_op jit(solution)/shard_map/ppermute | solution.py:476

commit v8 on v7

--- a/solution.py
+++ b/solution.py
@@ -166,7 +166,7 @@
 
 
 def build_kernel(first, held, own, *refs):
-    got, op = refs[: len(held)], refs[len(held)]
+    got, op = refs[: len(held)], refs[-1]
     size = own.shape[2]
     sources = [(ref, i) for ref, n in zip(got, held) for i in range(n)]
     for t, (ref, i) in enumerate(sources):
@@ -184,20 +184,21 @@
             op[t, level, size:, LANES:] = r
 
 
-def build(own, got, first, held):
+def build(own, got, first, held, after):
     size = own.shape[2]
     out = jax.ShapeDtypeStruct((sum(held), 2, 2 * size, 2 * LANES), BF16)
     return pl.pallas_call(
         functools.partial(build_kernel, first, held),
         out_shape=out,
-        in_specs=[whole(x.shape) for x in (own, *got)],
+        in_specs=[whole(x.shape) for x in (own, *got)]
+        + [pl.BlockSpec(memory_space=pl.ANY)] * len(after),
         out_specs=whole(out.shape),
         compiler_params=params(),
         cost_estimate=pl.CostEstimate(
             flops=8 * out.size, bytes_accessed=4 * out.size, transcendentals=0
         ),
         name="build",
-    )(own, *got)
+    )(own, *got, *after)
 
 
 def product_kernel(pieces, kept, after, *refs):
@@ -459,6 +460,25 @@
     )(where, *[state] * 4)
 
 
+def join_kernel(*refs):
+    *parts, _, out = refs
+    rows = parts[0].shape[0]
+    for i, part in enumerate(parts):
+        out[i * rows : (i + 1) * rows, :] = part[...]
+
+
+def join(parts, after):
+    rows, width = parts[0].shape
+    return pl.pallas_call(
+        join_kernel,
+        out_shape=jax.ShapeDtypeStruct((len(parts) * rows, width), parts[0].dtype),
+        in_specs=[whole(part.shape) for part in parts] + [pl.BlockSpec(memory_space=pl.ANY)],
+        out_specs=whole(None),
+        compiler_params=params(),
+        name="join",
+    )(*parts, after)
+
+
 def shards(mesh, spectral_state, inverse, term_weights, legendre, slot_column):
     terms, waves = mesh.shape["term"], mesh.shape["wave"]
     slots, cols, width = spectral_state.shape
@@ -481,37 +501,35 @@
     states = pick(where, spectral_state)
     received = [swap(states[bits], bits) for bits in range(1, 4)]
     turned, received[0] = lax.optimization_barrier((place_of, received[0]))
-    block = jnp.concatenate([states[0]] + received, axis=0)
-    steps = [3, 1] + list(range(4, outer)) + [2]
-    parts = [block] + [swap(block, q * 4) for q in steps[:-1]]
-    parts.append(swap(parts[1], 1 * 4))
-
     w_got = swap(term_weights, 1)
     far, own = (
         swap(lax.dynamic_index_in_dim(inverse, turned ^ bits, 1, keepdims=False), 1)
         for bits in (3, 1)
     )
-    mine = operator(where, term_weights, w_got, inverse, own)
-    groups = ((2, 1), (2,))
-    shares, near, got = [], [], []
-    first = 0
-    for group in groups:
-        start, messages = first, []
-        for n in group:
-            after = () if not shares else (shares[-1], mine)
-            shares.append(
-                share(where, term_weights, w_got, inverse, far, first, n, after)
-            )
-            messages.append(swap(shares[-1], 2))
-            first += n
-        after = [near[-1], got[-1][0]] if near else []
-        op = build(mine, messages, start, group)
-        if group is not groups[-1]:
-            made = product(parts, op, (0,), after)
-            sends = made[1:]
-        else:
-            made = product(parts, op, (0, 1), after)
-            sends = [fold(made[1], swap(made[-1], 1 * 4), got[-1][1:] if got else []), *made[2:-1]]
+    last = max(1, 2 * tiles // 5)
+    counts = [n for n in (last, tiles - 2 * last, last) if n]
+    shares, messages = [], []
+    for at, n in enumerate(counts):
+        first = sum(counts[:at])
+        after = () if not shares else (shares[-1], mine)[: at]
+        shares.append(share(where, term_weights, w_got, inverse, far, first, n, after))
+        messages.append(swap(shares[-1], 2))
+        if at == 0:
+            mine = operator(where, term_weights, w_got, inverse, own)
+            block = join([states[0]] + received, shares[0])
+            steps = [3, 1] + list(range(4, outer)) + [2]
+            parts = [block] + [swap(block, q * 4) for q in steps[:-1]]
+            parts.append(swap(parts[1], 1 * 4))
+    near, got = [], []
+    ends = [0, len(counts) - 1, len(counts)]
+    for start, end in zip(ends, ends[1:]):
+        after = [near[-1], got[-1][1]] if near else []
+        held = counts[start:end]
+        folded = sends[:1] if near else []
+        op = build(mine, messages[start:end], sum(counts[:start]), held, folded)
+        made = product(parts, op, (0, 1), after)
+        relayed = swap(made[-1], 1 * 4)
+        sends = [fold(made[1], relayed, got[-1] if got else []), *made[2:-1]]
         near.append(made[0])
         got.append([swap(send, q * 4) for send, q in zip(sends, steps)])
     make = synthesis if legendre.shape[2] // waves % LANES == 0 else plain_synthesis

time: 88.3 us -> 86.1 us (0.975)
  starting transfers between devices: 35.3 us -> 33.4 us
    ppermute x25, starting transfers between devices: 35.3 us -> 33.4 us  [swap(): return lax.ppermute(x, ('term', 'wave'), pairs)]
  transfers between devices with their start and end apart: 25 -> 25, of which waited for: 15 -> 11; matrix products, arithmetic and copies ran while one was open for 0% -> 0% of each run, Pallas kernels for 16% -> 17%
where the time goes in v8:
time: 86.1 us; the launch traced here: 86 us
  starting transfers between devices  33.4 us (39%)
  waiting for transfers between devices  30.3 us (35%)
  Pallas kernels  18.7 us (22%)
  local copies, waits for them, and re-layouts  3.44 us (4%)
    ppermute x25, starting transfers between devices, swap(): return lax.ppermute(x, ('term', 'wave'), pairs)  33.4 us
    ppermute x25, waiting for transfers between devices, swap(): return lax.ppermute(x, ('term', 'wave'), pairs)  30.3 us
    pallas_call x3, Pallas kernels, share(): pl.pallas_call(functools.partial(share_kernel, len(after)), out_shape=out...  5.27 us
    pallas_call x2, Pallas kernels, product(): pl.pallas_call(functools.partial(product_kernel, count, kept, len(after))...  3.86 us
    pallas_call x1, Pallas kernels, operator(): pl.pallas_call(own_kernel, out_shape=jax.ShapeDtypeStruct((tiles, 2, size...  2.91 us
    squeeze x1, local copies, waits for them, and re-layouts, shards(): lax.dynamic_index_in_dim(inverse, turned ^ bits, 1, keepdims=False)  2.36 us
    pallas_call x1, Pallas kernels, synthesis(): pl.pallas_call(functools.partial(synthesis_kernel, bands, [len(parts) for...  2.1 us
  transfers between devices with their start and end apart: 25, of which 11 were waited for; matrix products, arithmetic and copies ran while one was open for 0% of the time, Pallas kernels for 17%

profile of v8, /device:TPU:0, one launch (start us, length us, event | category | flops | bytes accessed | tf_op | source)
XLA Modules:
  0.0 86.0 jit_solution(16492709598204137055)
XLA Ops:
  0.0 0.1 stack.23.where
  0.1 1.0 %copy-done.1 = bf16[4,32,1280]{2,1,0:T(8,128)(2,1)S(1)} copy-done((bf16[4,32,1280]{2,1,0:T(8,128)(2,1)S(1)}, bf16[4,32,1280]{2,1,0:T(8,128)(2,1)}, u32[]{:S(2)}) %copy-start.1) | copy-done | bytes 327704
  1.1 0.6 pick.1
  1.6 0.5 collective-permute-start
  2.2 0.9 %collective-permute-done.refs_1_ = bf16[32,1280]{1,0:T(8,128)(2,1)S(1)} collective-permute-done((bf16[32,1280]{1,0:T(8,128)(2,1)S(1)}, bf16[32,1280]{1,0:T(8,128)(2,1)S(1)}, u32[]{:S(2)}, u32[]{:S(2)}) %collective-permute-start) | collective-permute-done | bytes 81952 | tf_op jit(solution)/shard_map/ppermute | solution.py:496
  3.1 2.4 %dynamic-slice_bitcast_fusion = (bf16[1,2,640,640]{3,2,1,0:T(8,128)(2,1)S(1)}, bf16[1,2,640,640]{3,2,1,0:T(8,128)(2,1)S(1)}) fusion(bf16[1,4,2,640,640]{4,3,2,1,0:T(8,128)(2,1)} %own.7, s32[]{:T(128)S(6)} %select_n.16, s32[]{:T(128)S(6)} %select_n.15), kind=kLoop, calls=%fused_computation | loop fusion | bytes 6553608 | tf_op jit(solution)/shard_map/jit(dynamic_index_in_dim)/squeeze | solution.py:506
  5.4 0.4 collective-permute-start.4
  5.9 0.2 collective-permute-start.8
  6.0 2.9 %collective-permute-start.1 = (bf16[32,1280]{1,0:T(8,128)(2,1)S(1)}, bf16[32,1280]{1,0:T(8,128)(2,1)S(1)}, u32[]{:S(2)}, u32[]{:S(2)}) collective-permute-start(bf16[32,1280]{1,0:T(8,128)(2,1)S(1)} %get-tuple-element.30), channel_id=1, source_target_pairs={{0,4},{1,5},{2,6},{3,7},{4,0},{5,1},{6,2},{7,3},{8,12},{9,13},{10,... | collective-permute-start | bytes 245768 | tf_op jit(solution)/shard_map/ppermute | solution.py:496
  8.9 0.0 collective-permute-start.2
  8.9 0.1 collective-permute-start.3
  9.0 2.3 %collective-permute-done.3.w_got = f32[1,2]{1,0:T(1,128)S(1)} collective-permute-done((f32[1,2]{1,0:T(1,128)S(1)}, f32[1,2]{1,0:T(1,128)S(1)}, u32[]{:S(2)}, u32[]{:S(2)}) %collective-permute-start.3) | collective-permute-done | bytes 40 | tf_op jit(solution)/shard_map/ppermute | solution.py:496
  11.4 0.0 collective-permute-done.4.got
  11.4 1.9 %share.3.refs_4_.refs_0_ = s16[2576,128]{1,0:T(8,128)(2,1)S(1)} custom-call(s32[5]{0:T(128)S(1)} %stack.23.where, f32[1,2]{1,0:T(1,128)S(1)} %copy-done.2, f32[1,2]{1,0:T(1,128)S(1)} %collective-permute-done.3.w_got, bf16[1,4,2,640,640]{4,3,2,1,0:T(8,128)(2,1)S(1)} %copy-done, bf16[1,2,640,640]{3,2,1,0:T(8,128)(2,1)S(1)} %collective-permute-done.4.got), custom_call_target="tpu_custom_call" | custom-call | flops 5242880 | bytes 2621440 | tf_op jit(solution)/shard_map/share/pallas_call | solution.py:91
  13.3 2.9 %collective-permute-start.9 = (s16[2576,128]{1,0:T(8,128)(2,1)S(1)}, s16[2576,128]{1,0:T(8,128)(2,1)S(1)}, u32[]{:S(2)}, u32[]{:S(2)}) collective-permute-start(s16[2576,128]{1,0:T(8,128)(2,1)S(1)} %share.3.refs_4_.refs_0_), channel_id=1, source_target_pairs={{0,4},{1,5},{2,6},{3,7},{4,0},{5,1},{6,2},{7,3},{8,12},{9,13},{10,... | collective-permute-start | bytes 1978376 | tf_op jit(solution)/shard_map/ppermute | solution.py:496
  16.2 0.0 collective-permute-done.1.refs_2_
  16.2 0.0 collective-permute-done.2.refs_3_
  16.3 3.7 %collective-permute-start.5 = (bf16[128,1280]{1,0:T(8,128)(2,1)S(1)}, bf16[128,1280]{1,0:T(8,128)(2,1)S(1)}, u32[]{:S(2)}, u32[]{:S(2)}) collective-permute-start(bf16[128,1280]{1,0:T(8,128)(2,1)S(1)} %join.1.refs_0_), channel_id=1, source_target_pairs={{0,24},{1,25},{2,26},{3,27},{4,28},{5,29},{6,30},{7,31},{8,16},{9,... | collective-permute-start | bytes 983048 | tf_op jit(solution)/shard_map/ppermute | solution.py:496
  19.9 1.4 %share.4.refs_0_ = s16[1296,128]{1,0:T(8,128)(2,1)S(1)} custom-call(s32[5]{0:T(128)S(1)} %stack.23.where, f32[1,2]{1,0:T(1,128)S(1)} %copy-done.2, f32[1,2]{1,0:T(1,128)S(1)} %collective-permute-done.3.w_got, bf16[1,4,2,640,640]{4,3,2,1,0:T(8,128)(2,1)S(1)} %copy-done, bf16[1,2,640,640]{3,2,1,0:T(8,128)(2,1)S(1)} %collective-permute-done.4.got, ...), custom_call_target="tpu_custom_call" | custom-call | flops 2621440 | bytes 1310720 | tf_op jit(solution)/shard_map/share/pallas_call | solution.py:91
  21.3 0.6 collective-permute-start.10
  21.9 0.0 collective-permute-start.6
  21.9 6.9 %collective-permute-done.5.refs_1_ = bf16[128,1280]{1,0:T(8,128)(2,1)S(1)} collective-permute-done((bf16[128,1280]{1,0:T(8,128)(2,1)S(1)}, bf16[128,1280]{1,0:T(8,128)(2,1)S(1)}, u32[]{:S(2)}, u32[]{:S(2)}) %collective-permute-start.5) | collective-permute-done | bytes 327712 | tf_op jit(solution)/shard_map/ppermute | solution.py:496
  28.8 5.7 %collective-permute-start.7 = (bf16[128,1280]{1,0:T(8,128)(2,1)S(1)}, bf16[128,1280]{1,0:T(8,128)(2,1)S(1)}, u32[]{:S(2)}, u32[]{:S(2)}) collective-permute-start(bf16[128,1280]{1,0:T(8,128)(2,1)S(1)} %collective-permute-done.5.refs_1_), channel_id=1, source_target_pairs={{0,8},{1,9},{2,10},{3,11},{4,12},{5,13},{6,14},{7,15},{8,0},{9,1},... | collective-permute-start | bytes 983048 | tf_op jit(solution)/shard_map/ppermute | solution.py:496
  34.4 0.0 collective-permute-done.8.got
  34.4 2.9 %operator.1.own.refs_1_ = f32[5,2,640,128]{3,2,1,0:T(8,128)S(1)} custom-call(s32[5]{0:T(128)S(1)} %stack.23.where, f32[1,2]{1,0:T(1,128)S(1)} %copy-done.2, f32[1,2]{1,0:T(1,128)S(1)} %collective-permute-done.3.w_got, bf16[1,4,2,640,640]{4,3,2,1,0:T(8,128)(2,1)S(1)} %copy-done, bf16[1,2,640,640]{3,2,1,0:T(8,128)(2,1)S(1)} %collective-permute-done.8.got), custom_call_target="tpu_custom_call" | custom-call | flops 13107200 | bytes 6553600 | tf_op jit(solution)/shard_map/operator/pallas_call | solution.py:126
  37.3 1.9 %share.5 = s16[2576,128]{1,0:T(8,128)(2,1)S(1)} custom-call(s32[5]{0:T(128)S(1)} %stack.23.where, f32[1,2]{1,0:T(1,128)S(1)} %copy-done.2, f32[1,2]{1,0:T(1,128)S(1)} %collective-permute-done.3.w_got, bf16[1,4,2,640,640]{4,3,2,1,0:T(8,128)(2,1)S(1)} %copy-done, bf16[1,2,640,640]{3,2,1,0:T(8,128)(2,1)S(1)} %collective-permute-done.4.got, ...), custom_call_target="tpu_custom_call" | custom-call | flops 5242880 | bytes 2621440 | tf_op jit(solution)/shard_map/share/pallas_call | solution.py:91
  39.3 0.6 collective-permute-start.11
  39.9 0.0 collective-permute-done.10.refs_1_
  39.9 0.8 build.2.refs_4_
  40.7 1.2 %collective-permute-done.7.refs_3_ = bf16[128,1280]{1,0:T(8,128)(2,1)S(1)} collective-permute-done((bf16[128,1280]{1,0:T(8,128)(2,1)S(1)}, bf16[128,1280]{1,0:T(8,128)(2,1)S(1)}, u32[]{:S(2)}, u32[]{:S(2)}) %collective-permute-start.7) | collective-permute-done | bytes 327712 | tf_op jit(solution)/shard_map/ppermute | solution.py:496
  41.8 2.3 %product.2 = (f32[3,128,256]{2,1,0:T(8,128)S(1)}, f32[3,128,256]{2,1,0:T(8,128)S(1)}, s16[784,128]{1,0:T(8,128)(2,1)S(1)}, s16[784,128]{1,0:T(8,128)(2,1)S(1)}) custom-call(bf16[128,1280]{1,0:T(8,128)(2,1)S(1)} %join.1.refs_0_, bf16[128,1280]{1,0:T(8,128)(2,1)S(1)} %collective-permute-done.5.refs_1_, bf16[128,1280]{1,0:T(8,128)(2,1)S(1)} %collective-permute-done.6.refs_2_, ...), custom_call_target="tpu_custom_call" | custom-call | flops 2013265920 | bytes 5242880 | tf_op jit(solution)/shard_map/product/pallas_call | solution.py:237
  44.1 1.8 %collective-permute-start.12 = (s16[784,128]{1,0:T(8,128)(2,1)S(1)}, s16[784,128]{1,0:T(8,128)(2,1)S(1)}, u32[]{:S(2)}, u32[]{:S(2)}) collective-permute-start(s16[784,128]{1,0:T(8,128)(2,1)S(1)} %get-tuple-element.35), channel_id=1, source_target_pairs={{0,8},{1,9},{2,10},{3,11},{4,12},{5,13},{6,14},{7,15},{8,0},{9,1},... | collective-permute-start | bytes 602120 | tf_op jit(solution)/shard_map/ppermute | solution.py:496
  45.9 0.3 collective-permute-start.13
  46.2 5.9 %collective-permute-done.12.got = s16[784,128]{1,0:T(8,128)(2,1)S(1)} collective-permute-done((s16[784,128]{1,0:T(8,128)(2,1)S(1)}, s16[784,128]{1,0:T(8,128)(2,1)S(1)}, u32[]{:S(2)}, u32[]{:S(2)}) %collective-permute-start.12) | collective-permute-done | bytes 200736 | tf_op jit(solution)/shard_map/ppermute | solution.py:496
  52.1 0.1 fold.2.refs_1_
  52.2 0.0 slice-start.1
  52.3 3.4 %collective-permute-start.14 = (s16[784,128]{1,0:T(8,128)(2,1)S(1)}, s16[784,128]{1,0:T(8,128)(2,1)S(1)}, u32[]{:S(2)}, u32[]{:S(2)}) collective-permute-start(s16[784,128]{1,0:T(8,128)(2,1)S(1)} %fold.2.refs_1_), channel_id=1, source_target_pairs={{0,24},{1,25},{2,26},{3,27},{4,28},{5,29},{6,30},{7,31},{8,16},{9,... | collective-permute-start | bytes 602120 | tf_op jit(solution)/shard_map/ppermute | solution.py:496
  55.6 0.0 collective-permute-done.11.refs_0_
  55.6 0.5 build.3.refs_4_
  56.2 1.6 %product.3 = (f32[2,128,256]{2,1,0:T(8,128)S(1)}, f32[2,128,256]{2,1,0:T(8,128)S(1)}, s16[528,128]{1,0:T(8,128)(2,1)S(1)}, s16[528,128]{1,0:T(8,128)(2,1)S(1)}) custom-call(bf16[128,1280]{1,0:T(8,128)(2,1)S(1)} %join.1.refs_0_, bf16[128,1280]{1,0:T(8,128)(2,1)S(1)} %collective-permute-done.5.refs_1_, bf16[128,1280]{1,0:T(8,128)(2,1)S(1)} %collective-permute-done.6.refs_2_, ...), custom_call_target="tpu_custom_call" | custom-call | flops 1342177280 | bytes 3932160 | tf_op jit(solution)/shard_map/product/pallas_call | solution.py:237
  57.8 0.1 collective-permute-start.15
  57.9 2.0 %collective-permute-start.17 = (s16[528,128]{1,0:T(8,128)(2,1)S(1)}, s16[528,128]{1,0:T(8,128)(2,1)S(1)}, u32[]{:S(2)}, u32[]{:S(2)}) collective-permute-start(s16[528,128]{1,0:T(8,128)(2,1)S(1)} %get-tuple-element.40), channel_id=1, source_target_pairs={{0,8},{1,9},{2,10},{3,11},{4,12},{5,13},{6,14},{7,15},{8,0},{9,1},... | collective-permute-start | bytes 405512 | tf_op jit(solution)/shard_map/ppermute | solution.py:496
  59.9 4.9 %collective-permute-done.15.got = s16[528,128]{1,0:T(8,128)(2,1)S(1)} collective-permute-done((s16[528,128]{1,0:T(8,128)(2,1)S(1)}, s16[528,128]{1,0:T(8,128)(2,1)S(1)}, u32[]{:S(2)}, u32[]{:S(2)}) %collective-permute-start.15) | collective-permute-done | bytes 135200 | tf_op jit(solution)/shard_map/ppermute | solution.py:496
  64.8 0.1 fold.3
  64.9 3.1 %collective-permute-start.16 = (s16[528,128]{1,0:T(8,128)(2,1)S(1)}, s16[528,128]{1,0:T(8,128)(2,1)S(1)}, u32[]{:S(2)}, u32[]{:S(2)}) collective-permute-start(s16[528,128]{1,0:T(8,128)(2,1)S(1)} %fold.3), channel_id=1, source_target_pairs={{0,24},{1,25},{2,26},{3,27},{4,28},{5,29},{6,30},{7,31},{8,16},{9,... | collective-permute-start | bytes 405512 | tf_op jit(solution)/shard_map/ppermute | solution.py:496
  68.0 0.8 table.1.refs_6_
  68.7 0.0 copy-start.3
  68.7 0.0 collective-permute-done.17.refs_5_
  68.8 3.1 %collective-permute-done.16.refs_4_ = s16[528,128]{1,0:T(8,128)(2,1)S(1)} collective-permute-done((s16[528,128]{1,0:T(8,128)(2,1)S(1)}, s16[528,128]{1,0:T(8,128)(2,1)S(1)}, u32[]{:S(2)}, u32[]{:S(2)}) %collective-permute-start.16) | collective-permute-done | bytes 135200 | tf_op jit(solution)/shard_map/ppermute | solution.py:496
  71.9 2.1 %synthesis.1 = (f32[2,32,640]{2,1,0:T(8,128)S(1)}, s16[336,128]{1,0:T(8,128)(2,1)S(1)}, s16[336,128]{1,0:T(8,128)(2,1)S(1)}, s16[336,128]{1,0:T(8,128)(2,1)S(1)}...) custom-call(s32[5]{0:T(128)S(1)} %stack.23.where, ...), custom_call_target="tpu_custom_call" | custom-call | flops 838860800 | bytes 2949120 | tf_op jit(solution)/shard_map/synthesis/pallas_call | solution.py:356
  74.0 1.5 %collective-permute-start.18 = (s16[336,128]{1,0:T(8,128)(2,1)S(1)}, s16[336,128]{1,0:T(8,128)(2,1)S(1)}, u32[]{:S(2)}, u32[]{:S(2)}) collective-permute-start(s16[336,128]{1,0:T(8,128)(2,1)S(1)} %get-tuple-element.41), channel_id=1, source_target_pairs={{0,5},{1,4},{2,7},{3,6},{4,1},{5,0},{6,3},{7,2},{8,13},{9,12},{10,... | collective-permute-start | bytes 258056 | tf_op jit(solution)/shard_map/ppermute | solution.py:496
  75.5 0.5 collective-permute-start.20
  76.0 2.4 %collective-permute-start.21 = (s16[336,128]{1,0:T(8,128)(2,1)S(1)}, s16[336,128]{1,0:T(8,128)(2,1)S(1)}, u32[]{:S(2)}, u32[]{:S(2)}) collective-permute-start(s16[336,128]{1,0:T(8,128)(2,1)S(1)} %get-tuple-element.44), channel_id=1, source_target_pairs={{0,3},{1,2},{2,1},{3,0},{4,7},{5,6},{6,5},{7,4},{8,11},{9,10},{10,... | collective-permute-start | bytes 258056 | tf_op jit(solution)/shard_map/ppermute | solution.py:496
  78.4 0.5 collective-permute-start.22
  78.9 0.5 collective-permute-done.18.refs_0_
  79.5 0.2 collective-permute-start.23
  79.6 1.6 %collective-permute-done.19.refs_1_ = s16[336,128]{1,0:T(8,128)(2,1)S(1)} collective-permute-done((s16[336,128]{1,0:T(8,128)(2,1)S(1)}, s16[336,128]{1,0:T(8,128)(2,1)S(1)}, u32[]{:S(2)}, u32[]{:S(2)}) %collective-permute-start.19) | collective-permute-done | bytes 86048 | tf_op jit(solution)/shard_map/ppermute | solution.py:496
  81.2 0.1 collective-permute-start.24
  81.3 0.0 collective-permute-done.20.refs_2_
  81.3 2.7 %collective-permute-done.21.refs_3_ = s16[336,128]{1,0:T(8,128)(2,1)S(1)} collective-permute-done((s16[336,128]{1,0:T(8,128)(2,1)S(1)}, s16[336,128]{1,0:T(8,128)(2,1)S(1)}, u32[]{:S(2)}, u32[]{:S(2)}) %collective-permute-start.21) | collective-permute-done | bytes 86048 | tf_op jit(solution)/shard_map/ppermute | solution.py:496
  84.0 0.0 collective-permute-done.22.refs_4_
  84.0 0.3 collective-permute-done.23.refs_5_
  84.3 0.0 collective-permute-done.24.refs_6_
  84.3 1.7 %place.1 = f32[8,2,32,640]{3,2,1,0:T(8,128)} custom-call(s32[5]{0:T(128)S(1)} %stack.23.where, s32[8]{0:T(128)S(1)} %copy-done.3, s16[336,128]{1,0:T(8,128)(2,1)S(1)} %collective-permute-done.18.refs_0_, s16[336,128]{1,0:T(8,128)(2,1)S(1)} %collective-permute-done.19.refs_1_, s16[336,128]{1,0:T(8,128)(2,1)S(1)} %collective-permute-done.20.refs_2_, ...), custom_call_target="tpu_custom_call" | custom-call | tf_op jit(solution)/shard_map/place/pallas_call | solution.py:429
  (16 shorter events, 0.1 us)
Async XLA Ops:
  0.1 1.0 %copy-start.1 = (bf16[4,32,1280]{2,1,0:T(8,128)(2,1)S(1)}, bf16[4,32,1280]{2,1,0:T(8,128)(2,1)}, u32[]{:S(2)}) copy-start(bf16[4,32,1280]{2,1,0:T(8,128)(2,1)} %refs_3_.1) | copy-start | bytes 983044
  1.6 1.4 %collective-permute-start = (bf16[32,1280]{1,0:T(8,128)(2,1)S(1)}, bf16[32,1280]{1,0:T(8,128)(2,1)S(1)}, u32[]{:S(2)}, u32[]{:S(2)}) collective-permute-start(bf16[32,1280]{1,0:T(8,128)(2,1)S(1)} %get-tuple-element.28), channel_id=1, source_target_pairs={{0,2},{1,3},{2,0},{3,1},{4,6},{5,7},{6,4},{7,5},{8,10},{9,11},{10,... | collective-permute-start | bytes 245768 | tf_op jit(solution)/shard_map/ppermute | solution.py:496
  3.1 5.8 %copy-start.2 = (f32[1,2]{1,0:T(1,128)S(1)}, f32[1,2]{1,0:T(1,128)}, u32[]{:S(2)}) copy-start(f32[1,2]{1,0:T(1,128)} %w_own.7) | copy-start | bytes 28
  3.1 8.3 %copy-start = (bf16[1,4,2,640,640]{4,3,2,1,0:T(8,128)(2,1)S(1)}, bf16[1,4,2,640,640]{4,3,2,1,0:T(8,128)(2,1)}, u32[]{:S(2)}) copy-start(bf16[1,4,2,640,640]{4,3,2,1,0:T(8,128)(2,1)} %own.7) | copy-start | bytes 19660804
  5.4 5.9 %collective-permute-start.4 = (bf16[1,2,640,640]{3,2,1,0:T(8,128)(2,1)S(1)}, bf16[1,2,640,640]{3,2,1,0:T(8,128)(2,1)S(1)}, u32[]{:S(2)}, u32[]{:S(2)}) collective-permute-start(bf16[1,2,640,640]{3,2,1,0:T(8,128)(2,1)S(1)} %get-tuple-element.50), channel_id=1, source_target_pairs={{0,2},{1,3},{2,0},{3,1},{4,6},{5,7},{6,4},{7,5},{8,10},{9,11},{10,... | collective-permute-start | bytes 4915208 | tf_op jit(solution)/shard_map/ppermute | solution.py:496
  5.9 28.6 %collective-permute-start.8 = (bf16[1,2,640,640]{3,2,1,0:T(8,128)(2,1)S(1)}, bf16[1,2,640,640]{3,2,1,0:T(8,128)(2,1)S(1)}, u32[]{:S(2)}, u32[]{:S(2)}) collective-permute-start(bf16[1,2,640,640]{3,2,1,0:T(8,128)(2,1)S(1)} %get-tuple-element.49), channel_id=1, source_target_pairs={{0,2},{1,3},{2,0},{3,1},{4,6},{5,7},{6,4},{7,5},{8,10},{9,11},{10,... | collective-permute-start | bytes 4915208 | tf_op jit(solution)/shard_map/ppermute | solution.py:496
  6.0 10.2 %collective-permute-start.1 = (bf16[32,1280]{1,0:T(8,128)(2,1)S(1)}, bf16[32,1280]{1,0:T(8,128)(2,1)S(1)}, u32[]{:S(2)}, u32[]{:S(2)}) collective-permute-start(bf16[32,1280]{1,0:T(8,128)(2,1)S(1)} %get-tuple-element.30), channel_id=1, source_target_pairs={{0,4},{1,5},{2,6},{3,7},{4,0},{5,1},{6,2},{7,3},{8,12},{9,13},{10,... | collective-permute-start | bytes 245768 | tf_op jit(solution)/shard_map/ppermute | solution.py:496
  8.9 7.4 %collective-permute-start.2 = (bf16[32,1280]{1,0:T(8,128)(2,1)S(1)}, bf16[32,1280]{1,0:T(8,128)(2,1)S(1)}, u32[]{:S(2)}, u32[]{:S(2)}) collective-permute-start(bf16[32,1280]{1,0:T(8,128)(2,1)S(1)} %get-tuple-element.31), channel_id=1, source_target_pairs={{0,6},{1,7},{2,4},{3,5},{4,2},{5,3},{6,0},{7,1},{8,14},{9,15},{10,... | collective-permute-start | bytes 245768 | tf_op jit(solution)/shard_map/ppermute | solution.py:496
  8.9 2.5 %collective-permute-start.3 = (f32[1,2]{1,0:T(1,128)S(1)}, f32[1,2]{1,0:T(1,128)S(1)}, u32[]{:S(2)}, u32[]{:S(2)}) collective-permute-start(f32[1,2]{1,0:T(1,128)S(1)} %copy-done.2), channel_id=1, source_target_pairs={{0,2},{1,3},{2,0},{3,1},{4,6},{5,7},{6,4},{7,5},{8,10},{9,11},{10,... | collective-permute-start | bytes 32 | tf_op jit(solution)/shard_map/ppermute | solution.py:496
  13.3 26.6 %collective-permute-start.9 = (s16[2576,128]{1,0:T(8,128)(2,1)S(1)}, s16[2576,128]{1,0:T(8,128)(2,1)S(1)}, u32[]{:S(2)}, u32[]{:S(2)}) collective-permute-start(s16[2576,128]{1,0:T(8,128)(2,1)S(1)} %share.3.refs_4_.refs_0_), channel_id=1, source_target_pairs={{0,4},{1,5},{2,6},{3,7},{4,0},{5,1},{6,2},{7,3},{8,12},{9,13},{10,... | collective-permute-start | bytes 1978376 | tf_op jit(solution)/shard_map/ppermute | solution.py:496
  16.3 12.5 %collective-permute-start.5 = (bf16[128,1280]{1,0:T(8,128)(2,1)S(1)}, bf16[128,1280]{1,0:T(8,128)(2,1)S(1)}, u32[]{:S(2)}, u32[]{:S(2)}) collective-permute-start(bf16[128,1280]{1,0:T(8,128)(2,1)S(1)} %join.1.refs_0_), channel_id=1, source_target_pairs={{0,24},{1,25},{2,26},{3,27},{4,28},{5,29},{6,30},{7,31},{8,16},{9,... | collective-permute-start | bytes 983048 | tf_op jit(solution)/shard_map/ppermute | solution.py:496
  21.3 18.5 %collective-permute-start.10 = (s16[1296,128]{1,0:T(8,128)(2,1)S(1)}, s16[1296,128]{1,0:T(8,128)(2,1)S(1)}, u32[]{:S(2)}, u32[]{:S(2)}) collective-permute-start(s16[1296,128]{1,0:T(8,128)(2,1)S(1)} %share.4.refs_0_), channel_id=1, source_target_pairs={{0,4},{1,5},{2,6},{3,7},{4,0},{5,1},{6,2},{7,3},{8,12},{9,13},{10,... | collective-permute-start | bytes 995336 | tf_op jit(solution)/shard_map/ppermute | solution.py:496
  21.9 18.7 %collective-permute-start.6 = (bf16[128,1280]{1,0:T(8,128)(2,1)S(1)}, bf16[128,1280]{1,0:T(8,128)(2,1)S(1)}, u32[]{:S(2)}, u32[]{:S(2)}) collective-permute-start(bf16[128,1280]{1,0:T(8,128)(2,1)S(1)} %join.1.refs_0_), channel_id=1, source_target_pairs={{0,8},{1,9},{2,10},{3,11},{4,12},{5,13},{6,14},{7,15},{8,0},{9,1},... | collective-permute-start | bytes 983048 | tf_op jit(solution)/shard_map/ppermute | solution.py:496
  28.8 13.1 %collective-permute-start.7 = (bf16[128,1280]{1,0:T(8,128)(2,1)S(1)}, bf16[128,1280]{1,0:T(8,128)(2,1)S(1)}, u32[]{:S(2)}, u32[]{:S(2)}) collective-permute-start(bf16[128,1280]{1,0:T(8,128)(2,1)S(1)} %collective-permute-done.5.refs_1_), channel_id=1, source_target_pairs={{0,8},{1,9},{2,10},{3,11},{4,12},{5,13},{6,14},{7,15},{8,0},{9,1},... | collective-permute-start | bytes 983048 | tf_op jit(solution)/shard_map/ppermute | solution.py:496
  39.3 16.3 %collective-permute-start.11 = (s16[2576,128]{1,0:T(8,128)(2,1)S(1)}, s16[2576,128]{1,0:T(8,128)(2,1)S(1)}, u32[]{:S(2)}, u32[]{:S(2)}) collective-permute-start(s16[2576,128]{1,0:T(8,128)(2,1)S(1)} %share.5), channel_id=1, source_target_pairs={{0,4},{1,5},{2,6},{3,7},{4,0},{5,1},{6,2},{7,3},{8,12},{9,13},{10,... | collective-permute-start | bytes 1978376 | tf_op jit(solution)/shard_map/ppermute | solution.py:496
  44.1 8.0 %collective-permute-start.12 = (s16[784,128]{1,0:T(8,128)(2,1)S(1)}, s16[784,128]{1,0:T(8,128)(2,1)S(1)}, u32[]{:S(2)}, u32[]{:S(2)}) collective-permute-start(s16[784,128]{1,0:T(8,128)(2,1)S(1)} %get-tuple-element.35), channel_id=1, source_target_pairs={{0,8},{1,9},{2,10},{3,11},{4,12},{5,13},{6,14},{7,15},{8,0},{9,1},... | collective-permute-start | bytes 602120 | tf_op jit(solution)/shard_map/ppermute | solution.py:496
  45.9 10.3 %collective-permute-start.13 = (s16[784,128]{1,0:T(8,128)(2,1)S(1)}, s16[784,128]{1,0:T(8,128)(2,1)S(1)}, u32[]{:S(2)}, u32[]{:S(2)}) collective-permute-start(s16[784,128]{1,0:T(8,128)(2,1)S(1)} %get-tuple-element.36), channel_id=1, source_target_pairs={{0,8},{1,9},{2,10},{3,11},{4,12},{5,13},{6,14},{7,15},{8,0},{9,1},... | collective-permute-start | bytes 602120 | tf_op jit(solution)/shard_map/ppermute | solution.py:496
  52.1 15.9 %slice-start = ((s8[6553600]{0:T(1024)(128)(4,1)}), s8[4194304]{0:T(1024)(128)(4,1)S(1)}, s32[]{:S(2)}) async-start(s8[6553600]{0:T(1024)(128)(4,1)} %bitcast.9), calls=%async_computation | async-start | bytes 8388608
  52.2 15.7 %slice-start.1 = ((s8[6553600]{0:T(1024)(128)(4,1)}), s8[2359296]{0:T(1024)(128)(4,1)S(1)}, s32[]{:S(2)}) async-start(s8[6553600]{0:T(1024)(128)(4,1)} %bitcast.9), calls=%async_computation.1 | async-start | bytes 4718592
  52.3 12.5 %collective-permute-start.14 = (s16[784,128]{1,0:T(8,128)(2,1)S(1)}, s16[784,128]{1,0:T(8,128)(2,1)S(1)}, u32[]{:S(2)}, u32[]{:S(2)}) collective-permute-start(s16[784,128]{1,0:T(8,128)(2,1)S(1)} %fold.2.refs_1_), channel_id=1, source_target_pairs={{0,24},{1,25},{2,26},{3,27},{4,28},{5,29},{6,30},{7,31},{8,16},{9,... | collective-permute-start | bytes 602120 | tf_op jit(solution)/shard_map/ppermute | solution.py:496
  57.8 7.0 %collective-permute-start.15 = (s16[528,128]{1,0:T(8,128)(2,1)S(1)}, s16[528,128]{1,0:T(8,128)(2,1)S(1)}, u32[]{:S(2)}, u32[]{:S(2)}) collective-permute-start(s16[528,128]{1,0:T(8,128)(2,1)S(1)} %get-tuple-element.39), channel_id=1, source_target_pairs={{0,8},{1,9},{2,10},{3,11},{4,12},{5,13},{6,14},{7,15},{8,0},{9,1},... | collective-permute-start | bytes 405512 | tf_op jit(solution)/shard_map/ppermute | solution.py:496
  57.9 10.9 %collective-permute-start.17 = (s16[528,128]{1,0:T(8,128)(2,1)S(1)}, s16[528,128]{1,0:T(8,128)(2,1)S(1)}, u32[]{:S(2)}, u32[]{:S(2)}) collective-permute-start(s16[528,128]{1,0:T(8,128)(2,1)S(1)} %get-tuple-element.40), channel_id=1, source_target_pairs={{0,8},{1,9},{2,10},{3,11},{4,12},{5,13},{6,14},{7,15},{8,0},{9,1},... | collective-permute-start | bytes 405512 | tf_op jit(solution)/shard_map/ppermute | solution.py:496
  64.9 7.0 %collective-permute-start.16 = (s16[528,128]{1,0:T(8,128)(2,1)S(1)}, s16[528,128]{1,0:T(8,128)(2,1)S(1)}, u32[]{:S(2)}, u32[]{:S(2)}) collective-permute-start(s16[528,128]{1,0:T(8,128)(2,1)S(1)} %fold.3), channel_id=1, source_target_pairs={{0,24},{1,25},{2,26},{3,27},{4,28},{5,29},{6,30},{7,31},{8,16},{9,... | collective-permute-start | bytes 405512 | tf_op jit(solution)/shard_map/ppermute | solution.py:496
  68.7 15.6 %copy-start.3 = (s32[8]{0:T(128)S(1)}, s32[8]{0:T(128)}, u32[]{:S(2)}) copy-start(s32[8]{0:T(128)} %column.1) | copy-start | bytes 100
  74.0 5.5 %collective-permute-start.18 = (s16[336,128]{1,0:T(8,128)(2,1)S(1)}, s16[336,128]{1,0:T(8,128)(2,1)S(1)}, u32[]{:S(2)}, u32[]{:S(2)}) collective-permute-start(s16[336,128]{1,0:T(8,128)(2,1)S(1)} %get-tuple-element.41), channel_id=1, source_target_pairs={{0,5},{1,4},{2,7},{3,6},{4,1},{5,0},{6,3},{7,2},{8,13},{9,12},{10,... | collective-permute-start | bytes 258056 | tf_op jit(solution)/shard_map/ppermute | solution.py:496
  75.5 5.7 %collective-permute-start.19 = (s16[336,128]{1,0:T(8,128)(2,1)S(1)}, s16[336,128]{1,0:T(8,128)(2,1)S(1)}, u32[]{:S(2)}, u32[]{:S(2)}) collective-permute-start(s16[336,128]{1,0:T(8,128)(2,1)S(1)} %get-tuple-element.42), channel_id=1, source_target_pairs={{0,7},{1,6},{2,5},{3,4},{4,3},{5,2},{6,1},{7,0},{8,15},{9,14},{10,... | collective-permute-start | bytes 258056 | tf_op jit(solution)/shard_map/ppermute | solution.py:496
  75.5 5.8 %collective-permute-start.20 = (s16[336,128]{1,0:T(8,128)(2,1)S(1)}, s16[336,128]{1,0:T(8,128)(2,1)S(1)}, u32[]{:S(2)}, u32[]{:S(2)}) collective-permute-start(s16[336,128]{1,0:T(8,128)(2,1)S(1)} %get-tuple-element.43), channel_id=1, source_target_pairs={{0,1},{1,0},{2,3},{3,2},{4,5},{5,4},{6,7},{7,6},{8,9},{9,8},{10,11... | collective-permute-start | bytes 258056 | tf_op jit(solution)/shard_map/ppermute | solution.py:496
  76.0 8.0 %collective-permute-start.21 = (s16[336,128]{1,0:T(8,128)(2,1)S(1)}, s16[336,128]{1,0:T(8,128)(2,1)S(1)}, u32[]{:S(2)}, u32[]{:S(2)}) collective-permute-start(s16[336,128]{1,0:T(8,128)(2,1)S(1)} %get-tuple-element.44), channel_id=1, source_target_pairs={{0,3},{1,2},{2,1},{3,0},{4,7},{5,6},{6,5},{7,4},{8,11},{9,10},{10,... | collective-permute-start | bytes 258056 | tf_op jit(solution)/shard_map/ppermute | solution.py:496
  78.4 5.6 %collective-permute-start.22 = (s16[336,128]{1,0:T(8,128)(2,1)S(1)}, s16[336,128]{1,0:T(8,128)(2,1)S(1)}, u32[]{:S(2)}, u32[]{:S(2)}) collective-permute-start(s16[336,128]{1,0:T(8,128)(2,1)S(1)} %get-tuple-element.45), channel_id=1, source_target_pairs={{0,4},{1,5},{2,6},{3,7},{4,0},{5,1},{6,2},{7,3},{8,12},{9,13},{10,... | collective-permute-start | bytes 258056 | tf_op jit(solution)/shard_map/ppermute | solution.py:496
  79.5 4.8 %collective-permute-start.23 = (s16[336,128]{1,0:T(8,128)(2,1)S(1)}, s16[336,128]{1,0:T(8,128)(2,1)S(1)}, u32[]{:S(2)}, u32[]{:S(2)}) collective-permute-start(s16[336,128]{1,0:T(8,128)(2,1)S(1)} %get-tuple-element.46), channel_id=1, source_target_pairs={{0,6},{1,7},{2,4},{3,5},{4,2},{5,3},{6,0},{7,1},{8,14},{9,15},{10,... | collective-permute-start | bytes 258056 | tf_op jit(solution)/shard_map/ppermute | solution.py:496
  81.2 3.1 %collective-permute-start.24 = (s16[336,128]{1,0:T(8,128)(2,1)S(1)}, s16[336,128]{1,0:T(8,128)(2,1)S(1)}, u32[]{:S(2)}, u32[]{:S(2)}) collective-permute-start(s16[336,128]{1,0:T(8,128)(2,1)S(1)} %get-tuple-element.47), channel_id=1, source_target_pairs={{0,2},{1,3},{2,0},{3,1},{4,6},{5,7},{6,4},{7,5},{8,10},{9,11},{10,... | collective-permute-start | bytes 258056 | tf_op jit(solution)/shard_map/ppermute | solution.py:496

commit v9 on v8

--- a/solution.py
+++ b/solution.py
@@ -499,9 +499,10 @@
     assert slots == 4
     where = jnp.stack([place_of ^ bits for bits in range(4)] + [wave]).astype(I32)
     states = pick(where, spectral_state)
+    turned, w_got, *states = lax.optimization_barrier(
+        (place_of, swap(term_weights, 1), *states)
+    )
     received = [swap(states[bits], bits) for bits in range(1, 4)]
-    turned, received[0] = lax.optimization_barrier((place_of, received[0]))
-    w_got = swap(term_weights, 1)
     far, own = (
         swap(lax.dynamic_index_in_dim(inverse, turned ^ bits, 1, keepdims=False), 1)
         for bits in (3, 1)
@@ -511,7 +512,7 @@
     shares, messages = [], []
     for at, n in enumerate(counts):
         first = sum(counts[:at])
-        after = () if not shares else (shares[-1], mine)[: at]
+        after = (shares[-1], mine) if shares else ()
         shares.append(share(where, term_weights, w_got, inverse, far, first, n, after))
         messages.append(swap(shares[-1], 2))
         if at == 0:

time: 86.1 us -> 83.5 us (0.970)
  waiting for transfers between devices: 30.3 us -> 26.2 us
  starting transfers between devices: 33.4 us -> 34.8 us
    ppermute x25, waiting for transfers between devices: 30.3 us -> 26.2 us  [swap(): return lax.ppermute(x, ('term', 'wave'), pairs)]
    ppermute x25, starting transfers between devices: 33.4 us -> 34.8 us  [swap(): return lax.ppermute(x, ('term', 'wave'), pairs)]
  transfers between devices with their start and end apart: 25 -> 25, of which waited for: 11 -> 10; matrix products, arithmetic and copies ran while one was open for 0% -> 0% of each run, Pallas kernels for 17% -> 18%
where the time goes in v9:
time: 83.5 us; the launch traced here: 83.3 us
  starting transfers between devices  34.8 us (42%)
  waiting for transfers between devices  26.2 us (31%)
  Pallas kernels  18.7 us (22%)
  local copies, waits for them, and re-layouts  3.45 us (4%)
    ppermute x25, starting transfers between devices, swap(): return lax.ppermute(x, ('term', 'wave'), pairs)  34.8 us
    ppermute x25, waiting for transfers between devices, swap(): return lax.ppermute(x, ('term', 'wave'), pairs)  26.2 us
    pallas_call x3, Pallas kernels, share(): pl.pallas_call(functools.partial(share_kernel, len(after)), out_shape=out...  5.27 us
    pallas_call x2, Pallas kernels, product(): pl.pallas_call(functools.partial(product_kernel, count, kept, len(after))...  3.86 us
    pallas_call x1, Pallas kernels, operator(): pl.pallas_call(own_kernel, out_shape=jax.ShapeDtypeStruct((tiles, 2, size...  2.91 us
    squeeze x1, local copies, waits for them, and re-layouts, shards(): lax.dynamic_index_in_dim(inverse, turned ^ bits, 1, keepdims=False)  2.36 us
    pallas_call x1, Pallas kernels, synthesis(): pl.pallas_call(functools.partial(synthesis_kernel, bands, [len(parts) for...  2.09 us
    pallas_call x1, Pallas kernels, place(): pl.pallas_call(functools.partial(place_kernel, count, slots, order), out_...  1.68 us
  transfers between devices with their start and end apart: 25, of which 10 were waited for; matrix products, arithmetic and copies ran while one was open for 0% of the time, Pallas kernels for 18%

profile of v9, /device:TPU:0, one launch (start us, length us, event | category | flops | bytes accessed | tf_op | source)
XLA Modules:
  0.0 83.3 jit_solution(2104399158010389743)
XLA Ops:
  0.0 0.5 collective-permute-start
  0.5 0.1 stack.23.where
  0.5 1.0 %copy-done.1 = bf16[4,32,1280]{2,1,0:T(8,128)(2,1)S(1)} copy-done((bf16[4,32,1280]{2,1,0:T(8,128)(2,1)S(1)}, bf16[4,32,1280]{2,1,0:T(8,128)(2,1)}, u32[]{:S(2)}) %copy-start.1) | copy-done | bytes 327704
  1.5 0.6 pick.1
  2.1 0.0 collective-permute-done.w_got
  2.1 0.0 copy-start
  2.1 0.0 copy-start.2
  2.1 2.4 %dynamic-slice_bitcast_fusion = (bf16[1,2,640,640]{3,2,1,0:T(8,128)(2,1)S(1)}, bf16[1,2,640,640]{3,2,1,0:T(8,128)(2,1)S(1)}) fusion(bf16[1,4,2,640,640]{4,3,2,1,0:T(8,128)(2,1)} %own.7, s32[]{:T(128)S(6)} %select_n.16, s32[]{:T(128)S(6)} %select_n.15), kind=kLoop, calls=%fused_computation | loop fusion | bytes 6553608 | tf_op jit(solution)/shard_map/jit(dynamic_index_in_dim)/squeeze | solution.py:507
  4.5 0.1 collective-permute-start.4
  4.6 0.5 collective-permute-start.8
  5.1 0.1 collective-permute-start.1
  5.2 2.9 %collective-permute-start.2 = (bf16[32,1280]{1,0:T(8,128)(2,1)S(1)}, bf16[32,1280]{1,0:T(8,128)(2,1)S(1)}, u32[]{:S(2)}, u32[]{:S(2)}) collective-permute-start(bf16[32,1280]{1,0:T(8,128)(2,1)S(1)} %get-tuple-element.37), channel_id=1, source_target_pairs={{0,4},{1,5},{2,6},{3,7},{4,0},{5,1},{6,2},{7,3},{8,12},{9,13},{10,... | collective-permute-start | bytes 245768 | tf_op jit(solution)/shard_map/ppermute | solution.py:496
  8.1 0.0 collective-permute-start.3
  8.1 0.0 collective-permute-done.4.got
  8.1 1.9 %share.3.refs_4_.refs_0_ = s16[2576,128]{1,0:T(8,128)(2,1)S(1)} custom-call(s32[5]{0:T(128)S(1)} %stack.23.where, f32[1,2]{1,0:T(1,128)S(1)} %copy-done.2, f32[1,2]{1,0:T(1,128)S(1)} %collective-permute-done.w_got, bf16[1,4,2,640,640]{4,3,2,1,0:T(8,128)(2,1)S(1)} %copy-done, bf16[1,2,640,640]{3,2,1,0:T(8,128)(2,1)S(1)} %collective-permute-done.4.got), custom_call_target="tpu_custom_call" | custom-call | flops 5242880 | bytes 2621440 | tf_op jit(solution)/shard_map/share/pallas_call | solution.py:91
  10.1 2.7 %collective-permute-start.9 = (s16[2576,128]{1,0:T(8,128)(2,1)S(1)}, s16[2576,128]{1,0:T(8,128)(2,1)S(1)}, u32[]{:S(2)}, u32[]{:S(2)}) collective-permute-start(s16[2576,128]{1,0:T(8,128)(2,1)S(1)} %share.3.refs_4_.refs_0_), channel_id=1, source_target_pairs={{0,4},{1,5},{2,6},{3,7},{4,0},{5,1},{6,2},{7,3},{8,12},{9,13},{10,... | collective-permute-start | bytes 1978376 | tf_op jit(solution)/shard_map/ppermute | solution.py:496
  12.8 0.0 collective-permute-done.1.refs_1_
  12.8 0.0 collective-permute-done.2.refs_2_
  12.8 0.1 collective-permute-done.3.refs_3_
  12.9 3.7 %collective-permute-start.5 = (bf16[128,1280]{1,0:T(8,128)(2,1)S(1)}, bf16[128,1280]{1,0:T(8,128)(2,1)S(1)}, u32[]{:S(2)}, u32[]{:S(2)}) collective-permute-start(bf16[128,1280]{1,0:T(8,128)(2,1)S(1)} %join.1.refs_0_), channel_id=1, source_target_pairs={{0,24},{1,25},{2,26},{3,27},{4,28},{5,29},{6,30},{7,31},{8,16},{9,... | collective-permute-start | bytes 983048 | tf_op jit(solution)/shard_map/ppermute | solution.py:496
  16.5 2.9 %operator.1.refs_1_.own = f32[5,2,640,128]{3,2,1,0:T(8,128)S(1)} custom-call(s32[5]{0:T(128)S(1)} %stack.23.where, f32[1,2]{1,0:T(1,128)S(1)} %copy-done.2, f32[1,2]{1,0:T(1,128)S(1)} %collective-permute-done.w_got, bf16[1,4,2,640,640]{4,3,2,1,0:T(8,128)(2,1)S(1)} %copy-done, bf16[1,2,640,640]{3,2,1,0:T(8,128)(2,1)S(1)} %collective-permute-done.8.got), custom_call_target="tpu_custom_call" | custom-call | flops 13107200 | bytes 6553600 | tf_op jit(solution)/shard_map/operator/pallas_call | solution.py:126
  19.4 1.4 %share.4.refs_0_ = s16[1296,128]{1,0:T(8,128)(2,1)S(1)} custom-call(s32[5]{0:T(128)S(1)} %stack.23.where, f32[1,2]{1,0:T(1,128)S(1)} %copy-done.2, f32[1,2]{1,0:T(1,128)S(1)} %collective-permute-done.w_got, bf16[1,4,2,640,640]{4,3,2,1,0:T(8,128)(2,1)S(1)} %copy-done, bf16[1,2,640,640]{3,2,1,0:T(8,128)(2,1)S(1)} %collective-permute-done.4.got, ...), custom_call_target="tpu_custom_call" | custom-call | flops 2621440 | bytes 1310720 | tf_op jit(solution)/shard_map/share/pallas_call | solution.py:91
  20.8 0.6 collective-permute-start.10
  21.5 0.0 collective-permute-start.6
  21.5 3.8 %collective-permute-done.5.refs_1_ = bf16[128,1280]{1,0:T(8,128)(2,1)S(1)} collective-permute-done((bf16[128,1280]{1,0:T(8,128)(2,1)S(1)}, bf16[128,1280]{1,0:T(8,128)(2,1)S(1)}, u32[]{:S(2)}, u32[]{:S(2)}) %collective-permute-start.5) | collective-permute-done | bytes 327712 | tf_op jit(solution)/shard_map/ppermute | solution.py:496
  25.3 5.9 %collective-permute-start.7 = (bf16[128,1280]{1,0:T(8,128)(2,1)S(1)}, bf16[128,1280]{1,0:T(8,128)(2,1)S(1)}, u32[]{:S(2)}, u32[]{:S(2)}) collective-permute-start(bf16[128,1280]{1,0:T(8,128)(2,1)S(1)} %collective-permute-done.5.refs_1_), channel_id=1, source_target_pairs={{0,8},{1,9},{2,10},{3,11},{4,12},{5,13},{6,14},{7,15},{8,0},{9,1},... | collective-permute-start | bytes 983048 | tf_op jit(solution)/shard_map/ppermute | solution.py:496
  31.2 1.9 %share.5 = s16[2576,128]{1,0:T(8,128)(2,1)S(1)} custom-call(s32[5]{0:T(128)S(1)} %stack.23.where, f32[1,2]{1,0:T(1,128)S(1)} %copy-done.2, f32[1,2]{1,0:T(1,128)S(1)} %collective-permute-done.w_got, bf16[1,4,2,640,640]{4,3,2,1,0:T(8,128)(2,1)S(1)} %copy-done, bf16[1,2,640,640]{3,2,1,0:T(8,128)(2,1)S(1)} %collective-permute-done.4.got, ...), custom_call_target="tpu_custom_call" | custom-call | flops 5242880 | bytes 2621440 | tf_op jit(solution)/shard_map/share/pallas_call | solution.py:91
  33.2 1.3 %collective-permute-start.11 = (s16[2576,128]{1,0:T(8,128)(2,1)S(1)}, s16[2576,128]{1,0:T(8,128)(2,1)S(1)}, u32[]{:S(2)}, u32[]{:S(2)}) collective-permute-start(s16[2576,128]{1,0:T(8,128)(2,1)S(1)} %share.5), channel_id=1, source_target_pairs={{0,4},{1,5},{2,6},{3,7},{4,0},{5,1},{6,2},{7,3},{8,12},{9,13},{10,... | collective-permute-start | bytes 1978376 | tf_op jit(solution)/shard_map/ppermute | solution.py:496
  34.4 1.1 %collective-permute-done.10.refs_1_ = s16[1296,128]{1,0:T(8,128)(2,1)S(1)} collective-permute-done((s16[1296,128]{1,0:T(8,128)(2,1)S(1)}, s16[1296,128]{1,0:T(8,128)(2,1)S(1)}, u32[]{:S(2)}, u32[]{:S(2)}) %collective-permute-start.10) | collective-permute-done | bytes 331808 | tf_op jit(solution)/shard_map/ppermute | solution.py:496
  35.5 0.8 build.2.refs_4_
  36.3 0.0 collective-permute-done.6.refs_2_
  36.3 2.5 %collective-permute-done.7.refs_3_ = bf16[128,1280]{1,0:T(8,128)(2,1)S(1)} collective-permute-done((bf16[128,1280]{1,0:T(8,128)(2,1)S(1)}, bf16[128,1280]{1,0:T(8,128)(2,1)S(1)}, u32[]{:S(2)}, u32[]{:S(2)}) %collective-permute-start.7) | collective-permute-done | bytes 327712 | tf_op jit(solution)/shard_map/ppermute | solution.py:496
  38.8 2.3 %product.2 = (f32[3,128,256]{2,1,0:T(8,128)S(1)}, f32[3,128,256]{2,1,0:T(8,128)S(1)}, s16[784,128]{1,0:T(8,128)(2,1)S(1)}, s16[784,128]{1,0:T(8,128)(2,1)S(1)}) custom-call(bf16[128,1280]{1,0:T(8,128)(2,1)S(1)} %join.1.refs_0_, bf16[128,1280]{1,0:T(8,128)(2,1)S(1)} %collective-permute-done.5.refs_1_, bf16[128,1280]{1,0:T(8,128)(2,1)S(1)} %collective-permute-done.6.refs_2_, ...), custom_call_target="tpu_custom_call" | custom-call | flops 2013265920 | bytes 5242880 | tf_op jit(solution)/shard_map/product/pallas_call | solution.py:237
  41.1 1.6 %collective-permute-start.12 = (s16[784,128]{1,0:T(8,128)(2,1)S(1)}, s16[784,128]{1,0:T(8,128)(2,1)S(1)}, u32[]{:S(2)}, u32[]{:S(2)}) collective-permute-start(s16[784,128]{1,0:T(8,128)(2,1)S(1)} %get-tuple-element.43), channel_id=1, source_target_pairs={{0,8},{1,9},{2,10},{3,11},{4,12},{5,13},{6,14},{7,15},{8,0},{9,1},... | collective-permute-start | bytes 602120 | tf_op jit(solution)/shard_map/ppermute | solution.py:496
  42.7 0.5 collective-permute-start.13
  43.2 5.9 %collective-permute-done.12.got = s16[784,128]{1,0:T(8,128)(2,1)S(1)} collective-permute-done((s16[784,128]{1,0:T(8,128)(2,1)S(1)}, s16[784,128]{1,0:T(8,128)(2,1)S(1)}, u32[]{:S(2)}, u32[]{:S(2)}) %collective-permute-start.12) | collective-permute-done | bytes 200736 | tf_op jit(solution)/shard_map/ppermute | solution.py:496
  49.1 0.1 fold.2.refs_1_
  49.2 0.0 slice-start.1
  49.2 3.3 %collective-permute-start.14 = (s16[784,128]{1,0:T(8,128)(2,1)S(1)}, s16[784,128]{1,0:T(8,128)(2,1)S(1)}, u32[]{:S(2)}, u32[]{:S(2)}) collective-permute-start(s16[784,128]{1,0:T(8,128)(2,1)S(1)} %fold.2.refs_1_), channel_id=1, source_target_pairs={{0,24},{1,25},{2,26},{3,27},{4,28},{5,29},{6,30},{7,31},{8,16},{9,... | collective-permute-start | bytes 602120 | tf_op jit(solution)/shard_map/ppermute | solution.py:496
  52.6 0.5 build.3.refs_4_
  53.1 1.6 %product.3 = (f32[2,128,256]{2,1,0:T(8,128)S(1)}, f32[2,128,256]{2,1,0:T(8,128)S(1)}, s16[528,128]{1,0:T(8,128)(2,1)S(1)}, s16[528,128]{1,0:T(8,128)(2,1)S(1)}) custom-call(bf16[128,1280]{1,0:T(8,128)(2,1)S(1)} %join.1.refs_0_, bf16[128,1280]{1,0:T(8,128)(2,1)S(1)} %collective-permute-done.5.refs_1_, bf16[128,1280]{1,0:T(8,128)(2,1)S(1)} %collective-permute-done.6.refs_2_, ...), custom_call_target="tpu_custom_call" | custom-call | flops 1342177280 | bytes 3932160 | tf_op jit(solution)/shard_map/product/pallas_call | solution.py:237
  54.7 0.1 collective-permute-start.15
  54.8 2.0 %collective-permute-start.17 = (s16[528,128]{1,0:T(8,128)(2,1)S(1)}, s16[528,128]{1,0:T(8,128)(2,1)S(1)}, u32[]{:S(2)}, u32[]{:S(2)}) collective-permute-start(s16[528,128]{1,0:T(8,128)(2,1)S(1)} %get-tuple-element.48), channel_id=1, source_target_pairs={{0,8},{1,9},{2,10},{3,11},{4,12},{5,13},{6,14},{7,15},{8,0},{9,1},... | collective-permute-start | bytes 405512 | tf_op jit(solution)/shard_map/ppermute | solution.py:496
  56.8 4.9 %collective-permute-done.15.got = s16[528,128]{1,0:T(8,128)(2,1)S(1)} collective-permute-done((s16[528,128]{1,0:T(8,128)(2,1)S(1)}, s16[528,128]{1,0:T(8,128)(2,1)S(1)}, u32[]{:S(2)}, u32[]{:S(2)}) %collective-permute-start.15) | collective-permute-done | bytes 135200 | tf_op jit(solution)/shard_map/ppermute | solution.py:496
  61.7 0.0 collective-permute-done.14.refs_0_.refs_2_
  61.7 0.1 fold.3
  61.8 3.3 %collective-permute-start.16 = (s16[528,128]{1,0:T(8,128)(2,1)S(1)}, s16[528,128]{1,0:T(8,128)(2,1)S(1)}, u32[]{:S(2)}, u32[]{:S(2)}) collective-permute-start(s16[528,128]{1,0:T(8,128)(2,1)S(1)} %fold.3), channel_id=1, source_target_pairs={{0,24},{1,25},{2,26},{3,27},{4,28},{5,29},{6,30},{7,31},{8,16},{9,... | collective-permute-start | bytes 405512 | tf_op jit(solution)/shard_map/ppermute | solution.py:496
  65.1 0.8 table.1.refs_6_
  65.9 0.0 copy-start.3
  65.9 0.0 collective-permute-done.17.refs_5_
  65.9 2.9 %collective-permute-done.16.refs_4_ = s16[528,128]{1,0:T(8,128)(2,1)S(1)} collective-permute-done((s16[528,128]{1,0:T(8,128)(2,1)S(1)}, s16[528,128]{1,0:T(8,128)(2,1)S(1)}, u32[]{:S(2)}, u32[]{:S(2)}) %collective-permute-start.16) | collective-permute-done | bytes 135200 | tf_op jit(solution)/shard_map/ppermute | solution.py:496
  68.8 2.1 %synthesis.1 = (f32[2,32,640]{2,1,0:T(8,128)S(1)}, s16[336,128]{1,0:T(8,128)(2,1)S(1)}, s16[336,128]{1,0:T(8,128)(2,1)S(1)}, s16[336,128]{1,0:T(8,128)(2,1)S(1)}...) custom-call(s32[5]{0:T(128)S(1)} %stack.23.where, ...), custom_call_target="tpu_custom_call" | custom-call | flops 838860800 | bytes 2949120 | tf_op jit(solution)/shard_map/synthesis/pallas_call | solution.py:356
  70.9 2.2 %collective-permute-start.18 = (s16[336,128]{1,0:T(8,128)(2,1)S(1)}, s16[336,128]{1,0:T(8,128)(2,1)S(1)}, u32[]{:S(2)}, u32[]{:S(2)}) collective-permute-start(s16[336,128]{1,0:T(8,128)(2,1)S(1)} %get-tuple-element.49), channel_id=1, source_target_pairs={{0,5},{1,4},{2,7},{3,6},{4,1},{5,0},{6,3},{7,2},{8,13},{9,12},{10,... | collective-permute-start | bytes 258056 | tf_op jit(solution)/shard_map/ppermute | solution.py:496
  73.1 0.0 collective-permute-start.19
  73.1 0.5 collective-permute-start.20
  73.6 1.7 %collective-permute-start.21 = (s16[336,128]{1,0:T(8,128)(2,1)S(1)}, s16[336,128]{1,0:T(8,128)(2,1)S(1)}, u32[]{:S(2)}, u32[]{:S(2)}) collective-permute-start(s16[336,128]{1,0:T(8,128)(2,1)S(1)} %get-tuple-element.52), channel_id=1, source_target_pairs={{0,3},{1,2},{2,1},{3,0},{4,7},{5,6},{6,5},{7,4},{8,11},{9,10},{10,... | collective-permute-start | bytes 258056 | tf_op jit(solution)/shard_map/ppermute | solution.py:496
  75.3 1.2 %collective-permute-start.22 = (s16[336,128]{1,0:T(8,128)(2,1)S(1)}, s16[336,128]{1,0:T(8,128)(2,1)S(1)}, u32[]{:S(2)}, u32[]{:S(2)}) collective-permute-start(s16[336,128]{1,0:T(8,128)(2,1)S(1)} %get-tuple-element.53), channel_id=1, source_target_pairs={{0,4},{1,5},{2,6},{3,7},{4,0},{5,1},{6,2},{7,3},{8,12},{9,13},{10,... | collective-permute-start | bytes 258056 | tf_op jit(solution)/shard_map/ppermute | solution.py:496
  76.6 0.0 collective-permute-start.23
  76.6 2.3 %collective-permute-done.19.refs_1_ = s16[336,128]{1,0:T(8,128)(2,1)S(1)} collective-permute-done((s16[336,128]{1,0:T(8,128)(2,1)S(1)}, s16[336,128]{1,0:T(8,128)(2,1)S(1)}, u32[]{:S(2)}, u32[]{:S(2)}) %collective-permute-start.19) | collective-permute-done | bytes 86048 | tf_op jit(solution)/shard_map/ppermute | solution.py:496
  78.9 0.7 collective-permute-done.20.refs_2_
  79.5 2.1 %collective-permute-done.21.refs_3_ = s16[336,128]{1,0:T(8,128)(2,1)S(1)} collective-permute-done((s16[336,128]{1,0:T(8,128)(2,1)S(1)}, s16[336,128]{1,0:T(8,128)(2,1)S(1)}, u32[]{:S(2)}, u32[]{:S(2)}) %collective-permute-start.21) | collective-permute-done | bytes 86048 | tf_op jit(solution)/shard_map/ppermute | solution.py:496
  81.6 0.0 collective-permute-done.22.refs_4_
  81.6 0.0 collective-permute-done.23.refs_5_
  81.6 1.7 %place.1 = f32[8,2,32,640]{3,2,1,0:T(8,128)} custom-call(s32[5]{0:T(128)S(1)} %stack.23.where, s32[8]{0:T(128)S(1)} %copy-done.3, s16[336,128]{1,0:T(8,128)(2,1)S(1)} %collective-permute-done.18.refs_0_, s16[336,128]{1,0:T(8,128)(2,1)S(1)} %collective-permute-done.19.refs_1_, s16[336,128]{1,0:T(8,128)(2,1)S(1)} %collective-permute-done.20.refs_2_, ...), custom_call_target="tpu_custom_call" | custom-call | tf_op jit(solution)/shard_map/place/pallas_call | solution.py:429
  (16 shorter events, 0.1 us)
Async XLA Ops:
  0.0 2.1 %collective-permute-start = (f32[1,2]{1,0:T(1,128)}, f32[1,2]{1,0:T(1,128)S(1)}, u32[]{:S(2)}, u32[]{:S(2)}) collective-permute-start(f32[1,2]{1,0:T(1,128)} %w_own.7), channel_id=1, source_target_pairs={{0,2},{1,3},{2,0},{3,1},{4,6},{5,7},{6,4},{7,5},{8,10},{9,11},{10,... | collective-permute-start | bytes 32 | tf_op jit(solution)/shard_map/ppermute | solution.py:496
  0.5 1.0 %copy-start.1 = (bf16[4,32,1280]{2,1,0:T(8,128)(2,1)S(1)}, bf16[4,32,1280]{2,1,0:T(8,128)(2,1)}, u32[]{:S(2)}) copy-start(bf16[4,32,1280]{2,1,0:T(8,128)(2,1)} %refs_3_.1) | copy-start | bytes 983044
  2.1 6.0 %copy-start = (bf16[1,4,2,640,640]{4,3,2,1,0:T(8,128)(2,1)S(1)}, bf16[1,4,2,640,640]{4,3,2,1,0:T(8,128)(2,1)}, u32[]{:S(2)}) copy-start(bf16[1,4,2,640,640]{4,3,2,1,0:T(8,128)(2,1)} %own.7) | copy-start | bytes 19660804
  2.1 6.0 %copy-start.2 = (f32[1,2]{1,0:T(1,128)S(1)}, f32[1,2]{1,0:T(1,128)}, u32[]{:S(2)}) copy-start(f32[1,2]{1,0:T(1,128)} %w_own.7) | copy-start | bytes 28
  4.5 3.6 %collective-permute-start.4 = (bf16[1,2,640,640]{3,2,1,0:T(8,128)(2,1)S(1)}, bf16[1,2,640,640]{3,2,1,0:T(8,128)(2,1)S(1)}, u32[]{:S(2)}, u32[]{:S(2)}) collective-permute-start(bf16[1,2,640,640]{3,2,1,0:T(8,128)(2,1)S(1)} %get-tuple-element.58), channel_id=1, source_target_pairs={{0,2},{1,3},{2,0},{3,1},{4,6},{5,7},{6,4},{7,5},{8,10},{9,11},{10,... | collective-permute-start | bytes 4915208 | tf_op jit(solution)/shard_map/ppermute | solution.py:496
  4.6 11.9 %collective-permute-start.8 = (bf16[1,2,640,640]{3,2,1,0:T(8,128)(2,1)S(1)}, bf16[1,2,640,640]{3,2,1,0:T(8,128)(2,1)S(1)}, u32[]{:S(2)}, u32[]{:S(2)}) collective-permute-start(bf16[1,2,640,640]{3,2,1,0:T(8,128)(2,1)S(1)} %get-tuple-element.57), channel_id=1, source_target_pairs={{0,2},{1,3},{2,0},{3,1},{4,6},{5,7},{6,4},{7,5},{8,10},{9,11},{10,... | collective-permute-start | bytes 4915208 | tf_op jit(solution)/shard_map/ppermute | solution.py:496
  5.1 7.7 %collective-permute-start.1 = (bf16[32,1280]{1,0:T(8,128)(2,1)S(1)}, bf16[32,1280]{1,0:T(8,128)(2,1)S(1)}, u32[]{:S(2)}, u32[]{:S(2)}) collective-permute-start(bf16[32,1280]{1,0:T(8,128)(2,1)S(1)} %get-tuple-element.36), channel_id=1, source_target_pairs={{0,2},{1,3},{2,0},{3,1},{4,6},{5,7},{6,4},{7,5},{8,10},{9,11},{10,... | collective-permute-start | bytes 245768 | tf_op jit(solution)/shard_map/ppermute | solution.py:496
  5.2 7.6 %collective-permute-start.2 = (bf16[32,1280]{1,0:T(8,128)(2,1)S(1)}, bf16[32,1280]{1,0:T(8,128)(2,1)S(1)}, u32[]{:S(2)}, u32[]{:S(2)}) collective-permute-start(bf16[32,1280]{1,0:T(8,128)(2,1)S(1)} %get-tuple-element.37), channel_id=1, source_target_pairs={{0,4},{1,5},{2,6},{3,7},{4,0},{5,1},{6,2},{7,3},{8,12},{9,13},{10,... | collective-permute-start | bytes 245768 | tf_op jit(solution)/shard_map/ppermute | solution.py:496
  8.1 4.7 %collective-permute-start.3 = (bf16[32,1280]{1,0:T(8,128)(2,1)S(1)}, bf16[32,1280]{1,0:T(8,128)(2,1)S(1)}, u32[]{:S(2)}, u32[]{:S(2)}) collective-permute-start(bf16[32,1280]{1,0:T(8,128)(2,1)S(1)} %get-tuple-element.38), channel_id=1, source_target_pairs={{0,6},{1,7},{2,4},{3,5},{4,2},{5,3},{6,0},{7,1},{8,14},{9,15},{10,... | collective-permute-start | bytes 245768 | tf_op jit(solution)/shard_map/ppermute | solution.py:496
  10.1 25.5 %collective-permute-start.9 = (s16[2576,128]{1,0:T(8,128)(2,1)S(1)}, s16[2576,128]{1,0:T(8,128)(2,1)S(1)}, u32[]{:S(2)}, u32[]{:S(2)}) collective-permute-start(s16[2576,128]{1,0:T(8,128)(2,1)S(1)} %share.3.refs_4_.refs_0_), channel_id=1, source_target_pairs={{0,4},{1,5},{2,6},{3,7},{4,0},{5,1},{6,2},{7,3},{8,12},{9,13},{10,... | collective-permute-start | bytes 1978376 | tf_op jit(solution)/shard_map/ppermute | solution.py:496
  12.9 12.5 %collective-permute-start.5 = (bf16[128,1280]{1,0:T(8,128)(2,1)S(1)}, bf16[128,1280]{1,0:T(8,128)(2,1)S(1)}, u32[]{:S(2)}, u32[]{:S(2)}) collective-permute-start(bf16[128,1280]{1,0:T(8,128)(2,1)S(1)} %join.1.refs_0_), channel_id=1, source_target_pairs={{0,24},{1,25},{2,26},{3,27},{4,28},{5,29},{6,30},{7,31},{8,16},{9,... | collective-permute-start | bytes 983048 | tf_op jit(solution)/shard_map/ppermute | solution.py:496
  20.8 14.7 %collective-permute-start.10 = (s16[1296,128]{1,0:T(8,128)(2,1)S(1)}, s16[1296,128]{1,0:T(8,128)(2,1)S(1)}, u32[]{:S(2)}, u32[]{:S(2)}) collective-permute-start(s16[1296,128]{1,0:T(8,128)(2,1)S(1)} %share.4.refs_0_), channel_id=1, source_target_pairs={{0,4},{1,5},{2,6},{3,7},{4,0},{5,1},{6,2},{7,3},{8,12},{9,13},{10,... | collective-permute-start | bytes 995336 | tf_op jit(solution)/shard_map/ppermute | solution.py:496
  21.5 14.8 %collective-permute-start.6 = (bf16[128,1280]{1,0:T(8,128)(2,1)S(1)}, bf16[128,1280]{1,0:T(8,128)(2,1)S(1)}, u32[]{:S(2)}, u32[]{:S(2)}) collective-permute-start(bf16[128,1280]{1,0:T(8,128)(2,1)S(1)} %join.1.refs_0_), channel_id=1, source_target_pairs={{0,8},{1,9},{2,10},{3,11},{4,12},{5,13},{6,14},{7,15},{8,0},{9,1},... | collective-permute-start | bytes 983048 | tf_op jit(solution)/shard_map/ppermute | solution.py:496
  25.3 13.5 %collective-permute-start.7 = (bf16[128,1280]{1,0:T(8,128)(2,1)S(1)}, bf16[128,1280]{1,0:T(8,128)(2,1)S(1)}, u32[]{:S(2)}, u32[]{:S(2)}) collective-permute-start(bf16[128,1280]{1,0:T(8,128)(2,1)S(1)} %collective-permute-done.5.refs_1_), channel_id=1, source_target_pairs={{0,8},{1,9},{2,10},{3,11},{4,12},{5,13},{6,14},{7,15},{8,0},{9,1},... | collective-permute-start | bytes 983048 | tf_op jit(solution)/shard_map/ppermute | solution.py:496
  33.2 19.4 %collective-permute-start.11 = (s16[2576,128]{1,0:T(8,128)(2,1)S(1)}, s16[2576,128]{1,0:T(8,128)(2,1)S(1)}, u32[]{:S(2)}, u32[]{:S(2)}) collective-permute-start(s16[2576,128]{1,0:T(8,128)(2,1)S(1)} %share.5), channel_id=1, source_target_pairs={{0,4},{1,5},{2,6},{3,7},{4,0},{5,1},{6,2},{7,3},{8,12},{9,13},{10,... | collective-permute-start | bytes 1978376 | tf_op jit(solution)/shard_map/ppermute | solution.py:496
  41.1 8.0 %collective-permute-start.12 = (s16[784,128]{1,0:T(8,128)(2,1)S(1)}, s16[784,128]{1,0:T(8,128)(2,1)S(1)}, u32[]{:S(2)}, u32[]{:S(2)}) collective-permute-start(s16[784,128]{1,0:T(8,128)(2,1)S(1)} %get-tuple-element.43), channel_id=1, source_target_pairs={{0,8},{1,9},{2,10},{3,11},{4,12},{5,13},{6,14},{7,15},{8,0},{9,1},... | collective-permute-start | bytes 602120 | tf_op jit(solution)/shard_map/ppermute | solution.py:496
  42.7 10.4 %collective-permute-start.13 = (s16[784,128]{1,0:T(8,128)(2,1)S(1)}, s16[784,128]{1,0:T(8,128)(2,1)S(1)}, u32[]{:S(2)}, u32[]{:S(2)}) collective-permute-start(s16[784,128]{1,0:T(8,128)(2,1)S(1)} %get-tuple-element.44), channel_id=1, source_target_pairs={{0,8},{1,9},{2,10},{3,11},{4,12},{5,13},{6,14},{7,15},{8,0},{9,1},... | collective-permute-start | bytes 602120 | tf_op jit(solution)/shard_map/ppermute | solution.py:496
  49.1 16.0 %slice-start = ((s8[6553600]{0:T(1024)(128)(4,1)}), s8[4194304]{0:T(1024)(128)(4,1)S(1)}, s32[]{:S(2)}) async-start(s8[6553600]{0:T(1024)(128)(4,1)} %bitcast.9), calls=%async_computation | async-start | bytes 8388608
  49.2 15.9 %slice-start.1 = ((s8[6553600]{0:T(1024)(128)(4,1)}), s8[2359296]{0:T(1024)(128)(4,1)S(1)}, s32[]{:S(2)}) async-start(s8[6553600]{0:T(1024)(128)(4,1)} %bitcast.9), calls=%async_computation.1 | async-start | bytes 4718592
  49.2 12.5 %collective-permute-start.14 = (s16[784,128]{1,0:T(8,128)(2,1)S(1)}, s16[784,128]{1,0:T(8,128)(2,1)S(1)}, u32[]{:S(2)}, u32[]{:S(2)}) collective-permute-start(s16[784,128]{1,0:T(8,128)(2,1)S(1)} %fold.2.refs_1_), channel_id=1, source_target_pairs={{0,24},{1,25},{2,26},{3,27},{4,28},{5,29},{6,30},{7,31},{8,16},{9,... | collective-permute-start | bytes 602120 | tf_op jit(solution)/shard_map/ppermute | solution.py:496
  54.7 7.0 %collective-permute-start.15 = (s16[528,128]{1,0:T(8,128)(2,1)S(1)}, s16[528,128]{1,0:T(8,128)(2,1)S(1)}, u32[]{:S(2)}, u32[]{:S(2)}) collective-permute-start(s16[528,128]{1,0:T(8,128)(2,1)S(1)} %get-tuple-element.47), channel_id=1, source_target_pairs={{0,8},{1,9},{2,10},{3,11},{4,12},{5,13},{6,14},{7,15},{8,0},{9,1},... | collective-permute-start | bytes 405512 | tf_op jit(solution)/shard_map/ppermute | solution.py:496
  54.8 11.1 %collective-permute-start.17 = (s16[528,128]{1,0:T(8,128)(2,1)S(1)}, s16[528,128]{1,0:T(8,128)(2,1)S(1)}, u32[]{:S(2)}, u32[]{:S(2)}) collective-permute-start(s16[528,128]{1,0:T(8,128)(2,1)S(1)} %get-tuple-element.48), channel_id=1, source_target_pairs={{0,8},{1,9},{2,10},{3,11},{4,12},{5,13},{6,14},{7,15},{8,0},{9,1},... | collective-permute-start | bytes 405512 | tf_op jit(solution)/shard_map/ppermute | solution.py:496
  61.8 6.9 %collective-permute-start.16 = (s16[528,128]{1,0:T(8,128)(2,1)S(1)}, s16[528,128]{1,0:T(8,128)(2,1)S(1)}, u32[]{:S(2)}, u32[]{:S(2)}) collective-permute-start(s16[528,128]{1,0:T(8,128)(2,1)S(1)} %fold.3), channel_id=1, source_target_pairs={{0,24},{1,25},{2,26},{3,27},{4,28},{5,29},{6,30},{7,31},{8,16},{9,... | collective-permute-start | bytes 405512 | tf_op jit(solution)/shard_map/ppermute | solution.py:496
  65.9 15.7 %copy-start.3 = (s32[8]{0:T(128)S(1)}, s32[8]{0:T(128)}, u32[]{:S(2)}) copy-start(s32[8]{0:T(128)} %column.1) | copy-start | bytes 100
  70.9 5.7 %collective-permute-start.18 = (s16[336,128]{1,0:T(8,128)(2,1)S(1)}, s16[336,128]{1,0:T(8,128)(2,1)S(1)}, u32[]{:S(2)}, u32[]{:S(2)}) collective-permute-start(s16[336,128]{1,0:T(8,128)(2,1)S(1)} %get-tuple-element.49), channel_id=1, source_target_pairs={{0,5},{1,4},{2,7},{3,6},{4,1},{5,0},{6,3},{7,2},{8,13},{9,12},{10,... | collective-permute-start | bytes 258056 | tf_op jit(solution)/shard_map/ppermute | solution.py:496
  73.1 5.8 %collective-permute-start.19 = (s16[336,128]{1,0:T(8,128)(2,1)S(1)}, s16[336,128]{1,0:T(8,128)(2,1)S(1)}, u32[]{:S(2)}, u32[]{:S(2)}) collective-permute-start(s16[336,128]{1,0:T(8,128)(2,1)S(1)} %get-tuple-element.50), channel_id=1, source_target_pairs={{0,7},{1,6},{2,5},{3,4},{4,3},{5,2},{6,1},{7,0},{8,15},{9,14},{10,... | collective-permute-start | bytes 258056 | tf_op jit(solution)/shard_map/ppermute | solution.py:496
  73.1 6.4 %collective-permute-start.20 = (s16[336,128]{1,0:T(8,128)(2,1)S(1)}, s16[336,128]{1,0:T(8,128)(2,1)S(1)}, u32[]{:S(2)}, u32[]{:S(2)}) collective-permute-start(s16[336,128]{1,0:T(8,128)(2,1)S(1)} %get-tuple-element.51), channel_id=1, source_target_pairs={{0,1},{1,0},{2,3},{3,2},{4,5},{5,4},{6,7},{7,6},{8,9},{9,8},{10,11... | collective-permute-start | bytes 258056 | tf_op jit(solution)/shard_map/ppermute | solution.py:496
  73.6 8.0 %collective-permute-start.21 = (s16[336,128]{1,0:T(8,128)(2,1)S(1)}, s16[336,128]{1,0:T(8,128)(2,1)S(1)}, u32[]{:S(2)}, u32[]{:S(2)}) collective-permute-start(s16[336,128]{1,0:T(8,128)(2,1)S(1)} %get-tuple-element.52), channel_id=1, source_target_pairs={{0,3},{1,2},{2,1},{3,0},{4,7},{5,6},{6,5},{7,4},{8,11},{9,10},{10,... | collective-permute-start | bytes 258056 | tf_op jit(solution)/shard_map/ppermute | solution.py:496
  75.3 6.3 %collective-permute-start.22 = (s16[336,128]{1,0:T(8,128)(2,1)S(1)}, s16[336,128]{1,0:T(8,128)(2,1)S(1)}, u32[]{:S(2)}, u32[]{:S(2)}) collective-permute-start(s16[336,128]{1,0:T(8,128)(2,1)S(1)} %get-tuple-element.53), channel_id=1, source_target_pairs={{0,4},{1,5},{2,6},{3,7},{4,0},{5,1},{6,2},{7,3},{8,12},{9,13},{10,... | collective-permute-start | bytes 258056 | tf_op jit(solution)/shard_map/ppermute | solution.py:496
  76.6 5.1 %collective-permute-start.23 = (s16[336,128]{1,0:T(8,128)(2,1)S(1)}, s16[336,128]{1,0:T(8,128)(2,1)S(1)}, u32[]{:S(2)}, u32[]{:S(2)}) collective-permute-start(s16[336,128]{1,0:T(8,128)(2,1)S(1)} %get-tuple-element.54), channel_id=1, source_target_pairs={{0,6},{1,7},{2,4},{3,5},{4,2},{5,3},{6,0},{7,1},{8,14},{9,15},{10,... | collective-permute-start | bytes 258056 | tf_op jit(solution)/shard_map/ppermute | solution.py:496
  78.9 2.7 %collective-permute-start.24 = (s16[336,128]{1,0:T(8,128)(2,1)S(1)}, s16[336,128]{1,0:T(8,128)(2,1)S(1)}, u32[]{:S(2)}, u32[]{:S(2)}) collective-permute-start(s16[336,128]{1,0:T(8,128)(2,1)S(1)} %get-tuple-element.55), channel_id=1, source_target_pairs={{0,2},{1,3},{2,0},{3,1},{4,6},{5,7},{6,4},{7,5},{8,10},{9,11},{10,... | collective-permute-start | bytes 258056 | tf_op jit(solution)/shard_map/ppermute | solution.py:496

commit v10 on v9

--- a/solution.py
+++ b/solution.py
@@ -402,10 +402,10 @@
     pieces, out, full, sems = refs[:count], refs[count], refs[count + 1], refs[count + 2]
     _, _, rows, lanes = full.shape
     copies = []
-    for i, piece in enumerate(pieces):
-        if len(piece.shape) == 3:
-            full[i] = piece[...]
-        else:
+    for i, piece in sorted(enumerate(pieces), key=lambda at: len(at[1].shape) != 3):
+        source = piece
+        if len(piece.shape) != 3:
+            source = full.at[i]
             strips = 2 * lanes // LANES
             table = scales(piece[strips * rows :, :])
             for strip in range(strips):
@@ -416,7 +416,7 @@
                 )
         d, bits = order[i]
         slot = column[(where[4] ^ d) * slots + where[bits]]
-        copies.append(pltpu.make_async_copy(full.at[i], out.at[slot], sems.at[i]))
+        copies.append(pltpu.make_async_copy(source, out.at[slot], sems.at[i]))
         copies[-1].start()
     for copy in copies:
         copy.wait()

time: 83.5 us -> 83.4 us (level)
  no operation moved by 1% of the time
where the time goes in v10:
time: 83.4 us; the launch traced here: 83.3 us
  starting transfers between devices  34.8 us (42%)
  waiting for transfers between devices  26.2 us (31%)
  Pallas kernels  18.7 us (22%)
  local copies, waits for them, and re-layouts  3.45 us (4%)
    ppermute x25, starting transfers between devices, swap(): return lax.ppermute(x, ('term', 'wave'), pairs)  34.8 us
    ppermute x25, waiting for transfers between devices, swap(): return lax.ppermute(x, ('term', 'wave'), pairs)  26.2 us
    pallas_call x3, Pallas kernels, share(): pl.pallas_call(functools.partial(share_kernel, len(after)), out_shape=out...  5.27 us
    pallas_call x2, Pallas kernels, product(): pl.pallas_call(functools.partial(product_kernel, count, kept, len(after))...  3.86 us
    pallas_call x1, Pallas kernels, operator(): pl.pallas_call(own_kernel, out_shape=jax.ShapeDtypeStruct((tiles, 2, size...  2.91 us
    squeeze x1, local copies, waits for them, and re-layouts, shards(): lax.dynamic_index_in_dim(inverse, turned ^ bits, 1, keepdims=False)  2.36 us
    pallas_call x1, Pallas kernels, synthesis(): pl.pallas_call(functools.partial(synthesis_kernel, bands, [len(parts) for...  2.09 us
  transfers between devices with their start and end apart: 25, of which 10 were waited for; matrix products, arithmetic and copies ran while one was open for 0% of the time, Pallas kernels for 18%

profile of v10, /device:TPU:0, one launch (start us, length us, event | category | flops | bytes accessed | tf_op | source)
XLA Modules:
  0.0 83.3 jit_solution(11798797797349140802)
XLA Ops:
  0.0 0.5 collective-permute-start
  0.5 0.1 stack.23.where
  0.5 1.0 %copy-done.1 = bf16[4,32,1280]{2,1,0:T(8,128)(2,1)S(1)} copy-done((bf16[4,32,1280]{2,1,0:T(8,128)(2,1)S(1)}, bf16[4,32,1280]{2,1,0:T(8,128)(2,1)}, u32[]{:S(2)}) %copy-start.1) | copy-done | bytes 327704
  1.5 0.6 pick.1
  2.1 0.0 collective-permute-done.w_got
  2.1 0.0 copy-start
  2.1 0.0 copy-start.2
  2.1 2.4 %dynamic-slice_bitcast_fusion = (bf16[1,2,640,640]{3,2,1,0:T(8,128)(2,1)S(1)}, bf16[1,2,640,640]{3,2,1,0:T(8,128)(2,1)S(1)}) fusion(bf16[1,4,2,640,640]{4,3,2,1,0:T(8,128)(2,1)} %own.7, s32[]{:T(128)S(6)} %select_n.16, s32[]{:T(128)S(6)} %select_n.15), kind=kLoop, calls=%fused_computation | loop fusion | bytes 6553608 | tf_op jit(solution)/shard_map/jit(dynamic_index_in_dim)/squeeze | solution.py:507
  4.5 0.1 collective-permute-start.4
  4.6 0.5 collective-permute-start.8
  5.1 0.1 collective-permute-start.1
  5.2 2.9 %collective-permute-start.2 = (bf16[32,1280]{1,0:T(8,128)(2,1)S(1)}, bf16[32,1280]{1,0:T(8,128)(2,1)S(1)}, u32[]{:S(2)}, u32[]{:S(2)}) collective-permute-start(bf16[32,1280]{1,0:T(8,128)(2,1)S(1)} %get-tuple-element.37), channel_id=1, source_target_pairs={{0,4},{1,5},{2,6},{3,7},{4,0},{5,1},{6,2},{7,3},{8,12},{9,13},{10,... | collective-permute-start | bytes 245768 | tf_op jit(solution)/shard_map/ppermute | solution.py:496
  8.1 0.0 collective-permute-start.3
  8.1 0.0 collective-permute-done.4.got
  8.1 1.9 %share.3.refs_4_.refs_0_ = s16[2576,128]{1,0:T(8,128)(2,1)S(1)} custom-call(s32[5]{0:T(128)S(1)} %stack.23.where, f32[1,2]{1,0:T(1,128)S(1)} %copy-done.2, f32[1,2]{1,0:T(1,128)S(1)} %collective-permute-done.w_got, bf16[1,4,2,640,640]{4,3,2,1,0:T(8,128)(2,1)S(1)} %copy-done, bf16[1,2,640,640]{3,2,1,0:T(8,128)(2,1)S(1)} %collective-permute-done.4.got), custom_call_target="tpu_custom_call" | custom-call | flops 5242880 | bytes 2621440 | tf_op jit(solution)/shard_map/share/pallas_call | solution.py:91
  10.1 2.7 %collective-permute-start.9 = (s16[2576,128]{1,0:T(8,128)(2,1)S(1)}, s16[2576,128]{1,0:T(8,128)(2,1)S(1)}, u32[]{:S(2)}, u32[]{:S(2)}) collective-permute-start(s16[2576,128]{1,0:T(8,128)(2,1)S(1)} %share.3.refs_4_.refs_0_), channel_id=1, source_target_pairs={{0,4},{1,5},{2,6},{3,7},{4,0},{5,1},{6,2},{7,3},{8,12},{9,13},{10,... | collective-permute-start | bytes 1978376 | tf_op jit(solution)/shard_map/ppermute | solution.py:496
  12.8 0.0 collective-permute-done.1.refs_1_
  12.8 0.0 collective-permute-done.2.refs_2_
  12.8 0.1 collective-permute-done.3.refs_3_
  12.9 3.7 %collective-permute-start.5 = (bf16[128,1280]{1,0:T(8,128)(2,1)S(1)}, bf16[128,1280]{1,0:T(8,128)(2,1)S(1)}, u32[]{:S(2)}, u32[]{:S(2)}) collective-permute-start(bf16[128,1280]{1,0:T(8,128)(2,1)S(1)} %join.1.refs_0_), channel_id=1, source_target_pairs={{0,24},{1,25},{2,26},{3,27},{4,28},{5,29},{6,30},{7,31},{8,16},{9,... | collective-permute-start | bytes 983048 | tf_op jit(solution)/shard_map/ppermute | solution.py:496
  16.5 2.9 %operator.1.refs_1_.own = f32[5,2,640,128]{3,2,1,0:T(8,128)S(1)} custom-call(s32[5]{0:T(128)S(1)} %stack.23.where, f32[1,2]{1,0:T(1,128)S(1)} %copy-done.2, f32[1,2]{1,0:T(1,128)S(1)} %collective-permute-done.w_got, bf16[1,4,2,640,640]{4,3,2,1,0:T(8,128)(2,1)S(1)} %copy-done, bf16[1,2,640,640]{3,2,1,0:T(8,128)(2,1)S(1)} %collective-permute-done.8.got), custom_call_target="tpu_custom_call" | custom-call | flops 13107200 | bytes 6553600 | tf_op jit(solution)/shard_map/operator/pallas_call | solution.py:126
  19.4 1.4 %share.4.refs_0_ = s16[1296,128]{1,0:T(8,128)(2,1)S(1)} custom-call(s32[5]{0:T(128)S(1)} %stack.23.where, f32[1,2]{1,0:T(1,128)S(1)} %copy-done.2, f32[1,2]{1,0:T(1,128)S(1)} %collective-permute-done.w_got, bf16[1,4,2,640,640]{4,3,2,1,0:T(8,128)(2,1)S(1)} %copy-done, bf16[1,2,640,640]{3,2,1,0:T(8,128)(2,1)S(1)} %collective-permute-done.4.got, ...), custom_call_target="tpu_custom_call" | custom-call | flops 2621440 | bytes 1310720 | tf_op jit(solution)/shard_map/share/pallas_call | solution.py:91
  20.8 0.6 collective-permute-start.10
  21.5 0.0 collective-permute-start.6
  21.5 3.8 %collective-permute-done.5.refs_1_ = bf16[128,1280]{1,0:T(8,128)(2,1)S(1)} collective-permute-done((bf16[128,1280]{1,0:T(8,128)(2,1)S(1)}, bf16[128,1280]{1,0:T(8,128)(2,1)S(1)}, u32[]{:S(2)}, u32[]{:S(2)}) %collective-permute-start.5) | collective-permute-done | bytes 327712 | tf_op jit(solution)/shard_map/ppermute | solution.py:496
  25.3 5.9 %collective-permute-start.7 = (bf16[128,1280]{1,0:T(8,128)(2,1)S(1)}, bf16[128,1280]{1,0:T(8,128)(2,1)S(1)}, u32[]{:S(2)}, u32[]{:S(2)}) collective-permute-start(bf16[128,1280]{1,0:T(8,128)(2,1)S(1)} %collective-permute-done.5.refs_1_), channel_id=1, source_target_pairs={{0,8},{1,9},{2,10},{3,11},{4,12},{5,13},{6,14},{7,15},{8,0},{9,1},... | collective-permute-start | bytes 983048 | tf_op jit(solution)/shard_map/ppermute | solution.py:496
  31.2 1.9 %share.5 = s16[2576,128]{1,0:T(8,128)(2,1)S(1)} custom-call(s32[5]{0:T(128)S(1)} %stack.23.where, f32[1,2]{1,0:T(1,128)S(1)} %copy-done.2, f32[1,2]{1,0:T(1,128)S(1)} %collective-permute-done.w_got, bf16[1,4,2,640,640]{4,3,2,1,0:T(8,128)(2,1)S(1)} %copy-done, bf16[1,2,640,640]{3,2,1,0:T(8,128)(2,1)S(1)} %collective-permute-done.4.got, ...), custom_call_target="tpu_custom_call" | custom-call | flops 5242880 | bytes 2621440 | tf_op jit(solution)/shard_map/share/pallas_call | solution.py:91
  33.2 1.3 %collective-permute-start.11 = (s16[2576,128]{1,0:T(8,128)(2,1)S(1)}, s16[2576,128]{1,0:T(8,128)(2,1)S(1)}, u32[]{:S(2)}, u32[]{:S(2)}) collective-permute-start(s16[2576,128]{1,0:T(8,128)(2,1)S(1)} %share.5), channel_id=1, source_target_pairs={{0,4},{1,5},{2,6},{3,7},{4,0},{5,1},{6,2},{7,3},{8,12},{9,13},{10,... | collective-permute-start | bytes 1978376 | tf_op jit(solution)/shard_map/ppermute | solution.py:496
  34.4 1.1 %collective-permute-done.10.refs_1_ = s16[1296,128]{1,0:T(8,128)(2,1)S(1)} collective-permute-done((s16[1296,128]{1,0:T(8,128)(2,1)S(1)}, s16[1296,128]{1,0:T(8,128)(2,1)S(1)}, u32[]{:S(2)}, u32[]{:S(2)}) %collective-permute-start.10) | collective-permute-done | bytes 331808 | tf_op jit(solution)/shard_map/ppermute | solution.py:496
  35.5 0.8 build.2.refs_4_
  36.3 0.0 collective-permute-done.6.refs_2_
  36.3 2.5 %collective-permute-done.7.refs_3_ = bf16[128,1280]{1,0:T(8,128)(2,1)S(1)} collective-permute-done((bf16[128,1280]{1,0:T(8,128)(2,1)S(1)}, bf16[128,1280]{1,0:T(8,128)(2,1)S(1)}, u32[]{:S(2)}, u32[]{:S(2)}) %collective-permute-start.7) | collective-permute-done | bytes 327712 | tf_op jit(solution)/shard_map/ppermute | solution.py:496
  38.8 2.3 %product.2 = (f32[3,128,256]{2,1,0:T(8,128)S(1)}, f32[3,128,256]{2,1,0:T(8,128)S(1)}, s16[784,128]{1,0:T(8,128)(2,1)S(1)}, s16[784,128]{1,0:T(8,128)(2,1)S(1)}) custom-call(bf16[128,1280]{1,0:T(8,128)(2,1)S(1)} %join.1.refs_0_, bf16[128,1280]{1,0:T(8,128)(2,1)S(1)} %collective-permute-done.5.refs_1_, bf16[128,1280]{1,0:T(8,128)(2,1)S(1)} %collective-permute-done.6.refs_2_, ...), custom_call_target="tpu_custom_call" | custom-call | flops 2013265920 | bytes 5242880 | tf_op jit(solution)/shard_map/product/pallas_call | solution.py:237
  41.1 1.6 %collective-permute-start.12 = (s16[784,128]{1,0:T(8,128)(2,1)S(1)}, s16[784,128]{1,0:T(8,128)(2,1)S(1)}, u32[]{:S(2)}, u32[]{:S(2)}) collective-permute-start(s16[784,128]{1,0:T(8,128)(2,1)S(1)} %get-tuple-element.43), channel_id=1, source_target_pairs={{0,8},{1,9},{2,10},{3,11},{4,12},{5,13},{6,14},{7,15},{8,0},{9,1},... | collective-permute-start | bytes 602120 | tf_op jit(solution)/shard_map/ppermute | solution.py:496
  42.7 0.5 collective-permute-start.13
  43.2 5.9 %collective-permute-done.12.got = s16[784,128]{1,0:T(8,128)(2,1)S(1)} collective-permute-done((s16[784,128]{1,0:T(8,128)(2,1)S(1)}, s16[784,128]{1,0:T(8,128)(2,1)S(1)}, u32[]{:S(2)}, u32[]{:S(2)}) %collective-permute-start.12) | collective-permute-done | bytes 200736 | tf_op jit(solution)/shard_map/ppermute | solution.py:496
  49.1 0.1 fold.2.refs_1_
  49.2 0.0 slice-start.1
  49.2 3.3 %collective-permute-start.14 = (s16[784,128]{1,0:T(8,128)(2,1)S(1)}, s16[784,128]{1,0:T(8,128)(2,1)S(1)}, u32[]{:S(2)}, u32[]{:S(2)}) collective-permute-start(s16[784,128]{1,0:T(8,128)(2,1)S(1)} %fold.2.refs_1_), channel_id=1, source_target_pairs={{0,24},{1,25},{2,26},{3,27},{4,28},{5,29},{6,30},{7,31},{8,16},{9,... | collective-permute-start | bytes 602120 | tf_op jit(solution)/shard_map/ppermute | solution.py:496
  52.6 0.5 build.3.refs_4_
  53.1 1.6 %product.3 = (f32[2,128,256]{2,1,0:T(8,128)S(1)}, f32[2,128,256]{2,1,0:T(8,128)S(1)}, s16[528,128]{1,0:T(8,128)(2,1)S(1)}, s16[528,128]{1,0:T(8,128)(2,1)S(1)}) custom-call(bf16[128,1280]{1,0:T(8,128)(2,1)S(1)} %join.1.refs_0_, bf16[128,1280]{1,0:T(8,128)(2,1)S(1)} %collective-permute-done.5.refs_1_, bf16[128,1280]{1,0:T(8,128)(2,1)S(1)} %collective-permute-done.6.refs_2_, ...), custom_call_target="tpu_custom_call" | custom-call | flops 1342177280 | bytes 3932160 | tf_op jit(solution)/shard_map/product/pallas_call | solution.py:237
  54.7 0.1 collective-permute-start.15
  54.8 2.0 %collective-permute-start.17 = (s16[528,128]{1,0:T(8,128)(2,1)S(1)}, s16[528,128]{1,0:T(8,128)(2,1)S(1)}, u32[]{:S(2)}, u32[]{:S(2)}) collective-permute-start(s16[528,128]{1,0:T(8,128)(2,1)S(1)} %get-tuple-element.48), channel_id=1, source_target_pairs={{0,8},{1,9},{2,10},{3,11},{4,12},{5,13},{6,14},{7,15},{8,0},{9,1},... | collective-permute-start | bytes 405512 | tf_op jit(solution)/shard_map/ppermute | solution.py:496
  56.8 4.9 %collective-permute-done.15.got = s16[528,128]{1,0:T(8,128)(2,1)S(1)} collective-permute-done((s16[528,128]{1,0:T(8,128)(2,1)S(1)}, s16[528,128]{1,0:T(8,128)(2,1)S(1)}, u32[]{:S(2)}, u32[]{:S(2)}) %collective-permute-start.15) | collective-permute-done | bytes 135200 | tf_op jit(solution)/shard_map/ppermute | solution.py:496
  61.7 0.0 collective-permute-done.14.refs_0_.refs_2_
  61.7 0.1 fold.3
  61.8 3.3 %collective-permute-start.16 = (s16[528,128]{1,0:T(8,128)(2,1)S(1)}, s16[528,128]{1,0:T(8,128)(2,1)S(1)}, u32[]{:S(2)}, u32[]{:S(2)}) collective-permute-start(s16[528,128]{1,0:T(8,128)(2,1)S(1)} %fold.3), channel_id=1, source_target_pairs={{0,24},{1,25},{2,26},{3,27},{4,28},{5,29},{6,30},{7,31},{8,16},{9,... | collective-permute-start | bytes 405512 | tf_op jit(solution)/shard_map/ppermute | solution.py:496
  65.1 0.8 table.1.refs_6_
  65.9 0.0 copy-start.3
  65.9 0.0 collective-permute-done.17.refs_5_
  65.9 2.9 %collective-permute-done.16.refs_4_ = s16[528,128]{1,0:T(8,128)(2,1)S(1)} collective-permute-done((s16[528,128]{1,0:T(8,128)(2,1)S(1)}, s16[528,128]{1,0:T(8,128)(2,1)S(1)}, u32[]{:S(2)}, u32[]{:S(2)}) %collective-permute-start.16) | collective-permute-done | bytes 135200 | tf_op jit(solution)/shard_map/ppermute | solution.py:496
  68.8 2.1 %synthesis.1 = (f32[2,32,640]{2,1,0:T(8,128)S(1)}, s16[336,128]{1,0:T(8,128)(2,1)S(1)}, s16[336,128]{1,0:T(8,128)(2,1)S(1)}, s16[336,128]{1,0:T(8,128)(2,1)S(1)}...) custom-call(s32[5]{0:T(128)S(1)} %stack.23.where, ...), custom_call_target="tpu_custom_call" | custom-call | flops 838860800 | bytes 2949120 | tf_op jit(solution)/shard_map/synthesis/pallas_call | solution.py:356
  70.9 2.2 %collective-permute-start.18 = (s16[336,128]{1,0:T(8,128)(2,1)S(1)}, s16[336,128]{1,0:T(8,128)(2,1)S(1)}, u32[]{:S(2)}, u32[]{:S(2)}) collective-permute-start(s16[336,128]{1,0:T(8,128)(2,1)S(1)} %get-tuple-element.49), channel_id=1, source_target_pairs={{0,5},{1,4},{2,7},{3,6},{4,1},{5,0},{6,3},{7,2},{8,13},{9,12},{10,... | collective-permute-start | bytes 258056 | tf_op jit(solution)/shard_map/ppermute | solution.py:496
  73.1 0.0 collective-permute-start.19
  73.1 0.5 collective-permute-start.20
  73.6 1.7 %collective-permute-start.21 = (s16[336,128]{1,0:T(8,128)(2,1)S(1)}, s16[336,128]{1,0:T(8,128)(2,1)S(1)}, u32[]{:S(2)}, u32[]{:S(2)}) collective-permute-start(s16[336,128]{1,0:T(8,128)(2,1)S(1)} %get-tuple-element.52), channel_id=1, source_target_pairs={{0,3},{1,2},{2,1},{3,0},{4,7},{5,6},{6,5},{7,4},{8,11},{9,10},{10,... | collective-permute-start | bytes 258056 | tf_op jit(solution)/shard_map/ppermute | solution.py:496
  75.3 1.2 %collective-permute-start.22 = (s16[336,128]{1,0:T(8,128)(2,1)S(1)}, s16[336,128]{1,0:T(8,128)(2,1)S(1)}, u32[]{:S(2)}, u32[]{:S(2)}) collective-permute-start(s16[336,128]{1,0:T(8,128)(2,1)S(1)} %get-tuple-element.53), channel_id=1, source_target_pairs={{0,4},{1,5},{2,6},{3,7},{4,0},{5,1},{6,2},{7,3},{8,12},{9,13},{10,... | collective-permute-start | bytes 258056 | tf_op jit(solution)/shard_map/ppermute | solution.py:496
  76.6 0.0 collective-permute-start.23
  76.6 2.3 %collective-permute-done.19.refs_1_ = s16[336,128]{1,0:T(8,128)(2,1)S(1)} collective-permute-done((s16[336,128]{1,0:T(8,128)(2,1)S(1)}, s16[336,128]{1,0:T(8,128)(2,1)S(1)}, u32[]{:S(2)}, u32[]{:S(2)}) %collective-permute-start.19) | collective-permute-done | bytes 86048 | tf_op jit(solution)/shard_map/ppermute | solution.py:496
  78.9 0.7 collective-permute-done.20.refs_2_
  79.5 2.1 %collective-permute-done.21.refs_3_ = s16[336,128]{1,0:T(8,128)(2,1)S(1)} collective-permute-done((s16[336,128]{1,0:T(8,128)(2,1)S(1)}, s16[336,128]{1,0:T(8,128)(2,1)S(1)}, u32[]{:S(2)}, u32[]{:S(2)}) %collective-permute-start.21) | collective-permute-done | bytes 86048 | tf_op jit(solution)/shard_map/ppermute | solution.py:496
  81.6 0.0 collective-permute-done.22.refs_4_
  81.6 0.0 collective-permute-done.23.refs_5_
  81.6 1.7 %place.1 = f32[8,2,32,640]{3,2,1,0:T(8,128)} custom-call(s32[5]{0:T(128)S(1)} %stack.23.where, s32[8]{0:T(128)S(1)} %copy-done.3, s16[336,128]{1,0:T(8,128)(2,1)S(1)} %collective-permute-done.18.refs_0_, s16[336,128]{1,0:T(8,128)(2,1)S(1)} %collective-permute-done.19.refs_1_, s16[336,128]{1,0:T(8,128)(2,1)S(1)} %collective-permute-done.20.refs_2_, ...), custom_call_target="tpu_custom_call" | custom-call | tf_op jit(solution)/shard_map/place/pallas_call | solution.py:429
  (16 shorter events, 0.1 us)
Async XLA Ops:
  0.0 2.1 %collective-permute-start = (f32[1,2]{1,0:T(1,128)}, f32[1,2]{1,0:T(1,128)S(1)}, u32[]{:S(2)}, u32[]{:S(2)}) collective-permute-start(f32[1,2]{1,0:T(1,128)} %w_own.7), channel_id=1, source_target_pairs={{0,2},{1,3},{2,0},{3,1},{4,6},{5,7},{6,4},{7,5},{8,10},{9,11},{10,... | collective-permute-start | bytes 32 | tf_op jit(solution)/shard_map/ppermute | solution.py:496
  0.5 1.0 %copy-start.1 = (bf16[4,32,1280]{2,1,0:T(8,128)(2,1)S(1)}, bf16[4,32,1280]{2,1,0:T(8,128)(2,1)}, u32[]{:S(2)}) copy-start(bf16[4,32,1280]{2,1,0:T(8,128)(2,1)} %refs_3_.1) | copy-start | bytes 983044
  2.1 6.0 %copy-start = (bf16[1,4,2,640,640]{4,3,2,1,0:T(8,128)(2,1)S(1)}, bf16[1,4,2,640,640]{4,3,2,1,0:T(8,128)(2,1)}, u32[]{:S(2)}) copy-start(bf16[1,4,2,640,640]{4,3,2,1,0:T(8,128)(2,1)} %own.7) | copy-start | bytes 19660804
  2.1 6.0 %copy-start.2 = (f32[1,2]{1,0:T(1,128)S(1)}, f32[1,2]{1,0:T(1,128)}, u32[]{:S(2)}) copy-start(f32[1,2]{1,0:T(1,128)} %w_own.7) | copy-start | bytes 28
  4.5 3.6 %collective-permute-start.4 = (bf16[1,2,640,640]{3,2,1,0:T(8,128)(2,1)S(1)}, bf16[1,2,640,640]{3,2,1,0:T(8,128)(2,1)S(1)}, u32[]{:S(2)}, u32[]{:S(2)}) collective-permute-start(bf16[1,2,640,640]{3,2,1,0:T(8,128)(2,1)S(1)} %get-tuple-element.58), channel_id=1, source_target_pairs={{0,2},{1,3},{2,0},{3,1},{4,6},{5,7},{6,4},{7,5},{8,10},{9,11},{10,... | collective-permute-start | bytes 4915208 | tf_op jit(solution)/shard_map/ppermute | solution.py:496
  4.6 11.9 %collective-permute-start.8 = (bf16[1,2,640,640]{3,2,1,0:T(8,128)(2,1)S(1)}, bf16[1,2,640,640]{3,2,1,0:T(8,128)(2,1)S(1)}, u32[]{:S(2)}, u32[]{:S(2)}) collective-permute-start(bf16[1,2,640,640]{3,2,1,0:T(8,128)(2,1)S(1)} %get-tuple-element.57), channel_id=1, source_target_pairs={{0,2},{1,3},{2,0},{3,1},{4,6},{5,7},{6,4},{7,5},{8,10},{9,11},{10,... | collective-permute-start | bytes 4915208 | tf_op jit(solution)/shard_map/ppermute | solution.py:496
  5.1 7.7 %collective-permute-start.1 = (bf16[32,1280]{1,0:T(8,128)(2,1)S(1)}, bf16[32,1280]{1,0:T(8,128)(2,1)S(1)}, u32[]{:S(2)}, u32[]{:S(2)}) collective-permute-start(bf16[32,1280]{1,0:T(8,128)(2,1)S(1)} %get-tuple-element.36), channel_id=1, source_target_pairs={{0,2},{1,3},{2,0},{3,1},{4,6},{5,7},{6,4},{7,5},{8,10},{9,11},{10,... | collective-permute-start | bytes 245768 | tf_op jit(solution)/shard_map/ppermute | solution.py:496
  5.2 7.6 %collective-permute-start.2 = (bf16[32,1280]{1,0:T(8,128)(2,1)S(1)}, bf16[32,1280]{1,0:T(8,128)(2,1)S(1)}, u32[]{:S(2)}, u32[]{:S(2)}) collective-permute-start(bf16[32,1280]{1,0:T(8,128)(2,1)S(1)} %get-tuple-element.37), channel_id=1, source_target_pairs={{0,4},{1,5},{2,6},{3,7},{4,0},{5,1},{6,2},{7,3},{8,12},{9,13},{10,... | collective-permute-start | bytes 245768 | tf_op jit(solution)/shard_map/ppermute | solution.py:496
  8.1 4.7 %collective-permute-start.3 = (bf16[32,1280]{1,0:T(8,128)(2,1)S(1)}, bf16[32,1280]{1,0:T(8,128)(2,1)S(1)}, u32[]{:S(2)}, u32[]{:S(2)}) collective-permute-start(bf16[32,1280]{1,0:T(8,128)(2,1)S(1)} %get-tuple-element.38), channel_id=1, source_target_pairs={{0,6},{1,7},{2,4},{3,5},{4,2},{5,3},{6,0},{7,1},{8,14},{9,15},{10,... | collective-permute-start | bytes 245768 | tf_op jit(solution)/shard_map/ppermute | solution.py:496
  10.1 25.5 %collective-permute-start.9 = (s16[2576,128]{1,0:T(8,128)(2,1)S(1)}, s16[2576,128]{1,0:T(8,128)(2,1)S(1)}, u32[]{:S(2)}, u32[]{:S(2)}) collective-permute-start(s16[2576,128]{1,0:T(8,128)(2,1)S(1)} %share.3.refs_4_.refs_0_), channel_id=1, source_target_pairs={{0,4},{1,5},{2,6},{3,7},{4,0},{5,1},{6,2},{7,3},{8,12},{9,13},{10,... | collective-permute-start | bytes 1978376 | tf_op jit(solution)/shard_map/ppermute | solution.py:496
  12.9 12.5 %collective-permute-start.5 = (bf16[128,1280]{1,0:T(8,128)(2,1)S(1)}, bf16[128,1280]{1,0:T(8,128)(2,1)S(1)}, u32[]{:S(2)}, u32[]{:S(2)}) collective-permute-start(bf16[128,1280]{1,0:T(8,128)(2,1)S(1)} %join.1.refs_0_), channel_id=1, source_target_pairs={{0,24},{1,25},{2,26},{3,27},{4,28},{5,29},{6,30},{7,31},{8,16},{9,... | collective-permute-start | bytes 983048 | tf_op jit(solution)/shard_map/ppermute | solution.py:496
  20.8 14.7 %collective-permute-start.10 = (s16[1296,128]{1,0:T(8,128)(2,1)S(1)}, s16[1296,128]{1,0:T(8,128)(2,1)S(1)}, u32[]{:S(2)}, u32[]{:S(2)}) collective-permute-start(s16[1296,128]{1,0:T(8,128)(2,1)S(1)} %share.4.refs_0_), channel_id=1, source_target_pairs={{0,4},{1,5},{2,6},{3,7},{4,0},{5,1},{6,2},{7,3},{8,12},{9,13},{10,... | collective-permute-start | bytes 995336 | tf_op jit(solution)/shard_map/ppermute | solution.py:496
  21.5 14.8 %collective-permute-start.6 = (bf16[128,1280]{1,0:T(8,128)(2,1)S(1)}, bf16[128,1280]{1,0:T(8,128)(2,1)S(1)}, u32[]{:S(2)}, u32[]{:S(2)}) collective-permute-start(bf16[128,1280]{1,0:T(8,128)(2,1)S(1)} %join.1.refs_0_), channel_id=1, source_target_pairs={{0,8},{1,9},{2,10},{3,11},{4,12},{5,13},{6,14},{7,15},{8,0},{9,1},... | collective-permute-start | bytes 983048 | tf_op jit(solution)/shard_map/ppermute | solution.py:496
  25.3 13.5 %collective-permute-start.7 = (bf16[128,1280]{1,0:T(8,128)(2,1)S(1)}, bf16[128,1280]{1,0:T(8,128)(2,1)S(1)}, u32[]{:S(2)}, u32[]{:S(2)}) collective-permute-start(bf16[128,1280]{1,0:T(8,128)(2,1)S(1)} %collective-permute-done.5.refs_1_), channel_id=1, source_target_pairs={{0,8},{1,9},{2,10},{3,11},{4,12},{5,13},{6,14},{7,15},{8,0},{9,1},... | collective-permute-start | bytes 983048 | tf_op jit(solution)/shard_map/ppermute | solution.py:496
  33.2 19.4 %collective-permute-start.11 = (s16[2576,128]{1,0:T(8,128)(2,1)S(1)}, s16[2576,128]{1,0:T(8,128)(2,1)S(1)}, u32[]{:S(2)}, u32[]{:S(2)}) collective-permute-start(s16[2576,128]{1,0:T(8,128)(2,1)S(1)} %share.5), channel_id=1, source_target_pairs={{0,4},{1,5},{2,6},{3,7},{4,0},{5,1},{6,2},{7,3},{8,12},{9,13},{10,... | collective-permute-start | bytes 1978376 | tf_op jit(solution)/shard_map/ppermute | solution.py:496
  41.1 8.0 %collective-permute-start.12 = (s16[784,128]{1,0:T(8,128)(2,1)S(1)}, s16[784,128]{1,0:T(8,128)(2,1)S(1)}, u32[]{:S(2)}, u32[]{:S(2)}) collective-permute-start(s16[784,128]{1,0:T(8,128)(2,1)S(1)} %get-tuple-element.43), channel_id=1, source_target_pairs={{0,8},{1,9},{2,10},{3,11},{4,12},{5,13},{6,14},{7,15},{8,0},{9,1},... | collective-permute-start | bytes 602120 | tf_op jit(solution)/shard_map/ppermute | solution.py:496
  42.7 10.4 %collective-permute-start.13 = (s16[784,128]{1,0:T(8,128)(2,1)S(1)}, s16[784,128]{1,0:T(8,128)(2,1)S(1)}, u32[]{:S(2)}, u32[]{:S(2)}) collective-permute-start(s16[784,128]{1,0:T(8,128)(2,1)S(1)} %get-tuple-element.44), channel_id=1, source_target_pairs={{0,8},{1,9},{2,10},{3,11},{4,12},{5,13},{6,14},{7,15},{8,0},{9,1},... | collective-permute-start | bytes 602120 | tf_op jit(solution)/shard_map/ppermute | solution.py:496
  49.1 16.0 %slice-start = ((s8[6553600]{0:T(1024)(128)(4,1)}), s8[4194304]{0:T(1024)(128)(4,1)S(1)}, s32[]{:S(2)}) async-start(s8[6553600]{0:T(1024)(128)(4,1)} %bitcast.9), calls=%async_computation | async-start | bytes 8388608
  49.2 15.9 %slice-start.1 = ((s8[6553600]{0:T(1024)(128)(4,1)}), s8[2359296]{0:T(1024)(128)(4,1)S(1)}, s32[]{:S(2)}) async-start(s8[6553600]{0:T(1024)(128)(4,1)} %bitcast.9), calls=%async_computation.1 | async-start | bytes 4718592
  49.2 12.5 %collective-permute-start.14 = (s16[784,128]{1,0:T(8,128)(2,1)S(1)}, s16[784,128]{1,0:T(8,128)(2,1)S(1)}, u32[]{:S(2)}, u32[]{:S(2)}) collective-permute-start(s16[784,128]{1,0:T(8,128)(2,1)S(1)} %fold.2.refs_1_), channel_id=1, source_target_pairs={{0,24},{1,25},{2,26},{3,27},{4,28},{5,29},{6,30},{7,31},{8,16},{9,... | collective-permute-start | bytes 602120 | tf_op jit(solution)/shard_map/ppermute | solution.py:496
  54.7 7.0 %collective-permute-start.15 = (s16[528,128]{1,0:T(8,128)(2,1)S(1)}, s16[528,128]{1,0:T(8,128)(2,1)S(1)}, u32[]{:S(2)}, u32[]{:S(2)}) collective-permute-start(s16[528,128]{1,0:T(8,128)(2,1)S(1)} %get-tuple-element.47), channel_id=1, source_target_pairs={{0,8},{1,9},{2,10},{3,11},{4,12},{5,13},{6,14},{7,15},{8,0},{9,1},... | collective-permute-start | bytes 405512 | tf_op jit(solution)/shard_map/ppermute | solution.py:496
  54.8 11.1 %collective-permute-start.17 = (s16[528,128]{1,0:T(8,128)(2,1)S(1)}, s16[528,128]{1,0:T(8,128)(2,1)S(1)}, u32[]{:S(2)}, u32[]{:S(2)}) collective-permute-start(s16[528,128]{1,0:T(8,128)(2,1)S(1)} %get-tuple-element.48), channel_id=1, source_target_pairs={{0,8},{1,9},{2,10},{3,11},{4,12},{5,13},{6,14},{7,15},{8,0},{9,1},... | collective-permute-start | bytes 405512 | tf_op jit(solution)/shard_map/ppermute | solution.py:496
  61.8 6.9 %collective-permute-start.16 = (s16[528,128]{1,0:T(8,128)(2,1)S(1)}, s16[528,128]{1,0:T(8,128)(2,1)S(1)}, u32[]{:S(2)}, u32[]{:S(2)}) collective-permute-start(s16[528,128]{1,0:T(8,128)(2,1)S(1)} %fold.3), channel_id=1, source_target_pairs={{0,24},{1,25},{2,26},{3,27},{4,28},{5,29},{6,30},{7,31},{8,16},{9,... | collective-permute-start | bytes 405512 | tf_op jit(solution)/shard_map/ppermute | solution.py:496
  65.9 15.7 %copy-start.3 = (s32[8]{0:T(128)S(1)}, s32[8]{0:T(128)}, u32[]{:S(2)}) copy-start(s32[8]{0:T(128)} %column.1) | copy-start | bytes 100
  70.9 5.7 %collective-permute-start.18 = (s16[336,128]{1,0:T(8,128)(2,1)S(1)}, s16[336,128]{1,0:T(8,128)(2,1)S(1)}, u32[]{:S(2)}, u32[]{:S(2)}) collective-permute-start(s16[336,128]{1,0:T(8,128)(2,1)S(1)} %get-tuple-element.49), channel_id=1, source_target_pairs={{0,5},{1,4},{2,7},{3,6},{4,1},{5,0},{6,3},{7,2},{8,13},{9,12},{10,... | collective-permute-start | bytes 258056 | tf_op jit(solution)/shard_map/ppermute | solution.py:496
  73.1 5.8 %collective-permute-start.19 = (s16[336,128]{1,0:T(8,128)(2,1)S(1)}, s16[336,128]{1,0:T(8,128)(2,1)S(1)}, u32[]{:S(2)}, u32[]{:S(2)}) collective-permute-start(s16[336,128]{1,0:T(8,128)(2,1)S(1)} %get-tuple-element.50), channel_id=1, source_target_pairs={{0,7},{1,6},{2,5},{3,4},{4,3},{5,2},{6,1},{7,0},{8,15},{9,14},{10,... | collective-permute-start | bytes 258056 | tf_op jit(solution)/shard_map/ppermute | solution.py:496
  73.1 6.4 %collective-permute-start.20 = (s16[336,128]{1,0:T(8,128)(2,1)S(1)}, s16[336,128]{1,0:T(8,128)(2,1)S(1)}, u32[]{:S(2)}, u32[]{:S(2)}) collective-permute-start(s16[336,128]{1,0:T(8,128)(2,1)S(1)} %get-tuple-element.51), channel_id=1, source_target_pairs={{0,1},{1,0},{2,3},{3,2},{4,5},{5,4},{6,7},{7,6},{8,9},{9,8},{10,11... | collective-permute-start | bytes 258056 | tf_op jit(solution)/shard_map/ppermute | solution.py:496
  73.6 8.0 %collective-permute-start.21 = (s16[336,128]{1,0:T(8,128)(2,1)S(1)}, s16[336,128]{1,0:T(8,128)(2,1)S(1)}, u32[]{:S(2)}, u32[]{:S(2)}) collective-permute-start(s16[336,128]{1,0:T(8,128)(2,1)S(1)} %get-tuple-element.52), channel_id=1, source_target_pairs={{0,3},{1,2},{2,1},{3,0},{4,7},{5,6},{6,5},{7,4},{8,11},{9,10},{10,... | collective-permute-start | bytes 258056 | tf_op jit(solution)/shard_map/ppermute | solution.py:496
  75.3 6.3 %collective-permute-start.22 = (s16[336,128]{1,0:T(8,128)(2,1)S(1)}, s16[336,128]{1,0:T(8,128)(2,1)S(1)}, u32[]{:S(2)}, u32[]{:S(2)}) collective-permute-start(s16[336,128]{1,0:T(8,128)(2,1)S(1)} %get-tuple-element.53), channel_id=1, source_target_pairs={{0,4},{1,5},{2,6},{3,7},{4,0},{5,1},{6,2},{7,3},{8,12},{9,13},{10,... | collective-permute-start | bytes 258056 | tf_op jit(solution)/shard_map/ppermute | solution.py:496
  76.6 5.1 %collective-permute-start.23 = (s16[336,128]{1,0:T(8,128)(2,1)S(1)}, s16[336,128]{1,0:T(8,128)(2,1)S(1)}, u32[]{:S(2)}, u32[]{:S(2)}) collective-permute-start(s16[336,128]{1,0:T(8,128)(2,1)S(1)} %get-tuple-element.54), channel_id=1, source_target_pairs={{0,6},{1,7},{2,4},{3,5},{4,2},{5,3},{6,0},{7,1},{8,14},{9,15},{10,... | collective-permute-start | bytes 258056 | tf_op jit(solution)/shard_map/ppermute | solution.py:496
  78.9 2.7 %collective-permute-start.24 = (s16[336,128]{1,0:T(8,128)(2,1)S(1)}, s16[336,128]{1,0:T(8,128)(2,1)S(1)}, u32[]{:S(2)}, u32[]{:S(2)}) collective-permute-start(s16[336,128]{1,0:T(8,128)(2,1)S(1)} %get-tuple-element.55), channel_id=1, source_target_pairs={{0,2},{1,3},{2,0},{3,1},{4,6},{5,7},{6,4},{7,5},{8,10},{9,11},{10,... | collective-permute-start | bytes 258056 | tf_op jit(solution)/shard_map/ppermute | solution.py:496

commit v11 on v10

--- a/solution.py
+++ b/solution.py
@@ -324,8 +324,9 @@
     for d in reversed(range(bands)):
         start = pl.multiple_of((where[4] ^ d) * band, LANES)
         columns = table[:, pl.ds(start, band)]
-        grid = jnp.dot(values[0], columns, preferred_element_type=F32)
-        grid += jnp.dot(values[1], columns, preferred_element_type=F32)
+        levels = values[...].reshape(4 * rows, values.shape[2])
+        grid = jnp.dot(levels, columns, preferred_element_type=F32)
+        grid = grid[: 2 * rows] + grid[2 * rows :]
         for side in range(4):
             out = outs[4 * d + side]
             if len(out.shape) == 3:

time: 83.4 us -> 83.3 us (level)
  no operation moved by 1% of the time
where the time goes in v11:
time: 83.3 us; the launch traced here: 83.2 us
  starting transfers between devices  34.8 us (42%)
  waiting for transfers between devices  26.2 us (31%)
  Pallas kernels  18.6 us (22%)
  local copies, waits for them, and re-layouts  3.45 us (4%)
    ppermute x25, starting transfers between devices, swap(): return lax.ppermute(x, ('term', 'wave'), pairs)  34.8 us
    ppermute x25, waiting for transfers between devices, swap(): return lax.ppermute(x, ('term', 'wave'), pairs)  26.2 us
    pallas_call x3, Pallas kernels, share(): pl.pallas_call(functools.partial(share_kernel, len(after)), out_shape=out...  5.27 us
    pallas_call x2, Pallas kernels, product(): pl.pallas_call(functools.partial(product_kernel, count, kept, len(after))...  3.86 us
    pallas_call x1, Pallas kernels, operator(): pl.pallas_call(own_kernel, out_shape=jax.ShapeDtypeStruct((tiles, 2, size...  2.91 us
    squeeze x1, local copies, waits for them, and re-layouts, shards(): lax.dynamic_index_in_dim(inverse, turned ^ bits, 1, keepdims=False)  2.36 us
    pallas_call x1, Pallas kernels, synthesis(): pl.pallas_call(functools.partial(synthesis_kernel, bands, [len(parts) for...  1.99 us
    pallas_call x1, Pallas kernels, place(): pl.pallas_call(functools.partial(place_kernel, count, slots, order), out_...  1.67 us
  transfers between devices with their start and end apart: 25, of which 10 were waited for; matrix products, arithmetic and copies ran while one was open for 0% of the time, Pallas kernels for 18%

profile of v11, /device:TPU:0, one launch (start us, length us, event | category | flops | bytes accessed | tf_op | source)
XLA Modules:
  0.0 83.2 jit_solution(1625515154392568783)
XLA Ops:
  0.0 0.5 collective-permute-start
  0.5 0.1 stack.23.where
  0.5 1.0 %copy-done.1 = bf16[4,32,1280]{2,1,0:T(8,128)(2,1)S(1)} copy-done((bf16[4,32,1280]{2,1,0:T(8,128)(2,1)S(1)}, bf16[4,32,1280]{2,1,0:T(8,128)(2,1)}, u32[]{:S(2)}) %copy-start.1) | copy-done | bytes 327704
  1.5 0.6 pick.1
  2.1 0.0 collective-permute-done.w_got
  2.1 0.0 copy-start
  2.1 0.0 copy-start.2
  2.1 2.4 %dynamic-slice_bitcast_fusion = (bf16[1,2,640,640]{3,2,1,0:T(8,128)(2,1)S(1)}, bf16[1,2,640,640]{3,2,1,0:T(8,128)(2,1)S(1)}) fusion(bf16[1,4,2,640,640]{4,3,2,1,0:T(8,128)(2,1)} %own.7, s32[]{:T(128)S(6)} %select_n.16, s32[]{:T(128)S(6)} %select_n.15), kind=kLoop, calls=%fused_computation | loop fusion | bytes 6553608 | tf_op jit(solution)/shard_map/jit(dynamic_index_in_dim)/squeeze | solution.py:508
  4.5 0.1 collective-permute-start.4
  4.6 0.5 collective-permute-start.8
  5.1 0.1 collective-permute-start.1
  5.2 2.9 %collective-permute-start.2 = (bf16[32,1280]{1,0:T(8,128)(2,1)S(1)}, bf16[32,1280]{1,0:T(8,128)(2,1)S(1)}, u32[]{:S(2)}, u32[]{:S(2)}) collective-permute-start(bf16[32,1280]{1,0:T(8,128)(2,1)S(1)} %get-tuple-element.37), channel_id=1, source_target_pairs={{0,4},{1,5},{2,6},{3,7},{4,0},{5,1},{6,2},{7,3},{8,12},{9,13},{10,... | collective-permute-start | bytes 245768 | tf_op jit(solution)/shard_map/ppermute | solution.py:497
  8.1 1.9 %share.3.refs_4_.refs_0_ = s16[2576,128]{1,0:T(8,128)(2,1)S(1)} custom-call(s32[5]{0:T(128)S(1)} %stack.23.where, f32[1,2]{1,0:T(1,128)S(1)} %copy-done.2, f32[1,2]{1,0:T(1,128)S(1)} %collective-permute-done.w_got, bf16[1,4,2,640,640]{4,3,2,1,0:T(8,128)(2,1)S(1)} %copy-done, bf16[1,2,640,640]{3,2,1,0:T(8,128)(2,1)S(1)} %collective-permute-done.4.got), custom_call_target="tpu_custom_call" | custom-call | flops 5242880 | bytes 2621440 | tf_op jit(solution)/shard_map/share/pallas_call | solution.py:91
  10.1 2.7 %collective-permute-start.9 = (s16[2576,128]{1,0:T(8,128)(2,1)S(1)}, s16[2576,128]{1,0:T(8,128)(2,1)S(1)}, u32[]{:S(2)}, u32[]{:S(2)}) collective-permute-start(s16[2576,128]{1,0:T(8,128)(2,1)S(1)} %share.3.refs_4_.refs_0_), channel_id=1, source_target_pairs={{0,4},{1,5},{2,6},{3,7},{4,0},{5,1},{6,2},{7,3},{8,12},{9,13},{10,... | collective-permute-start | bytes 1978376 | tf_op jit(solution)/shard_map/ppermute | solution.py:497
  12.8 0.0 collective-permute-done.1.refs_1_
  12.8 0.0 collective-permute-done.2.refs_2_
  12.8 0.1 collective-permute-done.3.refs_3_
  12.9 3.7 %collective-permute-start.5 = (bf16[128,1280]{1,0:T(8,128)(2,1)S(1)}, bf16[128,1280]{1,0:T(8,128)(2,1)S(1)}, u32[]{:S(2)}, u32[]{:S(2)}) collective-permute-start(bf16[128,1280]{1,0:T(8,128)(2,1)S(1)} %join.1.refs_0_), channel_id=1, source_target_pairs={{0,24},{1,25},{2,26},{3,27},{4,28},{5,29},{6,30},{7,31},{8,16},{9,... | collective-permute-start | bytes 983048 | tf_op jit(solution)/shard_map/ppermute | solution.py:497
  16.5 2.9 %operator.1.refs_1_.own = f32[5,2,640,128]{3,2,1,0:T(8,128)S(1)} custom-call(s32[5]{0:T(128)S(1)} %stack.23.where, f32[1,2]{1,0:T(1,128)S(1)} %copy-done.2, f32[1,2]{1,0:T(1,128)S(1)} %collective-permute-done.w_got, bf16[1,4,2,640,640]{4,3,2,1,0:T(8,128)(2,1)S(1)} %copy-done, bf16[1,2,640,640]{3,2,1,0:T(8,128)(2,1)S(1)} %collective-permute-done.8.got), custom_call_target="tpu_custom_call" | custom-call | flops 13107200 | bytes 6553600 | tf_op jit(solution)/shard_map/operator/pallas_call | solution.py:126
  19.4 1.4 %share.4.refs_0_ = s16[1296,128]{1,0:T(8,128)(2,1)S(1)} custom-call(s32[5]{0:T(128)S(1)} %stack.23.where, f32[1,2]{1,0:T(1,128)S(1)} %copy-done.2, f32[1,2]{1,0:T(1,128)S(1)} %collective-permute-done.w_got, bf16[1,4,2,640,640]{4,3,2,1,0:T(8,128)(2,1)S(1)} %copy-done, bf16[1,2,640,640]{3,2,1,0:T(8,128)(2,1)S(1)} %collective-permute-done.4.got, ...), custom_call_target="tpu_custom_call" | custom-call | flops 2621440 | bytes 1310720 | tf_op jit(solution)/shard_map/share/pallas_call | solution.py:91
  20.8 0.6 collective-permute-start.10
  21.5 0.0 collective-permute-start.6
  21.5 3.8 %collective-permute-done.5.refs_1_ = bf16[128,1280]{1,0:T(8,128)(2,1)S(1)} collective-permute-done((bf16[128,1280]{1,0:T(8,128)(2,1)S(1)}, bf16[128,1280]{1,0:T(8,128)(2,1)S(1)}, u32[]{:S(2)}, u32[]{:S(2)}) %collective-permute-start.5) | collective-permute-done | bytes 327712 | tf_op jit(solution)/shard_map/ppermute | solution.py:497
  25.3 5.9 %collective-permute-start.7 = (bf16[128,1280]{1,0:T(8,128)(2,1)S(1)}, bf16[128,1280]{1,0:T(8,128)(2,1)S(1)}, u32[]{:S(2)}, u32[]{:S(2)}) collective-permute-start(bf16[128,1280]{1,0:T(8,128)(2,1)S(1)} %collective-permute-done.5.refs_1_), channel_id=1, source_target_pairs={{0,8},{1,9},{2,10},{3,11},{4,12},{5,13},{6,14},{7,15},{8,0},{9,1},... | collective-permute-start | bytes 983048 | tf_op jit(solution)/shard_map/ppermute | solution.py:497
  31.2 1.9 %share.5 = s16[2576,128]{1,0:T(8,128)(2,1)S(1)} custom-call(s32[5]{0:T(128)S(1)} %stack.23.where, f32[1,2]{1,0:T(1,128)S(1)} %copy-done.2, f32[1,2]{1,0:T(1,128)S(1)} %collective-permute-done.w_got, bf16[1,4,2,640,640]{4,3,2,1,0:T(8,128)(2,1)S(1)} %copy-done, bf16[1,2,640,640]{3,2,1,0:T(8,128)(2,1)S(1)} %collective-permute-done.4.got, ...), custom_call_target="tpu_custom_call" | custom-call | flops 5242880 | bytes 2621440 | tf_op jit(solution)/shard_map/share/pallas_call | solution.py:91
  33.2 1.3 %collective-permute-start.11 = (s16[2576,128]{1,0:T(8,128)(2,1)S(1)}, s16[2576,128]{1,0:T(8,128)(2,1)S(1)}, u32[]{:S(2)}, u32[]{:S(2)}) collective-permute-start(s16[2576,128]{1,0:T(8,128)(2,1)S(1)} %share.5), channel_id=1, source_target_pairs={{0,4},{1,5},{2,6},{3,7},{4,0},{5,1},{6,2},{7,3},{8,12},{9,13},{10,... | collective-permute-start | bytes 1978376 | tf_op jit(solution)/shard_map/ppermute | solution.py:497
  34.4 1.1 %collective-permute-done.10.refs_1_ = s16[1296,128]{1,0:T(8,128)(2,1)S(1)} collective-permute-done((s16[1296,128]{1,0:T(8,128)(2,1)S(1)}, s16[1296,128]{1,0:T(8,128)(2,1)S(1)}, u32[]{:S(2)}, u32[]{:S(2)}) %collective-permute-start.10) | collective-permute-done | bytes 331808 | tf_op jit(solution)/shard_map/ppermute | solution.py:497
  35.5 0.8 build.2.refs_4_
  36.3 0.0 collective-permute-done.6.refs_2_
  36.3 2.5 %collective-permute-done.7.refs_3_ = bf16[128,1280]{1,0:T(8,128)(2,1)S(1)} collective-permute-done((bf16[128,1280]{1,0:T(8,128)(2,1)S(1)}, bf16[128,1280]{1,0:T(8,128)(2,1)S(1)}, u32[]{:S(2)}, u32[]{:S(2)}) %collective-permute-start.7) | collective-permute-done | bytes 327712 | tf_op jit(solution)/shard_map/ppermute | solution.py:497
  38.8 2.3 %product.2 = (f32[3,128,256]{2,1,0:T(8,128)S(1)}, f32[3,128,256]{2,1,0:T(8,128)S(1)}, s16[784,128]{1,0:T(8,128)(2,1)S(1)}, s16[784,128]{1,0:T(8,128)(2,1)S(1)}) custom-call(bf16[128,1280]{1,0:T(8,128)(2,1)S(1)} %join.1.refs_0_, bf16[128,1280]{1,0:T(8,128)(2,1)S(1)} %collective-permute-done.5.refs_1_, bf16[128,1280]{1,0:T(8,128)(2,1)S(1)} %collective-permute-done.6.refs_2_, ...), custom_call_target="tpu_custom_call" | custom-call | flops 2013265920 | bytes 5242880 | tf_op jit(solution)/shard_map/product/pallas_call | solution.py:237
  41.1 1.6 %collective-permute-start.12 = (s16[784,128]{1,0:T(8,128)(2,1)S(1)}, s16[784,128]{1,0:T(8,128)(2,1)S(1)}, u32[]{:S(2)}, u32[]{:S(2)}) collective-permute-start(s16[784,128]{1,0:T(8,128)(2,1)S(1)} %get-tuple-element.43), channel_id=1, source_target_pairs={{0,8},{1,9},{2,10},{3,11},{4,12},{5,13},{6,14},{7,15},{8,0},{9,1},... | collective-permute-start | bytes 602120 | tf_op jit(solution)/shard_map/ppermute | solution.py:497
  42.7 0.5 collective-permute-start.13
  43.2 5.9 %collective-permute-done.12.got = s16[784,128]{1,0:T(8,128)(2,1)S(1)} collective-permute-done((s16[784,128]{1,0:T(8,128)(2,1)S(1)}, s16[784,128]{1,0:T(8,128)(2,1)S(1)}, u32[]{:S(2)}, u32[]{:S(2)}) %collective-permute-start.12) | collective-permute-done | bytes 200736 | tf_op jit(solution)/shard_map/ppermute | solution.py:497
  49.1 0.1 fold.2.refs_1_
  49.2 0.0 slice-start.1
  49.2 3.3 %collective-permute-start.14 = (s16[784,128]{1,0:T(8,128)(2,1)S(1)}, s16[784,128]{1,0:T(8,128)(2,1)S(1)}, u32[]{:S(2)}, u32[]{:S(2)}) collective-permute-start(s16[784,128]{1,0:T(8,128)(2,1)S(1)} %fold.2.refs_1_), channel_id=1, source_target_pairs={{0,24},{1,25},{2,26},{3,27},{4,28},{5,29},{6,30},{7,31},{8,16},{9,... | collective-permute-start | bytes 602120 | tf_op jit(solution)/shard_map/ppermute | solution.py:497
  52.6 0.5 build.3.refs_4_
  53.1 1.6 %product.3 = (f32[2,128,256]{2,1,0:T(8,128)S(1)}, f32[2,128,256]{2,1,0:T(8,128)S(1)}, s16[528,128]{1,0:T(8,128)(2,1)S(1)}, s16[528,128]{1,0:T(8,128)(2,1)S(1)}) custom-call(bf16[128,1280]{1,0:T(8,128)(2,1)S(1)} %join.1.refs_0_, bf16[128,1280]{1,0:T(8,128)(2,1)S(1)} %collective-permute-done.5.refs_1_, bf16[128,1280]{1,0:T(8,128)(2,1)S(1)} %collective-permute-done.6.refs_2_, ...), custom_call_target="tpu_custom_call" | custom-call | flops 1342177280 | bytes 3932160 | tf_op jit(solution)/shard_map/product/pallas_call | solution.py:237
  54.7 0.1 collective-permute-start.15
  54.8 2.0 %collective-permute-start.17 = (s16[528,128]{1,0:T(8,128)(2,1)S(1)}, s16[528,128]{1,0:T(8,128)(2,1)S(1)}, u32[]{:S(2)}, u32[]{:S(2)}) collective-permute-start(s16[528,128]{1,0:T(8,128)(2,1)S(1)} %get-tuple-element.48), channel_id=1, source_target_pairs={{0,8},{1,9},{2,10},{3,11},{4,12},{5,13},{6,14},{7,15},{8,0},{9,1},... | collective-permute-start | bytes 405512 | tf_op jit(solution)/shard_map/ppermute | solution.py:497
  56.8 4.9 %collective-permute-done.15.got = s16[528,128]{1,0:T(8,128)(2,1)S(1)} collective-permute-done((s16[528,128]{1,0:T(8,128)(2,1)S(1)}, s16[528,128]{1,0:T(8,128)(2,1)S(1)}, u32[]{:S(2)}, u32[]{:S(2)}) %collective-permute-start.15) | collective-permute-done | bytes 135200 | tf_op jit(solution)/shard_map/ppermute | solution.py:497
  61.7 0.0 collective-permute-done.14.refs_0_.refs_2_
  61.7 0.1 fold.3
  61.8 3.3 %collective-permute-start.16 = (s16[528,128]{1,0:T(8,128)(2,1)S(1)}, s16[528,128]{1,0:T(8,128)(2,1)S(1)}, u32[]{:S(2)}, u32[]{:S(2)}) collective-permute-start(s16[528,128]{1,0:T(8,128)(2,1)S(1)} %fold.3), channel_id=1, source_target_pairs={{0,24},{1,25},{2,26},{3,27},{4,28},{5,29},{6,30},{7,31},{8,16},{9,... | collective-permute-start | bytes 405512 | tf_op jit(solution)/shard_map/ppermute | solution.py:497
  65.1 0.8 table.1.refs_6_
  65.9 0.0 copy-start.3
  65.9 0.0 collective-permute-done.17.refs_5_
  65.9 2.9 %collective-permute-done.16.refs_4_ = s16[528,128]{1,0:T(8,128)(2,1)S(1)} collective-permute-done((s16[528,128]{1,0:T(8,128)(2,1)S(1)}, s16[528,128]{1,0:T(8,128)(2,1)S(1)}, u32[]{:S(2)}, u32[]{:S(2)}) %collective-permute-start.16) | collective-permute-done | bytes 135200 | tf_op jit(solution)/shard_map/ppermute | solution.py:497
  68.8 2.0 %synthesis.1 = (f32[2,32,640]{2,1,0:T(8,128)S(1)}, s16[336,128]{1,0:T(8,128)(2,1)S(1)}, s16[336,128]{1,0:T(8,128)(2,1)S(1)}, s16[336,128]{1,0:T(8,128)(2,1)S(1)}...) custom-call(s32[5]{0:T(128)S(1)} %stack.23.where, ...), custom_call_target="tpu_custom_call" | custom-call | flops 838860800 | bytes 2949120 | tf_op jit(solution)/shard_map/synthesis/pallas_call | solution.py:357
  70.8 2.2 %collective-permute-start.18 = (s16[336,128]{1,0:T(8,128)(2,1)S(1)}, s16[336,128]{1,0:T(8,128)(2,1)S(1)}, u32[]{:S(2)}, u32[]{:S(2)}) collective-permute-start(s16[336,128]{1,0:T(8,128)(2,1)S(1)} %get-tuple-element.49), channel_id=1, source_target_pairs={{0,5},{1,4},{2,7},{3,6},{4,1},{5,0},{6,3},{7,2},{8,13},{9,12},{10,... | collective-permute-start | bytes 258056 | tf_op jit(solution)/shard_map/ppermute | solution.py:497
  73.0 0.5 collective-permute-start.20
  73.5 1.7 %collective-permute-start.21 = (s16[336,128]{1,0:T(8,128)(2,1)S(1)}, s16[336,128]{1,0:T(8,128)(2,1)S(1)}, u32[]{:S(2)}, u32[]{:S(2)}) collective-permute-start(s16[336,128]{1,0:T(8,128)(2,1)S(1)} %get-tuple-element.52), channel_id=1, source_target_pairs={{0,3},{1,2},{2,1},{3,0},{4,7},{5,6},{6,5},{7,4},{8,11},{9,10},{10,... | collective-permute-start | bytes 258056 | tf_op jit(solution)/shard_map/ppermute | solution.py:497
  75.2 1.2 %collective-permute-start.22 = (s16[336,128]{1,0:T(8,128)(2,1)S(1)}, s16[336,128]{1,0:T(8,128)(2,1)S(1)}, u32[]{:S(2)}, u32[]{:S(2)}) collective-permute-start(s16[336,128]{1,0:T(8,128)(2,1)S(1)} %get-tuple-element.53), channel_id=1, source_target_pairs={{0,4},{1,5},{2,6},{3,7},{4,0},{5,1},{6,2},{7,3},{8,12},{9,13},{10,... | collective-permute-start | bytes 258056 | tf_op jit(solution)/shard_map/ppermute | solution.py:497
  76.5 0.0 collective-permute-done.18.refs_0_
  76.5 0.0 collective-permute-start.23
  76.5 2.3 %collective-permute-done.19.refs_1_ = s16[336,128]{1,0:T(8,128)(2,1)S(1)} collective-permute-done((s16[336,128]{1,0:T(8,128)(2,1)S(1)}, s16[336,128]{1,0:T(8,128)(2,1)S(1)}, u32[]{:S(2)}, u32[]{:S(2)}) %collective-permute-start.19) | collective-permute-done | bytes 86048 | tf_op jit(solution)/shard_map/ppermute | solution.py:497
  78.8 0.0 collective-permute-start.24
  78.8 0.7 collective-permute-done.20.refs_2_
  79.4 2.1 %collective-permute-done.21.refs_3_ = s16[336,128]{1,0:T(8,128)(2,1)S(1)} collective-permute-done((s16[336,128]{1,0:T(8,128)(2,1)S(1)}, s16[336,128]{1,0:T(8,128)(2,1)S(1)}, u32[]{:S(2)}, u32[]{:S(2)}) %collective-permute-start.21) | collective-permute-done | bytes 86048 | tf_op jit(solution)/shard_map/ppermute | solution.py:497
  81.5 0.0 collective-permute-done.22.refs_4_
  81.5 0.0 collective-permute-done.23.refs_5_
  81.5 0.0 collective-permute-done.24.refs_6_
  81.5 1.7 %place.1 = f32[8,2,32,640]{3,2,1,0:T(8,128)} custom-call(s32[5]{0:T(128)S(1)} %stack.23.where, s32[8]{0:T(128)S(1)} %copy-done.3, s16[336,128]{1,0:T(8,128)(2,1)S(1)} %collective-permute-done.18.refs_0_, s16[336,128]{1,0:T(8,128)(2,1)S(1)} %collective-permute-done.19.refs_1_, s16[336,128]{1,0:T(8,128)(2,1)S(1)} %collective-permute-done.20.refs_2_, ...), custom_call_target="tpu_custom_call" | custom-call | tf_op jit(solution)/shard_map/place/pallas_call | solution.py:430
  (16 shorter events, 0.1 us)
Async XLA Ops:
  0.0 2.1 %collective-permute-start = (f32[1,2]{1,0:T(1,128)}, f32[1,2]{1,0:T(1,128)S(1)}, u32[]{:S(2)}, u32[]{:S(2)}) collective-permute-start(f32[1,2]{1,0:T(1,128)} %w_own.7), channel_id=1, source_target_pairs={{0,2},{1,3},{2,0},{3,1},{4,6},{5,7},{6,4},{7,5},{8,10},{9,11},{10,... | collective-permute-start | bytes 32 | tf_op jit(solution)/shard_map/ppermute | solution.py:497
  0.5 1.0 %copy-start.1 = (bf16[4,32,1280]{2,1,0:T(8,128)(2,1)S(1)}, bf16[4,32,1280]{2,1,0:T(8,128)(2,1)}, u32[]{:S(2)}) copy-start(bf16[4,32,1280]{2,1,0:T(8,128)(2,1)} %refs_3_.1) | copy-start | bytes 983044
  2.1 6.0 %copy-start = (bf16[1,4,2,640,640]{4,3,2,1,0:T(8,128)(2,1)S(1)}, bf16[1,4,2,640,640]{4,3,2,1,0:T(8,128)(2,1)}, u32[]{:S(2)}) copy-start(bf16[1,4,2,640,640]{4,3,2,1,0:T(8,128)(2,1)} %own.7) | copy-start | bytes 19660804
  2.1 6.0 %copy-start.2 = (f32[1,2]{1,0:T(1,128)S(1)}, f32[1,2]{1,0:T(1,128)}, u32[]{:S(2)}) copy-start(f32[1,2]{1,0:T(1,128)} %w_own.7) | copy-start | bytes 28
  4.5 3.6 %collective-permute-start.4 = (bf16[1,2,640,640]{3,2,1,0:T(8,128)(2,1)S(1)}, bf16[1,2,640,640]{3,2,1,0:T(8,128)(2,1)S(1)}, u32[]{:S(2)}, u32[]{:S(2)}) collective-permute-start(bf16[1,2,640,640]{3,2,1,0:T(8,128)(2,1)S(1)} %get-tuple-element.58), channel_id=1, source_target_pairs={{0,2},{1,3},{2,0},{3,1},{4,6},{5,7},{6,4},{7,5},{8,10},{9,11},{10,... | collective-permute-start | bytes 4915208 | tf_op jit(solution)/shard_map/ppermute | solution.py:497
  4.6 11.9 %collective-permute-start.8 = (bf16[1,2,640,640]{3,2,1,0:T(8,128)(2,1)S(1)}, bf16[1,2,640,640]{3,2,1,0:T(8,128)(2,1)S(1)}, u32[]{:S(2)}, u32[]{:S(2)}) collective-permute-start(bf16[1,2,640,640]{3,2,1,0:T(8,128)(2,1)S(1)} %get-tuple-element.57), channel_id=1, source_target_pairs={{0,2},{1,3},{2,0},{3,1},{4,6},{5,7},{6,4},{7,5},{8,10},{9,11},{10,... | collective-permute-start | bytes 4915208 | tf_op jit(solution)/shard_map/ppermute | solution.py:497
  5.1 7.7 %collective-permute-start.1 = (bf16[32,1280]{1,0:T(8,128)(2,1)S(1)}, bf16[32,1280]{1,0:T(8,128)(2,1)S(1)}, u32[]{:S(2)}, u32[]{:S(2)}) collective-permute-start(bf16[32,1280]{1,0:T(8,128)(2,1)S(1)} %get-tuple-element.36), channel_id=1, source_target_pairs={{0,2},{1,3},{2,0},{3,1},{4,6},{5,7},{6,4},{7,5},{8,10},{9,11},{10,... | collective-permute-start | bytes 245768 | tf_op jit(solution)/shard_map/ppermute | solution.py:497
  5.2 7.6 %collective-permute-start.2 = (bf16[32,1280]{1,0:T(8,128)(2,1)S(1)}, bf16[32,1280]{1,0:T(8,128)(2,1)S(1)}, u32[]{:S(2)}, u32[]{:S(2)}) collective-permute-start(bf16[32,1280]{1,0:T(8,128)(2,1)S(1)} %get-tuple-element.37), channel_id=1, source_target_pairs={{0,4},{1,5},{2,6},{3,7},{4,0},{5,1},{6,2},{7,3},{8,12},{9,13},{10,... | collective-permute-start | bytes 245768 | tf_op jit(solution)/shard_map/ppermute | solution.py:497
  8.1 4.7 %collective-permute-start.3 = (bf16[32,1280]{1,0:T(8,128)(2,1)S(1)}, bf16[32,1280]{1,0:T(8,128)(2,1)S(1)}, u32[]{:S(2)}, u32[]{:S(2)}) collective-permute-start(bf16[32,1280]{1,0:T(8,128)(2,1)S(1)} %get-tuple-element.38), channel_id=1, source_target_pairs={{0,6},{1,7},{2,4},{3,5},{4,2},{5,3},{6,0},{7,1},{8,14},{9,15},{10,... | collective-permute-start | bytes 245768 | tf_op jit(solution)/shard_map/ppermute | solution.py:497
  10.1 25.5 %collective-permute-start.9 = (s16[2576,128]{1,0:T(8,128)(2,1)S(1)}, s16[2576,128]{1,0:T(8,128)(2,1)S(1)}, u32[]{:S(2)}, u32[]{:S(2)}) collective-permute-start(s16[2576,128]{1,0:T(8,128)(2,1)S(1)} %share.3.refs_4_.refs_0_), channel_id=1, source_target_pairs={{0,4},{1,5},{2,6},{3,7},{4,0},{5,1},{6,2},{7,3},{8,12},{9,13},{10,... | collective-permute-start | bytes 1978376 | tf_op jit(solution)/shard_map/ppermute | solution.py:497
  12.9 12.5 %collective-permute-start.5 = (bf16[128,1280]{1,0:T(8,128)(2,1)S(1)}, bf16[128,1280]{1,0:T(8,128)(2,1)S(1)}, u32[]{:S(2)}, u32[]{:S(2)}) collective-permute-start(bf16[128,1280]{1,0:T(8,128)(2,1)S(1)} %join.1.refs_0_), channel_id=1, source_target_pairs={{0,24},{1,25},{2,26},{3,27},{4,28},{5,29},{6,30},{7,31},{8,16},{9,... | collective-permute-start | bytes 983048 | tf_op jit(solution)/shard_map/ppermute | solution.py:497
  20.8 14.7 %collective-permute-start.10 = (s16[1296,128]{1,0:T(8,128)(2,1)S(1)}, s16[1296,128]{1,0:T(8,128)(2,1)S(1)}, u32[]{:S(2)}, u32[]{:S(2)}) collective-permute-start(s16[1296,128]{1,0:T(8,128)(2,1)S(1)} %share.4.refs_0_), channel_id=1, source_target_pairs={{0,4},{1,5},{2,6},{3,7},{4,0},{5,1},{6,2},{7,3},{8,12},{9,13},{10,... | collective-permute-start | bytes 995336 | tf_op jit(solution)/shard_map/ppermute | solution.py:497
  21.5 14.8 %collective-permute-start.6 = (bf16[128,1280]{1,0:T(8,128)(2,1)S(1)}, bf16[128,1280]{1,0:T(8,128)(2,1)S(1)}, u32[]{:S(2)}, u32[]{:S(2)}) collective-permute-start(bf16[128,1280]{1,0:T(8,128)(2,1)S(1)} %join.1.refs_0_), channel_id=1, source_target_pairs={{0,8},{1,9},{2,10},{3,11},{4,12},{5,13},{6,14},{7,15},{8,0},{9,1},... | collective-permute-start | bytes 983048 | tf_op jit(solution)/shard_map/ppermute | solution.py:497
  25.3 13.5 %collective-permute-start.7 = (bf16[128,1280]{1,0:T(8,128)(2,1)S(1)}, bf16[128,1280]{1,0:T(8,128)(2,1)S(1)}, u32[]{:S(2)}, u32[]{:S(2)}) collective-permute-start(bf16[128,1280]{1,0:T(8,128)(2,1)S(1)} %collective-permute-done.5.refs_1_), channel_id=1, source_target_pairs={{0,8},{1,9},{2,10},{3,11},{4,12},{5,13},{6,14},{7,15},{8,0},{9,1},... | collective-permute-start | bytes 983048 | tf_op jit(solution)/shard_map/ppermute | solution.py:497
  33.2 19.4 %collective-permute-start.11 = (s16[2576,128]{1,0:T(8,128)(2,1)S(1)}, s16[2576,128]{1,0:T(8,128)(2,1)S(1)}, u32[]{:S(2)}, u32[]{:S(2)}) collective-permute-start(s16[2576,128]{1,0:T(8,128)(2,1)S(1)} %share.5), channel_id=1, source_target_pairs={{0,4},{1,5},{2,6},{3,7},{4,0},{5,1},{6,2},{7,3},{8,12},{9,13},{10,... | collective-permute-start | bytes 1978376 | tf_op jit(solution)/shard_map/ppermute | solution.py:497
  41.1 8.0 %collective-permute-start.12 = (s16[784,128]{1,0:T(8,128)(2,1)S(1)}, s16[784,128]{1,0:T(8,128)(2,1)S(1)}, u32[]{:S(2)}, u32[]{:S(2)}) collective-permute-start(s16[784,128]{1,0:T(8,128)(2,1)S(1)} %get-tuple-element.43), channel_id=1, source_target_pairs={{0,8},{1,9},{2,10},{3,11},{4,12},{5,13},{6,14},{7,15},{8,0},{9,1},... | collective-permute-start | bytes 602120 | tf_op jit(solution)/shard_map/ppermute | solution.py:497
  42.7 10.4 %collective-permute-start.13 = (s16[784,128]{1,0:T(8,128)(2,1)S(1)}, s16[784,128]{1,0:T(8,128)(2,1)S(1)}, u32[]{:S(2)}, u32[]{:S(2)}) collective-permute-start(s16[784,128]{1,0:T(8,128)(2,1)S(1)} %get-tuple-element.44), channel_id=1, source_target_pairs={{0,8},{1,9},{2,10},{3,11},{4,12},{5,13},{6,14},{7,15},{8,0},{9,1},... | collective-permute-start | bytes 602120 | tf_op jit(solution)/shard_map/ppermute | solution.py:497
  49.1 16.0 %slice-start = ((s8[6553600]{0:T(1024)(128)(4,1)}), s8[4194304]{0:T(1024)(128)(4,1)S(1)}, s32[]{:S(2)}) async-start(s8[6553600]{0:T(1024)(128)(4,1)} %bitcast.9), calls=%async_computation | async-start | bytes 8388608
  49.2 15.9 %slice-start.1 = ((s8[6553600]{0:T(1024)(128)(4,1)}), s8[2359296]{0:T(1024)(128)(4,1)S(1)}, s32[]{:S(2)}) async-start(s8[6553600]{0:T(1024)(128)(4,1)} %bitcast.9), calls=%async_computation.1 | async-start | bytes 4718592
  49.2 12.5 %collective-permute-start.14 = (s16[784,128]{1,0:T(8,128)(2,1)S(1)}, s16[784,128]{1,0:T(8,128)(2,1)S(1)}, u32[]{:S(2)}, u32[]{:S(2)}) collective-permute-start(s16[784,128]{1,0:T(8,128)(2,1)S(1)} %fold.2.refs_1_), channel_id=1, source_target_pairs={{0,24},{1,25},{2,26},{3,27},{4,28},{5,29},{6,30},{7,31},{8,16},{9,... | collective-permute-start | bytes 602120 | tf_op jit(solution)/shard_map/ppermute | solution.py:497
  54.7 7.0 %collective-permute-start.15 = (s16[528,128]{1,0:T(8,128)(2,1)S(1)}, s16[528,128]{1,0:T(8,128)(2,1)S(1)}, u32[]{:S(2)}, u32[]{:S(2)}) collective-permute-start(s16[528,128]{1,0:T(8,128)(2,1)S(1)} %get-tuple-element.47), channel_id=1, source_target_pairs={{0,8},{1,9},{2,10},{3,11},{4,12},{5,13},{6,14},{7,15},{8,0},{9,1},... | collective-permute-start | bytes 405512 | tf_op jit(solution)/shard_map/ppermute | solution.py:497
  54.8 11.1 %collective-permute-start.17 = (s16[528,128]{1,0:T(8,128)(2,1)S(1)}, s16[528,128]{1,0:T(8,128)(2,1)S(1)}, u32[]{:S(2)}, u32[]{:S(2)}) collective-permute-start(s16[528,128]{1,0:T(8,128)(2,1)S(1)} %get-tuple-element.48), channel_id=1, source_target_pairs={{0,8},{1,9},{2,10},{3,11},{4,12},{5,13},{6,14},{7,15},{8,0},{9,1},... | collective-permute-start | bytes 405512 | tf_op jit(solution)/shard_map/ppermute | solution.py:497
  61.8 6.9 %collective-permute-start.16 = (s16[528,128]{1,0:T(8,128)(2,1)S(1)}, s16[528,128]{1,0:T(8,128)(2,1)S(1)}, u32[]{:S(2)}, u32[]{:S(2)}) collective-permute-start(s16[528,128]{1,0:T(8,128)(2,1)S(1)} %fold.3), channel_id=1, source_target_pairs={{0,24},{1,25},{2,26},{3,27},{4,28},{5,29},{6,30},{7,31},{8,16},{9,... | collective-permute-start | bytes 405512 | tf_op jit(solution)/shard_map/ppermute | solution.py:497
  65.9 15.6 %copy-start.3 = (s32[8]{0:T(128)S(1)}, s32[8]{0:T(128)}, u32[]{:S(2)}) copy-start(s32[8]{0:T(128)} %column.1) | copy-start | bytes 100
  70.8 5.7 %collective-permute-start.18 = (s16[336,128]{1,0:T(8,128)(2,1)S(1)}, s16[336,128]{1,0:T(8,128)(2,1)S(1)}, u32[]{:S(2)}, u32[]{:S(2)}) collective-permute-start(s16[336,128]{1,0:T(8,128)(2,1)S(1)} %get-tuple-element.49), channel_id=1, source_target_pairs={{0,5},{1,4},{2,7},{3,6},{4,1},{5,0},{6,3},{7,2},{8,13},{9,12},{10,... | collective-permute-start | bytes 258056 | tf_op jit(solution)/shard_map/ppermute | solution.py:497
  73.0 5.8 %collective-permute-start.19 = (s16[336,128]{1,0:T(8,128)(2,1)S(1)}, s16[336,128]{1,0:T(8,128)(2,1)S(1)}, u32[]{:S(2)}, u32[]{:S(2)}) collective-permute-start(s16[336,128]{1,0:T(8,128)(2,1)S(1)} %get-tuple-element.50), channel_id=1, source_target_pairs={{0,7},{1,6},{2,5},{3,4},{4,3},{5,2},{6,1},{7,0},{8,15},{9,14},{10,... | collective-permute-start | bytes 258056 | tf_op jit(solution)/shard_map/ppermute | solution.py:497
  73.0 6.5 %collective-permute-start.20 = (s16[336,128]{1,0:T(8,128)(2,1)S(1)}, s16[336,128]{1,0:T(8,128)(2,1)S(1)}, u32[]{:S(2)}, u32[]{:S(2)}) collective-permute-start(s16[336,128]{1,0:T(8,128)(2,1)S(1)} %get-tuple-element.51), channel_id=1, source_target_pairs={{0,1},{1,0},{2,3},{3,2},{4,5},{5,4},{6,7},{7,6},{8,9},{9,8},{10,11... | collective-permute-start | bytes 258056 | tf_op jit(solution)/shard_map/ppermute | solution.py:497
  73.5 8.0 %collective-permute-start.21 = (s16[336,128]{1,0:T(8,128)(2,1)S(1)}, s16[336,128]{1,0:T(8,128)(2,1)S(1)}, u32[]{:S(2)}, u32[]{:S(2)}) collective-permute-start(s16[336,128]{1,0:T(8,128)(2,1)S(1)} %get-tuple-element.52), channel_id=1, source_target_pairs={{0,3},{1,2},{2,1},{3,0},{4,7},{5,6},{6,5},{7,4},{8,11},{9,10},{10,... | collective-permute-start | bytes 258056 | tf_op jit(solution)/shard_map/ppermute | solution.py:497
  75.2 6.3 %collective-permute-start.22 = (s16[336,128]{1,0:T(8,128)(2,1)S(1)}, s16[336,128]{1,0:T(8,128)(2,1)S(1)}, u32[]{:S(2)}, u32[]{:S(2)}) collective-permute-start(s16[336,128]{1,0:T(8,128)(2,1)S(1)} %get-tuple-element.53), channel_id=1, source_target_pairs={{0,4},{1,5},{2,6},{3,7},{4,0},{5,1},{6,2},{7,3},{8,12},{9,13},{10,... | collective-permute-start | bytes 258056 | tf_op jit(solution)/shard_map/ppermute | solution.py:497
  76.5 5.1 %collective-permute-start.23 = (s16[336,128]{1,0:T(8,128)(2,1)S(1)}, s16[336,128]{1,0:T(8,128)(2,1)S(1)}, u32[]{:S(2)}, u32[]{:S(2)}) collective-permute-start(s16[336,128]{1,0:T(8,128)(2,1)S(1)} %get-tuple-element.54), channel_id=1, source_target_pairs={{0,6},{1,7},{2,4},{3,5},{4,2},{5,3},{6,0},{7,1},{8,14},{9,15},{10,... | collective-permute-start | bytes 258056 | tf_op jit(solution)/shard_map/ppermute | solution.py:497
  78.8 2.7 %collective-permute-start.24 = (s16[336,128]{1,0:T(8,128)(2,1)S(1)}, s16[336,128]{1,0:T(8,128)(2,1)S(1)}, u32[]{:S(2)}, u32[]{:S(2)}) collective-permute-start(s16[336,128]{1,0:T(8,128)(2,1)S(1)} %get-tuple-element.55), channel_id=1, source_target_pairs={{0,2},{1,3},{2,0},{3,1},{4,6},{5,7},{6,4},{7,5},{8,10},{9,11},{10,... | collective-permute-start | bytes 258056 | tf_op jit(solution)/shard_map/ppermute | solution.py:497
